TPU v7x, 32 devices: a whole 2x2x4 slice. The times are simulated.
32 devices in a mesh: clip: 4 (over y, x), fsdp: 8 (over z, core).
Axes of the slice: x: 2, y: 2, z: 4, core: 2. Of those that a mesh axis runs over, the one named last changes fastest.
Arguments:
- sample: bfloat16 [4096, 5120], P('clip', 'fsdp'), may hold values from -150 to 150
- noise: bfloat16 [4096, 5120], P('clip', 'fsdp'), may hold values from -6 to 6
- gen_branch: bfloat16 [4096, 5120], P('clip', 'fsdp'), may hold values from -6 to 6
- step: int32 [4], P('clip'), may hold values from 20 to 979
- teacher_mod: float32 [4, 2, 5120], P('clip'), may hold values from -3 to 3
- fake_mod: float32 [4, 2, 5120], P('clip'), may hold values from -3 to 3
- teacher_weight: bfloat16 [5120, 5120], P('clip', 'fsdp'), may hold values from -0.078125 to 0.078125
- fake_weight: bfloat16 [5120, 5120], P('clip', 'fsdp'), may hold values from -0.078125 to 0.078125
- gen_gate: float32 [4, 5120], P('clip', 'fsdp'), may hold values from -4 to 4
Outputs:
- branch_cot: bfloat16 [4096, 5120], P('clip', 'fsdp')
- gate_grad: float32 [4, 5120], P('clip', 'fsdp')
- fake_grad: float32 [5120, 5120], P('clip', 'fsdp')
All inputs are finite; a program needn't handle non-finite values. Where the computation divides by a largest or mean magnitude, that divisor is 1e-20 or more.
Results may differ from a plain program's by a relative error of at most 0.017.
Values may be sent and summed in bfloat16 or wider, within the bound.
No kernel may reach another device: no remote copies, remote signals or barrier semaphores. Data moves between devices by JAX's collectives and lax.ppermute only.
A program may use at most 128 MiB of HBM per device.

v0:
```python
import math

import jax
import jax.numpy as jnp
from jax import lax
from jax.sharding import PartitionSpec as P

EPS = 1e-06


def per_device(
    sample, noise, gen_branch, step, teacher_mod, fake_mod, teacher_weight, fake_weight, gen_gate
):
    clip_rows = sample.shape[0]
    width = sample.shape[1] * lax.axis_size("fsdp")
    total_tokens = clip_rows * lax.axis_size("clip")
    frac = step.astype(jnp.float32)[0] / 1000.0
    sigma = 5.0 * frac / (1.0 + 4.0 * frac)
    sample32 = sample.astype(jnp.float32)
    noise32 = noise.astype(jnp.float32)
    noised = ((1.0 - sigma) * sample32 + sigma * noise32).astype(jnp.bfloat16)
    noised32 = noised.astype(jnp.float32)
    partial_sum = jnp.sum(noised32, axis=1)
    partial_power = jnp.sum(noised32 * noised32, axis=1)
    row_sum, row_total = lax.psum((partial_sum, partial_power), "fsdp")
    center = row_sum / width
    variance = jnp.maximum(row_total / width - center * center, 0.0)
    row_factor = lax.rsqrt(variance + EPS)
    local_normed = ((noised32 - center[:, None]) * row_factor[:, None]).astype(jnp.bfloat16)
    normed = lax.all_gather(local_normed, "fsdp", axis=1, tiled=True)
    normed32 = normed.astype(jnp.float32)
    teacher_in = (normed32 * (1.0 + teacher_mod[0, 1]) + teacher_mod[0, 0]).astype(jnp.bfloat16)
    fake_in = (normed32 * (1.0 + fake_mod[0, 1]) + fake_mod[0, 0]).astype(jnp.bfloat16)
    left_fake = fake_in
    teacher_velocity = jnp.dot(
        teacher_in,
        lax.all_gather(teacher_weight, "clip", axis=0, tiled=True),
        preferred_element_type=jnp.float32,
    )
    fake_velocity = jnp.dot(
        left_fake,
        lax.all_gather(fake_weight, "clip", axis=0, tiled=True),
        preferred_element_type=jnp.float32,
    )
    target = noise32 - sample32
    teacher_estimate = noised32 - sigma * teacher_velocity
    fake_estimate = noised32 - sigma * fake_velocity
    local_gap = jnp.sum(jnp.abs(sample32 - teacher_estimate))
    gap_value = lax.psum(local_gap, "fsdp") / (clip_rows * width)
    push = (fake_estimate - teacher_estimate) / (gap_value + EPS)
    branch_cot = (gen_gate * push).astype(jnp.bfloat16)
    gate_grad = jnp.sum(push * gen_branch.astype(jnp.float32), axis=0, keepdims=True) / math.sqrt(
        clip_rows
    )
    velocity_error = ((fake_velocity - target) / math.sqrt(total_tokens)).astype(jnp.bfloat16)
    left_fake = fake_in
    fake_grad = lax.psum_scatter(
        lax.dot_general(
            left_fake, velocity_error, (((0,), (0,)), ((), ())), preferred_element_type=jnp.float32
        ).astype(jnp.bfloat16),
        "clip",
        scatter_dimension=0,
        tiled=True,
    ).astype(jnp.float32)
    return (branch_cot, gate_grad, fake_grad)


def solution(mesh):
    placed = (
        P("clip", "fsdp"),
        P("clip", "fsdp"),
        P("clip", "fsdp"),
        P("clip"),
        P("clip", None, None),
        P("clip", None, None),
        P("clip", "fsdp"),
        P("clip", "fsdp"),
        P("clip", "fsdp"),
    )
    return jax.shard_map(
        per_device,
        mesh=mesh,
        in_specs=placed,
        out_specs=(P("clip", "fsdp"), P("clip", "fsdp"), P("clip", "fsdp")),
        check_vma=False,
    )
```

profile of v0, /device:TPU:0, one launch (start us, length us, event | category | flops | bytes accessed | tf_op | source)
XLA Modules:
  0.0 367.8 jit_solution(4829083452065140367)
XLA Ops:
  7.2 0.0 all-gather.8.cloned.1.call-start
  7.2 0.7 all-gather.8.cloned.1.call-update
  7.9 0.0 all-gather.4.cloned.1.call-start
  8.6 2.5 convert_reduce_fusion
  11.2 18.3 %all-reduce = (f32[1024]{0:T(1024)S(1)}, f32[1024]{0:T(1024)S(1)}) all-reduce(f32[1024]{0:T(1024)S(1)} %get-tuple-element.4, f32[1024]{0:T(1024)S(1)} %get-tuple-element.3), channel_id=1, replica_groups=mesh['clip'=4,'fsdp'=8] {'fsdp'}, use_global_device_ids=true, to_apply=%region_3.0 | all-reduce | flops 2048 | bytes 16384 | tf_op jit(solution)/shard_map/psum | solution.py:25
  29.5 0.0 copy-start.3
  29.6 0.0 copy-start.4
  29.6 0.0 copy-start.1
  29.6 1.5 fusion.19
  31.1 0.0 all-gather.4.cloned.1.call-update
  31.1 0.0 all-gather.6.cloned.1.call-start
  31.1 0.7 all-gather.6.cloned.1.call-update
  31.8 0.0 reduce-scatter.2.cloned.1.call-start
  31.9 0.0 copy-done.3
  31.9 0.0 copy-done.4
  32.0 52.9 %all-gather.8.cloned.1.call-done = bf16[5120,640]{1,0:T(8,128)(2,1)} async-done(((bf16[1280,640]{1,0:T(8,128)(2,1)}), bf16[5120,640]{1,0:T(8,128)(2,1)}) %all-gather.8.cloned.1.call-update) | async-done | bytes 6553616 | tf_op jit(solution)/shard_map/all_gather | solution.py:37
  84.9 101.6 %all-gather.4.cloned.1.call-done = bf16[1024,5120]{1,0:T(8,128)(2,1)} async-done(((bf16[1024,640]{1,0:T(8,128)(2,1)}), bf16[1024,5120]{1,0:T(8,128)(2,1)}) %all-gather.4.cloned.1.call-update) | async-done | bytes 10485776 | tf_op jit(solution)/shard_map/all_gather | solution.py:30
  186.5 0.0 copy-done.1
  186.5 14.7 %fusion.14 = (f32[]{:T(128)}, f32[1024,640]{1,0:T(8,128)}) fusion(bf16[1024,640]{1,0:T(8,128)(2,1)S(1)} %copy-done.1, bf16[1024,640]{1,0:T(8,128)(2,1)S(1)} %get-tuple-element.9, f32[]{:T(128)} %bitcast, bf16[5120,640]{1,0:T(8,128)(2,1)} %all-gather.8.cloned.1.call-done, bf16[1024,5120]{1,0:T(8,128)(2,1)} %all-gather.4.cloned.1.call-done, ...), kind=kOutput, calls=%fused_computation.23 | convolution fusion | flops 6736445440 | bytes 22323208 | tf_op jit(solution)/shard_map/dot_general | solution.py:35
  201.2 14.5 %psum.23 = f32[]{:T(128)} all-reduce(f32[]{:T(128)} %get-tuple-element.16), channel_id=1, replica_groups=mesh['clip'=4,'fsdp'=8] {'fsdp'}, use_global_device_ids=true, to_apply=%region_5.0 | all-reduce | flops 1 | bytes 8 | tf_op jit(solution)/shard_map/psum | solution.py:49
  216.3 42.8 %all-gather.6.cloned.1.call-done = bf16[5120,640]{1,0:T(8,128)(2,1)} async-done(((bf16[1280,640]{1,0:T(8,128)(2,1)}), bf16[5120,640]{1,0:T(8,128)(2,1)}) %all-gather.6.cloned.1.call-update) | async-done | bytes 6553616 | tf_op jit(solution)/shard_map/all_gather | solution.py:42
  259.1 0.0 copy-start.2
  259.1 0.0 copy-start.6
  259.1 15.1 %multiply_reduce_fusion = (f32[640]{0:T(1024)S(1)}, f32[1024,640]{1,0:T(8,128)}, f32[1024,640]{1,0:T(8,128)S(1)}) fusion(bf16[1024,640]{1,0:T(8,128)(2,1)} %param.11, f32[]{:T(128)S(6)} %add.78, f32[1024,640]{1,0:T(8,128)} %get-tuple-element.17, f32[]{:T(128)} %bitcast, bf16[1024,640]{1,0:T(8,128)(2,1)S(1)} %get-tuple-element.9, ...), kind=kOutput, calls=%fused_computation.32 | convolution fusion | flops 6738411008 | bytes 27568648 | tf_op jit(solution)/shard_map/dot_general | solution.py:40
  274.3 0.0 copy-done.2
  274.3 0.0 copy-done.6
  274.3 11.1 %convolution_convert_fusion = bf16[5120,640]{1,0:T(8,128)(2,1)} fusion(bf16[1024,5120]{1,0:T(8,128)(2,1)S(1)} %copy-done.6, f32[5120]{0:T(1024)S(1)} %bitcast.10, f32[5120]{0:T(1024)S(1)} %bitcast.8, f32[1024,640]{1,0:T(8,128)S(1)} %get-tuple-element.18, bf16[1024,640]{1,0:T(8,128)(2,1)S(1)} %copy-done.1, bf16[1024,640]{1,0:T(8,128)(2,1)S(1)} %copy-done.2), kind=kOutput, calls=%fused_computation.9 | convolution fusion | flops 6739066880 | bytes 22323200 | tf_op jit(solution)/shard_map/dot_general | solution.py:58
  285.4 0.0 copy-start.5
  285.4 0.0 copy-start
  285.4 0.0 reduce-scatter.2.cloned.1.call-update
  285.4 0.7 copy-done.5
  286.1 0.6 div.45
  286.7 0.5 copy-done
  287.2 1.2 multiply_convert_fusion
  288.4 69.6 %reduce-scatter.2.cloned.1.call-done = bf16[1280,640]{1,0:T(8,128)(2,1)} async-done(((bf16[5120,640]{1,0:T(8,128)(2,1)}), bf16[1280,640]{1,0:T(8,128)(2,1)}) %reduce-scatter.2.cloned.1.call-update) | async-done | bytes 1638416 | tf_op jit(solution)/shard_map/reduce_scatter | solution.py:57
  358.0 3.3 convert_element_type.55
  (5 shorter events, 0.1 us)
Async XLA Ops:
  7.2 77.8 %all-gather.8.cloned.1.call-start = ((), (), s32[]{:S(2)}) async-start(), calls=%async_computation.3 | async-start | bytes 8192000 | tf_op jit(solution)/shard_map/all_gather | solution.py:37
  7.9 178.6 %all-gather.4.cloned.1.call-start = ((), (), s32[]{:S(2)}) async-start(), calls=%async_computation.1 | async-start | bytes 11796480 | tf_op jit(solution)/shard_map/all_gather | solution.py:30
  29.5 2.3 copy-start.3
  29.6 2.4 copy-start.4
  29.6 156.9 %copy-start.1 = (bf16[1024,640]{1,0:T(8,128)(2,1)S(1)}, bf16[1024,640]{1,0:T(8,128)(2,1)}, u32[]{:S(2)}) copy-start(bf16[1024,640]{1,0:T(8,128)(2,1)} %param.9) | copy-start | bytes 3932164
  31.1 228.0 %all-gather.6.cloned.1.call-start = ((), (), s32[]{:S(2)}) async-start(), calls=%async_computation.2 | async-start | bytes 8192000 | tf_op jit(solution)/shard_map/all_gather | solution.py:42
  31.8 326.1 %reduce-scatter.2.cloned.1.call-start = ((), (), s32[]{:S(2)}) async-start(), calls=%async_computation.4 | async-start | bytes 8192000 | tf_op jit(solution)/shard_map/reduce_scatter | solution.py:57
  259.1 15.2 %copy-start.2 = (bf16[1024,640]{1,0:T(8,128)(2,1)S(1)}, bf16[1024,640]{1,0:T(8,128)(2,1)}, u32[]{:S(2)}) copy-start(bf16[1024,640]{1,0:T(8,128)(2,1)} %param.10) | copy-start | bytes 3932164
  259.1 15.2 %copy-start.6 = (bf16[1024,5120]{1,0:T(8,128)(2,1)S(1)}, bf16[1024,5120]{1,0:T(8,128)(2,1)}, u32[]{:S(2)}) copy-start(bf16[1024,5120]{1,0:T(8,128)(2,1)} %all-gather.4.cloned.1.call-done) | copy-start | bytes 31457284
  285.4 0.7 copy-start.5
  285.4 1.8 copy-start
Sparse Core Ops, SparseCore 0:
  9.8 75.0 all-gather.7
  87.1 99.3 all-gather.3
  188.3 70.7 all-gather.5
  285.5 72.3 reduce-scatter.1
where the time goes:
time: 368 us
  waiting for transfers between devices  268 us (73%)
  matrix products  40.9 us (11%)
  blocking collectives  32.8 us (9%)
  between operations  15.2 us (4%)
  other arithmetic  8.73 us (2%)
    all_gather x1, waiting for transfers between devices, per_device(): normed = lax.all_gather(local_normed, 'fsdp', axis=1, tiled=True)  102 us
    reduce_scatter x1, waiting for transfers between devices, per_device(): lax.psum_scatter(lax.dot_general(left_fake, velocity_error, (((0,), (0,))...  69.6 us
    all_gather x1, waiting for transfers between devices, per_device(): lax.all_gather(teacher_weight, 'clip', axis=0, tiled=True)  52.9 us
    all_gather x1, waiting for transfers between devices, per_device(): lax.all_gather(fake_weight, 'clip', axis=0, tiled=True)  42.8 us
    psum x1, blocking collectives, per_device(): row_sum, row_total = lax.psum((partial_sum, partial_power), 'fsdp')  18.3 us
    dot_general x1, matrix products, per_device(): jnp.dot(left_fake, lax.all_gather(fake_weight, 'clip', axis=0, tiled=True...  15.1 us
    dot_general x1, matrix products, per_device(): jnp.dot(teacher_in, lax.all_gather(teacher_weight, 'clip', axis=0, tiled=...  14.7 us
    psum x1, blocking collectives, per_device(): gap_value = lax.psum(local_gap, 'fsdp') / (clip_rows * width)  14.5 us
  transfers between devices with their start and end apart: 4, of which 4 were waited for; matrix products, arithmetic and copies ran while one was open for 6% of the time, Pallas kernels for 0%

commit v1 on v0

v1 whole, which is shorter than its diff:
```python
import math

import jax
import jax.numpy as jnp
from jax import lax
from jax.sharding import PartitionSpec as P

EPS = 1e-06
BF16 = jnp.bfloat16
F32 = jnp.float32


def swap_clip(value, bit, count):
    return lax.ppermute(value, "clip", [(i, i ^ bit) for i in range(count)])


def swap_core(value, count):
    return lax.ppermute(value, "fsdp", [(i, i ^ 1) for i in range(count)])


def ring_next(count):
    order = list(range(0, count, 2)) + list(range(count - 1, 0, -2))
    if count % 2:
        order = list(range(0, count, 2)) + list(range(count - 2, 0, -2))
    return {order[i]: order[(i + 1) % count] for i in range(count)}


def gather_halves(weight, count):
    bits = [1 << i for i in range(count.bit_length() - 1)]
    rows = weight.shape[0] // 2
    pieces = {}
    for half, order in ((0, bits), (1, bits[::-1])):
        held = {0: weight[half * rows : (half + 1) * rows]}
        for bit in order:
            held.update({mask ^ bit: swap_clip(block, bit, count) for mask, block in held.items()})
        for mask, block in held.items():
            pieces[mask, half] = block
    return pieces


def assemble(pieces, clip, rows):
    full = jnp.zeros((rows * len(pieces), next(iter(pieces.values())).shape[1]), BF16)
    for (mask, half), block in pieces.items():
        full = lax.dynamic_update_slice(full, block, (((clip ^ mask) * 2 + half) * rows, 0))
    return full


def per_device(
    sample, noise, gen_branch, step, teacher_mod, fake_mod, teacher_weight, fake_weight, gen_gate
):
    clips = lax.axis_size("clip")
    shards = lax.axis_size("fsdp")
    clip = lax.axis_index("clip")
    shard = lax.axis_index("fsdp")
    clip_rows, cols = sample.shape
    width = cols * shards
    total_tokens = clip_rows * clips
    half_rows = fake_weight.shape[0] // 2

    frac = step.astype(F32)[0] / 1000.0
    sigma = 5.0 * frac / (1.0 + 4.0 * frac)
    sample32 = sample.astype(F32)
    noise32 = noise.astype(F32)
    noised = ((1.0 - sigma) * sample32 + sigma * noise32).astype(BF16)
    noised32 = noised.astype(F32)

    fake_pieces = gather_halves(fake_weight, clips)
    teacher_pieces = gather_halves(teacher_weight, clips)

    after = ring_next(shards // 2)
    ring = [(2 * a + core, 2 * b + core) for a, b in after.items() for core in range(2)]
    before = jnp.array([a for a, _ in sorted(after.items(), key=lambda pair: pair[1])], jnp.int32)
    place = shard // 2
    parts = 2
    part_rows = clip_rows // parts
    blocks = []
    travel = [noised[i * part_rows : (i + 1) * part_rows] for i in range(parts)]
    for hop in range(shards // 2):
        if hop:
            travel = [lax.ppermute(piece, "fsdp", ring) for piece in travel]
            place = before[place]
        for i, piece in enumerate(travel):
            blocks.append((i, 2 * place + shard % 2, piece))
            blocks.append((i, 2 * place + 1 - shard % 2, swap_core(piece, shards)))

    partial = jnp.stack([jnp.sum(noised32, axis=1), jnp.sum(noised32 * noised32, axis=1)])
    row_sum, row_total = lax.psum(partial, "fsdp")
    center = row_sum / width
    variance = jnp.maximum(row_total / width - center * center, 0.0)
    row_factor = lax.rsqrt(variance + EPS)

    fake_in = jnp.zeros((clip_rows, width), BF16)
    teacher_in = jnp.zeros((clip_rows, width), BF16)
    for i, source, piece in blocks:
        part = slice(i * part_rows, (i + 1) * part_rows)
        spread = piece.astype(F32) - center[part, None]
        normed32 = (spread * row_factor[part, None]).astype(BF16).astype(F32)
        spot = (i * part_rows, source * cols)
        fake_cut = lax.dynamic_slice(fake_mod[0], (0, source * cols), (2, cols))
        teacher_cut = lax.dynamic_slice(teacher_mod[0], (0, source * cols), (2, cols))
        fake_in = lax.dynamic_update_slice(
            fake_in, (normed32 * (1.0 + fake_cut[1]) + fake_cut[0]).astype(BF16), spot
        )
        teacher_in = lax.dynamic_update_slice(
            teacher_in, (normed32 * (1.0 + teacher_cut[1]) + teacher_cut[0]).astype(BF16), spot
        )

    target = noise32 - sample32
    fake_velocity = jnp.dot(
        fake_in, assemble(fake_pieces, clip, half_rows), preferred_element_type=F32
    )
    velocity_error = ((fake_velocity - target) / math.sqrt(total_tokens)).astype(BF16)

    bits = [1 << i for i in range(clips.bit_length() - 1)]

    def term(mask, half):
        left = lax.dynamic_slice(
            fake_in, (0, ((clip ^ mask) * 2 + half) * half_rows), (clip_rows, half_rows)
        )
        return lax.dot_general(
            left, velocity_error, (((0,), (0,)), ((), ())), preferred_element_type=F32
        )

    sums = []
    for half, order in ((0, bits), (1, bits[::-1])):
        held = {mask: term(mask, half) for mask in range(clips)}
        for bit in order:
            sent = {mask: held.pop(mask) for mask in list(held) if mask & bit}
            for mask, block in sent.items():
                held[mask ^ bit] = held[mask ^ bit] + swap_clip(
                    block.astype(BF16), bit, clips
                ).astype(F32)
        sums.append(held[0])
    fake_grad = jnp.concatenate(sums, axis=0)

    teacher_velocity = jnp.dot(
        teacher_in, assemble(teacher_pieces, clip, half_rows), preferred_element_type=F32
    )
    teacher_estimate = noised32 - sigma * teacher_velocity
    fake_estimate = noised32 - sigma * fake_velocity
    local_gap = jnp.sum(jnp.abs(sample32 - teacher_estimate))
    gap_value = lax.psum(local_gap, "fsdp") / (clip_rows * width)
    push = (fake_estimate - teacher_estimate) / (gap_value + EPS)
    branch_cot = (gen_gate * push).astype(BF16)
    gate_grad = jnp.sum(push * gen_branch.astype(F32), axis=0, keepdims=True) / math.sqrt(clip_rows)
    return (branch_cot, gate_grad, fake_grad)


def solution(mesh):
    placed = (
        P("clip", "fsdp"),
        P("clip", "fsdp"),
        P("clip", "fsdp"),
        P("clip"),
        P("clip", None, None),
        P("clip", None, None),
        P("clip", "fsdp"),
        P("clip", "fsdp"),
        P("clip", "fsdp"),
    )
    return jax.shard_map(
        per_device,
        mesh=mesh,
        in_specs=placed,
        out_specs=(P("clip", "fsdp"), P("clip", "fsdp"), P("clip", "fsdp")),
        check_vma=False,
    )
```

time: 368 us -> 329 us (0.89)
  waiting for transfers between devices: 268 us -> 141 us
  local copies, waits for them, and re-layouts: 1.73 us -> 36.3 us
  other arithmetic: 8.73 us -> 36 us
  starting transfers between devices: 0.16 us -> 23 us
  matrix products: 40.9 us -> 49.5 us
  between operations: 15.2 us -> 8.26 us
    all_gather x3 -> x0, waiting for transfers between devices: 197 us -> none  [the longest x1 102 us: per_device(): normed = lax.all_gather(local_normed, 'fsdp', axis=1, tiled=True)]
    ppermute x0 -> x32, waiting for transfers between devices: none -> 141 us  [the longest x18 126 us: swap_clip(): return lax.ppermute(value, 'clip', [(i, i ^ bit) for i in range(count)])]
    reduce_scatter x1 -> x0, waiting for transfers between devices: 69.6 us -> none  [per_device(): lax.psum_scatter(lax.dot_general(left_fake, velocity_error, (((0,), (0,))...]
    dynamic_update_slice x0 -> x17, other arithmetic: none -> 29.9 us  [the longest x16 28.7 us: per_device(): lax.dynamic_update_slice(fake_in, (normed32 * (1.0 + fake_cut[1]) + fake_...]
    ppermute x0 -> x32, starting transfers between devices: none -> 23 us  [the longest x18 21.8 us: swap_clip(): return lax.ppermute(value, 'clip', [(i, i ^ bit) for i in range(count)])]
    dynamic_update_slice x0 -> x14, local copies, waits for them, and re-layouts: none -> 14.1 us  [assemble(): lax.dynamic_update_slice(full, block, (((clip ^ mask) * 2 + half) * rows,...]
    another operation x0 -> x4, local copies, waits for them, and re-layouts: none -> 11.5 us
    dot_general x3 -> x10, matrix products: 40.9 us -> 49.5 us  [the longest x8 20.5 us: term(): lax.dot_general(left, velocity_error, (((0,), (0,)), ((), ())), preferred...]
  transfers between devices with their start and end apart: 4 -> 32, of which waited for: 4 -> 12; matrix products, arithmetic and copies ran while one was open for 6% -> 20% of each run, Pallas kernels for 0% -> 0%
where the time goes in v1:
time: 329 us; the launch traced here: 328 us
  waiting for transfers between devices  141 us (43%)
  matrix products  49.5 us (15%)
  local copies, waits for them, and re-layouts  36.3 us (11%)
  other arithmetic  36 us (11%)
  blocking collectives  33.5 us (10%)
  starting transfers between devices  23 us (7%)
  between operations  8.26 us (3%)
    ppermute x18, waiting for transfers between devices, swap_clip(): return lax.ppermute(value, 'clip', [(i, i ^ bit) for i in range(count)])  126 us
    dynamic_update_slice x16, other arithmetic, per_device(): lax.dynamic_update_slice(fake_in, (normed32 * (1.0 + fake_cut[1]) + fake_...  28.7 us
    ppermute x18, starting transfers between devices, swap_clip(): return lax.ppermute(value, 'clip', [(i, i ^ bit) for i in range(count)])  21.8 us
    dot_general x8, matrix products, term(): lax.dot_general(left, velocity_error, (((0,), (0,)), ((), ())), preferred...  20.5 us
    psum x1, blocking collectives, per_device(): row_sum, row_total = lax.psum(partial, 'fsdp')  18.3 us
    dot_general x1, matrix products, per_device(): jnp.dot(fake_in, assemble(fake_pieces, clip, half_rows), preferred_elemen...  16.2 us
    psum x1, blocking collectives, per_device(): gap_value = lax.psum(local_gap, 'fsdp') / (clip_rows * width)  15.2 us
    ppermute x6, waiting for transfers between devices, per_device(): travel = [lax.ppermute(piece, 'fsdp', ring) for piece in travel]  15 us
  transfers between devices with their start and end apart: 32, of which 12 were waited for; matrix products, arithmetic and copies ran while one was open for 20% of the time, Pallas kernels for 0%

profile of v1, /device:TPU:0, one launch (start us, length us, event | category | flops | bytes accessed | tf_op | source)
XLA Modules:
  0.0 328.0 jit_solution(774606575413023668)
XLA Ops:
  11.0 2.6 convert_reduce_fusion
  13.6 18.3 %psum.14 = f32[2,1024]{1,0:T(2,128)S(1)} all-reduce(f32[2,1024]{1,0:T(2,128)S(1)} %pad_maximum_fusion.1), channel_id=1, replica_groups=mesh['clip'=4,'fsdp'=8] {'fsdp'}, use_global_device_ids=true, to_apply=%region_2.3 | all-reduce | flops 2048 | bytes 16384 | tf_op jit(solution)/shard_map/psum | solution.py:87
  32.2 5.3 %broadcast.118.clone = bf16[1024,5120]{1,0:T(8,128)(2,1)} broadcast(bf16[]{:T(256)} %constant.116.clone.1), dimensions={} | broadcast | bytes 10485762 | tf_op jit(solution)/shard_map/broadcast.6
  46.6 2.7 copy-done.2
  50.1 5.1 %broadcast.118.clone.1 = bf16[1024,5120]{1,0:T(8,128)(2,1)} broadcast(bf16[]{:T(256)} %constant.116.clone.1), dimensions={} | broadcast | bytes 10485762 | tf_op jit(solution)/shard_map/broadcast.6
  58.0 2.7 fusion.119
  60.7 1.8 fusion.117
  63.1 2.2 constant_dynamic-update-slice_fusion.6
  65.3 14.9 %collective-permute-done.14 = bf16[640,640]{1,0:T(8,128)(2,1)} collective-permute-done((bf16[640,640]{1,0:T(8,128)(2,1)}, bf16[640,640]{1,0:T(8,128)(2,1)}, u32[]{:S(2)}, u32[]{:S(2)}) %collective-permute-start.14) | collective-permute-done | bytes 819232 | tf_op jit(solution)/shard_map/ppermute | solution.py:14
  81.7 2.1 constant_dynamic-update-slice_fusion.14
  84.4 2.1 constant_dynamic-update-slice_fusion.5
  86.6 2.1 constant_dynamic-update-slice_fusion.13
  90.2 2.8 fusion.115
  93.0 2.7 fusion.113
  96.2 1.6 fusion.111
  97.8 4.7 %collective-permute-done.4 = bf16[512,640]{1,0:T(8,128)(2,1)S(1)} collective-permute-done((bf16[512,640]{1,0:T(8,128)(2,1)}, bf16[512,640]{1,0:T(8,128)(2,1)S(1)}, u32[]{:S(2)}, u32[]{:S(2)}) %collective-permute-start.4) | collective-permute-done | bytes 655392 | tf_op jit(solution)/shard_map/ppermute | solution.py:80
  104.0 1.5 fusion.109
  105.5 30.9 %collective-permute-done.22 = bf16[640,640]{1,0:T(8,128)(2,1)S(1)} collective-permute-done((bf16[640,640]{1,0:T(8,128)(2,1)}, bf16[640,640]{1,0:T(8,128)(2,1)S(1)}, u32[]{:S(2)}, u32[]{:S(2)}) %collective-permute-start.22) | collective-permute-done | bytes 819232 | tf_op jit(solution)/shard_map/ppermute | solution.py:14
  139.0 13.7 %collective-permute-done.16 = bf16[640,640]{1,0:T(8,128)(2,1)S(1)} collective-permute-done((bf16[640,640]{1,0:T(8,128)(2,1)}, bf16[640,640]{1,0:T(8,128)(2,1)S(1)}, u32[]{:S(2)}, u32[]{:S(2)}) %collective-permute-start.16) | collective-permute-done | bytes 819232 | tf_op jit(solution)/shard_map/ppermute | solution.py:14
  160.3 14.9 %collective-permute-done.25 = bf16[640,640]{1,0:T(8,128)(2,1)S(1)} collective-permute-done((bf16[640,640]{1,0:T(8,128)(2,1)S(1)}, bf16[640,640]{1,0:T(8,128)(2,1)S(1)}, u32[]{:S(2)}, u32[]{:S(2)}) %collective-permute-start.25) | collective-permute-done | bytes 819232 | tf_op jit(solution)/shard_map/ppermute | solution.py:14
  175.3 14.0 %collective-permute-done.19 = bf16[640,640]{1,0:T(8,128)(2,1)S(1)} collective-permute-done((bf16[640,640]{1,0:T(8,128)(2,1)S(1)}, bf16[640,640]{1,0:T(8,128)(2,1)S(1)}, u32[]{:S(2)}, u32[]{:S(2)}) %collective-permute-start.19) | collective-permute-done | bytes 819232 | tf_op jit(solution)/shard_map/ppermute | solution.py:14
  190.8 1.6 fusion.107
  192.4 1.6 fusion.105
  193.9 1.5 fusion.103
  195.5 1.6 fusion.101
  197.1 10.4 %collective-permute-done.12 = bf16[512,640]{1,0:T(8,128)(2,1)S(1)} collective-permute-done((bf16[512,640]{1,0:T(8,128)(2,1)S(1)}, bf16[512,640]{1,0:T(8,128)(2,1)S(1)}, u32[]{:S(2)}, u32[]{:S(2)}) %collective-permute-start.12) | collective-permute-done | bytes 655392 | tf_op jit(solution)/shard_map/ppermute | solution.py:80
  207.4 1.6 fusion.99
  209.0 1.5 fusion.97
  210.6 1.6 fusion.95
  212.1 1.6 fusion.93
  213.8 1.6 fusion.91
  215.4 12.8 %fusion.3 = (f32[]{:T(128)}, f32[1024,640]{1,0:T(8,128)}) fusion(bf16[1024,640]{1,0:T(8,128)(2,1)S(1)} %copy-done.6, bf16[1024,640]{1,0:T(8,128)(2,1)S(1)} %get-tuple-element.39, f32[]{:T(128)} %bitcast, bf16[1024,5120]{1,0:T(8,128)(2,1)} %get-tuple-element.53, bf16[5120,640]{1,0:T(8,128)(2,1)S(1)} %constant_dynamic-update-slice_fusion), kind=kOutput, calls=%fused_computation.12 | convolution fusion | flops 6715473920 | bytes 22282248 | tf_op jit(solution)/shard_map/dot_general | solution.py:136
  228.2 15.2 %psum.15 = f32[]{:T(128)} all-reduce(f32[]{:T(128)} %get-tuple-element.86), channel_id=1, replica_groups=mesh['clip'=4,'fsdp'=8] {'fsdp'}, use_global_device_ids=true, to_apply=%region_4.5 | all-reduce | flops 1 | bytes 8 | tf_op jit(solution)/shard_map/psum | solution.py:142
  244.0 16.2 %multiply_reduce_fusion = (f32[640]{0:T(1024)S(1)}, f32[1024,640]{1,0:T(8,128)S(1)}, bf16[1024,640]{1,0:T(8,128)(2,1)S(1)}) fusion(bf16[1024,640]{1,0:T(8,128)(2,1)} %param.12, f32[]{:T(128)S(6)} %add.803, f32[1024,640]{1,0:T(8,128)} %get-tuple-element.87, f32[]{:T(128)} %bitcast, bf16[1024,640]{1,0:T(8,128)(2,1)S(1)} %get-tuple-element.39, ...), kind=kOutput, calls=%fused_computation.19 | convolution fusion | flops 6721371648 | bytes 28838408 | tf_op jit(solution)/shard_map/dot_general | solution.py:109
  260.3 2.6 convolution_convert_fusion.2
  264.4 2.6 convolution_convert_fusion
  266.9 1.6 collective-permute-start.30
  268.5 2.6 convolution_convert_fusion.3
  271.7 2.6 convolution_convert_fusion.1
  274.8 9.2 %collective-permute-done.27 = bf16[640,640]{1,0:T(8,128)(2,1)S(1)} collective-permute-done((bf16[640,640]{1,0:T(8,128)(2,1)S(1)}, bf16[640,640]{1,0:T(8,128)(2,1)S(1)}, u32[]{:S(2)}, u32[]{:S(2)}) %collective-permute-start.27) | collective-permute-done | bytes 819232 | tf_op jit(solution)/shard_map/ppermute | solution.py:14
  284.1 2.5 add_convert_fusion.1
  286.6 1.6 collective-permute-start.28
  288.2 2.5 add_convert_fusion
  294.2 7.5 %collective-permute-done.26 = bf16[640,640]{1,0:T(8,128)(2,1)S(1)} collective-permute-done((bf16[640,640]{1,0:T(8,128)(2,1)S(1)}, bf16[640,640]{1,0:T(8,128)(2,1)S(1)}, u32[]{:S(2)}, u32[]{:S(2)}) %collective-permute-start.26) | collective-permute-done | bytes 819232 | tf_op jit(solution)/shard_map/ppermute | solution.py:14
  301.6 19.2 %collective-permute-done.28 = bf16[640,640]{1,0:T(8,128)(2,1)S(1)} collective-permute-done((bf16[640,640]{1,0:T(8,128)(2,1)S(1)}, bf16[640,640]{1,0:T(8,128)(2,1)S(1)}, u32[]{:S(2)}, u32[]{:S(2)}) %collective-permute-start.28) | collective-permute-done | bytes 819232 | tf_op jit(solution)/shard_map/ppermute | solution.py:14
  320.9 2.6 convert_add_fusion.1
  323.5 2.6 convert_add_fusion
  326.0 1.9 pad_maximum_fusion
  (103 shorter events, 40.7 us)
Async XLA Ops:
  11.0 21.0 %copy-start.9 = (f32[1,2,5120]{2,1,0:T(2,128)S(1)}, f32[1,2,5120]{2,1,0:T(2,128)}, u32[]{:S(2)}) copy-start(f32[1,2,5120]{2,1,0:T(2,128)} %param.15) | copy-start | bytes 122884
  38.9 17.6 %collective-permute-start = (bf16[512,640]{1,0:T(8,128)(2,1)}, bf16[512,640]{1,0:T(8,128)(2,1)}, u32[]{:S(2)}, u32[]{:S(2)}) collective-permute-start(bf16[512,640]{1,0:T(8,128)(2,1)} %get-tuple-element.51), channel_id=1, source_target_pairs={{0,1},{1,0},{2,3},{3,2},{4,5},{5,4},{6,7},{7,6},{8,9},{9,8},{10,11... | collective-permute-start | bytes 1966088 | tf_op jit(solution)/shard_map/ppermute | solution.py:18
  38.9 47.6 %collective-permute-start.2 = (bf16[512,640]{1,0:T(8,128)(2,1)}, bf16[512,640]{1,0:T(8,128)(2,1)}, u32[]{:S(2)}, u32[]{:S(2)}) collective-permute-start(bf16[512,640]{1,0:T(8,128)(2,1)} %get-tuple-element.51), channel_id=1, source_target_pairs={{0,4},{1,5},{4,6},{5,7},{6,2},{7,3},{2,0},{3,1},{8,12},{9,13},{12,... | collective-permute-start | bytes 1966088 | tf_op jit(solution)/shard_map/ppermute | solution.py:80
  38.9 1.4 copy-start.3
  41.7 3.5 %copy-start = (bf16[5120,640]{1,0:T(8,128)(2,1)}, bf16[5120,640]{1,0:T(8,128)(2,1)S(1)}, u32[]{:S(2)}) copy-start(bf16[5120,640]{1,0:T(8,128)(2,1)S(1)} %get-tuple-element.45) | copy-start | bytes 19660804
  41.7 3.5 %copy-start.4 = (bf16[1280,640]{1,0:T(8,128)(2,1)S(1)}, bf16[1280,640]{1,0:T(8,128)(2,1)}, u32[]{:S(2)}) copy-start(bf16[1280,640]{1,0:T(8,128)(2,1)} %param.17) | copy-start | bytes 4915204
  41.7 21.4 %collective-permute-start.20 = (bf16[640,640]{1,0:T(8,128)(2,1)}, bf16[640,640]{1,0:T(8,128)(2,1)}, u32[]{:S(2)}, u32[]{:S(2)}) collective-permute-start(bf16[640,640]{1,0:T(8,128)(2,1)} %get-tuple-element.46), channel_id=1, source_target_pairs={{0,8},{8,0},{16,24},{24,16},{1,9},{9,1},{17,25},{25,17},{2,10},{10... | collective-permute-start | bytes 2457608 | tf_op jit(solution)/shard_map/ppermute | solution.py:14
  43.2 40.7 %collective-permute-start.21 = (bf16[640,640]{1,0:T(8,128)(2,1)}, bf16[640,640]{1,0:T(8,128)(2,1)}, u32[]{:S(2)}, u32[]{:S(2)}) collective-permute-start(bf16[640,640]{1,0:T(8,128)(2,1)} %get-tuple-element.46), channel_id=1, source_target_pairs={{0,16},{8,24},{16,0},{24,8},{1,17},{9,25},{17,1},{25,9},{2,18},{10... | collective-permute-start | bytes 2457608 | tf_op jit(solution)/shard_map/ppermute | solution.py:14
  45.2 4.8 %copy-start.10 = (f32[1,2,5120]{2,1,0:T(2,128)S(1)}, f32[1,2,5120]{2,1,0:T(2,128)}, u32[]{:S(2)}) copy-start(f32[1,2,5120]{2,1,0:T(2,128)} %param.14) | copy-start | bytes 122884
  46.6 2.7 copy-start.2
  49.3 30.9 %collective-permute-start.14 = (bf16[640,640]{1,0:T(8,128)(2,1)}, bf16[640,640]{1,0:T(8,128)(2,1)}, u32[]{:S(2)}, u32[]{:S(2)}) collective-permute-start(bf16[640,640]{1,0:T(8,128)(2,1)} %get-tuple-element.43), channel_id=1, source_target_pairs={{0,8},{8,0},{16,24},{24,16},{1,9},{9,1},{17,25},{25,17},{2,10},{10... | collective-permute-start | bytes 2457608 | tf_op jit(solution)/shard_map/ppermute | solution.py:14
  56.5 30.0 %collective-permute-start.15 = (bf16[640,640]{1,0:T(8,128)(2,1)}, bf16[640,640]{1,0:T(8,128)(2,1)}, u32[]{:S(2)}, u32[]{:S(2)}) collective-permute-start(bf16[640,640]{1,0:T(8,128)(2,1)} %get-tuple-element.43), channel_id=1, source_target_pairs={{0,16},{8,24},{16,0},{24,8},{1,17},{9,25},{17,1},{25,9},{2,18},{10... | collective-permute-start | bytes 2457608 | tf_op jit(solution)/shard_map/ppermute | solution.py:14
  60.7 2.4 copy-start.11
  63.0 25.7 %collective-permute-start.1 = (bf16[512,640]{1,0:T(8,128)(2,1)}, bf16[512,640]{1,0:T(8,128)(2,1)}, u32[]{:S(2)}, u32[]{:S(2)}) collective-permute-start(bf16[512,640]{1,0:T(8,128)(2,1)} %get-tuple-element.49), channel_id=1, source_target_pairs={{0,1},{1,0},{2,3},{3,2},{4,5},{5,4},{6,7},{7,6},{8,9},{9,8},{10,11... | collective-permute-start | bytes 1966088 | tf_op jit(solution)/shard_map/ppermute | solution.py:18
  63.0 17.2 %copy-start.7 = (bf16[640,640]{1,0:T(8,128)(2,1)S(1)}, bf16[640,640]{1,0:T(8,128)(2,1)}, u32[]{:S(2)}) copy-start(bf16[640,640]{1,0:T(8,128)(2,1)} %get-tuple-element.44) | copy-start | bytes 2457604
  63.1 20.8 %copy-start.8 = (bf16[640,640]{1,0:T(8,128)(2,1)S(1)}, bf16[640,640]{1,0:T(8,128)(2,1)}, u32[]{:S(2)}) copy-start(bf16[640,640]{1,0:T(8,128)(2,1)} %get-tuple-element.41) | copy-start | bytes 2457604
  80.2 57.9 %collective-permute-start.23 = (bf16[640,640]{1,0:T(8,128)(2,1)S(1)}, bf16[640,640]{1,0:T(8,128)(2,1)S(1)}, u32[]{:S(2)}, u32[]{:S(2)}) collective-permute-start(bf16[640,640]{1,0:T(8,128)(2,1)S(1)} %copy-done.7), channel_id=1, source_target_pairs={{0,16},{8,24},{16,0},{24,8},{1,17},{9,25},{17,1},{25,9},{2,18},{10... | collective-permute-start | bytes 2457608 | tf_op jit(solution)/shard_map/ppermute | solution.py:14
  83.9 54.4 %collective-permute-start.17 = (bf16[640,640]{1,0:T(8,128)(2,1)S(1)}, bf16[640,640]{1,0:T(8,128)(2,1)S(1)}, u32[]{:S(2)}, u32[]{:S(2)}) collective-permute-start(bf16[640,640]{1,0:T(8,128)(2,1)S(1)} %copy-done.8), channel_id=1, source_target_pairs={{0,16},{8,24},{16,0},{24,8},{1,17},{9,25},{17,1},{25,9},{2,18},{10... | collective-permute-start | bytes 2457608 | tf_op jit(solution)/shard_map/ppermute | solution.py:14
  86.5 16.0 %collective-permute-start.4 = (bf16[512,640]{1,0:T(8,128)(2,1)}, bf16[512,640]{1,0:T(8,128)(2,1)S(1)}, u32[]{:S(2)}, u32[]{:S(2)}) collective-permute-start(bf16[512,640]{1,0:T(8,128)(2,1)} %get-tuple-element.49), channel_id=1, source_target_pairs={{0,4},{1,5},{4,6},{5,7},{6,2},{7,3},{2,0},{3,1},{8,12},{9,13},{12,... | collective-permute-start | bytes 1966088 | tf_op jit(solution)/shard_map/ppermute | solution.py:80
  86.5 9.2 %collective-permute-start.3 = (bf16[512,640]{1,0:T(8,128)(2,1)}, bf16[512,640]{1,0:T(8,128)(2,1)S(1)}, u32[]{:S(2)}, u32[]{:S(2)}) collective-permute-start(bf16[512,640]{1,0:T(8,128)(2,1)} %collective-permute-done.2), channel_id=1, source_target_pairs={{0,1},{1,0},{2,3},{3,2},{4,5},{5,4},{6,7},{7,6},{8,9},{9,8},{10,11... | collective-permute-start | bytes 1966088 | tf_op jit(solution)/shard_map/ppermute | solution.py:18
  88.7 47.8 %collective-permute-start.22 = (bf16[640,640]{1,0:T(8,128)(2,1)}, bf16[640,640]{1,0:T(8,128)(2,1)S(1)}, u32[]{:S(2)}, u32[]{:S(2)}) collective-permute-start(bf16[640,640]{1,0:T(8,128)(2,1)} %collective-permute-done.20), channel_id=1, source_target_pairs={{0,16},{8,24},{16,0},{24,8},{1,17},{9,25},{17,1},{25,9},{2,18},{10... | collective-permute-start | bytes 2457608 | tf_op jit(solution)/shard_map/ppermute | solution.py:14
  90.2 47.7 %copy-start.1 = (bf16[5120,640]{1,0:T(8,128)(2,1)S(1)}, bf16[5120,640]{1,0:T(8,128)(2,1)}, u32[]{:S(2)}) copy-start(bf16[5120,640]{1,0:T(8,128)(2,1)} %constant_dynamic-update-slice_fusion.5) | copy-start | bytes 19660804
  95.7 57.0 %collective-permute-start.16 = (bf16[640,640]{1,0:T(8,128)(2,1)}, bf16[640,640]{1,0:T(8,128)(2,1)S(1)}, u32[]{:S(2)}, u32[]{:S(2)}) collective-permute-start(bf16[640,640]{1,0:T(8,128)(2,1)} %collective-permute-done.14), channel_id=1, source_target_pairs={{0,16},{8,24},{16,0},{24,8},{1,17},{9,25},{17,1},{25,9},{2,18},{10... | collective-permute-start | bytes 2457608 | tf_op jit(solution)/shard_map/ppermute | solution.py:14
  102.5 53.7 %collective-permute-start.24 = (bf16[640,640]{1,0:T(8,128)(2,1)S(1)}, bf16[640,640]{1,0:T(8,128)(2,1)S(1)}, u32[]{:S(2)}, u32[]{:S(2)}) collective-permute-start(bf16[640,640]{1,0:T(8,128)(2,1)S(1)} %copy-done.7), channel_id=1, source_target_pairs={{0,8},{8,0},{16,24},{24,16},{1,9},{9,1},{17,25},{25,17},{2,10},{10... | collective-permute-start | bytes 2457608 | tf_op jit(solution)/shard_map/ppermute | solution.py:14
  136.5 21.2 %collective-permute-start.18 = (bf16[640,640]{1,0:T(8,128)(2,1)S(1)}, bf16[640,640]{1,0:T(8,128)(2,1)S(1)}, u32[]{:S(2)}, u32[]{:S(2)}) collective-permute-start(bf16[640,640]{1,0:T(8,128)(2,1)S(1)} %copy-done.8), channel_id=1, source_target_pairs={{0,8},{8,0},{16,24},{24,16},{1,9},{9,1},{17,25},{25,17},{2,10},{10... | collective-permute-start | bytes 2457608 | tf_op jit(solution)/shard_map/ppermute | solution.py:14
  138.1 19.6 %collective-permute-start.6 = (bf16[512,640]{1,0:T(8,128)(2,1)}, bf16[512,640]{1,0:T(8,128)(2,1)S(1)}, u32[]{:S(2)}, u32[]{:S(2)}) collective-permute-start(bf16[512,640]{1,0:T(8,128)(2,1)} %collective-permute-done.2), channel_id=1, source_target_pairs={{0,4},{1,5},{4,6},{5,7},{6,2},{7,3},{2,0},{3,1},{8,12},{9,13},{12,... | collective-permute-start | bytes 1966088 | tf_op jit(solution)/shard_map/ppermute | solution.py:80
  138.3 16.9 %copy-start.5 = (bf16[1280,640]{1,0:T(8,128)(2,1)S(1)}, bf16[1280,640]{1,0:T(8,128)(2,1)}, u32[]{:S(2)}) copy-start(bf16[1280,640]{1,0:T(8,128)(2,1)} %param.17) | copy-start | bytes 4915204
  138.3 36.9 %collective-permute-start.25 = (bf16[640,640]{1,0:T(8,128)(2,1)S(1)}, bf16[640,640]{1,0:T(8,128)(2,1)S(1)}, u32[]{:S(2)}, u32[]{:S(2)}) collective-permute-start(bf16[640,640]{1,0:T(8,128)(2,1)S(1)} %collective-permute-done.23), channel_id=1, source_target_pairs={{0,8},{8,0},{16,24},{24,16},{1,9},{9,1},{17,25},{25,17},{2,10},{10... | collective-permute-start | bytes 2457608 | tf_op jit(solution)/shard_map/ppermute | solution.py:14
  152.7 36.5 %collective-permute-start.19 = (bf16[640,640]{1,0:T(8,128)(2,1)S(1)}, bf16[640,640]{1,0:T(8,128)(2,1)S(1)}, u32[]{:S(2)}, u32[]{:S(2)}) collective-permute-start(bf16[640,640]{1,0:T(8,128)(2,1)S(1)} %collective-permute-done.17), channel_id=1, source_target_pairs={{0,8},{8,0},{16,24},{24,16},{1,9},{9,1},{17,25},{25,17},{2,10},{10... | collective-permute-start | bytes 2457608 | tf_op jit(solution)/shard_map/ppermute | solution.py:14
  156.2 34.6 %collective-permute-start.5 = (bf16[512,640]{1,0:T(8,128)(2,1)S(1)}, bf16[512,640]{1,0:T(8,128)(2,1)S(1)}, u32[]{:S(2)}, u32[]{:S(2)}) collective-permute-start(bf16[512,640]{1,0:T(8,128)(2,1)S(1)} %collective-permute-done.4), channel_id=1, source_target_pairs={{0,1},{1,0},{2,3},{3,2},{4,5},{5,4},{6,7},{7,6},{8,9},{9,8},{10,11... | collective-permute-start | bytes 1966088 | tf_op jit(solution)/shard_map/ppermute | solution.py:18
  157.6 32.6 %collective-permute-start.8 = (bf16[512,640]{1,0:T(8,128)(2,1)S(1)}, bf16[512,640]{1,0:T(8,128)(2,1)S(1)}, u32[]{:S(2)}, u32[]{:S(2)}) collective-permute-start(bf16[512,640]{1,0:T(8,128)(2,1)S(1)} %collective-permute-done.4), channel_id=1, source_target_pairs={{0,4},{1,5},{4,6},{5,7},{6,2},{7,3},{2,0},{3,1},{8,12},{9,13},{12,... | collective-permute-start | bytes 1966088 | tf_op jit(solution)/shard_map/ppermute | solution.py:80
  157.6 32.6 %collective-permute-start.10 = (bf16[512,640]{1,0:T(8,128)(2,1)S(1)}, bf16[512,640]{1,0:T(8,128)(2,1)S(1)}, u32[]{:S(2)}, u32[]{:S(2)}) collective-permute-start(bf16[512,640]{1,0:T(8,128)(2,1)S(1)} %collective-permute-done.6), channel_id=1, source_target_pairs={{0,4},{1,5},{4,6},{5,7},{6,2},{7,3},{2,0},{3,1},{8,12},{9,13},{12,... | collective-permute-start | bytes 1966088 | tf_op jit(solution)/shard_map/ppermute | solution.py:80
  175.2 18.7 %collective-permute-start.7 = (bf16[512,640]{1,0:T(8,128)(2,1)S(1)}, bf16[512,640]{1,0:T(8,128)(2,1)S(1)}, u32[]{:S(2)}, u32[]{:S(2)}) collective-permute-start(bf16[512,640]{1,0:T(8,128)(2,1)S(1)} %collective-permute-done.6), channel_id=1, source_target_pairs={{0,1},{1,0},{2,3},{3,2},{4,5},{5,4},{6,7},{7,6},{8,9},{9,8},{10,11... | collective-permute-start | bytes 1966088 | tf_op jit(solution)/shard_map/ppermute | solution.py:18
  190.3 17.2 %collective-permute-start.9 = (bf16[512,640]{1,0:T(8,128)(2,1)S(1)}, bf16[512,640]{1,0:T(8,128)(2,1)S(1)}, u32[]{:S(2)}, u32[]{:S(2)}) collective-permute-start(bf16[512,640]{1,0:T(8,128)(2,1)S(1)} %collective-permute-done.8), channel_id=1, source_target_pairs={{0,1},{1,0},{2,3},{3,2},{4,5},{5,4},{6,7},{7,6},{8,9},{9,8},{10,11... | collective-permute-start | bytes 1966088 | tf_op jit(solution)/shard_map/ppermute | solution.py:18
  190.3 17.1 %collective-permute-start.12 = (bf16[512,640]{1,0:T(8,128)(2,1)S(1)}, bf16[512,640]{1,0:T(8,128)(2,1)S(1)}, u32[]{:S(2)}, u32[]{:S(2)}) collective-permute-start(bf16[512,640]{1,0:T(8,128)(2,1)S(1)} %collective-permute-done.8), channel_id=1, source_target_pairs={{0,4},{1,5},{4,6},{5,7},{6,2},{7,3},{2,0},{3,1},{8,12},{9,13},{12,... | collective-permute-start | bytes 1966088 | tf_op jit(solution)/shard_map/ppermute | solution.py:80
  190.3 20.3 %collective-permute-start.11 = (bf16[512,640]{1,0:T(8,128)(2,1)S(1)}, bf16[512,640]{1,0:T(8,128)(2,1)S(1)}, u32[]{:S(2)}, u32[]{:S(2)}) collective-permute-start(bf16[512,640]{1,0:T(8,128)(2,1)S(1)} %collective-permute-done.10), channel_id=1, source_target_pairs={{0,1},{1,0},{2,3},{3,2},{4,5},{5,4},{6,7},{7,6},{8,9},{9,8},{10,11... | collective-permute-start | bytes 1966088 | tf_op jit(solution)/shard_map/ppermute | solution.py:18
  207.4 6.3 %collective-permute-start.13 = (bf16[512,640]{1,0:T(8,128)(2,1)S(1)}, bf16[512,640]{1,0:T(8,128)(2,1)S(1)}, u32[]{:S(2)}, u32[]{:S(2)}) collective-permute-start(bf16[512,640]{1,0:T(8,128)(2,1)S(1)} %collective-permute-done.12), channel_id=1, source_target_pairs={{0,1},{1,0},{2,3},{3,2},{4,5},{5,4},{6,7},{7,6},{8,9},{9,8},{10,11... | collective-permute-start | bytes 1966088 | tf_op jit(solution)/shard_map/ppermute | solution.py:18
  213.8 1.6 copy-start.6
  262.8 21.2 %collective-permute-start.27 = (bf16[640,640]{1,0:T(8,128)(2,1)S(1)}, bf16[640,640]{1,0:T(8,128)(2,1)S(1)}, u32[]{:S(2)}, u32[]{:S(2)}) collective-permute-start(bf16[640,640]{1,0:T(8,128)(2,1)S(1)} %convolution_convert_fusion.2), channel_id=1, source_target_pairs={{0,8},{8,0},{16,24},{24,16},{1,9},{9,1},{17,25},{25,17},{2,10},{10... | collective-permute-start | bytes 2457608 | tf_op jit(solution)/shard_map/ppermute | solution.py:14
  266.9 21.3 %collective-permute-start.30 = (bf16[640,640]{1,0:T(8,128)(2,1)S(1)}, bf16[640,640]{1,0:T(8,128)(2,1)S(1)}, u32[]{:S(2)}, u32[]{:S(2)}) collective-permute-start(bf16[640,640]{1,0:T(8,128)(2,1)S(1)} %convolution_convert_fusion), channel_id=1, source_target_pairs={{0,16},{8,24},{16,0},{24,8},{1,17},{9,25},{17,1},{25,9},{2,18},{10... | collective-permute-start | bytes 2457608 | tf_op jit(solution)/shard_map/ppermute | solution.py:14
  271.1 30.6 %collective-permute-start.26 = (bf16[640,640]{1,0:T(8,128)(2,1)S(1)}, bf16[640,640]{1,0:T(8,128)(2,1)S(1)}, u32[]{:S(2)}, u32[]{:S(2)}) collective-permute-start(bf16[640,640]{1,0:T(8,128)(2,1)S(1)} %convolution_convert_fusion.3), channel_id=1, source_target_pairs={{0,8},{8,0},{16,24},{24,16},{1,9},{9,1},{17,25},{25,17},{2,10},{10... | collective-permute-start | bytes 2457608 | tf_op jit(solution)/shard_map/ppermute | solution.py:14
  274.3 49.2 %collective-permute-start.29 = (bf16[640,640]{1,0:T(8,128)(2,1)S(1)}, bf16[640,640]{1,0:T(8,128)(2,1)S(1)}, u32[]{:S(2)}, u32[]{:S(2)}) collective-permute-start(bf16[640,640]{1,0:T(8,128)(2,1)S(1)} %convolution_convert_fusion.1), channel_id=1, source_target_pairs={{0,16},{8,24},{16,0},{24,8},{1,17},{9,25},{17,1},{25,9},{2,18},{10... | collective-permute-start | bytes 2457608 | tf_op jit(solution)/shard_map/ppermute | solution.py:14
  286.6 34.2 %collective-permute-start.28 = (bf16[640,640]{1,0:T(8,128)(2,1)S(1)}, bf16[640,640]{1,0:T(8,128)(2,1)S(1)}, u32[]{:S(2)}, u32[]{:S(2)}) collective-permute-start(bf16[640,640]{1,0:T(8,128)(2,1)S(1)} %add_convert_fusion.1), channel_id=1, source_target_pairs={{0,16},{8,24},{16,0},{24,8},{1,17},{9,25},{17,1},{25,9},{2,18},{10... | collective-permute-start | bytes 2457608 | tf_op jit(solution)/shard_map/ppermute | solution.py:14
  290.8 32.7 %collective-permute-start.31 = (bf16[640,640]{1,0:T(8,128)(2,1)S(1)}, bf16[640,640]{1,0:T(8,128)(2,1)S(1)}, u32[]{:S(2)}, u32[]{:S(2)}) collective-permute-start(bf16[640,640]{1,0:T(8,128)(2,1)S(1)} %add_convert_fusion), channel_id=1, source_target_pairs={{0,8},{8,0},{16,24},{24,16},{1,9},{9,1},{17,25},{25,17},{2,10},{10... | collective-permute-start | bytes 2457608 | tf_op jit(solution)/shard_map/ppermute | solution.py:14

commit v2 on v0

v2 whole, which is shorter than its diff:
```python
import functools
import math

import jax
import jax.numpy as jnp
from jax import lax
from jax.experimental import pallas as pl
from jax.experimental.pallas import tpu as pltpu
from jax.sharding import PartitionSpec as P

EPS = 1e-06
BF16 = jnp.bfloat16
F32 = jnp.float32
VMEM_BYTES = 48 * 1024 * 1024
CHUNKS = 2
TILE = 256
ANY = pl.BlockSpec(memory_space=pl.ANY)
SMEM = pl.BlockSpec(memory_space=pltpu.SMEM)


def after(value, *earlier):
    return lax.optimization_barrier((value, *earlier))[0]


def swap_clip(value, bit, count):
    return lax.ppermute(value, "clip", [(i, i ^ bit) for i in range(count)])


def clip_orders(count):
    bits = [1 << i for i in range(count.bit_length() - 1)]
    return ((0, bits), (1, bits[::-1]))


def gather_halves(weight, count, early=(), late=()):
    rows = weight.shape[0] // 2
    pieces = {}
    for half, order in clip_orders(count):
        own = weight[half * rows : (half + 1) * rows]
        held = {0: own}
        for bit in order:
            for mask in list(held):
                block = held[mask]
                if mask == 0:
                    block = after(own, *(early if bit == order[0] else late))
                held[mask ^ bit] = swap_clip(block, bit, count)
        for mask, block in held.items():
            pieces[mask, half] = block
    return pieces


def project_kernel(
    fake, start, masks, where, scalars, mod, sample, other, gathered, weight, *refs
):
    blocks, refs = refs[: (masks - 1) * 2], refs[(masks - 1) * 2 :]
    if fake:
        refs = refs[3 if start else 0 :]
        velocity, inputs, error = refs[:3]
        refs = refs[3:]
    else:
        refs = refs[1 if start else 0 :]
        velocity, gap = refs[:2]
        refs = refs[2:]
    held, full, total, wrong, sems, wsems, osems, *tiles = refs
    places, rows, depth = held.shape
    cols = total.shape[1]
    shards = gathered.shape[0]
    group = depth // cols
    count = len(tiles)
    tile = rows // count
    half_rows = weight.shape[0] // 2
    width = places * depth
    loads = []
    for mask in range(masks):
        for half in range(2):
            if mask:
                source = blocks[(mask - 1) * 2 + half]
            else:
                source = weight.at[pl.ds(half * half_rows, half_rows)]
            spot = pl.multiple_of((where[mask] * 2 + half) * half_rows, half_rows)
            target = full.at[pl.ds(spot, half_rows)]
            loads.append(pltpu.make_async_copy(source, target, wsems.at[mask * 2 + half]))
    arrivals = []
    for i in range(count):
        at = pl.ds(i * tile, tile)
        arrivals.append([
            pltpu.make_async_copy(
                gathered.at[f, at],
                held.at[f // group, at, pl.ds(f % group * cols, cols)],
                sems.at[i * shards + f],
            )
            for f in range(shards)
        ])
    for copy in arrivals[0] + loads:
        copy.start()
    for copies in arrivals[1:]:
        for copy in copies:
            copy.start()
    slab = tile // places

    def normalise(i, step):
        low = pl.multiple_of(step * slab, slab)
        at = pl.ds(i * tile + low, slab)
        sums = jnp.zeros((slab, 1), F32)
        for p in range(places):
            sums += jnp.sum(held[p, at, :].astype(F32), axis=1, keepdims=True)
        center = sums * (1.0 / width)
        power = jnp.zeros((slab, 1), F32)
        for p in range(places):
            spread = held[p, at, :].astype(F32) - center
            power += jnp.sum(spread * spread, axis=1, keepdims=True)
        factor = lax.rsqrt(power * (1.0 / width) + EPS)
        for p in range(places):
            spread = held[p, at, :].astype(F32) - center
            normed = (spread * factor).astype(BF16).astype(F32)
            put = (normed * (1.0 + mod[p, 1:2, :]) + mod[p, 0:1, :]).astype(BF16)
            tiles[i][p, pl.ds(low, slab), :] = put

    for copy in arrivals[0]:
        copy.wait()

    @pl.loop(0, places)
    def _(step):
        normalise(0, step)

    for copy in loads:
        copy.wait()
    drains = []

    def drain(source, target, index):
        drains.append(pltpu.make_async_copy(source, target, osems.at[index]))
        drains[-1].start()

    if not fake:
        gap[...] = jnp.zeros_like(gap)
    for i in range(count):
        at = pl.ds(i * tile, tile)
        out_at = pl.ds(start + i * tile, tile)
        if fake:
            drain(tiles[i], inputs.at[:, out_at, :], 3 * i)
        if i + 1 < count:
            for copy in arrivals[i + 1]:
                copy.wait()
        total[at, :] = jnp.zeros((tile, cols), F32)

        @pl.loop(0, places)
        def _(step):
            total[at, :] += jnp.dot(
                tiles[i][step],
                full[pl.ds(pl.multiple_of(step * depth, depth), depth), :],
                preferred_element_type=F32,
            )
            if i + 1 < count:
                normalise(i + 1, step)

        drain(total.at[at], velocity.at[out_at], 3 * i + 1)
        piece = 64

        @pl.loop(0, tile // piece)
        def _(step):
            low = pl.ds(pl.multiple_of(i * tile + step * piece, piece), piece)
            if fake:
                target = other[low, :].astype(F32) - sample[low, :].astype(F32)
                wrong[low, :] = ((total[low, :] - target) * scalars[1]).astype(BF16)
            else:
                estimate = other[low, :].astype(F32) - scalars[0] * total[low, :]
                away = jnp.abs(sample[low, :].astype(F32) - estimate)
                gap[...] += jnp.sum(away.reshape(piece // 8, 8, cols), axis=0)

        if fake:
            drain(wrong.at[at], error.at[out_at], 3 * i + 2)
    for copy in drains:
        copy.wait()


def project(fake, chunk, where, scalars, mod, sample, other, gathered, weight, blocks, earlier):
    clip_rows, cols = sample.shape
    shards, rows, _ = gathered.shape
    masks = len(blocks) // 2 + 1
    places, _, depth = mod.shape
    width = places * depth
    tile = min(TILE, rows)
    count = rows // tile
    window = pl.BlockSpec((rows, cols), lambda i: (chunk, 0))
    scratch = [
        pltpu.VMEM((places, rows, depth), BF16),
        pltpu.VMEM((width, cols), BF16),
        pltpu.VMEM((rows, cols), F32),
        pltpu.VMEM((rows, cols), BF16),
        pltpu.SemaphoreType.DMA((count * shards,)),
        pltpu.SemaphoreType.DMA((masks * 2,)),
        pltpu.SemaphoreType.DMA((3 * count,)),
    ] + [pltpu.VMEM((places, tile, depth), BF16)] * count
    out_shape = [jax.ShapeDtypeStruct((clip_rows, cols), F32)]
    out_specs = [ANY]
    if fake:
        out_shape.append(jax.ShapeDtypeStruct((places, clip_rows, depth), BF16))
        out_shape.append(jax.ShapeDtypeStruct((clip_rows, cols), BF16))
        out_specs += [ANY, ANY]
    else:
        out_shape.append(jax.ShapeDtypeStruct((8, cols), F32))
        out_specs.append(pl.BlockSpec((8, cols), lambda i: (0, 0)))
    first = 7 + len(blocks)
    return pl.pallas_call(
        functools.partial(project_kernel, fake, chunk * rows, masks),
        grid=(1,),
        out_shape=out_shape,
        in_specs=[SMEM, SMEM, pl.BlockSpec((places, 2, depth), lambda i: (0, 0, 0)), window, window]
        + [ANY] * (2 + len(blocks) + len(earlier)),
        out_specs=out_specs,
        scratch_shapes=scratch,
        input_output_aliases={first + i: i for i in range(len(earlier))},
        compiler_params=pltpu.CompilerParams(vmem_limit_bytes=VMEM_BYTES),
        cost_estimate=pl.CostEstimate(
            flops=2 * rows * width * cols,
            bytes_accessed=2 * (2 * rows * width + width * cols + 4 * rows * cols),
            transcendentals=0,
        ),
        name="project_fake" if fake else "project_teacher",
    )(where, scalars, mod, sample, other, gathered, weight, *blocks, *earlier)


def per_device(
    sample, noise, gen_branch, step, teacher_mod, fake_mod, teacher_weight, fake_weight, gen_gate
):
    clips = lax.axis_size("clip")
    shards = lax.axis_size("fsdp")
    clip = lax.axis_index("clip")
    clip_rows, cols = sample.shape
    width = cols * shards
    total_tokens = clip_rows * clips
    half_rows = fake_weight.shape[0] // 2
    group = 1 if cols % 128 else 2
    rows = clip_rows // CHUNKS

    frac = step.astype(F32)[0] / 1000.0
    sigma = 5.0 * frac / (1.0 + 4.0 * frac)
    noised = ((1.0 - sigma) * sample.astype(F32) + sigma * noise.astype(F32)).astype(BF16)
    gathered = [
        lax.all_gather(noised[i * rows : (i + 1) * rows], "fsdp") for i in range(CHUNKS)
    ]

    orders = clip_orders(clips)
    keys = [(mask, half) for mask in range(1, clips) for half in range(2)]
    fake_pieces = gather_halves(fake_weight, clips)
    crossed = [fake_pieces[order[-1], half] for half, order in orders]
    relayed = [fake_pieces[clips - 1, half] for half, order in orders]
    teacher_pieces = gather_halves(teacher_weight, clips, crossed, relayed)
    direct = [teacher_pieces[order[0], half] for half, order in orders]

    where = jnp.stack([clip ^ mask for mask in range(clips)]).astype(jnp.int32)
    scalars = jnp.stack([sigma, jnp.float32(1.0 / math.sqrt(total_tokens))])

    def by_place(mod):
        return jnp.swapaxes(mod[0].reshape(2, shards // group, group * cols), 0, 1)

    fake_by_place = by_place(fake_mod)
    teacher_by_place = by_place(teacher_mod)
    done = ()
    for i in range(CHUNKS):
        tokens = after(gathered[i], *direct) if i == 0 else gathered[i]
        done = project(
            True, i, where, scalars, fake_by_place, sample, noise, tokens,
            fake_weight, [fake_pieces[key] for key in keys], done,
        )
    fake_velocity, fake_in, error = done

    def term(mask, half):
        place = clip ^ mask
        if group == 2:
            left = lax.dynamic_slice(
                fake_in, (place, 0, half * cols), (1, clip_rows, cols)
            )[0]
        else:
            left = lax.dynamic_index_in_dim(fake_in, place * 2 + half, 0, keepdims=False)
        return lax.dot_general(left, error, (((0,), (0,)), ((), ())), preferred_element_type=F32)

    sent = {}
    for mask in range(clips - 1, 0, -1):
        for half, order in orders:
            if mask & order[0]:
                sent[half, mask] = term(mask, half).astype(BF16)
    ready = list(sent.values())
    sums = []
    for half, order in orders:
        mine = {mask: term(mask, half) for mask in range(clips) if not mask & order[0]}
        for bit in order:
            if bit == order[0]:
                going = {mask: block for (h, mask), block in sent.items() if h == half}
            else:
                going = {mask: mine.pop(mask).astype(BF16) for mask in list(mine) if mask & bit}
            for mask, block in going.items():
                mine[mask ^ bit] = mine[mask ^ bit] + swap_clip(block, bit, clips).astype(F32)
        sums.append(mine[0])
    fake_grad = jnp.concatenate(sums, axis=0)

    done = ()
    away = 0.0
    for i in range(CHUNKS):
        tokens = after(gathered[i], *ready) if i == 0 else gathered[i]
        velocity, gap = project(
            False, i, where, scalars, teacher_by_place, sample, noised, tokens,
            teacher_weight, [teacher_pieces[key] for key in keys], done,
        )
        done = (velocity,)
        away = away + gap
    gap_value = lax.psum(jnp.sum(away), "fsdp") / (clip_rows * width)
    push = sigma * (velocity - fake_velocity) / (gap_value + EPS)
    branch_cot = (gen_gate * push).astype(BF16)
    gate_grad = jnp.sum(push * gen_branch.astype(F32), axis=0, keepdims=True) / math.sqrt(clip_rows)
    return (branch_cot, gate_grad, fake_grad)


def solution(mesh):
    placed = (
        P("clip", "fsdp"),
        P("clip", "fsdp"),
        P("clip", "fsdp"),
        P("clip"),
        P("clip", None, None),
        P("clip", None, None),
        P("clip", "fsdp"),
        P("clip", "fsdp"),
        P("clip", "fsdp"),
    )
    return jax.shard_map(
        per_device,
        mesh=mesh,
        in_specs=placed,
        out_specs=(P("clip", "fsdp"), P("clip", "fsdp"), P("clip", "fsdp")),
        check_vma=False,
    )
```

time: 368 us -> 246 us (0.67)
  waiting for transfers between devices: 268 us -> 92.2 us
  Pallas kernels: 0 us -> 56 us
  starting transfers between devices: 0.16 us -> 23.6 us
  blocking collectives: 32.8 us -> 14.2 us
  matrix products: 40.9 us -> 25.9 us
  local copies, waits for them, and re-layouts: 1.73 us -> 10.8 us
    all_gather x3 -> x2, waiting for transfers between devices: 197 us -> 19.8 us  [per_device(): lax.all_gather(noised[i * rows:(i + 1) * rows], 'fsdp')]
    ppermute x0 -> x18, waiting for transfers between devices: none -> 71.8 us  [swap_clip(): return lax.ppermute(value, 'clip', [(i, i ^ bit) for i in range(count)])]
    reduce_scatter x1 -> x0, waiting for transfers between devices: 69.6 us -> none  [per_device(): lax.psum_scatter(lax.dot_general(left_fake, velocity_error, (((0,), (0,))...]
    pallas_call x0 -> x4, Pallas kernels: none -> 56 us  [project(): pl.pallas_call(functools.partial(project_kernel, fake, chunk * rows, mask...]
    ppermute x0 -> x18, starting transfers between devices: none -> 23.5 us  [swap_clip(): return lax.ppermute(value, 'clip', [(i, i ^ bit) for i in range(count)])]
    psum x2 -> x1, blocking collectives: 32.8 us -> 14.2 us  [per_device(): gap_value = lax.psum(jnp.sum(away), 'fsdp') / (clip_rows * width)]
    dot_general x3 -> x8, matrix products: 40.9 us -> 25.9 us  [term(): lax.dot_general(left, error, (((0,), (0,)), ((), ())), preferred_element_...]
    unnamed x14 -> x34, local copies, waits for them, and re-layouts: 1.15 us -> 7.52 us
  transfers between devices with their start and end apart: 4 -> 20, of which waited for: 4 -> 7; matrix products, arithmetic and copies ran while one was open for 6% -> 11% of each run, Pallas kernels for 0% -> 23%
where the time goes in v2:
time: 246 us; the launch traced here: 245 us
  waiting for transfers between devices  92.2 us (37%)
  Pallas kernels  56 us (23%)
  matrix products  25.9 us (11%)
  starting transfers between devices  23.6 us (10%)
  between operations  15.6 us (6%)
  blocking collectives  14.2 us (6%)
  local copies, waits for them, and re-layouts  10.8 us (4%)
  other arithmetic  6.61 us (3%)
    ppermute x18, waiting for transfers between devices, swap_clip(): return lax.ppermute(value, 'clip', [(i, i ^ bit) for i in range(count)])  71.8 us
    pallas_call x4, Pallas kernels, project(): pl.pallas_call(functools.partial(project_kernel, fake, chunk * rows, mask...  56 us
    dot_general x8, matrix products, term(): lax.dot_general(left, error, (((0,), (0,)), ((), ())), preferred_element_...  25.9 us
    ppermute x18, starting transfers between devices, swap_clip(): return lax.ppermute(value, 'clip', [(i, i ^ bit) for i in range(count)])  23.5 us
    all_gather x2, waiting for transfers between devices, per_device(): lax.all_gather(noised[i * rows:(i + 1) * rows], 'fsdp')  19.8 us
    psum x1, blocking collectives, per_device(): gap_value = lax.psum(jnp.sum(away), 'fsdp') / (clip_rows * width)  14.2 us
    unnamed x34, local copies, waits for them, and re-layouts  7.52 us
  transfers between devices with their start and end apart: 20, of which 7 were waited for; matrix products, arithmetic and copies ran while one was open for 11% of the time, Pallas kernels for 23%

profile of v2, /device:TPU:0, one launch (start us, length us, event | category | flops | bytes accessed | tf_op | source)
XLA Modules:
  0.0 245.0 jit_solution(3812207100270760848)
XLA Ops:
  7.9 2.2 add_convert_fusion.other
  10.1 1.0 copy-done.8
  11.2 1.2 fusion.30
  12.4 0.7 all-gather.5.cloned.1.call-update
  13.3 3.0 %collective-permute-start.3 = (bf16[640,640]{1,0:T(8,128)(2,1)S(1)}, bf16[640,640]{1,0:T(8,128)(2,1)S(1)}, u32[]{:S(2)}, u32[]{:S(2)}) collective-permute-start(bf16[640,640]{1,0:T(8,128)(2,1)S(1)} %get-tuple-element.40), channel_id=1, source_target_pairs={{0,8},{8,0},{16,24},{24,16},{1,9},{9,1},{17,25},{25,17},{2,10},{10... | collective-permute-start | bytes 2457608 | tf_op jit(solution)/shard_map/ppermute | solution.py:26
  16.3 1.5 collective-permute-start.5
  18.5 1.4 fusion.28
  19.8 15.6 %collective-permute-done.3.refs_0_ = bf16[640,640]{1,0:T(8,128)(2,1)S(1)} collective-permute-done((bf16[640,640]{1,0:T(8,128)(2,1)S(1)}, bf16[640,640]{1,0:T(8,128)(2,1)S(1)}, u32[]{:S(2)}, u32[]{:S(2)}) %collective-permute-start.3) | collective-permute-done | bytes 819232 | tf_op jit(solution)/shard_map/ppermute | solution.py:26
  35.4 2.1 collective-permute-start.4
  37.5 1.5 collective-permute-start.6
  39.0 16.1 %collective-permute-done.refs_2_ = bf16[640,640]{1,0:T(8,128)(2,1)S(1)} collective-permute-done((bf16[640,640]{1,0:T(8,128)(2,1)S(1)}, bf16[640,640]{1,0:T(8,128)(2,1)S(1)}, u32[]{:S(2)}, u32[]{:S(2)}) %collective-permute-start) | collective-permute-done | bytes 819232 | tf_op jit(solution)/shard_map/ppermute | solution.py:26
  55.1 0.9 copy-done
  56.0 0.9 copy-done.3
  57.0 2.0 collective-permute-start.9
  59.1 13.6 %collective-permute-done.4.refs_4_ = bf16[640,640]{1,0:T(8,128)(2,1)} collective-permute-done((bf16[640,640]{1,0:T(8,128)(2,1)S(1)}, bf16[640,640]{1,0:T(8,128)(2,1)}, u32[]{:S(2)}, u32[]{:S(2)}) %collective-permute-start.4) | collective-permute-done | bytes 819232 | tf_op jit(solution)/shard_map/ppermute | solution.py:26
  72.8 2.0 collective-permute-start.8
  74.8 13.3 %collective-permute-done.2.refs_0_ = bf16[640,640]{1,0:T(8,128)(2,1)S(1)} collective-permute-done((bf16[640,640]{1,0:T(8,128)(2,1)}, bf16[640,640]{1,0:T(8,128)(2,1)S(1)}, u32[]{:S(2)}, u32[]{:S(2)}) %collective-permute-start.2) | collective-permute-done | bytes 819232 | tf_op jit(solution)/shard_map/ppermute | solution.py:26
  88.1 2.1 collective-permute-start.10
  90.2 1.5 collective-permute-start.11
  91.7 1.2 copy-done.1
  92.8 1.2 copy-done.4
  94.0 14.0 %project_fake.2 = (f32[1024,640]{1,0:T(8,128)}, bf16[4,1024,1280]{2,1,0:T(8,128)(2,1)}, bf16[1024,640]{1,0:T(8,128)(2,1)}) custom-call(s32[4]{0:T(128)S(1)} %pad_add_fusion.where, f32[2]{0:T(128)S(1)} %pad_maximum_fusion.1.scalars, f32[4,2,1280]{2,1,0:T(2,128)S(1)} %bitcast.45, bf16[1024,640]{1,0:T(8,128)(2,1)} %sample.7, bf16[1024,640]{1,0:T(8,128)(2,1)} %other.3, ...), custom_call_target="tpu_custom_call" | custom-call | flops 3355443200 | bytes 19660800 | tf_op jit(solution)/shard_map/project_fake/pallas_call | solution.py:203
  108.0 19.8 %all-gather.5.cloned.1.call-done = bf16[4096,640]{1,0:T(8,128)(2,1)} async-done(((bf16[512,640]{1,0:T(8,128)(2,1)}), bf16[4096,640]{1,0:T(8,128)(2,1)}) %all-gather.5.cloned.1.call-update) | async-done | bytes 5242896 | tf_op jit(solution)/shard_map/all_gather | solution.py:239
  127.8 1.1 copy-done.2
  128.9 1.1 copy-done.5
  130.1 14.0 %project_fake.3 = (f32[1024,640]{1,0:T(8,128)}, bf16[4,1024,1280]{2,1,0:T(8,128)(2,1)}, bf16[1024,640]{1,0:T(8,128)(2,1)}) custom-call(s32[4]{0:T(128)S(1)} %pad_add_fusion.where, f32[2]{0:T(128)S(1)} %pad_maximum_fusion.1.scalars, f32[4,2,1280]{2,1,0:T(2,128)S(1)} %bitcast.46, ...), custom_call_target="tpu_custom_call", output_to_operand_aliasing={{0}: (13, {}), {1}: (14, {}), {2}: (15, {})} | custom-call | flops 3355443200 | bytes 19660800 | tf_op jit(solution)/shard_map/project_fake/pallas_call | solution.py:203
  144.1 4.0 %convolution_convert_fusion.3 = bf16[640,640]{1,0:T(8,128)(2,1)} fusion(bf16[1024,640]{1,0:T(8,128)(2,1)} %get-tuple-element.28, bf16[4,1024,1280]{2,1,0:T(8,128)(2,1)} %get-tuple-element.27, s32[]{:T(128)S(6)} %select_n.16), kind=kOutput, calls=%fused_computation.12 | convolution fusion | flops 839270400 | bytes 3440644 | tf_op jit(solution)/shard_map/dot_general | solution.py:275
  148.0 1.5 collective-permute-start.13
  149.5 3.5 %convolution_convert_fusion.2 = bf16[640,640]{1,0:T(8,128)(2,1)} fusion(bf16[1024,640]{1,0:T(8,128)(2,1)S(1)} %copy-done.14, bf16[4,1024,1280]{2,1,0:T(8,128)(2,1)} %get-tuple-element.27, s32[]{:T(128)S(6)} %select_n.16), kind=kOutput, calls=%fused_computation.11 | convolution fusion | flops 839270400 | bytes 3440644 | tf_op jit(solution)/shard_map/dot_general | solution.py:275
  153.0 3.5 %convolution_convert_fusion = bf16[640,640]{1,0:T(8,128)(2,1)} fusion(bf16[1024,640]{1,0:T(8,128)(2,1)S(1)} %copy-done.14, bf16[4,1024,1280]{2,1,0:T(8,128)(2,1)} %get-tuple-element.27, s32[]{:T(128)S(6)} %select_n.18), kind=kOutput, calls=%fused_computation.9 | convolution fusion | flops 839270400 | bytes 3440644 | tf_op jit(solution)/shard_map/dot_general | solution.py:275
  156.5 3.5 %convolution_convert_fusion.1 = bf16[640,640]{1,0:T(8,128)(2,1)} fusion(bf16[1024,640]{1,0:T(8,128)(2,1)S(1)} %copy-done.14, bf16[4,1024,1280]{2,1,0:T(8,128)(2,1)} %get-tuple-element.27, s32[]{:T(128)S(6)} %select_n.17), kind=kOutput, calls=%fused_computation.10 | convolution fusion | flops 839270400 | bytes 3440644 | tf_op jit(solution)/shard_map/dot_general | solution.py:275
  160.0 0.6 collective-permute-start.12
  160.5 1.5 collective-permute-start.16
  162.0 14.1 %project_teacher.2 = (f32[1024,640]{1,0:T(8,128)}, f32[8,640]{1,0:T(8,128)S(1)}) custom-call(s32[4]{0:T(128)S(1)} %pad_add_fusion.where, f32[2]{0:T(128)S(1)} %pad_maximum_fusion.1.scalars, f32[4,2,1280]{2,1,0:T(2,128)S(1)} %bitcast.47, bf16[1024,640]{1,0:T(8,128)(2,1)} %sample.7, bf16[1024,640]{1,0:T(8,128)(2,1)} %copy-done.8, ...), custom_call_target="tpu_custom_call" | custom-call | flops 3355443200 | bytes 19660800 | tf_op jit(solution)/shard_map/project_teacher/pallas_call | solution.py:203
  176.2 13.9 %project_teacher.3 = (f32[1024,640]{1,0:T(8,128)}, f32[8,640]{1,0:T(8,128)S(1)}) custom-call(s32[4]{0:T(128)S(1)} %pad_add_fusion.where, f32[2]{0:T(128)S(1)} %pad_maximum_fusion.1.scalars, f32[4,2,1280]{2,1,0:T(2,128)S(1)} %bitcast.48, bf16[1024,640]{1,0:T(8,128)(2,1)} %sample.7, bf16[1024,640]{1,0:T(8,128)(2,1)} %copy-done.8, ...), custom_call_target="tpu_custom_call", output_to_operand_aliasing={{0}: (13, {})} | custom-call | flops 3355443200 | bytes 19660800 | tf_op jit(solution)/shard_map/project_teacher/pallas_call | solution.py:203
  190.1 0.6 add_reduce_fusion
  191.2 14.2 %psum.7 = f32[]{:T(128)} all-reduce(f32[]{:T(128)} %add_reduce_fusion), channel_id=1, replica_groups=mesh['clip'=4,'fsdp'=8] {'fsdp'}, use_global_device_ids=true, to_apply=%region_1.0 | all-reduce | flops 1 | bytes 8 | tf_op jit(solution)/shard_map/psum | solution.py:306
  206.1 3.3 %add_convert_fusion.2 = bf16[640,640]{1,0:T(8,128)(2,1)S(1)} fusion(bf16[640,640]{1,0:T(8,128)(2,1)} %collective-permute-done.13, bf16[1024,640]{1,0:T(8,128)(2,1)} %get-tuple-element.28, bf16[4,1024,1280]{2,1,0:T(8,128)(2,1)} %get-tuple-element.27, s32[]{:T(128)S(6)} %select_n.17), kind=kOutput, calls=%fused_computation.8 | convolution fusion | flops 840089600 | bytes 4259844 | tf_op jit(solution)/shard_map/dot_general | solution.py:275
  209.4 1.5 collective-permute-start.14
  211.0 2.9 %add_convert_fusion.1 = bf16[640,640]{1,0:T(8,128)(2,1)S(1)} fusion(bf16[640,640]{1,0:T(8,128)(2,1)} %collective-permute-done.16, bf16[1024,640]{1,0:T(8,128)(2,1)S(1)} %copy-done.15, bf16[4,1024,1280]{2,1,0:T(8,128)(2,1)} %get-tuple-element.27, s32[]{:T(128)S(6)} %select_n.18), kind=kOutput, calls=%fused_computation.6 | convolution fusion | flops 840089600 | bytes 4259844 | tf_op jit(solution)/shard_map/dot_general | solution.py:275
  213.9 1.5 collective-permute-start.17
  215.4 1.7 multiply_reduce_fusion
  217.1 0.6 div.31
  217.7 11.8 %collective-permute-done.14 = bf16[640,640]{1,0:T(8,128)(2,1)S(1)} collective-permute-done((bf16[640,640]{1,0:T(8,128)(2,1)S(1)}, bf16[640,640]{1,0:T(8,128)(2,1)S(1)}, u32[]{:S(2)}, u32[]{:S(2)}) %collective-permute-start.14) | collective-permute-done | bytes 819232 | tf_op jit(solution)/shard_map/ppermute | solution.py:26
  229.5 2.8 %convert_add_fusion.1 = f32[640,640]{1,0:T(8,128)S(1)} fusion(bf16[640,640]{1,0:T(8,128)(2,1)S(1)} %collective-permute-done.14, bf16[640,640]{1,0:T(8,128)(2,1)} %collective-permute-done.12, bf16[1024,640]{1,0:T(8,128)(2,1)S(1)} %copy-done.15, bf16[4,1024,1280]{2,1,0:T(8,128)(2,1)} %get-tuple-element.27, s32[]{:T(128)S(6)} %select_n.19), kind=kOutput, calls=%fused_computation.7 | convolution fusion | flops 840499200 | bytes 5898244 | tf_op jit(solution)/shard_map/dot_general | solution.py:275
  232.3 1.4 collective-permute-done.17
  233.7 2.5 %convert_add_fusion = f32[640,640]{1,0:T(8,128)S(1)} fusion(bf16[640,640]{1,0:T(8,128)(2,1)S(1)} %collective-permute-done.17, bf16[640,640]{1,0:T(8,128)(2,1)S(1)} %collective-permute-done.15, bf16[1024,640]{1,0:T(8,128)(2,1)S(1)} %copy-done.15, bf16[4,1024,1280]{2,1,0:T(8,128)(2,1)} %get-tuple-element.27, s32[]{:T(128)S(6)} %select_n.19), kind=kOutput, calls=%fused_computation.5 | convolution fusion | flops 840499200 | bytes 5898244 | tf_op jit(solution)/shard_map/dot_general | solution.py:275
  236.2 1.9 pad_maximum_fusion
  (53 shorter events, 1.8 us)
Async XLA Ops:
  7.2 84.5 %all-gather.7.cloned.1.call-start = ((), (), s32[]{:S(2)}) async-start(), calls=%async_computation.1 | async-start | bytes 5898240 | tf_op jit(solution)/shard_map/all_gather | solution.py:239
  10.1 1.1 copy-start.8
  11.2 2.0 copy-start.9
  12.4 115.4 %all-gather.5.cloned.1.call-start = ((), (), s32[]{:S(2)}) async-start(), calls=%async_computation | async-start | bytes 5898240 | tf_op jit(solution)/shard_map/all_gather | solution.py:239
  13.2 5.3 %copy-start.10 = (bf16[1280,640]{1,0:T(8,128)(2,1)S(1)}, bf16[1280,640]{1,0:T(8,128)(2,1)}, u32[]{:S(2)}) copy-start(bf16[1280,640]{1,0:T(8,128)(2,1)} %weight.7) | copy-start | bytes 4915204
  13.3 22.1 %collective-permute-start.3 = (bf16[640,640]{1,0:T(8,128)(2,1)S(1)}, bf16[640,640]{1,0:T(8,128)(2,1)S(1)}, u32[]{:S(2)}, u32[]{:S(2)}) collective-permute-start(bf16[640,640]{1,0:T(8,128)(2,1)S(1)} %get-tuple-element.40), channel_id=1, source_target_pairs={{0,8},{8,0},{16,24},{24,16},{1,9},{9,1},{17,25},{25,17},{2,10},{10... | collective-permute-start | bytes 2457608 | tf_op jit(solution)/shard_map/ppermute | solution.py:26
  16.3 42.6 %copy-start.16 = (f32[1,640]{1,0:T(1,128)S(1)}, f32[1,640]{1,0:T(1,128)}, u32[]{:S(2)}) copy-start(f32[1,640]{1,0:T(1,128)} %param.17) | copy-start | bytes 7684
  16.3 75.3 %copy-start.6 = (f32[1,2,5120]{2,1,0:T(2,128)S(1)}, f32[1,2,5120]{2,1,0:T(2,128)}, u32[]{:S(2)}) copy-start(f32[1,2,5120]{2,1,0:T(2,128)} %param.14) | copy-start | bytes 122884
  16.3 21.2 %collective-permute-start.5 = (bf16[640,640]{1,0:T(8,128)(2,1)S(1)}, bf16[640,640]{1,0:T(8,128)(2,1)S(1)}, u32[]{:S(2)}, u32[]{:S(2)}) collective-permute-start(bf16[640,640]{1,0:T(8,128)(2,1)S(1)} %get-tuple-element.39), channel_id=1, source_target_pairs={{0,16},{8,24},{16,0},{24,8},{1,17},{9,25},{17,1},{25,9},{2,18},{10... | collective-permute-start | bytes 2457608 | tf_op jit(solution)/shard_map/ppermute | solution.py:26
  17.9 37.2 %collective-permute-start = (bf16[640,640]{1,0:T(8,128)(2,1)S(1)}, bf16[640,640]{1,0:T(8,128)(2,1)S(1)}, u32[]{:S(2)}, u32[]{:S(2)}) collective-permute-start(bf16[640,640]{1,0:T(8,128)(2,1)S(1)} %get-tuple-element.40), channel_id=1, source_target_pairs={{0,16},{8,24},{16,0},{24,8},{1,17},{9,25},{17,1},{25,9},{2,18},{10... | collective-permute-start | bytes 2457608 | tf_op jit(solution)/shard_map/ppermute | solution.py:26
  18.4 37.6 %collective-permute-start.1 = (bf16[640,640]{1,0:T(8,128)(2,1)S(1)}, bf16[640,640]{1,0:T(8,128)(2,1)S(1)}, u32[]{:S(2)}, u32[]{:S(2)}) collective-permute-start(bf16[640,640]{1,0:T(8,128)(2,1)S(1)} %get-tuple-element.39), channel_id=1, source_target_pairs={{0,8},{8,0},{16,24},{24,16},{1,9},{9,1},{17,25},{25,17},{2,10},{10... | collective-permute-start | bytes 2457608 | tf_op jit(solution)/shard_map/ppermute | solution.py:26
  35.4 37.3 %collective-permute-start.4 = (bf16[640,640]{1,0:T(8,128)(2,1)S(1)}, bf16[640,640]{1,0:T(8,128)(2,1)}, u32[]{:S(2)}, u32[]{:S(2)}) collective-permute-start(bf16[640,640]{1,0:T(8,128)(2,1)S(1)} %collective-permute-done.3.refs_0_), channel_id=1, source_target_pairs={{0,16},{8,24},{16,0},{24,8},{1,17},{9,25},{17,1},{25,9},{2,18},{10... | collective-permute-start | bytes 2457608 | tf_op jit(solution)/shard_map/ppermute | solution.py:26
  37.5 35.2 %collective-permute-start.6 = (bf16[640,640]{1,0:T(8,128)(2,1)S(1)}, bf16[640,640]{1,0:T(8,128)(2,1)}, u32[]{:S(2)}, u32[]{:S(2)}) collective-permute-start(bf16[640,640]{1,0:T(8,128)(2,1)S(1)} %collective-permute-done.5.refs_3_), channel_id=1, source_target_pairs={{0,8},{8,0},{16,24},{24,16},{1,9},{9,1},{17,25},{25,17},{2,10},{10... | collective-permute-start | bytes 2457608 | tf_op jit(solution)/shard_map/ppermute | solution.py:26
  55.1 0.9 copy-start
  56.0 0.9 copy-start.3
  56.9 31.2 %collective-permute-start.2 = (bf16[640,640]{1,0:T(8,128)(2,1)}, bf16[640,640]{1,0:T(8,128)(2,1)S(1)}, u32[]{:S(2)}, u32[]{:S(2)}) collective-permute-start(bf16[640,640]{1,0:T(8,128)(2,1)} %get-tuple-element.21), channel_id=1, source_target_pairs={{0,8},{8,0},{16,24},{24,16},{1,9},{9,1},{17,25},{25,17},{2,10},{10... | collective-permute-start | bytes 2457608 | tf_op jit(solution)/shard_map/ppermute | solution.py:26
  57.0 33.2 %collective-permute-start.9 = (bf16[640,640]{1,0:T(8,128)(2,1)}, bf16[640,640]{1,0:T(8,128)(2,1)S(1)}, u32[]{:S(2)}, u32[]{:S(2)}) collective-permute-start(bf16[640,640]{1,0:T(8,128)(2,1)} %get-tuple-element.20), channel_id=1, source_target_pairs={{0,16},{8,24},{16,0},{24,8},{1,17},{9,25},{17,1},{25,9},{2,18},{10... | collective-permute-start | bytes 2457608 | tf_op jit(solution)/shard_map/ppermute | solution.py:26
  72.7 87.3 %collective-permute-start.7 = (bf16[640,640]{1,0:T(8,128)(2,1)}, bf16[640,640]{1,0:T(8,128)(2,1)}, u32[]{:S(2)}, u32[]{:S(2)}) collective-permute-start(bf16[640,640]{1,0:T(8,128)(2,1)} %get-tuple-element.20), channel_id=1, source_target_pairs={{0,8},{8,0},{16,24},{24,16},{1,9},{9,1},{17,25},{25,17},{2,10},{10... | collective-permute-start | bytes 2457608 | tf_op jit(solution)/shard_map/ppermute | solution.py:26
  72.8 87.8 %collective-permute-start.8 = (bf16[640,640]{1,0:T(8,128)(2,1)}, bf16[640,640]{1,0:T(8,128)(2,1)}, u32[]{:S(2)}, u32[]{:S(2)}) collective-permute-start(bf16[640,640]{1,0:T(8,128)(2,1)} %get-tuple-element.21), channel_id=1, source_target_pairs={{0,16},{8,24},{16,0},{24,8},{1,17},{9,25},{17,1},{25,9},{2,18},{10... | collective-permute-start | bytes 2457608 | tf_op jit(solution)/shard_map/ppermute | solution.py:26
  88.1 74.0 %collective-permute-start.10 = (bf16[640,640]{1,0:T(8,128)(2,1)S(1)}, bf16[640,640]{1,0:T(8,128)(2,1)}, u32[]{:S(2)}, u32[]{:S(2)}) collective-permute-start(bf16[640,640]{1,0:T(8,128)(2,1)S(1)} %collective-permute-done.2.refs_0_), channel_id=1, source_target_pairs={{0,16},{8,24},{16,0},{24,8},{1,17},{9,25},{17,1},{25,9},{2,18},{10... | collective-permute-start | bytes 2457608 | tf_op jit(solution)/shard_map/ppermute | solution.py:26
  90.2 71.9 %collective-permute-start.11 = (bf16[640,640]{1,0:T(8,128)(2,1)S(1)}, bf16[640,640]{1,0:T(8,128)(2,1)}, u32[]{:S(2)}, u32[]{:S(2)}) collective-permute-start(bf16[640,640]{1,0:T(8,128)(2,1)S(1)} %collective-permute-done.9.refs_3_), channel_id=1, source_target_pairs={{0,8},{8,0},{16,24},{24,16},{1,9},{9,1},{17,25},{25,17},{2,10},{10... | collective-permute-start | bytes 2457608 | tf_op jit(solution)/shard_map/ppermute | solution.py:26
  91.7 1.2 copy-start.1
  92.8 1.2 copy-start.4
  127.8 1.1 copy-start.2
  128.9 1.1 copy-start.5
  144.1 5.4 %copy-start.14 = (bf16[1024,640]{1,0:T(8,128)(2,1)S(1)}, bf16[1024,640]{1,0:T(8,128)(2,1)}, u32[]{:S(2)}) copy-start(bf16[1024,640]{1,0:T(8,128)(2,1)} %get-tuple-element.28) | copy-start | bytes 3932164
  148.0 58.1 %collective-permute-start.13 = (bf16[640,640]{1,0:T(8,128)(2,1)}, bf16[640,640]{1,0:T(8,128)(2,1)}, u32[]{:S(2)}, u32[]{:S(2)}) collective-permute-start(bf16[640,640]{1,0:T(8,128)(2,1)} %convolution_convert_fusion.3), channel_id=1, source_target_pairs={{0,8},{8,0},{16,24},{24,16},{1,9},{9,1},{17,25},{25,17},{2,10},{10... | collective-permute-start | bytes 2457608 | tf_op jit(solution)/shard_map/ppermute | solution.py:26
  156.5 5.6 %copy-start.7 = (f32[1,2,5120]{2,1,0:T(2,128)S(1)}, f32[1,2,5120]{2,1,0:T(2,128)}, u32[]{:S(2)}) copy-start(f32[1,2,5120]{2,1,0:T(2,128)} %param.13) | copy-start | bytes 122884
  160.0 57.7 %collective-permute-start.12 = (bf16[640,640]{1,0:T(8,128)(2,1)}, bf16[640,640]{1,0:T(8,128)(2,1)}, u32[]{:S(2)}, u32[]{:S(2)}) collective-permute-start(bf16[640,640]{1,0:T(8,128)(2,1)} %convolution_convert_fusion), channel_id=1, source_target_pairs={{0,8},{8,0},{16,24},{24,16},{1,9},{9,1},{17,25},{25,17},{2,10},{10... | collective-permute-start | bytes 2457608 | tf_op jit(solution)/shard_map/ppermute | solution.py:26
  160.5 50.4 %collective-permute-start.16 = (bf16[640,640]{1,0:T(8,128)(2,1)}, bf16[640,640]{1,0:T(8,128)(2,1)}, u32[]{:S(2)}, u32[]{:S(2)}) collective-permute-start(bf16[640,640]{1,0:T(8,128)(2,1)} %convolution_convert_fusion.2), channel_id=1, source_target_pairs={{0,16},{8,24},{16,0},{24,8},{1,17},{9,25},{17,1},{25,9},{2,18},{10... | collective-permute-start | bytes 2457608 | tf_op jit(solution)/shard_map/ppermute | solution.py:26
  190.7 41.6 %collective-permute-start.15 = (bf16[640,640]{1,0:T(8,128)(2,1)}, bf16[640,640]{1,0:T(8,128)(2,1)S(1)}, u32[]{:S(2)}, u32[]{:S(2)}) collective-permute-start(bf16[640,640]{1,0:T(8,128)(2,1)} %convolution_convert_fusion.1), channel_id=1, source_target_pairs={{0,16},{8,24},{16,0},{24,8},{1,17},{9,25},{17,1},{25,9},{2,18},{10... | collective-permute-start | bytes 2457608 | tf_op jit(solution)/shard_map/ppermute | solution.py:26
  206.1 4.8 %copy-start.15 = (bf16[1024,640]{1,0:T(8,128)(2,1)S(1)}, bf16[1024,640]{1,0:T(8,128)(2,1)}, u32[]{:S(2)}) copy-start(bf16[1024,640]{1,0:T(8,128)(2,1)} %get-tuple-element.28) | copy-start | bytes 3932164
  209.4 6.0 %copy-start.13 = (bf16[1024,640]{1,0:T(8,128)(2,1)S(1)}, bf16[1024,640]{1,0:T(8,128)(2,1)}, u32[]{:S(2)}) copy-start(bf16[1024,640]{1,0:T(8,128)(2,1)} %param.11) | copy-start | bytes 3932164
  209.4 20.1 %collective-permute-start.14 = (bf16[640,640]{1,0:T(8,128)(2,1)S(1)}, bf16[640,640]{1,0:T(8,128)(2,1)S(1)}, u32[]{:S(2)}, u32[]{:S(2)}) collective-permute-start(bf16[640,640]{1,0:T(8,128)(2,1)S(1)} %add_convert_fusion.2), channel_id=1, source_target_pairs={{0,16},{8,24},{16,0},{24,8},{1,17},{9,25},{17,1},{25,9},{2,18},{10... | collective-permute-start | bytes 2457608 | tf_op jit(solution)/shard_map/ppermute | solution.py:26
  210.9 4.5 %copy-start.11 = (f32[1024,640]{1,0:T(8,128)S(1)}, f32[1024,640]{1,0:T(8,128)}, u32[]{:S(2)}) copy-start(f32[1024,640]{1,0:T(8,128)} %get-tuple-element.32) | copy-start | bytes 7864324
  210.9 4.5 %copy-start.12 = (f32[1024,640]{1,0:T(8,128)S(1)}, f32[1024,640]{1,0:T(8,128)}, u32[]{:S(2)}) copy-start(f32[1024,640]{1,0:T(8,128)} %get-tuple-element.31) | copy-start | bytes 7864324
  213.9 19.8 %collective-permute-start.17 = (bf16[640,640]{1,0:T(8,128)(2,1)S(1)}, bf16[640,640]{1,0:T(8,128)(2,1)S(1)}, u32[]{:S(2)}, u32[]{:S(2)}) collective-permute-start(bf16[640,640]{1,0:T(8,128)(2,1)S(1)} %add_convert_fusion.1), channel_id=1, source_target_pairs={{0,8},{8,0},{16,24},{24,16},{1,9},{9,1},{17,25},{25,17},{2,10},{10... | collective-permute-start | bytes 2457608 | tf_op jit(solution)/shard_map/ppermute | solution.py:26
Sparse Core Ops, SparseCore 0:
  12.5 58.7 all-gather.6
  72.9 54.8 all-gather.4

commit v3 on v0

v3 whole, which is shorter than its diff:
```python
import functools
import math

import jax
import jax.numpy as jnp
from jax import lax
from jax.experimental import pallas as pl
from jax.experimental.pallas import tpu as pltpu
from jax.sharding import PartitionSpec as P

EPS = 1e-06
BF16 = jnp.bfloat16
F32 = jnp.float32
VMEM_BYTES = 48 * 1024 * 1024
CHUNKS = 2
GATES = {'relay': ('cA1', 'own', 'B1'), 'teacher': ('parts', 'parts1'), 'B2': ('A2',), 'A3': ('far0', 'far1'), 'B3': ('A3', 't00', 't01', 'sums'), 'cB1': ('far0', 'far1'), 'cA2': ('far0', 'far1'), 'cB2': ('far0', 'far1'), 'cA3': ('early',), 'cB3': ('early',), 'teacher relay': ('early',)}
ANY = pl.BlockSpec(memory_space=pl.ANY)
SMEM = pl.BlockSpec(memory_space=pltpu.SMEM)
VMEM = pl.BlockSpec(memory_space=pltpu.VMEM)


def after(value, *earlier):
    return lax.optimization_barrier((value, *earlier))[0]


def swap_clip(value, bit, count):
    return lax.ppermute(value, "clip", [(i, i ^ bit) for i in range(count)])


def clip_orders(count):
    bits = [1 << i for i in range(count.bit_length() - 1)]
    return ((0, bits), (1, bits[::-1]))


def neighbour_blocks(weight, count):
    return {bit: swap_clip(weight, bit, count) for bit in clip_orders(count)[0][1]}


def relay_parts(direct, rows):
    parts = {}
    for half in range(2):
        for bit, block in direct.items():
            parts[bit, half] = block[half * rows : (half + 1) * rows]
    return parts


def relay_blocks(parts, count):
    pieces = {}
    for half, order in clip_orders(count):
        held = {}
        for bit in order:
            for mask in list(held):
                held[mask ^ bit] = swap_clip(held[mask], bit, count)
            held[bit] = parts[bit, half]
        for mask, block in held.items():
            pieces[mask, half] = block
    return pieces


def scale_kernel(keys, where, mod, weight, *refs):
    blocks, refs = refs[: len(keys)], refs[len(keys) :]
    out, sums, full, sems, osems = refs
    half_rows = weight.shape[0] // 2
    cols = weight.shape[1]
    loads, drains = [], []
    for index, (mask, half) in enumerate([(0, 0), (0, 1)] + keys):
        ref = weight if mask == 0 else blocks[index - 2]
        source = ref.at[pl.ds(half * half_rows, half_rows)] if ref.shape[0] > half_rows else ref
        spot = pl.multiple_of((where[mask] * 2 + half) * half_rows, half_rows)
        at = pl.ds(spot, half_rows)
        loads.append((pltpu.make_async_copy(source, full.at[at], sems.at[index]), spot))
        drains.append(pltpu.make_async_copy(full.at[at], out.at[at], osems.at[index]))
        loads[-1][0].start()
    tile = 160
    sums[...] = jnp.zeros_like(sums)
    for (load, spot), drain in zip(loads, drains):
        load.wait()

        @pl.loop(0, half_rows // tile)
        def _(step):
            at = pl.ds(pl.multiple_of(spot + step * tile, tile), tile)
            value = full[at, :].astype(F32)
            shifted = value * mod[at, 0:1]
            scaled = (value * (1.0 + mod[at, 1:2])).astype(BF16)
            full[at, :] = scaled
            sums[0] += jnp.sum(scaled.astype(F32).reshape(tile // 8, 8, cols), axis=0)
            sums[1] += jnp.sum(shifted.reshape(tile // 8, 8, cols), axis=0)

        drain.start()
    for i in range(2):
        sums[i] = jnp.broadcast_to(jnp.sum(sums[i], axis=0, keepdims=True), (8, cols))
    for drain in drains:
        drain.wait()


def scale(where, mod, weight, blocks):
    cols = weight.shape[1]
    half_rows = weight.shape[0] // 2
    count = len(blocks) + 2
    width = half_rows * count
    return pl.pallas_call(
        functools.partial(scale_kernel, list(blocks)),
        out_shape=(
            jax.ShapeDtypeStruct((width, cols), BF16),
            jax.ShapeDtypeStruct((2, 8, cols), F32),
        ),
        in_specs=[SMEM, VMEM] + [ANY] * (1 + len(blocks)),
        out_specs=(ANY, VMEM),
        scratch_shapes=[
            pltpu.VMEM((width, cols), BF16),
            pltpu.SemaphoreType.DMA((count,)),
            pltpu.SemaphoreType.DMA((count,)),
        ],
        compiler_params=pltpu.CompilerParams(vmem_limit_bytes=VMEM_BYTES),
        cost_estimate=pl.CostEstimate(
            flops=1, bytes_accessed=1, transcendentals=0
        ),
        name="scale",
    )(where, mod, weight, *blocks.values())


def project_kernel(
    first, last, hops, core_at, where, scalars, sums, sample, other, scaled, *refs
):
    count = len(hops)
    pieces, refs = refs[: sum(len(hop) for hop in hops)], refs[sum(len(hop) for hop in hops) :]
    if not first:
        carry, means, powers, _, *refs = refs
    if last:
        velocity, inputs, flipped, centers, factors, edge, *refs = refs
    else:
        velocity, inputs, centers, factors, *refs = refs
    held, full, tail, sems, wsems, osems = refs
    rows, depth = held.shape[1:]
    cols = velocity.shape[1]
    group = depth // cols
    core = where[core_at]
    loads, arrivals, drains = [], [], []
    index = 0
    for n, hop in enumerate(hops):
        copies = []
        for low, side, place in hop:
            owner = core if side == 0 else 1 - core
            ref = pieces[index]
            at = pl.ds(low, ref.shape[0])
            if group == 2:
                lanes = pl.ds(pl.multiple_of(owner * cols, cols), cols)
                spot = held.at[n, at, lanes]
            else:
                spot = held.at[2 * n + owner, at]
            copies.append(pltpu.make_async_copy(ref, spot, sems.at[index]))
            index += 1
        arrivals.append(copies)
        place = where[hop[0][2]]
        span = 2 * cols
        loads.append(
            pltpu.make_async_copy(
                scaled.at[pl.ds(pl.multiple_of(place * span, span), span)], full.at[n], wsems.at[n]
            )
        )
        parts = 2 // group
        drains.append(
            pltpu.make_async_copy(
                held.at[pl.ds(n * parts, parts)],
                inputs.at[pl.ds(place * parts, parts)],
                osems.at[n],
            )
        )
    for copies, load in zip(arrivals, loads):
        for copy in copies:
            copy.start()
        load.start()
    slots = held.shape[0]
    for n in range(count):
        for copy in arrivals[n]:
            copy.wait()
        loads[n].wait()
        drains[n].start()
        for part in range(2 // group):
            slot = n * (2 // group) + part
            term = jnp.dot(
                held[slot], full[n, pl.ds(part * depth, depth), :], preferred_element_type=F32
            )
            if n or part:
                velocity[...] += term
            elif first:
                velocity[...] = term
            else:
                velocity[...] = carry[...] + term
    piece = 128
    many = slots * depth
    total = many if first else many * (scaled.shape[0] // many)
    if last:
        tail[...] = jnp.zeros_like(tail)

    @pl.loop(0, rows // piece)
    def _(step):
        low = pl.multiple_of(step * piece, piece)
        at = pl.ds(low, piece)
        sum_ = jnp.zeros((piece, 1), F32)
        for slot in range(slots):
            sum_ += jnp.sum(held[slot, at, :].astype(F32), axis=1, keepdims=True)
        mean = sum_ * (1.0 / many)
        power = jnp.zeros((piece, 1), F32)
        for slot in range(slots):
            spread = held[slot, at, :].astype(F32) - mean
            power += jnp.sum(spread * spread, axis=1, keepdims=True)
        if not first:
            others = scaled.shape[0] - many
            apart = means[at, 0:1] - mean
            power += powers[at, 0:1] + apart * apart * (many * others / scaled.shape[0])
            mean += apart * (others / scaled.shape[0])
        if last:
            by = lax.rsqrt(power * (1.0 / scaled.shape[0]) + EPS)
            power = by
            value = by * (velocity[at, :] - mean * sums[0, 0:1, :]) + sums[1, 0:1, :]
            velocity[at, :] = value
            target = other[at, :].astype(F32) - sample[at, :].astype(F32)
            wrong = (value - target) * scalars[1]
            sent = (by * wrong).astype(BF16).astype(F32)
            flipped[:, at] = jnp.transpose(sent).astype(BF16)
            tail[0] += jnp.sum((mean * sent).reshape(piece // 8, 8, cols), axis=0)
            tail[1] += jnp.sum(wrong.reshape(piece // 8, 8, cols), axis=0)
        centers[at, :] = jnp.broadcast_to(mean, (piece, 128))
        factors[at, :] = jnp.broadcast_to(power, (piece, 128))

    if last:
        ends = [jnp.sum(jnp.transpose(tail[i]), axis=1, keepdims=True) for i in range(2)]
        edge[...] = jnp.concatenate(ends, axis=1)
    for copy in drains:
        copy.wait()


def project(where, scalars, sums, sample, other, scaled, hops, earlier, last):
    clip_rows, cols = sample.shape
    width = scaled.shape[0]
    group = 1 if cols % 128 else 2
    depth = group * cols
    places = width // depth
    slots = len(hops) * 2 // group
    first = not earlier
    pieces = [piece for hop, _ in hops for piece, _, _ in hop]
    plan = [[(low, side, place) for _, low, side in hop] for hop, place in hops]
    wide = jax.ShapeDtypeStruct((clip_rows, 128), F32)
    out_shape = [
        jax.ShapeDtypeStruct((clip_rows, cols), F32),
        jax.ShapeDtypeStruct((places, clip_rows, depth), BF16),
    ]
    if last:
        out_shape.append(jax.ShapeDtypeStruct((cols, clip_rows), BF16))
    out_shape += [wide, wide]
    if last:
        out_shape.append(jax.ShapeDtypeStruct((cols, 2), F32))
    if not first:
        velocity, inputs, means, powers = earlier
        earlier = [velocity, means, powers, inputs]
    return pl.pallas_call(
        functools.partial(project_kernel, first, last, plan, where.shape[0] - 1),
        out_shape=out_shape,
        in_specs=[SMEM, SMEM] + [VMEM] * 3 + [ANY] * (1 + len(pieces)) + ([] if first else [VMEM] * 3 + [ANY]),
        out_specs=[VMEM, ANY] + [VMEM] * (len(out_shape) - 2),
        scratch_shapes=[
            pltpu.VMEM((slots, clip_rows, depth), BF16),
            pltpu.VMEM((len(hops), 2 * cols, cols), BF16),
            pltpu.VMEM((2, 8, cols), F32),
            pltpu.SemaphoreType.DMA((len(pieces),)),
            pltpu.SemaphoreType.DMA((len(hops),)),
            pltpu.SemaphoreType.DMA((len(hops),)),
        ],
        input_output_aliases={} if first else {6 + len(pieces) + 3: 1},
        compiler_params=pltpu.CompilerParams(vmem_limit_bytes=VMEM_BYTES),
        cost_estimate=pl.CostEstimate(
            flops=1, bytes_accessed=1,
            transcendentals=0,
        ),
        name="project",
    )(where, scalars, sums, sample, other, scaled, *pieces, *earlier)


def outer_kernel(picks, mod, edge, flipped, inputs, *outs):
    del picks
    term = jnp.dot(flipped[...], inputs[0], preferred_element_type=F32)
    term = (term - edge[:, 0:1]) * (1.0 + mod[0, 1:2, :]) + edge[:, 1:2] * mod[0, 0:1, :]
    for i, out in enumerate(outs):

        @pl.when(pl.program_id(0) == i)
        def _():
            out[...] = term.astype(out.dtype)


def outer(picks, mod, edge, flipped, inputs, dtype):
    cols, rows = flipped.shape
    count = len(picks)
    group = inputs.shape[2] // cols

    def spot(i, picks):
        return (picks[i] // group, 0, lax.rem(picks[i], group))

    return pl.pallas_call(
        outer_kernel,
        out_shape=[jax.ShapeDtypeStruct((cols, cols), dtype)] * count,
        grid_spec=pltpu.PrefetchScalarGridSpec(
            num_scalar_prefetch=1,
            grid=(count,),
            in_specs=[
                pl.BlockSpec((1, 2, cols), spot),
                pl.BlockSpec((cols, 2), lambda i, picks: (0, 0)),
                pl.BlockSpec((cols, rows), lambda i, picks: (0, 0)),
                pl.BlockSpec((1, rows, cols), spot),
            ],
            out_specs=[pl.BlockSpec((cols, cols), lambda i, picks: (0, 0))] * count,
        ),
        compiler_params=pltpu.CompilerParams(vmem_limit_bytes=VMEM_BYTES),
        cost_estimate=pl.CostEstimate(
            flops=1, bytes_accessed=1,
            transcendentals=0,
        ),
        name="outer",
    )(jnp.stack(picks).astype(jnp.int32), mod, edge, flipped, inputs)


def finish_kernel(terms, *refs):
    *parts, out = refs
    for half in range(2):
        total = parts[half * terms][...]
        for ref in parts[half * terms + 1 : (half + 1) * terms]:
            total += ref[...].astype(F32)
        out[half] = jnp.transpose(total)


def finish(halves):
    cols = halves[0][0].shape[0]
    lanes = 128 if cols % 128 == 0 else cols
    parts = [part for half in halves for part in half]
    return pl.pallas_call(
        functools.partial(finish_kernel, len(halves[0])),
        grid=(cols // lanes,),
        out_shape=jax.ShapeDtypeStruct((2, cols, cols), F32),
        in_specs=[pl.BlockSpec((cols, lanes), lambda i: (0, i))] * len(parts),
        out_specs=pl.BlockSpec((2, lanes, cols), lambda i: (0, i, 0)),
        compiler_params=pltpu.CompilerParams(vmem_limit_bytes=VMEM_BYTES),
        name="finish",
    )(*parts).reshape(2 * cols, cols)


def per_device(
    sample, noise, gen_branch, step, teacher_mod, fake_mod, teacher_weight, fake_weight, gen_gate
):
    clips = lax.axis_size("clip")
    shards = lax.axis_size("fsdp")
    clip = lax.axis_index("clip")
    shard = lax.axis_index("fsdp")
    clip_rows, cols = sample.shape
    width = cols * shards
    total_tokens = clip_rows * clips
    hops = shards // 2
    group = 1 if cols % 128 else 2
    rows = clip_rows // CHUNKS
    orders = clip_orders(clips)

    frac = step.astype(F32)[0] / 1000.0
    sigma = 5.0 * frac / (1.0 + 4.0 * frac)
    noised = ((1.0 - sigma) * sample.astype(F32) + sigma * noise.astype(F32)).astype(BF16)

    order = list(range(0, hops, 2)) + list(range(hops - 1 - hops % 2, 0, -2))
    ring = [
        (2 * order[i] + core, 2 * order[(i + 1) % hops] + core)
        for i in range(hops)
        for core in range(2)
    ]
    line = shard // 2
    rank = jnp.where(line % 2 == 0, line // 2, hops - 1 - line // 2)
    places = []
    for hop in range(hops):
        at = (rank + hops - hop) % hops
        places.append(jnp.where(2 * at < hops, 2 * at, 2 * (hops - 1 - at) + 1))
    swap = [(i, i ^ 1) for i in range(shards)]
    half_rows = fake_weight.shape[0] // 2
    far = [key for key in ((m, h) for m in range(clips) for h in range(2)) if key[0] & (key[0] - 1)]
    seen = {}

    def gated(name, value):
        names = [other for other in GATES.get(name, ()) if other in seen]
        return after(value, *(seen[other] for other in names))

    def hop_to(hop, i):
        name = "AB"[i] + str(hop)
        source = seen["AB"[i] + str(hop - 1)] if hop > 1 else noised[i * rows : (i + 1) * rows]
        seen[name] = lax.ppermute(gated(name, source), "fsdp", ring)

    def cross(hop, i):
        name = "AB"[i] + str(hop)
        seen["c" + name] = lax.ppermute(gated("c" + name, seen[name]), "fsdp", swap)

    fake_direct = neighbour_blocks(fake_weight, clips)
    for i, block in enumerate(fake_direct.values()):
        seen["f" + str(i)] = block
    for i in range(CHUNKS):
        hop_to(1, i)
    seen["own"] = lax.ppermute(noised, "fsdp", swap)
    for i in range(CHUNKS):
        cross(1, i)
    for i in range(CHUNKS):
        hop_to(2, i)
    parts = relay_parts({bit: gated("relay", block) for bit, block in fake_direct.items()}, half_rows)
    seen["parts"] = list(parts.values())[0]
    seen["parts1"] = list(parts.values())[-1]
    fake_blocks = relay_blocks(parts, clips)
    for mask, block in fake_direct.items():
        fake_blocks[mask, 0] = fake_blocks[mask, 1] = block
    seen["far0"], seen["far1"] = fake_blocks[far[0]], fake_blocks[far[1]]
    scalars = jnp.stack([sigma, jnp.float32(1.0 / math.sqrt(total_tokens))])
    owners = jnp.stack([clip ^ mask for mask in range(clips)]).astype(jnp.int32)
    where = jnp.stack(places + [shard % 2]).astype(jnp.int32)
    scaled, sums = scale(owners, jnp.transpose(fake_mod[0]), fake_weight, fake_blocks)
    seen["sums"] = sums
    teacher_parts = {}
    own = gated("teacher", teacher_weight)
    own = [own[:half_rows], own[half_rows:]]
    for phase in range(len(orders[0][1])):
        for half, order in orders:
            block = swap_clip(gated("teacher" + str(min(phase, 1)), own[half]), order[phase], clips)
            teacher_parts[order[phase], half] = block
            seen["t" + str(phase) + str(half)] = block
    tokens = [([(noised, 0, 0), (seen["own"], 0, 1)], 0)]

    def add_hop(hop):
        pieces = []
        for i in range(CHUNKS):
            name = "AB"[i] + str(hop)
            pieces += [(seen[name], i * rows, 0), (seen["c" + name], i * rows, 1)]
        tokens.append((pieces, hop))

    add_hop(1)
    for hop in range(2, hops):
        for i in range(CHUNKS):
            if hop > 2:
                hop_to(hop, i)
            if hop < hops - 1:
                cross(hop, i)
        if hop < hops - 1:
            add_hop(hop)
    done = project(where, scalars, sums, sample, noise, scaled, tokens, (), False)
    seen["early"] = done[2]
    for key, block in teacher_parts.items():
        teacher_parts[key] = gated("teacher relay", block)
    teacher_blocks = relay_blocks(teacher_parts, clips)
    for i in range(CHUNKS):
        cross(hops - 1, i)
    add_hop(hops - 1)
    fake_velocity, inputs, flipped, centers, factors, edge = project(
        where, scalars, sums, sample, noise, scaled, tokens[-1:], done, True
    )
    by_place = jnp.swapaxes(fake_mod[0].reshape(2, shards // group, group * cols), 0, 1)
    flipped = after(flipped, *(teacher_blocks[key] for key in far))

    def terms(keys, left, dtype):
        picks = [(clip ^ mask) * 2 + half for mask, half in keys]
        return dict(zip(keys, outer(picks, by_place, edge, left, inputs, dtype)))

    held = {}
    going = [(mask, half) for half, order in orders for mask in range(clips) if mask & order[0]]
    held.update(terms([key for key in going if key[0] & (key[0] - 1)], flipped, BF16))
    held.update(terms([key for key in going if key not in held], flipped, BF16))
    ready = list(held.values())
    keys = [key for m in range(clips) for key in [(m, 0), (m, 1)] if key not in held]
    held.update(terms(keys, after(flipped, *ready), F32))
    halves = []
    firsts, seconds = [], []
    for half, order in orders:
        mine = {mask: [block] for (mask, h), block in held.items() if h == half}
        for bit in order:
            for mask in [mask for mask in mine if mask & bit]:
                block = sum(part.astype(F32) for part in mine.pop(mask)).astype(BF16)
                got = swap_clip(block, bit, clips)
                if bit == order[0]:
                    (firsts if mask & (mask - 1) else seconds).append(got)
                mine[mask ^ bit].append(got)
        halves.append(mine[0])
    fake_grad = finish(halves)

    scaled, sums = scale(
        owners, jnp.transpose(teacher_mod[0]), after(teacher_weight, *ready), teacher_blocks
    )
    depth = group * cols
    velocity = 0.0
    for p in range(width // depth):
        left = inputs[p]
        if p == width // depth // 2:
            left = after(left, *firsts)
        right = scaled[p * depth : (p + 1) * depth]
        velocity = velocity + jnp.dot(left, right, preferred_element_type=F32)
    velocity = factors[:, :1] * (velocity - centers[:, :1] * sums[0, :1]) + sums[1, :1]
    away = sample.astype(F32) - (noised.astype(F32) - sigma * velocity)
    away = after(jnp.sum(jnp.abs(away)).reshape(1, 1), *seconds)
    bit = 1
    while bit < shards:
        away = away + lax.ppermute(away, "fsdp", [(i, i ^ bit) for i in range(shards)])
        bit *= 2
    gap_value = away / (clip_rows * width)
    push = sigma * (velocity - fake_velocity) / (gap_value + EPS)
    branch_cot = (gen_gate * push).astype(BF16)
    gate_grad = jnp.sum(push * gen_branch.astype(F32), axis=0, keepdims=True) / math.sqrt(clip_rows)
    return (branch_cot, gate_grad, fake_grad)


def solution(mesh):
    placed = (
        P("clip", "fsdp"),
        P("clip", "fsdp"),
        P("clip", "fsdp"),
        P("clip"),
        P("clip", None, None),
        P("clip", None, None),
        P("clip", "fsdp"),
        P("clip", "fsdp"),
        P("clip", "fsdp"),
    )
    return jax.shard_map(
        per_device,
        mesh=mesh,
        in_specs=placed,
        out_specs=(P("clip", "fsdp"), P("clip", "fsdp"), P("clip", "fsdp")),
        check_vma=False,
    )
```

time: 368 us -> 220 us (0.60)
  waiting for transfers between devices: 268 us -> 51.6 us
  Pallas kernels: 0 us -> 72.5 us
  starting transfers between devices: 0.16 us -> 41 us
  blocking collectives: 32.8 us -> 0 us
  local copies, waits for them, and re-layouts: 1.73 us -> 25.1 us
  matrix products: 40.9 us -> 19.1 us
  between operations: 15.2 us -> 4.26 us
    all_gather x3 -> x0, waiting for transfers between devices: 197 us -> none  [the longest x1 102 us: per_device(): normed = lax.all_gather(local_normed, 'fsdp', axis=1, tiled=True)]
    pallas_call x0 -> x8, Pallas kernels: none -> 72.5 us  [the longest x2 31.7 us: project(): pl.pallas_call(functools.partial(project_kernel, first, last, plan, where...]
    reduce_scatter x1 -> x0, waiting for transfers between devices: 69.6 us -> none  [per_device(): lax.psum_scatter(lax.dot_general(left_fake, velocity_error, (((0,), (0,))...]
    ppermute x0 -> x32, waiting for transfers between devices: none -> 51.6 us  [the longest x6 45.6 us: hop_to(): seen[name] = lax.ppermute(gated(name, source), 'fsdp', ring)]
    ppermute x0 -> x32, starting transfers between devices: none -> 41 us  [the longest x16 19.9 us: swap_clip(): return lax.ppermute(value, 'clip', [(i, i ^ bit) for i in range(count)])]
    psum x2 -> x0, blocking collectives: 32.8 us -> none  [the longest x1 18.3 us: per_device(): row_sum, row_total = lax.psum((partial_sum, partial_power), 'fsdp')]
    dot_general x3 -> x4, matrix products: 40.9 us -> 19.1 us  [per_device(): velocity = velocity + jnp.dot(left, right, preferred_element_type=F32)]
    unnamed x14 -> x62, local copies, waits for them, and re-layouts: 1.15 us -> 19 us
  transfers between devices with their start and end apart: 4 -> 32, of which waited for: 4 -> 10; matrix products, arithmetic and copies ran while one was open for 6% -> 16% of each run, Pallas kernels for 0% -> 27%
where the time goes in v3:
time: 220 us
  Pallas kernels  72.5 us (33%)
  waiting for transfers between devices  51.6 us (23%)
  starting transfers between devices  41 us (19%)
  local copies, waits for them, and re-layouts  25.1 us (11%)
  matrix products  19.1 us (9%)
  other arithmetic  6.02 us (3%)
  between operations  4.26 us (2%)
    ppermute x6, waiting for transfers between devices, hop_to(): seen[name] = lax.ppermute(gated(name, source), 'fsdp', ring)  45.6 us
    pallas_call x2, Pallas kernels, project(): pl.pallas_call(functools.partial(project_kernel, first, last, plan, where...  31.7 us
    ppermute x16, starting transfers between devices, swap_clip(): return lax.ppermute(value, 'clip', [(i, i ^ bit) for i in range(count)])  19.9 us
    dot_general x4, matrix products, per_device(): velocity = velocity + jnp.dot(left, right, preferred_element_type=F32)  19.1 us
    unnamed x62, local copies, waits for them, and re-layouts  19 us
    pallas_call x3, Pallas kernels, outer(): pl.pallas_call(outer_kernel, out_shape=[jax.ShapeDtypeStruct((cols, cols)...  18.1 us
    pallas_call x2, Pallas kernels, scale(): pl.pallas_call(functools.partial(scale_kernel, list(blocks)), out_shape=(...  17.6 us
    ppermute x6, starting transfers between devices, hop_to(): seen[name] = lax.ppermute(gated(name, source), 'fsdp', ring)  15.7 us
  transfers between devices with their start and end apart: 32, of which 10 were waited for; matrix products, arithmetic and copies ran while one was open for 16% of the time, Pallas kernels for 27%

profile of v3, /device:TPU:0, one launch (start us, length us, event | category | flops | bytes accessed | tf_op | source)
XLA Modules:
  0.0 219.6 jit_solution(2089803281934894298)
XLA Ops:
  0.6 3.0 %collective-permute-start = (bf16[1280,640]{1,0:T(8,128)(2,1)}, bf16[1280,640]{1,0:T(8,128)(2,1)S(1)}, u32[]{:S(2)}, u32[]{:S(2)}) collective-permute-start(bf16[1280,640]{1,0:T(8,128)(2,1)} %weight.1), channel_id=1, source_target_pairs={{0,8},{8,0},{16,24},{24,16},{1,9},{9,1},{17,25},{25,17},{2,10},{10... | collective-permute-start | bytes 4915208 | tf_op jit(solution)/shard_map/ppermute | solution.py:27
  3.6 1.5 collective-permute-start.6
  5.8 2.2 %fusion.1.refs_0_ = bf16[1024,640]{1,0:T(8,128)(2,1)S(1)} fusion(bf16[1024,640]{1,0:T(8,128)(2,1)} %sample.3, bf16[1024,640]{1,0:T(8,128)(2,1)} %other.3, f32[]{:T(128)S(6)} %sub.57, f32[]{:T(128)} %bitcast), kind=kLoop, calls=%fused_computation.3 | loop fusion | flops 3932160 | bytes 3932168 | tf_op jit(solution)/shard_map/convert_element_type | solution.py:363
  8.2 2.6 %collective-permute-start.1 = (bf16[512,640]{1,0:T(8,128)(2,1)S(1)}, bf16[512,640]{1,0:T(8,128)(2,1)S(1)}, u32[]{:S(2)}, u32[]{:S(2)}) collective-permute-start(bf16[512,640]{1,0:T(8,128)(2,1)S(1)} %get-tuple-element.92), channel_id=1, source_target_pairs={{0,4},{1,5},{4,6},{5,7},{6,2},{7,3},{2,0},{3,1},{8,12},{9,13},{12,... | collective-permute-start | bytes 1966088 | tf_op jit(solution)/shard_map/ppermute | solution.py:389
  10.9 1.6 collective-permute-start.4
  12.4 13.6 %collective-permute-done.1.refs_2_ = bf16[512,640]{1,0:T(8,128)(2,1)S(1)} collective-permute-done((bf16[512,640]{1,0:T(8,128)(2,1)S(1)}, bf16[512,640]{1,0:T(8,128)(2,1)S(1)}, u32[]{:S(2)}, u32[]{:S(2)}) %collective-permute-start.1) | collective-permute-done | bytes 655392 | tf_op jit(solution)/shard_map/ppermute | solution.py:389
  26.0 12.3 %collective-permute-done.4.refs_4_ = bf16[512,640]{1,0:T(8,128)(2,1)} collective-permute-done((bf16[512,640]{1,0:T(8,128)(2,1)S(1)}, bf16[512,640]{1,0:T(8,128)(2,1)}, u32[]{:S(2)}, u32[]{:S(2)}) %collective-permute-start.4) | collective-permute-done | bytes 655392 | tf_op jit(solution)/shard_map/ppermute | solution.py:389
  40.3 1.3 collective-permute-start.5
  41.6 1.2 copy-done.20
  42.9 1.6 collective-permute-start.7
  44.4 2.6 %collective-permute-start.8 = (bf16[512,640]{1,0:T(8,128)(2,1)S(1)}, bf16[512,640]{1,0:T(8,128)(2,1)}, u32[]{:S(2)}, u32[]{:S(2)}) collective-permute-start(bf16[512,640]{1,0:T(8,128)(2,1)S(1)} %collective-permute-done.1.refs_2_), channel_id=1, source_target_pairs={{0,4},{1,5},{4,6},{5,7},{6,2},{7,3},{2,0},{3,1},{8,12},{9,13},{12,... | collective-permute-start | bytes 1966088 | tf_op jit(solution)/shard_map/ppermute | solution.py:389
  47.0 1.3 fusion.18
  49.1 1.5 collective-permute-start.15
  50.6 9.0 %collective-permute-done.8.refs_6_ = bf16[512,640]{1,0:T(8,128)(2,1)} collective-permute-done((bf16[512,640]{1,0:T(8,128)(2,1)S(1)}, bf16[512,640]{1,0:T(8,128)(2,1)}, u32[]{:S(2)}, u32[]{:S(2)}) %collective-permute-start.8) | collective-permute-done | bytes 655392 | tf_op jit(solution)/shard_map/ppermute | solution.py:389
  59.6 3.5 %collective-permute-start.12 = (bf16[512,640]{1,0:T(8,128)(2,1)}, bf16[512,640]{1,0:T(8,128)(2,1)}, u32[]{:S(2)}, u32[]{:S(2)}) collective-permute-start(bf16[512,640]{1,0:T(8,128)(2,1)} %collective-permute-done.4.refs_4_), channel_id=1, source_target_pairs={{0,4},{1,5},{4,6},{5,7},{6,2},{7,3},{2,0},{3,1},{8,12},{9,13},{12,... | collective-permute-start | bytes 1966088 | tf_op jit(solution)/shard_map/ppermute | solution.py:389
  65.0 2.8 %collective-permute-start.9 = (bf16[512,640]{1,0:T(8,128)(2,1)}, bf16[512,640]{1,0:T(8,128)(2,1)}, u32[]{:S(2)}, u32[]{:S(2)}) collective-permute-start(bf16[512,640]{1,0:T(8,128)(2,1)} %collective-permute-done.8.refs_6_), channel_id=1, source_target_pairs={{0,4},{1,5},{4,6},{5,7},{6,2},{7,3},{2,0},{3,1},{8,12},{9,13},{12,... | collective-permute-start | bytes 1966088 | tf_op jit(solution)/shard_map/ppermute | solution.py:389
  67.8 10.7 %collective-permute-done.12.refs_8_ = bf16[512,640]{1,0:T(8,128)(2,1)} collective-permute-done((bf16[512,640]{1,0:T(8,128)(2,1)}, bf16[512,640]{1,0:T(8,128)(2,1)}, u32[]{:S(2)}, u32[]{:S(2)}) %collective-permute-start.12) | collective-permute-done | bytes 655392 | tf_op jit(solution)/shard_map/ppermute | solution.py:389
  79.4 1.5 collective-permute-start.22
  80.9 2.3 %copy.15 = f32[1,2,5120]{1,2,0:T(8,128)} copy(f32[1,2,5120]{2,1,0:T(2,128)S(1)} %copy-done.12) | data formatting | bytes 81920 | tf_op args[5]
  83.3 1.1 copy-done.5
  84.4 1.1 copy-done.7
  85.6 8.4 %scale.2 = (bf16[5120,640]{1,0:T(8,128)(2,1)}, f32[2,8,640]{2,1,0:T(8,128)S(1)}) custom-call(s32[4]{0:T(128)S(1)} %pad_add_fusion.where, f32[5120,2]{1,0:T(8,128)} %bitcast.48, bf16[1280,640]{1,0:T(8,128)(2,1)S(1)} %copy-done.2, bf16[1280,640]{1,0:T(8,128)(2,1)S(1)} %collective-permute-done.refs_0_.refs_5_, bf16[640,640]{1,0:T(8,128)(2,1)S(1)} %copy-done.5, ...), custom_call_target="tpu_custom_call" | custom-call | flops 1 | bytes 1 | tf_op jit(solution)/shard_map/scale/pallas_call | solution.py:101
  94.0 2.6 %collective-permute-start.17 = (bf16[512,640]{1,0:T(8,128)(2,1)}, bf16[512,640]{1,0:T(8,128)(2,1)S(1)}, u32[]{:S(2)}, u32[]{:S(2)}) collective-permute-start(bf16[512,640]{1,0:T(8,128)(2,1)} %collective-permute-done.12.refs_8_), channel_id=1, source_target_pairs={{0,4},{1,5},{4,6},{5,7},{6,2},{7,3},{2,0},{3,1},{8,12},{9,13},{12,... | collective-permute-start | bytes 1966088 | tf_op jit(solution)/shard_map/ppermute | solution.py:389
  98.5 1.1 copy-done.11
  99.6 18.4 %project.2 = (f32[1024,640]{1,0:T(8,128)}, bf16[4,1024,1280]{2,1,0:T(8,128)(2,1)}, f32[1024,128]{1,0:T(8,128)S(1)}, f32[1024,128]{1,0:T(8,128)S(1)}) custom-call(s32[5]{0:T(128)S(1)} %stack.75.where, f32[2]{0:T(128)S(1)} %pad_maximum_fusion.scalars, f32[2,8,640]{2,1,0:T(8,128)S(1)} %get-tuple-element.45.sums, bf16[1024,640]{1,0:T(8,128)(2,1)} %sample.3, ...), custom_call_target="tpu_custom_call" | custom-call | flops 1 | bytes 1 | tf_op jit(solution)/shard_map/project/pallas_call | solution.py:257
  120.6 1.4 collective-permute-start.19
  122.5 2.3 %copy.16 = f32[1,2,5120]{1,2,0:T(8,128)} copy(f32[1,2,5120]{2,1,0:T(2,128)S(1)} %copy-done.28) | data formatting | bytes 81920 | tf_op args[4]
  127.2 13.3 %project.3 = (f32[1024,640]{1,0:T(8,128)}, bf16[4,1024,1280]{2,1,0:T(8,128)(2,1)}, bf16[640,1024]{1,0:T(8,128)(2,1)}, f32[1024,128]{1,0:T(8,128)S(1)}, f32[1024,128]{1,0:T(8,128)S(1)}, /*index=5*/f32[640,2]{1,0:T(8,128)S(1)}) custom-call(s32[5]{0:T(128)S(1)} %stack.75.where, f32[2]{0:T(128)S(1)} %pad_maximum_fusion.scalars, ...), custom_call_target="tpu_custom_call", output_to_operand_aliasing={{1}: (13, {})} | custom-call | flops 1 | bytes 1 | tf_op jit(solution)/shard_map/project/pallas_call | solution.py:257
  140.6 1.3 copy-done
  141.9 4.5 %outer.4 = (bf16[640,640]{1,0:T(8,128)(2,1)S(1)}, bf16[640,640]{1,0:T(8,128)(2,1)S(1)}) custom-call(s32[2]{0:T(128)S(1)} %pad_add_fusion.2.picks, f32[4,2,1280]{2,1,0:T(2,128)S(1)} %bitcast.44, f32[640,2]{1,0:T(8,128)S(1)} %get-tuple-element.60.edge, bf16[640,1024]{1,0:T(8,128)(2,1)S(1)} %copy-done, bf16[4,1024,1280]{2,1,0:T(8,128)(2,1)} %get-tuple-element.59.inputs), custom_call_target="tpu_custom_call" | custom-call | flops 1 | bytes 1 | tf_op jit(solution)/shard_map/outer/pallas_call | solution.py:299
  146.4 4.5 %outer.3 = (bf16[640,640]{1,0:T(8,128)(2,1)S(1)}, bf16[640,640]{1,0:T(8,128)(2,1)S(1)}) custom-call(s32[2]{0:T(128)S(1)} %pad_add_fusion.1.picks, f32[4,2,1280]{2,1,0:T(2,128)S(1)} %bitcast.45, f32[640,2]{1,0:T(8,128)S(1)} %get-tuple-element.60.edge, bf16[640,1024]{1,0:T(8,128)(2,1)S(1)} %copy-done, bf16[4,1024,1280]{2,1,0:T(8,128)(2,1)} %get-tuple-element.59.inputs), custom_call_target="tpu_custom_call" | custom-call | flops 1 | bytes 1 | tf_op jit(solution)/shard_map/outer/pallas_call | solution.py:299
  153.7 1.4 collective-permute-start.26
  155.1 3.4 %slice_bitcast_fusion = bf16[1024,1280]{1,0:T(8,128)(2,1)} fusion(bf16[4,1024,1280]{2,1,0:T(8,128)(2,1)} %get-tuple-element.59.inputs), kind=kLoop, calls=%fused_computation.17 | loop fusion | bytes 5242880 | tf_op jit(solution)/shard_map/squeeze | solution.py:488
  158.5 9.2 %scale.3 = (bf16[5120,640]{1,0:T(8,128)(2,1)}, f32[2,8,640]{2,1,0:T(8,128)S(1)}) custom-call(s32[4]{0:T(128)S(1)} %pad_add_fusion.where, f32[5120,2]{1,0:T(8,128)} %bitcast.47, bf16[1280,640]{1,0:T(8,128)(2,1)} %weight.2, bf16[640,640]{1,0:T(8,128)(2,1)} %collective-permute-done.15.refs_0_, bf16[640,640]{1,0:T(8,128)(2,1)S(1)} %collective-permute-done.19.refs_1_, ...), custom_call_target="tpu_custom_call" | custom-call | flops 1 | bytes 1 | tf_op jit(solution)/shard_map/scale/pallas_call | solution.py:101
  167.7 4.5 %fusion.6 = f32[1024,640]{1,0:T(8,128)S(1)} fusion(bf16[4,1024,1280]{2,1,0:T(8,128)(2,1)} %get-tuple-element.59.inputs, bf16[5120,640]{1,0:T(8,128)(2,1)} %get-tuple-element.72), kind=kOutput, calls=%fused_computation.8 | convolution fusion | flops 1677721600 | bytes 6881280 | tf_op jit(solution)/shard_map/dot_general | solution.py:492
  172.6 9.0 %outer.5 = (f32[640,640]{1,0:T(8,128)S(1)}, f32[640,640]{1,0:T(8,128)S(1)}, f32[640,640]{1,0:T(8,128)}, f32[640,640]{1,0:T(8,128)}) custom-call(s32[4]{0:T(128)S(1)} %pad_add_fusion.3.picks, f32[4,2,1280]{2,1,0:T(2,128)S(1)} %bitcast.46, f32[640,2]{1,0:T(8,128)S(1)} %get-tuple-element.60.edge, bf16[640,1024]{1,0:T(8,128)(2,1)S(1)} %copy-done.1, ...), custom_call_target="tpu_custom_call" | custom-call | flops 1 | bytes 1 | tf_op jit(solution)/shard_map/outer/pallas_call | solution.py:299
  181.7 5.1 %fusion.8 = f32[1024,640]{1,0:T(8,128)S(1)} fusion(bf16[4,1024,1280]{2,1,0:T(8,128)(2,1)} %get-tuple-element.59.inputs, bf16[5120,640]{1,0:T(8,128)(2,1)} %get-tuple-element.72), kind=kOutput, calls=%fused_computation.10 | convolution fusion | flops 1677721600 | bytes 6881280 | tf_op jit(solution)/shard_map/dot_general | solution.py:492
  186.8 1.5 add_convert_fusion
  188.3 1.1 collective-permute-start.31
  190.2 3.8 %fusion.14 = f32[1024,640]{1,0:T(8,128)S(1)} fusion(bf16[1024,1280]{1,0:T(8,128)(2,1)S(1)} %copy-done.23, bf16[5120,640]{1,0:T(8,128)(2,1)} %get-tuple-element.72), kind=kOutput, calls=%fused_computation.23 | convolution fusion | flops 1677721600 | bytes 6881280 | tf_op jit(solution)/shard_map/dot_general | solution.py:492
  194.0 5.8 %fusion.3 = (f32[]{:T(128)}, f32[1024,640]{1,0:T(8,128)S(1)}) fusion(bf16[1024,640]{1,0:T(8,128)(2,1)S(1)} %copy-done.17, bf16[1024,640]{1,0:T(8,128)(2,1)S(1)} %copy-done.19, f32[]{:T(128)} %bitcast, f32[640]{0:T(1024)S(1)} %get-tuple-element.84, f32[640]{0:T(1024)S(1)} %get-tuple-element.83, f32[1024]{0:T(1024)S(1)} %get-tuple-element.93, ...), kind=kOutput, calls=%fused_computation.5 | convolution fusion | flops 1686896640 | bytes 17380868 | tf_op jit(solution)/shard_map/dot_general | solution.py:492
  199.8 1.4 collective-permute-done.27
  202.5 1.4 collective-permute-start.28
  203.9 2.3 %collective-permute-done.28 = f32[1,1]{1,0:T(1,128)} collective-permute-done((f32[1,1]{1,0:T(1,128)}, f32[1,1]{1,0:T(1,128)}, u32[]{:S(2)}, u32[]{:S(2)}) %collective-permute-start.28) | collective-permute-done | bytes 36 | tf_op jit(solution)/shard_map/ppermute | solution.py:498
  206.8 2.9 %collective-permute-start.29 = (f32[1,1]{1,0:T(1,128)}, f32[1,1]{1,0:T(1,128)}, u32[]{:S(2)}, u32[]{:S(2)}) collective-permute-start(f32[1,1]{1,0:T(1,128)} %add.126), channel_id=1, source_target_pairs={{0,4},{1,5},{2,6},{3,7},{4,0},{5,1},{6,2},{7,3},{8,12},{9,13},{10,... | collective-permute-start | bytes 20 | tf_op jit(solution)/shard_map/ppermute | solution.py:498
  209.8 1.7 collective-permute-done.29
  212.1 1.7 multiply_reduce_fusion
  214.5 5.1 %finish.1 = f32[2,640,640]{2,1,0:T(8,128)} custom-call(f32[640,640]{1,0:T(8,128)S(1)} %get-tuple-element.79.refs_0_, bf16[640,640]{1,0:T(8,128)(2,1)S(1)} %collective-permute-done.25.refs_1_, bf16[640,640]{1,0:T(8,128)(2,1)S(1)} %collective-permute-done.30.refs_2_, f32[640,640]{1,0:T(8,128)} %copy-done.3, ...), custom_call_target="tpu_custom_call" | custom-call | tf_op jit(solution)/shard_map/finish/pallas_call | solution.py:335
  (110 shorter events, 17.9 us)
Async XLA Ops:
  0.6 39.6 %collective-permute-start = (bf16[1280,640]{1,0:T(8,128)(2,1)}, bf16[1280,640]{1,0:T(8,128)(2,1)S(1)}, u32[]{:S(2)}, u32[]{:S(2)}) collective-permute-start(bf16[1280,640]{1,0:T(8,128)(2,1)} %weight.1), channel_id=1, source_target_pairs={{0,8},{8,0},{16,24},{24,16},{1,9},{9,1},{17,25},{25,17},{2,10},{10... | collective-permute-start | bytes 4915208 | tf_op jit(solution)/shard_map/ppermute | solution.py:27
  3.6 37.9 %collective-permute-start.6 = (bf16[1280,640]{1,0:T(8,128)(2,1)}, bf16[1280,640]{1,0:T(8,128)(2,1)S(1)}, u32[]{:S(2)}, u32[]{:S(2)}) collective-permute-start(bf16[1280,640]{1,0:T(8,128)(2,1)} %weight.1), channel_id=1, source_target_pairs={{0,16},{8,24},{16,0},{24,8},{1,17},{9,25},{17,1},{25,9},{2,18},{10... | collective-permute-start | bytes 4915208 | tf_op jit(solution)/shard_map/ppermute | solution.py:27
  8.1 34.8 %copy-start.18 = (bf16[1024,640]{1,0:T(8,128)(2,1)}, bf16[1024,640]{1,0:T(8,128)(2,1)S(1)}, u32[]{:S(2)}) copy-start(bf16[1024,640]{1,0:T(8,128)(2,1)S(1)} %fusion.1.refs_0_) | copy-start | bytes 3932164
  8.1 38.9 %copy-start.21 = (bf16[1280,640]{1,0:T(8,128)(2,1)S(1)}, bf16[1280,640]{1,0:T(8,128)(2,1)}, u32[]{:S(2)}) copy-start(bf16[1280,640]{1,0:T(8,128)(2,1)} %weight.2) | copy-start | bytes 4915204
  8.2 17.8 %collective-permute-start.1 = (bf16[512,640]{1,0:T(8,128)(2,1)S(1)}, bf16[512,640]{1,0:T(8,128)(2,1)S(1)}, u32[]{:S(2)}, u32[]{:S(2)}) collective-permute-start(bf16[512,640]{1,0:T(8,128)(2,1)S(1)} %get-tuple-element.92), channel_id=1, source_target_pairs={{0,4},{1,5},{4,6},{5,7},{6,2},{7,3},{2,0},{3,1},{8,12},{9,13},{12,... | collective-permute-start | bytes 1966088 | tf_op jit(solution)/shard_map/ppermute | solution.py:389
  10.9 28.3 %collective-permute-start.3 = (bf16[1024,640]{1,0:T(8,128)(2,1)S(1)}, bf16[1024,640]{1,0:T(8,128)(2,1)S(1)}, u32[]{:S(2)}, u32[]{:S(2)}) collective-permute-start(bf16[1024,640]{1,0:T(8,128)(2,1)S(1)} %fusion.1.refs_0_), channel_id=1, source_target_pairs={{0,1},{1,0},{2,3},{3,2},{4,5},{5,4},{6,7},{7,6},{8,9},{9,8},{10,11... | collective-permute-start | bytes 3932168 | tf_op jit(solution)/shard_map/ppermute | solution.py:400
  10.9 27.5 %collective-permute-start.4 = (bf16[512,640]{1,0:T(8,128)(2,1)S(1)}, bf16[512,640]{1,0:T(8,128)(2,1)}, u32[]{:S(2)}, u32[]{:S(2)}) collective-permute-start(bf16[512,640]{1,0:T(8,128)(2,1)S(1)} %get-tuple-element.91), channel_id=1, source_target_pairs={{0,4},{1,5},{4,6},{5,7},{6,2},{7,3},{2,0},{3,1},{8,12},{9,13},{12,... | collective-permute-start | bytes 1966088 | tf_op jit(solution)/shard_map/ppermute | solution.py:389
  26.0 22.3 %copy-start.8 = (bf16[512,640]{1,0:T(8,128)(2,1)}, bf16[512,640]{1,0:T(8,128)(2,1)S(1)}, u32[]{:S(2)}) copy-start(bf16[512,640]{1,0:T(8,128)(2,1)S(1)} %collective-permute-done.1.refs_2_) | copy-start | bytes 1966084
  26.0 12.3 %collective-permute-start.2 = (bf16[512,640]{1,0:T(8,128)(2,1)S(1)}, bf16[512,640]{1,0:T(8,128)(2,1)S(1)}, u32[]{:S(2)}, u32[]{:S(2)}) collective-permute-start(bf16[512,640]{1,0:T(8,128)(2,1)S(1)} %collective-permute-done.1.refs_2_), channel_id=1, source_target_pairs={{0,1},{1,0},{2,3},{3,2},{4,5},{5,4},{6,7},{7,6},{8,9},{9,8},{10,11... | collective-permute-start | bytes 1966088 | tf_op jit(solution)/shard_map/ppermute | solution.py:393
  40.3 40.6 %copy-start.12 = (f32[1,2,5120]{2,1,0:T(2,128)S(1)}, f32[1,2,5120]{2,1,0:T(2,128)}, u32[]{:S(2)}) copy-start(f32[1,2,5120]{2,1,0:T(2,128)} %param.14) | copy-start | bytes 122884
  40.3 22.7 %collective-permute-start.5 = (bf16[640,640]{1,0:T(8,128)(2,1)S(1)}, bf16[640,640]{1,0:T(8,128)(2,1)S(1)}, u32[]{:S(2)}, u32[]{:S(2)}) collective-permute-start(bf16[640,640]{1,0:T(8,128)(2,1)S(1)} %slice.56), channel_id=1, source_target_pairs={{0,16},{8,24},{16,0},{24,8},{1,17},{9,25},{17,1},{25,9},{2,18},{10... | collective-permute-start | bytes 2457608 | tf_op jit(solution)/shard_map/ppermute | solution.py:27
  42.8 40.4 %copy-start.2 = (bf16[1280,640]{1,0:T(8,128)(2,1)S(1)}, bf16[1280,640]{1,0:T(8,128)(2,1)}, u32[]{:S(2)}) copy-start(bf16[1280,640]{1,0:T(8,128)(2,1)} %weight.1) | copy-start | bytes 4915204
  42.9 21.2 %collective-permute-start.7 = (bf16[640,640]{1,0:T(8,128)(2,1)S(1)}, bf16[640,640]{1,0:T(8,128)(2,1)S(1)}, u32[]{:S(2)}, u32[]{:S(2)}) collective-permute-start(bf16[640,640]{1,0:T(8,128)(2,1)S(1)} %slice.57), channel_id=1, source_target_pairs={{0,8},{8,0},{16,24},{24,16},{1,9},{9,1},{17,25},{25,17},{2,10},{10... | collective-permute-start | bytes 2457608 | tf_op jit(solution)/shard_map/ppermute | solution.py:27
  44.4 15.1 %collective-permute-start.8 = (bf16[512,640]{1,0:T(8,128)(2,1)S(1)}, bf16[512,640]{1,0:T(8,128)(2,1)}, u32[]{:S(2)}, u32[]{:S(2)}) collective-permute-start(bf16[512,640]{1,0:T(8,128)(2,1)S(1)} %collective-permute-done.1.refs_2_), channel_id=1, source_target_pairs={{0,4},{1,5},{4,6},{5,7},{6,2},{7,3},{2,0},{3,1},{8,12},{9,13},{12,... | collective-permute-start | bytes 1966088 | tf_op jit(solution)/shard_map/ppermute | solution.py:389
  48.3 30.2 %collective-permute-start.16 = (bf16[640,640]{1,0:T(8,128)(2,1)}, bf16[640,640]{1,0:T(8,128)(2,1)}, u32[]{:S(2)}, u32[]{:S(2)}) collective-permute-start(bf16[640,640]{1,0:T(8,128)(2,1)} %get-tuple-element.89), channel_id=1, source_target_pairs={{0,16},{8,24},{16,0},{24,8},{1,17},{9,25},{17,1},{25,9},{2,18},{10... | collective-permute-start | bytes 2457608 | tf_op jit(solution)/shard_map/ppermute | solution.py:27
  49.1 30.3 %collective-permute-start.15 = (bf16[640,640]{1,0:T(8,128)(2,1)}, bf16[640,640]{1,0:T(8,128)(2,1)}, u32[]{:S(2)}, u32[]{:S(2)}) collective-permute-start(bf16[640,640]{1,0:T(8,128)(2,1)} %get-tuple-element.90), channel_id=1, source_target_pairs={{0,8},{8,0},{16,24},{24,16},{1,9},{9,1},{17,25},{25,17},{2,10},{10... | collective-permute-start | bytes 2457608 | tf_op jit(solution)/shard_map/ppermute | solution.py:27
  59.6 19.0 %collective-permute-start.12 = (bf16[512,640]{1,0:T(8,128)(2,1)}, bf16[512,640]{1,0:T(8,128)(2,1)}, u32[]{:S(2)}, u32[]{:S(2)}) collective-permute-start(bf16[512,640]{1,0:T(8,128)(2,1)} %collective-permute-done.4.refs_4_), channel_id=1, source_target_pairs={{0,4},{1,5},{4,6},{5,7},{6,2},{7,3},{2,0},{3,1},{8,12},{9,13},{12,... | collective-permute-start | bytes 1966088 | tf_op jit(solution)/shard_map/ppermute | solution.py:389
  65.0 29.0 %collective-permute-start.9 = (bf16[512,640]{1,0:T(8,128)(2,1)}, bf16[512,640]{1,0:T(8,128)(2,1)}, u32[]{:S(2)}, u32[]{:S(2)}) collective-permute-start(bf16[512,640]{1,0:T(8,128)(2,1)} %collective-permute-done.8.refs_6_), channel_id=1, source_target_pairs={{0,4},{1,5},{4,6},{5,7},{6,2},{7,3},{2,0},{3,1},{8,12},{9,13},{12,... | collective-permute-start | bytes 1966088 | tf_op jit(solution)/shard_map/ppermute | solution.py:389
  67.8 29.0 %collective-permute-start.10 = (bf16[512,640]{1,0:T(8,128)(2,1)}, bf16[512,640]{1,0:T(8,128)(2,1)}, u32[]{:S(2)}, u32[]{:S(2)}) collective-permute-start(bf16[512,640]{1,0:T(8,128)(2,1)} %collective-permute-done.4.refs_4_), channel_id=1, source_target_pairs={{0,1},{1,0},{2,3},{3,2},{4,5},{5,4},{6,7},{7,6},{8,9},{9,8},{10,11... | collective-permute-start | bytes 1966088 | tf_op jit(solution)/shard_map/ppermute | solution.py:393
  78.6 18.8 %collective-permute-start.13 = (bf16[512,640]{1,0:T(8,128)(2,1)}, bf16[512,640]{1,0:T(8,128)(2,1)}, u32[]{:S(2)}, u32[]{:S(2)}) collective-permute-start(bf16[512,640]{1,0:T(8,128)(2,1)} %collective-permute-done.12.refs_8_), channel_id=1, source_target_pairs={{0,1},{1,0},{2,3},{3,2},{4,5},{5,4},{6,7},{7,6},{8,9},{9,8},{10,11... | collective-permute-start | bytes 1966088 | tf_op jit(solution)/shard_map/ppermute | solution.py:393
  78.6 18.8 %collective-permute-start.11 = (bf16[512,640]{1,0:T(8,128)(2,1)}, bf16[512,640]{1,0:T(8,128)(2,1)}, u32[]{:S(2)}, u32[]{:S(2)}) collective-permute-start(bf16[512,640]{1,0:T(8,128)(2,1)} %collective-permute-done.8.refs_6_), channel_id=1, source_target_pairs={{0,1},{1,0},{2,3},{3,2},{4,5},{5,4},{6,7},{7,6},{8,9},{9,8},{10,11... | collective-permute-start | bytes 1966088 | tf_op jit(solution)/shard_map/ppermute | solution.py:393
  79.4 42.6 %collective-permute-start.22 = (bf16[640,640]{1,0:T(8,128)(2,1)}, bf16[640,640]{1,0:T(8,128)(2,1)}, u32[]{:S(2)}, u32[]{:S(2)}) collective-permute-start(bf16[640,640]{1,0:T(8,128)(2,1)} %get-tuple-element.89), channel_id=1, source_target_pairs={{0,8},{8,0},{16,24},{24,16},{1,9},{9,1},{17,25},{25,17},{2,10},{10... | collective-permute-start | bytes 2457608 | tf_op jit(solution)/shard_map/ppermute | solution.py:27
  94.0 27.9 %collective-permute-start.17 = (bf16[512,640]{1,0:T(8,128)(2,1)}, bf16[512,640]{1,0:T(8,128)(2,1)S(1)}, u32[]{:S(2)}, u32[]{:S(2)}) collective-permute-start(bf16[512,640]{1,0:T(8,128)(2,1)} %collective-permute-done.12.refs_8_), channel_id=1, source_target_pairs={{0,4},{1,5},{4,6},{5,7},{6,2},{7,3},{2,0},{3,1},{8,12},{9,13},{12,... | collective-permute-start | bytes 1966088 | tf_op jit(solution)/shard_map/ppermute | solution.py:389
  96.8 28.2 %collective-permute-start.21 = (bf16[640,640]{1,0:T(8,128)(2,1)}, bf16[640,640]{1,0:T(8,128)(2,1)S(1)}, u32[]{:S(2)}, u32[]{:S(2)}) collective-permute-start(bf16[640,640]{1,0:T(8,128)(2,1)} %get-tuple-element.90), channel_id=1, source_target_pairs={{0,16},{8,24},{16,0},{24,8},{1,17},{9,25},{17,1},{25,9},{2,18},{10... | collective-permute-start | bytes 2457608 | tf_op jit(solution)/shard_map/ppermute | solution.py:27
  99.6 22.9 %copy-start.28 = (f32[1,2,5120]{2,1,0:T(2,128)S(1)}, f32[1,2,5120]{2,1,0:T(2,128)}, u32[]{:S(2)}) copy-start(f32[1,2,5120]{2,1,0:T(2,128)} %param.13) | copy-start | bytes 122884
  119.6 5.2 %copy-start.29 = (f32[1,640]{1,0:T(1,128)S(1)}, f32[1,640]{1,0:T(1,128)}, u32[]{:S(2)}) copy-start(f32[1,640]{1,0:T(1,128)} %param.17) | copy-start | bytes 7684
  119.6 21.0 %collective-permute-start.20 = (bf16[640,640]{1,0:T(8,128)(2,1)}, bf16[640,640]{1,0:T(8,128)(2,1)S(1)}, u32[]{:S(2)}, u32[]{:S(2)}) collective-permute-start(bf16[640,640]{1,0:T(8,128)(2,1)} %collective-permute-done.16.refs_3_), channel_id=1, source_target_pairs={{0,8},{8,0},{16,24},{24,16},{1,9},{9,1},{17,25},{25,17},{2,10},{10... | collective-permute-start | bytes 2457608 | tf_op jit(solution)/shard_map/ppermute | solution.py:27
  120.6 20.0 %collective-permute-start.19 = (bf16[640,640]{1,0:T(8,128)(2,1)}, bf16[640,640]{1,0:T(8,128)(2,1)S(1)}, u32[]{:S(2)}, u32[]{:S(2)}) collective-permute-start(bf16[640,640]{1,0:T(8,128)(2,1)} %collective-permute-done.15.refs_0_), channel_id=1, source_target_pairs={{0,16},{8,24},{16,0},{24,8},{1,17},{9,25},{17,1},{25,9},{2,18},{10... | collective-permute-start | bytes 2457608 | tf_op jit(solution)/shard_map/ppermute | solution.py:27
  122.0 3.1 %collective-permute-start.14 = (bf16[512,640]{1,0:T(8,128)(2,1)}, bf16[512,640]{1,0:T(8,128)(2,1)}, u32[]{:S(2)}, u32[]{:S(2)}) collective-permute-start(bf16[512,640]{1,0:T(8,128)(2,1)} %collective-permute-done.9.refs_0_), channel_id=1, source_target_pairs={{0,1},{1,0},{2,3},{3,2},{4,5},{5,4},{6,7},{7,6},{8,9},{9,8},{10,11... | collective-permute-start | bytes 1966088 | tf_op jit(solution)/shard_map/ppermute | solution.py:393
  122.0 3.2 %collective-permute-start.18 = (bf16[512,640]{1,0:T(8,128)(2,1)S(1)}, bf16[512,640]{1,0:T(8,128)(2,1)}, u32[]{:S(2)}, u32[]{:S(2)}) collective-permute-start(bf16[512,640]{1,0:T(8,128)(2,1)S(1)} %collective-permute-done.17.refs_2_), channel_id=1, source_target_pairs={{0,1},{1,0},{2,3},{3,2},{4,5},{5,4},{6,7},{7,6},{8,9},{9,8},{10,11... | collective-permute-start | bytes 1966088 | tf_op jit(solution)/shard_map/ppermute | solution.py:393
  150.9 35.8 %collective-permute-start.24 = (bf16[640,640]{1,0:T(8,128)(2,1)S(1)}, bf16[640,640]{1,0:T(8,128)(2,1)}, u32[]{:S(2)}, u32[]{:S(2)}) collective-permute-start(bf16[640,640]{1,0:T(8,128)(2,1)S(1)} %get-tuple-element.66), channel_id=1, source_target_pairs={{0,16},{8,24},{16,0},{24,8},{1,17},{9,25},{17,1},{25,9},{2,18},{10... | collective-permute-start | bytes 2457608 | tf_op jit(solution)/shard_map/ppermute | solution.py:27
  151.7 37.7 %collective-permute-start.23 = (bf16[640,640]{1,0:T(8,128)(2,1)S(1)}, bf16[640,640]{1,0:T(8,128)(2,1)S(1)}, u32[]{:S(2)}, u32[]{:S(2)}) collective-permute-start(bf16[640,640]{1,0:T(8,128)(2,1)S(1)} %get-tuple-element.65), channel_id=1, source_target_pairs={{0,8},{8,0},{16,24},{24,16},{1,9},{9,1},{17,25},{25,17},{2,10},{10... | collective-permute-start | bytes 2457608 | tf_op jit(solution)/shard_map/ppermute | solution.py:27
  152.7 47.2 %collective-permute-start.25 = (bf16[640,640]{1,0:T(8,128)(2,1)S(1)}, bf16[640,640]{1,0:T(8,128)(2,1)S(1)}, u32[]{:S(2)}, u32[]{:S(2)}) collective-permute-start(bf16[640,640]{1,0:T(8,128)(2,1)S(1)} %get-tuple-element.67), channel_id=1, source_target_pairs={{0,8},{8,0},{16,24},{24,16},{1,9},{9,1},{17,25},{25,17},{2,10},{10... | collective-permute-start | bytes 2457608 | tf_op jit(solution)/shard_map/ppermute | solution.py:27
  153.7 46.1 %collective-permute-start.26 = (bf16[640,640]{1,0:T(8,128)(2,1)S(1)}, bf16[640,640]{1,0:T(8,128)(2,1)S(1)}, u32[]{:S(2)}, u32[]{:S(2)}) collective-permute-start(bf16[640,640]{1,0:T(8,128)(2,1)S(1)} %get-tuple-element.68), channel_id=1, source_target_pairs={{0,16},{8,24},{16,0},{24,8},{1,17},{9,25},{17,1},{25,9},{2,18},{10... | collective-permute-start | bytes 2457608 | tf_op jit(solution)/shard_map/ppermute | solution.py:27
  167.7 4.9 %copy-start.1 = (bf16[640,1024]{1,0:T(8,128)(2,1)S(1)}, bf16[640,1024]{1,0:T(8,128)(2,1)}, u32[]{:S(2)}) copy-start(bf16[640,1024]{1,0:T(8,128)(2,1)} %get-tuple-element.78.flipped) | copy-start | bytes 3932164
  181.6 5.1 %copy-start.3 = (f32[640,640]{1,0:T(8,128)}, f32[640,640]{1,0:T(8,128)S(1)}, u32[]{:S(2)}) copy-start(f32[640,640]{1,0:T(8,128)S(1)} %get-tuple-element.81.refs_3_) | copy-start | bytes 4915204
  181.7 5.1 %copy-start.25 = (f32[640,640]{1,0:T(8,128)S(1)}, f32[640,640]{1,0:T(8,128)}, u32[]{:S(2)}) copy-start(f32[640,640]{1,0:T(8,128)} %get-tuple-element.82) | copy-start | bytes 4915204
  186.7 2.7 %copy-start.24 = (f32[640,640]{1,0:T(8,128)S(1)}, f32[640,640]{1,0:T(8,128)}, u32[]{:S(2)}) copy-start(f32[640,640]{1,0:T(8,128)} %get-tuple-element.80) | copy-start | bytes 4915204
  186.8 3.4 %copy-start.23 = (bf16[1024,1280]{1,0:T(8,128)(2,1)S(1)}, bf16[1024,1280]{1,0:T(8,128)(2,1)}, u32[]{:S(2)}) copy-start(bf16[1024,1280]{1,0:T(8,128)(2,1)} %slice_bitcast_fusion) | copy-start | bytes 7864324
  188.3 26.2 %collective-permute-start.31 = (bf16[640,640]{1,0:T(8,128)(2,1)S(1)}, bf16[640,640]{1,0:T(8,128)(2,1)S(1)}, u32[]{:S(2)}, u32[]{:S(2)}) collective-permute-start(bf16[640,640]{1,0:T(8,128)(2,1)S(1)} %add_convert_fusion), channel_id=1, source_target_pairs={{0,8},{8,0},{16,24},{24,16},{1,9},{9,1},{17,25},{25,17},{2,10},{10... | collective-permute-start | bytes 2457608 | tf_op jit(solution)/shard_map/ppermute | solution.py:27
  189.6 4.4 %copy-start.17 = (bf16[1024,640]{1,0:T(8,128)(2,1)S(1)}, bf16[1024,640]{1,0:T(8,128)(2,1)}, u32[]{:S(2)}) copy-start(bf16[1024,640]{1,0:T(8,128)(2,1)} %sample.3) | copy-start | bytes 3932164
  189.6 4.4 %copy-start.19 = (bf16[1024,640]{1,0:T(8,128)(2,1)S(1)}, bf16[1024,640]{1,0:T(8,128)(2,1)}, u32[]{:S(2)}) copy-start(bf16[1024,640]{1,0:T(8,128)(2,1)} %copy-done.18) | copy-start | bytes 3932164
  189.6 24.9 %collective-permute-start.30 = (bf16[640,640]{1,0:T(8,128)(2,1)S(1)}, bf16[640,640]{1,0:T(8,128)(2,1)S(1)}, u32[]{:S(2)}, u32[]{:S(2)}) collective-permute-start(bf16[640,640]{1,0:T(8,128)(2,1)S(1)} %add_convert_fusion.1), channel_id=1, source_target_pairs={{0,16},{8,24},{16,0},{24,8},{1,17},{9,25},{17,1},{25,9},{2,18},{10... | collective-permute-start | bytes 2457608 | tf_op jit(solution)/shard_map/ppermute | solution.py:27
  194.0 18.1 %copy-start.22 = (f32[1024,640]{1,0:T(8,128)S(1)}, f32[1024,640]{1,0:T(8,128)}, u32[]{:S(2)}) copy-start(f32[1024,640]{1,0:T(8,128)} %get-tuple-element.76) | copy-start | bytes 7864324
  194.0 18.1 %copy-start.26 = (bf16[1024,640]{1,0:T(8,128)(2,1)S(1)}, bf16[1024,640]{1,0:T(8,128)(2,1)}, u32[]{:S(2)}) copy-start(bf16[1024,640]{1,0:T(8,128)(2,1)} %param.11) | copy-start | bytes 3932164
  199.8 1.4 collective-permute-start.27
  202.5 3.7 %collective-permute-start.28 = (f32[1,1]{1,0:T(1,128)}, f32[1,1]{1,0:T(1,128)}, u32[]{:S(2)}, u32[]{:S(2)}) collective-permute-start(f32[1,1]{1,0:T(1,128)} %add.125), channel_id=1, source_target_pairs={{0,2},{1,3},{2,0},{3,1},{4,6},{5,7},{6,4},{7,5},{8,10},{9,11},{10,... | collective-permute-start | bytes 20 | tf_op jit(solution)/shard_map/ppermute | solution.py:498
  206.8 4.6 %collective-permute-start.29 = (f32[1,1]{1,0:T(1,128)}, f32[1,1]{1,0:T(1,128)}, u32[]{:S(2)}, u32[]{:S(2)}) collective-permute-start(f32[1,1]{1,0:T(1,128)} %add.126), channel_id=1, source_target_pairs={{0,4},{1,5},{2,6},{3,7},{4,0},{5,1},{6,2},{7,3},{8,12},{9,13},{10,... | collective-permute-start | bytes 20 | tf_op jit(solution)/shard_map/ppermute | solution.py:498
  (14 other events, 14.4 us)

commit v4 on v3

--- a/solution.py
+++ b/solution.py
@@ -11,9 +11,9 @@
 EPS = 1e-06
 BF16 = jnp.bfloat16
 F32 = jnp.float32
-VMEM_BYTES = 48 * 1024 * 1024
+MIB = 1024 * 1024
 CHUNKS = 2
-GATES = {'relay': ('cA1', 'own', 'B1'), 'teacher': ('parts', 'parts1'), 'B2': ('A2',), 'A3': ('far0', 'far1'), 'B3': ('A3', 't00', 't01', 'sums'), 'cB1': ('far0', 'far1'), 'cA2': ('far0', 'far1'), 'cB2': ('far0', 'far1'), 'cA3': ('early',), 'cB3': ('early',), 'teacher relay': ('early',)}
+GATES = {'relay': ('cA1',), 'teacher': ('parts', 'parts1'), 'teacher1': ('far0', 'far1'), 'A2': ('B1',), 'B2': ('A2',), 'A3': ('far0', 'far1'), 'B3': ('A3', 'sums'), 'cB1': ('f0', 'f1'), 'cA2': ('soon',), 'cB2': ('sums',), 'cB3': ('early',), 'teacher relay': ('sums',)}
 ANY = pl.BlockSpec(memory_space=pl.ANY)
 SMEM = pl.BlockSpec(memory_space=pltpu.SMEM)
 VMEM = pl.BlockSpec(memory_space=pltpu.VMEM)
@@ -111,7 +111,9 @@
             pltpu.SemaphoreType.DMA((count,)),
             pltpu.SemaphoreType.DMA((count,)),
         ],
-        compiler_params=pltpu.CompilerParams(vmem_limit_bytes=VMEM_BYTES),
+        compiler_params=pltpu.CompilerParams(
+            vmem_limit_bytes=2 * width * (cols + 256) + 8 * MIB
+        ),
         cost_estimate=pl.CostEstimate(
             flops=1, bytes_accessed=1, transcendentals=0
         ),
@@ -120,21 +122,22 @@
 
 
 def project_kernel(
-    first, last, hops, core_at, where, scalars, sums, sample, other, scaled, *refs
+    prior, last, hops, where, scalars, sums, sample, other, scaled, *refs
 ):
-    count = len(hops)
-    pieces, refs = refs[: sum(len(hop) for hop in hops)], refs[sum(len(hop) for hop in hops) :]
-    if not first:
-        carry, means, powers, _, *refs = refs
+    count = sum(len(hop) for hop in hops)
+    pieces, refs = refs[:count], refs[count:]
+    if prior:
+        carry, carried, _, *refs = refs
     if last:
-        velocity, inputs, flipped, centers, factors, edge, *refs = refs
+        velocity, inputs, stats, flipped, edge, *refs = refs
     else:
-        velocity, inputs, centers, factors, *refs = refs
-    held, full, tail, sems, wsems, osems = refs
-    rows, depth = held.shape[1:]
+        velocity, inputs, stats, *refs = refs
+    held, full, moments, tail, sems, wsems, osems = refs
+    slots, rows, depth = held.shape
     cols = velocity.shape[1]
-    group = depth // cols
-    core = where[core_at]
+    width = scaled.shape[0]
+    parts = 2 * cols // depth
+    core = where[where.shape[0] - 1]
     loads, arrivals, drains = [], [], []
     index = 0
     for n, hop in enumerate(hops):
@@ -143,7 +146,7 @@
             owner = core if side == 0 else 1 - core
             ref = pieces[index]
             at = pl.ds(low, ref.shape[0])
-            if group == 2:
+            if parts == 1:
                 lanes = pl.ds(pl.multiple_of(owner * cols, cols), cols)
                 spot = held.at[n, at, lanes]
             else:
@@ -158,7 +161,6 @@
                 scaled.at[pl.ds(pl.multiple_of(place * span, span), span)], full.at[n], wsems.at[n]
             )
         )
-        parts = 2 // group
         drains.append(
             pltpu.make_async_copy(
                 held.at[pl.ds(n * parts, parts)],
@@ -170,49 +172,51 @@
         for copy in copies:
             copy.start()
         load.start()
-    slots = held.shape[0]
-    for n in range(count):
+    piece = 256
+    lane = lax.broadcasted_iota(jnp.int32, (piece, 128), 1)
+    for n in range(len(hops)):
         for copy in arrivals[n]:
             copy.wait()
         loads[n].wait()
         drains[n].start()
-        for part in range(2 // group):
-            slot = n * (2 // group) + part
+        for part in range(parts):
+            slot = n * parts + part
             term = jnp.dot(
                 held[slot], full[n, pl.ds(part * depth, depth), :], preferred_element_type=F32
             )
-            if n or part:
+            if slot:
                 velocity[...] += term
-            elif first:
+            elif prior:
+                velocity[...] = carry[...] + term
+            else:
                 velocity[...] = term
-            else:
-                velocity[...] = carry[...] + term
-    piece = 128
-    many = slots * depth
-    total = many if first else many * (scaled.shape[0] // many)
-    if last:
+            for low in range(0, rows, piece):
+                at = pl.ds(low, piece)
+                if slot == 0 and prior:
+                    moments[at, :] = carried[at, :]
+                elif slot == 0:
+                    near = held[0, at, :128].astype(F32)
+                    near = jnp.sum(near, axis=1, keepdims=True) * (1.0 / 128)
+                    moments[at, :] = jnp.where(lane == 0, near, 0.0)
+                spread = held[slot, at, :].astype(F32) - moments[at, 0:1]
+                sum_ = jnp.sum(spread, axis=1, keepdims=True)
+                power = jnp.sum(spread * spread, axis=1, keepdims=True)
+                more = jnp.where(lane == 1, sum_, jnp.where(lane == 2, power, 0.0))
+                moments[at, :] += more
+    if not last:
+        stats[...] = moments[...]
+    else:
         tail[...] = jnp.zeros_like(tail)
 
-    @pl.loop(0, rows // piece)
-    def _(step):
-        low = pl.multiple_of(step * piece, piece)
-        at = pl.ds(low, piece)
-        sum_ = jnp.zeros((piece, 1), F32)
-        for slot in range(slots):
-            sum_ += jnp.sum(held[slot, at, :].astype(F32), axis=1, keepdims=True)
-        mean = sum_ * (1.0 / many)
-        power = jnp.zeros((piece, 1), F32)
-        for slot in range(slots):
-            spread = held[slot, at, :].astype(F32) - mean
-            power += jnp.sum(spread * spread, axis=1, keepdims=True)
-        if not first:
-            others = scaled.shape[0] - many
-            apart = means[at, 0:1] - mean
-            power += powers[at, 0:1] + apart * apart * (many * others / scaled.shape[0])
-            mean += apart * (others / scaled.shape[0])
-        if last:
-            by = lax.rsqrt(power * (1.0 / scaled.shape[0]) + EPS)
-            power = by
+        @pl.loop(0, rows // piece)
+        def _(step):
+            low = pl.multiple_of(step * piece, piece)
+            at = pl.ds(low, piece)
+            away = moments[at, 1:2] * (1.0 / width)
+            power = jnp.maximum(moments[at, 2:3] * (1.0 / width) - away * away, 0.0)
+            mean = moments[at, 0:1] + away
+            by = lax.rsqrt(power + EPS)
+            stats[at, :] = jnp.where(lane == 0, mean, by)
             value = by * (velocity[at, :] - mean * sums[0, 0:1, :]) + sums[1, 0:1, :]
             velocity[at, :] = value
             target = other[at, :].astype(F32) - sample[at, :].astype(F32)
@@ -221,98 +225,104 @@
             flipped[:, at] = jnp.transpose(sent).astype(BF16)
             tail[0] += jnp.sum((mean * sent).reshape(piece // 8, 8, cols), axis=0)
             tail[1] += jnp.sum(wrong.reshape(piece // 8, 8, cols), axis=0)
-        centers[at, :] = jnp.broadcast_to(mean, (piece, 128))
-        factors[at, :] = jnp.broadcast_to(power, (piece, 128))
-
-    if last:
+
         ends = [jnp.sum(jnp.transpose(tail[i]), axis=1, keepdims=True) for i in range(2)]
         edge[...] = jnp.concatenate(ends, axis=1)
     for copy in drains:
         copy.wait()
 
 
-def project(where, scalars, sums, sample, other, scaled, hops, earlier, last):
+def project(where, scalars, sums, sample, other, scaled, hops, prior, earlier, last):
     clip_rows, cols = sample.shape
     width = scaled.shape[0]
     group = 1 if cols % 128 else 2
     depth = group * cols
     places = width // depth
     slots = len(hops) * 2 // group
-    first = not earlier
     pieces = [piece for hop, _ in hops for piece, _, _ in hop]
     plan = [[(low, side, place) for _, low, side in hop] for hop, place in hops]
-    wide = jax.ShapeDtypeStruct((clip_rows, 128), F32)
     out_shape = [
         jax.ShapeDtypeStruct((clip_rows, cols), F32),
         jax.ShapeDtypeStruct((places, clip_rows, depth), BF16),
+        jax.ShapeDtypeStruct((clip_rows, 128), F32),
     ]
     if last:
         out_shape.append(jax.ShapeDtypeStruct((cols, clip_rows), BF16))
-    out_shape += [wide, wide]
-    if last:
         out_shape.append(jax.ShapeDtypeStruct((cols, 2), F32))
-    if not first:
-        velocity, inputs, means, powers = earlier
-        earlier = [velocity, means, powers, inputs]
+    if prior:
+        velocity, inputs, stats = earlier
+        earlier = [velocity, stats, inputs]
+    need = 2 * slots * depth * (clip_rows + cols) + clip_rows * cols * 20 + clip_rows * 128 * 16
     return pl.pallas_call(
-        functools.partial(project_kernel, first, last, plan, where.shape[0] - 1),
+        functools.partial(project_kernel, prior, last, plan),
         out_shape=out_shape,
-        in_specs=[SMEM, SMEM] + [VMEM] * 3 + [ANY] * (1 + len(pieces)) + ([] if first else [VMEM] * 3 + [ANY]),
+        in_specs=[SMEM, SMEM] + [VMEM] * 3 + [ANY] * (1 + len(pieces))
+        + ([VMEM, VMEM, ANY] if prior else []),
         out_specs=[VMEM, ANY] + [VMEM] * (len(out_shape) - 2),
         scratch_shapes=[
             pltpu.VMEM((slots, clip_rows, depth), BF16),
             pltpu.VMEM((len(hops), 2 * cols, cols), BF16),
+            pltpu.VMEM((clip_rows, 128), F32),
             pltpu.VMEM((2, 8, cols), F32),
             pltpu.SemaphoreType.DMA((len(pieces),)),
             pltpu.SemaphoreType.DMA((len(hops),)),
             pltpu.SemaphoreType.DMA((len(hops),)),
         ],
-        input_output_aliases={} if first else {6 + len(pieces) + 3: 1},
-        compiler_params=pltpu.CompilerParams(vmem_limit_bytes=VMEM_BYTES),
-        cost_estimate=pl.CostEstimate(
-            flops=1, bytes_accessed=1,
-            transcendentals=0,
-        ),
+        input_output_aliases={6 + len(pieces) + 2: 1} if prior else {},
+        compiler_params=pltpu.CompilerParams(vmem_limit_bytes=need + 8 * MIB),
+        cost_estimate=pl.CostEstimate(flops=1, bytes_accessed=1, transcendentals=0),
         name="project",
     )(where, scalars, sums, sample, other, scaled, *pieces, *earlier)
 
 
 def outer_kernel(picks, mod, edge, flipped, inputs, *outs):
     del picks
-    term = jnp.dot(flipped[...], inputs[0], preferred_element_type=F32)
-    term = (term - edge[:, 0:1]) * (1.0 + mod[0, 1:2, :]) + edge[:, 1:2] * mod[0, 0:1, :]
-    for i, out in enumerate(outs):
-
-        @pl.when(pl.program_id(0) == i)
-        def _():
-            out[...] = term.astype(out.dtype)
-
-
-def outer(picks, mod, edge, flipped, inputs, dtype):
+    cols = flipped.shape[0]
+    if inputs.shape[0] == 1:
+        term = jnp.dot(flipped[...], inputs[0], preferred_element_type=F32)
+        terms = [term[:, half * cols : (half + 1) * cols] for half in range(2)]
+        mods = [mod[0, :, half * cols : (half + 1) * cols] for half in range(2)]
+    else:
+        terms = [jnp.dot(flipped[...], inputs[h], preferred_element_type=F32) for h in range(2)]
+        mods = [mod[0], mod[1]]
+    for half in range(2):
+        shift, gain = mods[half][0:1, :], 1.0 + mods[half][1:2, :]
+        term = (terms[half] - edge[:, 0:1]) * gain + edge[:, 1:2] * shift
+        for i, out in enumerate(outs[half::2]):
+
+            @pl.when(pl.program_id(0) == i)
+            def _():
+                out[...] = term.astype(out.dtype)
+
+
+def outer(picks, mod, edge, flipped, inputs, dtypes):
     cols, rows = flipped.shape
     count = len(picks)
     group = inputs.shape[2] // cols
 
     def spot(i, picks):
-        return (picks[i] // group, 0, lax.rem(picks[i], group))
+        return (picks[i], 0, 0)
 
     return pl.pallas_call(
         outer_kernel,
-        out_shape=[jax.ShapeDtypeStruct((cols, cols), dtype)] * count,
+        out_shape=[jax.ShapeDtypeStruct((cols, cols), dtype) for dtype in dtypes],
         grid_spec=pltpu.PrefetchScalarGridSpec(
             num_scalar_prefetch=1,
             grid=(count,),
             in_specs=[
-                pl.BlockSpec((1, 2, cols), spot),
+                pl.BlockSpec((2 // group, 2, group * cols), spot),
                 pl.BlockSpec((cols, 2), lambda i, picks: (0, 0)),
                 pl.BlockSpec((cols, rows), lambda i, picks: (0, 0)),
-                pl.BlockSpec((1, rows, cols), spot),
+                pl.BlockSpec((2 // group, rows, group * cols), spot),
             ],
-            out_specs=[pl.BlockSpec((cols, cols), lambda i, picks: (0, 0))] * count,
+            out_specs=[pl.BlockSpec((cols, cols), lambda i, picks: (0, 0))] * (2 * count),
         ),
-        compiler_params=pltpu.CompilerParams(vmem_limit_bytes=VMEM_BYTES),
+        compiler_params=pltpu.CompilerParams(
+            vmem_limit_bytes=cols * (rows * 16 + cols * (16 * count + 16)) + 6 * MIB
+        ),
         cost_estimate=pl.CostEstimate(
-            flops=1, bytes_accessed=1,
+            flops=4 * rows * cols * cols * count,
+            bytes_accessed=4 * rows * cols * (count + 1) + 4 * cols * cols * count,
             transcendentals=0,
         ),
         name="outer",
@@ -338,7 +348,7 @@
         out_shape=jax.ShapeDtypeStruct((2, cols, cols), F32),
         in_specs=[pl.BlockSpec((cols, lanes), lambda i: (0, i))] * len(parts),
         out_specs=pl.BlockSpec((2, lanes, cols), lambda i: (0, i, 0)),
-        compiler_params=pltpu.CompilerParams(vmem_limit_bytes=VMEM_BYTES),
+        compiler_params=pltpu.CompilerParams(vmem_limit_bytes=cols * cols * 16 + 8 * MIB),
         name="finish",
     )(*parts).reshape(2 * cols, cols)
 
@@ -440,7 +450,15 @@
                 cross(hop, i)
         if hop < hops - 1:
             add_hop(hop)
-    done = project(where, scalars, sums, sample, noise, scaled, tokens, (), False)
+    cut = max(1, hops - 2)
+    done = project(
+        where, scalars, sums, sample, noise, scaled, tokens[:cut], 0, (), False
+    )
+    seen["soon"] = done[2]
+    if cut < hops - 1:
+        done = project(
+            where, scalars, sums, sample, noise, scaled, tokens[cut:], 2 * cols * cut, done, False
+        )
     seen["early"] = done[2]
     for key, block in teacher_parts.items():
         teacher_parts[key] = gated("teacher relay", block)
@@ -448,33 +466,41 @@
     for i in range(CHUNKS):
         cross(hops - 1, i)
     add_hop(hops - 1)
-    fake_velocity, inputs, flipped, centers, factors, edge = project(
-        where, scalars, sums, sample, noise, scaled, tokens[-1:], done, True
+    fake_velocity, inputs, stats, flipped, edge = project(
+        where, scalars, sums, sample, noise, scaled, tokens[-1:], 2 * cols * (hops - 1), done, True
     )
     by_place = jnp.swapaxes(fake_mod[0].reshape(2, shards // group, group * cols), 0, 1)
     flipped = after(flipped, *(teacher_blocks[key] for key in far))
 
-    def terms(keys, left, dtype):
-        picks = [(clip ^ mask) * 2 + half for mask, half in keys]
-        return dict(zip(keys, outer(picks, by_place, edge, left, inputs, dtype)))
+    def going(mask):
+        return [bool(mask & order[0]) for _, order in orders]
 
     held = {}
-    going = [(mask, half) for half, order in orders for mask in range(clips) if mask & order[0]]
-    held.update(terms([key for key in going if key[0] & (key[0] - 1)], flipped, BF16))
-    held.update(terms([key for key in going if key not in held], flipped, BF16))
+
+    def terms(masks, left):
+        dtypes = [BF16 if out else F32 for mask in masks for out in going(mask)]
+        got = outer([clip ^ mask for mask in masks], by_place, edge, left, inputs, dtypes)
+        held.update(zip([(mask, half) for mask in masks for half in range(2)], got))
+
+    ranks = [[m for m in range(clips) if sum(going(m)) == n] for n in (2, 1, 0)]
+    terms(ranks[0], flipped)
+    if ranks[1]:
+        terms(ranks[1], flipped)
     ready = list(held.values())
-    keys = [key for m in range(clips) for key in [(m, 0), (m, 1)] if key not in held]
-    held.update(terms(keys, after(flipped, *ready), F32))
     halves = []
-    firsts, seconds = [], []
+    sent = {key: swap_clip(held[key], orders[key[1]][1][0], clips) for key in held if going(key[0])[key[1]]}
+    firsts = [sent[key] for key in sent if key[0] in ranks[0]]
+    seconds = [sent[key] for key in sent if key[0] not in ranks[0]]
+    terms(ranks[2], after(flipped, *firsts))
     for half, order in orders:
         mine = {mask: [block] for (mask, h), block in held.items() if h == half}
         for bit in order:
             for mask in [mask for mask in mine if mask & bit]:
-                block = sum(part.astype(F32) for part in mine.pop(mask)).astype(BF16)
-                got = swap_clip(block, bit, clips)
+                block = mine.pop(mask)
                 if bit == order[0]:
-                    (firsts if mask & (mask - 1) else seconds).append(got)
+                    got = sent[mask, half]
+                else:
+                    got = swap_clip(sum(part.astype(F32) for part in block).astype(BF16), bit, clips)
                 mine[mask ^ bit].append(got)
         halves.append(mine[0])
     fake_grad = finish(halves)
@@ -486,11 +512,10 @@
     velocity = 0.0
     for p in range(width // depth):
         left = inputs[p]
-        if p == width // depth // 2:
-            left = after(left, *firsts)
+        left = after(left, *firsts) if p == 0 else after(left, velocity)
         right = scaled[p * depth : (p + 1) * depth]
         velocity = velocity + jnp.dot(left, right, preferred_element_type=F32)
-    velocity = factors[:, :1] * (velocity - centers[:, :1] * sums[0, :1]) + sums[1, :1]
+    velocity = stats[:, 1:2] * (velocity - stats[:, 0:1] * sums[0, :1]) + sums[1, :1]
     away = sample.astype(F32) - (noised.astype(F32) - sigma * velocity)
     away = after(jnp.sum(jnp.abs(away)).reshape(1, 1), *seconds)
     bit = 1

time: 220 us -> 229 us (1.041)
  local copies, waits for them, and re-layouts: 25.1 us -> 58.2 us
  Pallas kernels: 72.5 us -> 50 us
  waiting for transfers between devices: 51.6 us -> 60.6 us
  matrix products: 19.1 us -> 11.9 us
  starting transfers between devices: 41 us -> 37.7 us
    unnamed x62 -> x98, local copies, waits for them, and re-layouts: 19 us -> 49.9 us
    ppermute x16, waiting for transfers between devices: 0.5 us -> 10.3 us  [swap_clip(): return lax.ppermute(value, 'clip', [(i, i ^ bit) for i in range(count)])]
    pallas_call x2 -> x3, Pallas kernels: 31.7 us -> 22 us  [project(): pl.pallas_call(functools.partial(project_kernel, prior, last, plan), out_...]
    pallas_call x3, Pallas kernels: 18.1 us -> 10.2 us  [outer(): pl.pallas_call(outer_kernel, out_shape=[jax.ShapeDtypeStruct((cols, cols)...]
    dot_general x4, matrix products: 19.1 us -> 11.9 us  [per_device(): velocity = velocity + jnp.dot(left, right, preferred_element_type=F32)]
    pallas_call x2, Pallas kernels: 17.6 us -> 14.1 us  [scale(): pl.pallas_call(functools.partial(scale_kernel, list(blocks)), out_shape=(...]
  transfers between devices with their start and end apart: 32 -> 32, of which waited for: 10 -> 12; matrix products, arithmetic and copies ran while one was open for 16% -> 14% of each run, Pallas kernels for 27% -> 19%
where the time goes in v4:
time: 229 us; the launch traced here: 228 us
  waiting for transfers between devices  60.6 us (26%)
  local copies, waits for them, and re-layouts  58.2 us (25%)
  Pallas kernels  50 us (22%)
  starting transfers between devices  37.7 us (16%)
  matrix products  11.9 us (5%)
  other arithmetic  5.58 us (2%)
  between operations  4.26 us (2%)
    unnamed x98, local copies, waits for them, and re-layouts  49.9 us
    ppermute x6, waiting for transfers between devices, hop_to(): seen[name] = lax.ppermute(gated(name, source), 'fsdp', ring)  43.5 us
    pallas_call x3, Pallas kernels, project(): pl.pallas_call(functools.partial(project_kernel, prior, last, plan), out_...  22 us
    ppermute x16, starting transfers between devices, swap_clip(): return lax.ppermute(value, 'clip', [(i, i ^ bit) for i in range(count)])  18.1 us
    ppermute x6, starting transfers between devices, hop_to(): seen[name] = lax.ppermute(gated(name, source), 'fsdp', ring)  15.6 us
    pallas_call x2, Pallas kernels, scale(): pl.pallas_call(functools.partial(scale_kernel, list(blocks)), out_shape=(...  14.1 us
    dot_general x4, matrix products, per_device(): velocity = velocity + jnp.dot(left, right, preferred_element_type=F32)  11.9 us
    ppermute x16, waiting for transfers between devices, swap_clip(): return lax.ppermute(value, 'clip', [(i, i ^ bit) for i in range(count)])  10.3 us
  transfers between devices with their start and end apart: 32, of which 12 were waited for; matrix products, arithmetic and copies ran while one was open for 14% of the time, Pallas kernels for 19%

profile of v4, /device:TPU:0, one launch (start us, length us, event | category | flops | bytes accessed | tf_op | source)
XLA Modules:
  0.0 228.2 jit_solution(4531899834173824624)
XLA Ops:
  0.6 3.0 %collective-permute-start = (bf16[1280,640]{1,0:T(8,128)(2,1)}, bf16[1280,640]{1,0:T(8,128)(2,1)S(1)}, u32[]{:S(2)}, u32[]{:S(2)}) collective-permute-start(bf16[1280,640]{1,0:T(8,128)(2,1)} %weight.1), channel_id=1, source_target_pairs={{0,8},{8,0},{16,24},{24,16},{1,9},{9,1},{17,25},{25,17},{2,10},{10... | collective-permute-start | bytes 4915208 | tf_op jit(solution)/shard_map/ppermute | solution.py:27
  5.8 3.3 %fusion.1.refs_0_ = bf16[1024,640]{1,0:T(8,128)(2,1)} fusion(bf16[1024,640]{1,0:T(8,128)(2,1)} %sample.5, bf16[1024,640]{1,0:T(8,128)(2,1)} %other.5, f32[]{:T(128)S(6)} %sub.57, f32[]{:T(128)} %bitcast), kind=kLoop, calls=%fused_computation.3 | loop fusion | flops 3932160 | bytes 3932168 | tf_op jit(solution)/shard_map/convert_element_type | solution.py:373
  9.1 1.5 fusion.19
  10.6 2.6 %collective-permute-start.1 = (bf16[512,640]{1,0:T(8,128)(2,1)S(1)}, bf16[512,640]{1,0:T(8,128)(2,1)S(1)}, u32[]{:S(2)}, u32[]{:S(2)}) collective-permute-start(bf16[512,640]{1,0:T(8,128)(2,1)S(1)} %get-tuple-element.112), channel_id=1, source_target_pairs={{0,4},{1,5},{4,6},{5,7},{6,2},{7,3},{2,0},{3,1},{8,12},{9,13},{12,... | collective-permute-start | bytes 1966088 | tf_op jit(solution)/shard_map/ppermute | solution.py:399
  13.3 1.6 collective-permute-start.6
  14.9 13.6 %collective-permute-done.1.refs_2_ = bf16[512,640]{1,0:T(8,128)(2,1)S(1)} collective-permute-done((bf16[512,640]{1,0:T(8,128)(2,1)S(1)}, bf16[512,640]{1,0:T(8,128)(2,1)S(1)}, u32[]{:S(2)}, u32[]{:S(2)}) %collective-permute-start.1) | collective-permute-done | bytes 655392 | tf_op jit(solution)/shard_map/ppermute | solution.py:399
  28.5 12.3 %collective-permute-done.6.refs_4_ = bf16[512,640]{1,0:T(8,128)(2,1)S(1)} collective-permute-done((bf16[512,640]{1,0:T(8,128)(2,1)S(1)}, bf16[512,640]{1,0:T(8,128)(2,1)S(1)}, u32[]{:S(2)}, u32[]{:S(2)}) %collective-permute-start.6) | collective-permute-done | bytes 655392 | tf_op jit(solution)/shard_map/ppermute | solution.py:399
  40.8 3.4 %collective-permute-start.7 = (bf16[512,640]{1,0:T(8,128)(2,1)S(1)}, bf16[512,640]{1,0:T(8,128)(2,1)}, u32[]{:S(2)}, u32[]{:S(2)}) collective-permute-start(bf16[512,640]{1,0:T(8,128)(2,1)S(1)} %collective-permute-done.1.refs_2_), channel_id=1, source_target_pairs={{0,4},{1,5},{4,6},{5,7},{6,2},{7,3},{2,0},{3,1},{8,12},{9,13},{12,... | collective-permute-start | bytes 1966088 | tf_op jit(solution)/shard_map/ppermute | solution.py:399
  46.3 10.3 %collective-permute-done.7.refs_0_ = bf16[512,640]{1,0:T(8,128)(2,1)} collective-permute-done((bf16[512,640]{1,0:T(8,128)(2,1)S(1)}, bf16[512,640]{1,0:T(8,128)(2,1)}, u32[]{:S(2)}, u32[]{:S(2)}) %collective-permute-start.7) | collective-permute-done | bytes 655392 | tf_op jit(solution)/shard_map/ppermute | solution.py:399
  56.6 3.5 %collective-permute-start.10 = (bf16[512,640]{1,0:T(8,128)(2,1)S(1)}, bf16[512,640]{1,0:T(8,128)(2,1)}, u32[]{:S(2)}, u32[]{:S(2)}) collective-permute-start(bf16[512,640]{1,0:T(8,128)(2,1)S(1)} %collective-permute-done.6.refs_4_), channel_id=1, source_target_pairs={{0,4},{1,5},{4,6},{5,7},{6,2},{7,3},{2,0},{3,1},{8,12},{9,13},{12,... | collective-permute-start | bytes 1966088 | tf_op jit(solution)/shard_map/ppermute | solution.py:399
  64.3 1.8 collective-permute-done.5.refs_4_
  68.0 7.3 %collective-permute-done.10.refs_2_ = bf16[512,640]{1,0:T(8,128)(2,1)} collective-permute-done((bf16[512,640]{1,0:T(8,128)(2,1)S(1)}, bf16[512,640]{1,0:T(8,128)(2,1)}, u32[]{:S(2)}, u32[]{:S(2)}) %collective-permute-start.10) | collective-permute-done | bytes 655392 | tf_op jit(solution)/shard_map/ppermute | solution.py:399
  75.8 2.3 %copy.16 = f32[1,2,5120]{1,2,0:T(8,128)} copy(f32[1,2,5120]{2,1,0:T(2,128)S(1)} %copy-done.40) | data formatting | bytes 81920 | tf_op args[5]
  78.2 1.7 copy-done.11
  86.5 7.3 %scale.2 = (bf16[5120,640]{1,0:T(8,128)(2,1)S(1)}, f32[2,8,640]{2,1,0:T(8,128)S(1)}) custom-call(s32[4]{0:T(128)S(1)} %pad_add_fusion.where, f32[5120,2]{1,0:T(8,128)S(1)} %bitcast.35, bf16[1280,640]{1,0:T(8,128)(2,1)S(1)} %copy-done.22, bf16[1280,640]{1,0:T(8,128)(2,1)S(1)} %copy-done.13, bf16[640,640]{1,0:T(8,128)(2,1)S(1)} %copy-done.24, ...), custom_call_target="tpu_custom_call" | custom-call | flops 1 | bytes 1 | tf_op jit(solution)/shard_map/scale/pallas_call | solution.py:101
  93.8 2.8 %copy-done.4 = bf16[5120,640]{1,0:T(8,128)(2,1)} copy-done((bf16[5120,640]{1,0:T(8,128)(2,1)}, bf16[5120,640]{1,0:T(8,128)(2,1)S(1)}, u32[]{:S(2)}) %copy-start.4) | copy-done | bytes 6553624
  96.6 1.5 collective-permute-start.23
  98.6 3.5 %collective-permute-start.11 = (bf16[512,640]{1,0:T(8,128)(2,1)}, bf16[512,640]{1,0:T(8,128)(2,1)}, u32[]{:S(2)}, u32[]{:S(2)}) collective-permute-start(bf16[512,640]{1,0:T(8,128)(2,1)} %collective-permute-done.10.refs_2_), channel_id=1, source_target_pairs={{0,4},{1,5},{4,6},{5,7},{6,2},{7,3},{2,0},{3,1},{8,12},{9,13},{12,... | collective-permute-start | bytes 1966088 | tf_op jit(solution)/shard_map/ppermute | solution.py:399
  106.5 2.9 %copy-done.5 = bf16[5120,640]{1,0:T(8,128)(2,1)S(1)} copy-done((bf16[5120,640]{1,0:T(8,128)(2,1)S(1)}, bf16[5120,640]{1,0:T(8,128)(2,1)}, u32[]{:S(2)}) %copy-start.5) | copy-done | bytes 6553624
  113.7 8.9 %project.3 = (f32[1024,640]{1,0:T(8,128)S(1)}, bf16[4,1024,1280]{2,1,0:T(8,128)(2,1)}, f32[1024,128]{1,0:T(8,128)S(1)}) custom-call(s32[5]{0:T(128)S(1)} %stack.49.where, f32[2]{0:T(128)S(1)} %pad_maximum_fusion.scalars, f32[2,8,640]{2,1,0:T(8,128)S(1)} %get-tuple-element.52.sums, bf16[1024,640]{1,0:T(8,128)(2,1)S(1)} %copy-done.9, ...), custom_call_target="tpu_custom_call" | custom-call | flops 1 | bytes 1 | tf_op jit(solution)/shard_map/project/pallas_call | solution.py:256
  122.6 4.0 %copy-done = bf16[4,1024,1280]{2,1,0:T(8,128)(2,1)S(1)} copy-done((bf16[4,1024,1280]{2,1,0:T(8,128)(2,1)S(1)}, bf16[4,1024,1280]{2,1,0:T(8,128)(2,1)}, u32[]{:S(2)}) %copy-start) | copy-done | bytes 10485784
  126.6 5.0 %project.4 = (f32[1024,640]{1,0:T(8,128)S(1)}, bf16[4,1024,1280]{2,1,0:T(8,128)(2,1)S(1)}, f32[1024,128]{1,0:T(8,128)S(1)}) custom-call(s32[5]{0:T(128)S(1)} %stack.49.where, f32[2]{0:T(128)S(1)} %pad_maximum_fusion.scalars, f32[2,8,640]{2,1,0:T(8,128)S(1)} %get-tuple-element.52.sums, ...), custom_call_target="tpu_custom_call", output_to_operand_aliasing={{1}: (12, {})} | custom-call | flops 1 | bytes 1 | tf_op jit(solution)/shard_map/project/pallas_call | solution.py:256
  131.6 4.0 %copy-done.1 = bf16[4,1024,1280]{2,1,0:T(8,128)(2,1)} copy-done((bf16[4,1024,1280]{2,1,0:T(8,128)(2,1)}, bf16[4,1024,1280]{2,1,0:T(8,128)(2,1)S(1)}, u32[]{:S(2)}) %copy-start.1) | copy-done | bytes 10485784
  138.5 3.0 %copy.17 = f32[1,2,5120]{1,2,0:T(8,128)} copy(f32[1,2,5120]{2,1,0:T(2,128)} %param.13) | data formatting | bytes 81920 | tf_op args[4]
  141.7 2.9 %copy-done.7 = bf16[5120,640]{1,0:T(8,128)(2,1)S(1)} copy-done((bf16[5120,640]{1,0:T(8,128)(2,1)S(1)}, bf16[5120,640]{1,0:T(8,128)(2,1)}, u32[]{:S(2)}) %copy-start.7) | copy-done | bytes 6553624
  144.5 1.7 copy-done.21
  147.3 8.1 %project.5 = (f32[1024,640]{1,0:T(8,128)S(1)}, bf16[4,1024,1280]{2,1,0:T(8,128)(2,1)}, f32[1024,128]{1,0:T(8,128)S(1)}, bf16[640,1024]{1,0:T(8,128)(2,1)S(1)}, f32[640,2]{1,0:T(8,128)S(1)}) custom-call(s32[5]{0:T(128)S(1)} %stack.49.where, f32[2]{0:T(128)S(1)} %pad_maximum_fusion.scalars, ...), custom_call_target="tpu_custom_call", output_to_operand_aliasing={{1}: (12, {})} | custom-call | flops 1 | bytes 1 | tf_op jit(solution)/shard_map/project/pallas_call | solution.py:256
  155.4 1.6 copy-done.18
  157.0 4.0 %copy-done.2 = bf16[4,1024,1280]{2,1,0:T(8,128)(2,1)S(1)} copy-done((bf16[4,1024,1280]{2,1,0:T(8,128)(2,1)S(1)}, bf16[4,1024,1280]{2,1,0:T(8,128)(2,1)}, u32[]{:S(2)}) %copy-start.2) | copy-done | bytes 10485784
  160.9 2.0 outer.3
  162.9 1.6 collective-permute-start.22
  164.9 4.2 %slice_bitcast_fusion = (bf16[1024,1280]{1,0:T(8,128)(2,1)}, bf16[1024,1280]{1,0:T(8,128)(2,1)}, bf16[1024,1280]{1,0:T(8,128)(2,1)}, bf16[1024,1280]{1,0:T(8,128)(2,1)}) fusion(bf16[4,1024,1280]{2,1,0:T(8,128)(2,1)S(1)} %copy-done.3), kind=kLoop, calls=%fused_computation.10 | loop fusion | bytes 20971520 | tf_op jit(solution)/shard_map/squeeze | solution.py:514
  169.6 6.3 %outer.4 = (bf16[640,640]{1,0:T(8,128)(2,1)}, f32[640,640]{1,0:T(8,128)S(1)}, f32[640,640]{1,0:T(8,128)S(1)}, bf16[640,640]{1,0:T(8,128)(2,1)S(1)}) custom-call(s32[2]{0:T(128)S(1)} %pad_add_fusion.1.picks, f32[4,2,1280]{2,1,0:T(2,128)S(1)} %bitcast.37, f32[640,2]{1,0:T(8,128)S(1)} %get-tuple-element.69.edge, ...), custom_call_target="tpu_custom_call" | custom-call | flops 3355443200 | bytes 11141120 | tf_op jit(solution)/shard_map/outer/pallas_call | solution.py:306
  178.9 6.8 %scale.3 = (bf16[5120,640]{1,0:T(8,128)(2,1)S(1)}, f32[2,8,640]{2,1,0:T(8,128)S(1)}) custom-call(s32[4]{0:T(128)S(1)} %pad_add_fusion.where, f32[5120,2]{1,0:T(8,128)S(1)} %bitcast.34, bf16[1280,640]{1,0:T(8,128)(2,1)S(1)} %copy-done.17, bf16[640,640]{1,0:T(8,128)(2,1)} %collective-permute-done.17.refs_0_, bf16[640,640]{1,0:T(8,128)(2,1)} %collective-permute-done.18.refs_1_, ...), custom_call_target="tpu_custom_call" | custom-call | flops 1 | bytes 1 | tf_op jit(solution)/shard_map/scale/pallas_call | solution.py:101
  187.0 3.1 %collective-permute-done.21 = bf16[640,640]{1,0:T(8,128)(2,1)S(1)} collective-permute-done((bf16[640,640]{1,0:T(8,128)(2,1)S(1)}, bf16[640,640]{1,0:T(8,128)(2,1)S(1)}, u32[]{:S(2)}, u32[]{:S(2)}) %collective-permute-start.21) | collective-permute-done | bytes 819232 | tf_op jit(solution)/shard_map/ppermute | solution.py:27
  190.3 1.6 collective-permute-start.30
  191.9 2.2 fusion.10
  194.2 2.2 fusion.12
  196.4 2.2 fusion.15
  198.7 1.9 outer.5
  200.6 5.2 %fusion.3 = (f32[]{:T(128)}, f32[1024,640]{1,0:T(8,128)S(1)}) fusion(bf16[1024,640]{1,0:T(8,128)(2,1)S(1)} %copy-done.9, bf16[1024,640]{1,0:T(8,128)(2,1)} %fusion.1.refs_0_, f32[]{:T(128)} %bitcast, f32[640]{0:T(1024)S(1)} %get-tuple-element.100, f32[640]{0:T(1024)S(1)} %get-tuple-element.99, f32[1024]{0:T(1024)S(1)} %get-tuple-element.98, ...), kind=kOutput, calls=%fused_computation.5 | convolution fusion | flops 1685585920 | bytes 12137988 | tf_op jit(solution)/shard_map/dot_general | solution.py:517
  205.8 1.9 collective-permute-done.25.refs_1_
  211.8 2.3 %collective-permute-done.28 = f32[1,1]{1,0:T(1,128)} collective-permute-done((f32[1,1]{1,0:T(1,128)}, f32[1,1]{1,0:T(1,128)}, u32[]{:S(2)}, u32[]{:S(2)}) %collective-permute-start.28) | collective-permute-done | bytes 36 | tf_op jit(solution)/shard_map/ppermute | solution.py:523
  214.8 1.6 collective-permute-start.29
  216.3 3.0 %collective-permute-done.29 = f32[1,1]{1,0:T(1,128)} collective-permute-done((f32[1,1]{1,0:T(1,128)}, f32[1,1]{1,0:T(1,128)}, u32[]{:S(2)}, u32[]{:S(2)}) %collective-permute-start.29) | collective-permute-done | bytes 36 | tf_op jit(solution)/shard_map/ppermute | solution.py:523
  220.0 1.8 multiply_reduce_fusion
  222.4 2.0 collective-permute-done.31.refs_5_
  224.4 3.7 %finish.1 = f32[2,640,640]{2,1,0:T(8,128)} custom-call(f32[640,640]{1,0:T(8,128)S(1)} %get-tuple-element.95.refs_0_, bf16[640,640]{1,0:T(8,128)(2,1)S(1)} %collective-permute-done.25.refs_1_, bf16[640,640]{1,0:T(8,128)(2,1)S(1)} %collective-permute-done.30.refs_2_, f32[640,640]{1,0:T(8,128)S(1)} %get-tuple-element.96.refs_3_, ...), custom_call_target="tpu_custom_call" | custom-call | tf_op jit(solution)/shard_map/finish/pallas_call | solution.py:345
  (145 shorter events, 39.0 us)
Async XLA Ops:
  0.6 44.4 %collective-permute-start = (bf16[1280,640]{1,0:T(8,128)(2,1)}, bf16[1280,640]{1,0:T(8,128)(2,1)S(1)}, u32[]{:S(2)}, u32[]{:S(2)}) collective-permute-start(bf16[1280,640]{1,0:T(8,128)(2,1)} %weight.1), channel_id=1, source_target_pairs={{0,8},{8,0},{16,24},{24,16},{1,9},{9,1},{17,25},{25,17},{2,10},{10... | collective-permute-start | bytes 4915208 | tf_op jit(solution)/shard_map/ppermute | solution.py:27
  3.6 42.0 %collective-permute-start.4 = (bf16[1280,640]{1,0:T(8,128)(2,1)}, bf16[1280,640]{1,0:T(8,128)(2,1)S(1)}, u32[]{:S(2)}, u32[]{:S(2)}) collective-permute-start(bf16[1280,640]{1,0:T(8,128)(2,1)} %weight.1), channel_id=1, source_target_pairs={{0,16},{8,24},{16,0},{24,8},{1,17},{9,25},{17,1},{25,9},{2,18},{10... | collective-permute-start | bytes 4915208 | tf_op jit(solution)/shard_map/ppermute | solution.py:27
  9.1 51.0 %copy-start.16 = (bf16[1280,640]{1,0:T(8,128)(2,1)S(1)}, bf16[1280,640]{1,0:T(8,128)(2,1)}, u32[]{:S(2)}) copy-start(bf16[1280,640]{1,0:T(8,128)(2,1)} %weight.2) | copy-start | bytes 4915204
  10.6 17.8 %collective-permute-start.1 = (bf16[512,640]{1,0:T(8,128)(2,1)S(1)}, bf16[512,640]{1,0:T(8,128)(2,1)S(1)}, u32[]{:S(2)}, u32[]{:S(2)}) collective-permute-start(bf16[512,640]{1,0:T(8,128)(2,1)S(1)} %get-tuple-element.112), channel_id=1, source_target_pairs={{0,4},{1,5},{4,6},{5,7},{6,2},{7,3},{2,0},{3,1},{8,12},{9,13},{12,... | collective-permute-start | bytes 1966088 | tf_op jit(solution)/shard_map/ppermute | solution.py:399
  13.3 27.5 %collective-permute-start.6 = (bf16[512,640]{1,0:T(8,128)(2,1)S(1)}, bf16[512,640]{1,0:T(8,128)(2,1)S(1)}, u32[]{:S(2)}, u32[]{:S(2)}) collective-permute-start(bf16[512,640]{1,0:T(8,128)(2,1)S(1)} %get-tuple-element.111), channel_id=1, source_target_pairs={{0,4},{1,5},{4,6},{5,7},{6,2},{7,3},{2,0},{3,1},{8,12},{9,13},{12,... | collective-permute-start | bytes 1966088 | tf_op jit(solution)/shard_map/ppermute | solution.py:399
  28.5 17.2 %copy-start.27 = (bf16[512,640]{1,0:T(8,128)(2,1)}, bf16[512,640]{1,0:T(8,128)(2,1)S(1)}, u32[]{:S(2)}) copy-start(bf16[512,640]{1,0:T(8,128)(2,1)S(1)} %collective-permute-done.1.refs_2_) | copy-start | bytes 1966084
  28.5 15.7 %collective-permute-start.2 = (bf16[512,640]{1,0:T(8,128)(2,1)S(1)}, bf16[512,640]{1,0:T(8,128)(2,1)S(1)}, u32[]{:S(2)}, u32[]{:S(2)}) collective-permute-start(bf16[512,640]{1,0:T(8,128)(2,1)S(1)} %collective-permute-done.1.refs_2_), channel_id=1, source_target_pairs={{0,1},{1,0},{2,3},{3,2},{4,5},{5,4},{6,7},{7,6},{8,9},{9,8},{10,11... | collective-permute-start | bytes 1966088 | tf_op jit(solution)/shard_map/ppermute | solution.py:403
  40.8 20.7 %copy-start.29 = (bf16[512,640]{1,0:T(8,128)(2,1)}, bf16[512,640]{1,0:T(8,128)(2,1)S(1)}, u32[]{:S(2)}) copy-start(bf16[512,640]{1,0:T(8,128)(2,1)S(1)} %collective-permute-done.6.refs_4_) | copy-start | bytes 1966084
  40.8 15.9 %collective-permute-start.7 = (bf16[512,640]{1,0:T(8,128)(2,1)S(1)}, bf16[512,640]{1,0:T(8,128)(2,1)}, u32[]{:S(2)}, u32[]{:S(2)}) collective-permute-start(bf16[512,640]{1,0:T(8,128)(2,1)S(1)} %collective-permute-done.1.refs_2_), channel_id=1, source_target_pairs={{0,4},{1,5},{4,6},{5,7},{6,2},{7,3},{2,0},{3,1},{8,12},{9,13},{12,... | collective-permute-start | bytes 1966088 | tf_op jit(solution)/shard_map/ppermute | solution.py:399
  45.0 16.4 %copy-start.12 = (bf16[1280,640]{1,0:T(8,128)(2,1)}, bf16[1280,640]{1,0:T(8,128)(2,1)S(1)}, u32[]{:S(2)}) copy-start(bf16[1280,640]{1,0:T(8,128)(2,1)S(1)} %collective-permute-done.refs_0_.refs_5_) | copy-start | bytes 4915204
  45.1 30.8 %copy-start.40 = (f32[1,2,5120]{2,1,0:T(2,128)S(1)}, f32[1,2,5120]{2,1,0:T(2,128)}, u32[]{:S(2)}) copy-start(f32[1,2,5120]{2,1,0:T(2,128)} %param.14) | copy-start | bytes 122884
  45.1 18.3 %collective-permute-start.3 = (bf16[640,640]{1,0:T(8,128)(2,1)S(1)}, bf16[640,640]{1,0:T(8,128)(2,1)S(1)}, u32[]{:S(2)}, u32[]{:S(2)}) collective-permute-start(bf16[640,640]{1,0:T(8,128)(2,1)S(1)} %slice.55), channel_id=1, source_target_pairs={{0,16},{8,24},{16,0},{24,8},{1,17},{9,25},{17,1},{25,9},{2,18},{10... | collective-permute-start | bytes 2457608 | tf_op jit(solution)/shard_map/ppermute | solution.py:27
  45.7 32.5 %copy-start.14 = (bf16[1280,640]{1,0:T(8,128)(2,1)}, bf16[1280,640]{1,0:T(8,128)(2,1)S(1)}, u32[]{:S(2)}) copy-start(bf16[1280,640]{1,0:T(8,128)(2,1)S(1)} %collective-permute-done.4.refs_2_.refs_3_) | copy-start | bytes 4915204
  45.7 20.3 %collective-permute-start.5 = (bf16[640,640]{1,0:T(8,128)(2,1)S(1)}, bf16[640,640]{1,0:T(8,128)(2,1)S(1)}, u32[]{:S(2)}, u32[]{:S(2)}) collective-permute-start(bf16[640,640]{1,0:T(8,128)(2,1)S(1)} %slice.56), channel_id=1, source_target_pairs={{0,8},{8,0},{16,24},{24,16},{1,9},{9,1},{17,25},{25,17},{2,10},{10... | collective-permute-start | bytes 2457608 | tf_op jit(solution)/shard_map/ppermute | solution.py:27
  46.3 50.2 %collective-permute-start.14 = (bf16[1024,640]{1,0:T(8,128)(2,1)}, bf16[1024,640]{1,0:T(8,128)(2,1)}, u32[]{:S(2)}, u32[]{:S(2)}) collective-permute-start(bf16[1024,640]{1,0:T(8,128)(2,1)} %fusion.1.refs_0_), channel_id=1, source_target_pairs={{0,1},{1,0},{2,3},{3,2},{4,5},{5,4},{6,7},{7,6},{8,9},{9,8},{10,11... | collective-permute-start | bytes 3932168 | tf_op jit(solution)/shard_map/ppermute | solution.py:410
  56.6 18.7 %collective-permute-start.10 = (bf16[512,640]{1,0:T(8,128)(2,1)S(1)}, bf16[512,640]{1,0:T(8,128)(2,1)}, u32[]{:S(2)}, u32[]{:S(2)}) collective-permute-start(bf16[512,640]{1,0:T(8,128)(2,1)S(1)} %collective-permute-done.6.refs_4_), channel_id=1, source_target_pairs={{0,4},{1,5},{4,6},{5,7},{6,2},{7,3},{2,0},{3,1},{8,12},{9,13},{12,... | collective-permute-start | bytes 1966088 | tf_op jit(solution)/shard_map/ppermute | solution.py:399
  61.4 37.2 %collective-permute-start.17 = (bf16[640,640]{1,0:T(8,128)(2,1)}, bf16[640,640]{1,0:T(8,128)(2,1)}, u32[]{:S(2)}, u32[]{:S(2)}) collective-permute-start(bf16[640,640]{1,0:T(8,128)(2,1)} %get-tuple-element.83), channel_id=1, source_target_pairs={{0,8},{8,0},{16,24},{24,16},{1,9},{9,1},{17,25},{25,17},{2,10},{10... | collective-permute-start | bytes 2457608 | tf_op jit(solution)/shard_map/ppermute | solution.py:27
  64.3 33.8 %collective-permute-start.12 = (bf16[512,640]{1,0:T(8,128)(2,1)}, bf16[512,640]{1,0:T(8,128)(2,1)}, u32[]{:S(2)}, u32[]{:S(2)}) collective-permute-start(bf16[512,640]{1,0:T(8,128)(2,1)} %collective-permute-done.7.refs_0_), channel_id=1, source_target_pairs={{0,1},{1,0},{2,3},{3,2},{4,5},{5,4},{6,7},{7,6},{8,9},{9,8},{10,11... | collective-permute-start | bytes 1966088 | tf_op jit(solution)/shard_map/ppermute | solution.py:403
  66.9 31.2 %collective-permute-start.8 = (bf16[512,640]{1,0:T(8,128)(2,1)}, bf16[512,640]{1,0:T(8,128)(2,1)}, u32[]{:S(2)}, u32[]{:S(2)}) collective-permute-start(bf16[512,640]{1,0:T(8,128)(2,1)} %collective-permute-done.7.refs_0_), channel_id=1, source_target_pairs={{0,4},{1,5},{4,6},{5,7},{6,2},{7,3},{2,0},{3,1},{8,12},{9,13},{12,... | collective-permute-start | bytes 1966088 | tf_op jit(solution)/shard_map/ppermute | solution.py:399
  75.3 26.8 %collective-permute-start.19 = (bf16[640,640]{1,0:T(8,128)(2,1)}, bf16[640,640]{1,0:T(8,128)(2,1)}, u32[]{:S(2)}, u32[]{:S(2)}) collective-permute-start(bf16[640,640]{1,0:T(8,128)(2,1)} %get-tuple-element.85), channel_id=1, source_target_pairs={{0,16},{8,24},{16,0},{24,8},{1,17},{9,25},{17,1},{25,9},{2,18},{10... | collective-permute-start | bytes 2457608 | tf_op jit(solution)/shard_map/ppermute | solution.py:27
  86.5 11.6 %copy-start.30 = (bf16[512,640]{1,0:T(8,128)(2,1)S(1)}, bf16[512,640]{1,0:T(8,128)(2,1)}, u32[]{:S(2)}) copy-start(bf16[512,640]{1,0:T(8,128)(2,1)} %copy-done.29) | copy-start | bytes 1966084
  86.5 20.0 %copy-start.8 = (bf16[1024,640]{1,0:T(8,128)(2,1)S(1)}, bf16[1024,640]{1,0:T(8,128)(2,1)}, u32[]{:S(2)}) copy-start(bf16[1024,640]{1,0:T(8,128)(2,1)} %other.5) | copy-start | bytes 3932164
  86.5 20.0 %copy-start.9 = (bf16[1024,640]{1,0:T(8,128)(2,1)S(1)}, bf16[1024,640]{1,0:T(8,128)(2,1)}, u32[]{:S(2)}) copy-start(bf16[1024,640]{1,0:T(8,128)(2,1)} %sample.5) | copy-start | bytes 3932164
  96.6 41.4 %collective-permute-start.23 = (bf16[640,640]{1,0:T(8,128)(2,1)}, bf16[640,640]{1,0:T(8,128)(2,1)S(1)}, u32[]{:S(2)}, u32[]{:S(2)}) collective-permute-start(bf16[640,640]{1,0:T(8,128)(2,1)} %get-tuple-element.83), channel_id=1, source_target_pairs={{0,16},{8,24},{16,0},{24,8},{1,17},{9,25},{17,1},{25,9},{2,18},{10... | collective-permute-start | bytes 2457608 | tf_op jit(solution)/shard_map/ppermute | solution.py:27
  98.1 4.5 %collective-permute-start.15 = (bf16[512,640]{1,0:T(8,128)(2,1)S(1)}, bf16[512,640]{1,0:T(8,128)(2,1)S(1)}, u32[]{:S(2)}, u32[]{:S(2)}) collective-permute-start(bf16[512,640]{1,0:T(8,128)(2,1)S(1)} %copy-done.30), channel_id=1, source_target_pairs={{0,1},{1,0},{2,3},{3,2},{4,5},{5,4},{6,7},{7,6},{8,9},{9,8},{10,11... | collective-permute-start | bytes 1966088 | tf_op jit(solution)/shard_map/ppermute | solution.py:403
  98.1 5.9 %collective-permute-start.13 = (bf16[512,640]{1,0:T(8,128)(2,1)}, bf16[512,640]{1,0:T(8,128)(2,1)S(1)}, u32[]{:S(2)}, u32[]{:S(2)}) collective-permute-start(bf16[512,640]{1,0:T(8,128)(2,1)} %collective-permute-done.10.refs_2_), channel_id=1, source_target_pairs={{0,1},{1,0},{2,3},{3,2},{4,5},{5,4},{6,7},{7,6},{8,9},{9,8},{10,11... | collective-permute-start | bytes 1966088 | tf_op jit(solution)/shard_map/ppermute | solution.py:403
  98.6 39.4 %collective-permute-start.11 = (bf16[512,640]{1,0:T(8,128)(2,1)}, bf16[512,640]{1,0:T(8,128)(2,1)}, u32[]{:S(2)}, u32[]{:S(2)}) collective-permute-start(bf16[512,640]{1,0:T(8,128)(2,1)} %collective-permute-done.10.refs_2_), channel_id=1, source_target_pairs={{0,4},{1,5},{4,6},{5,7},{6,2},{7,3},{2,0},{3,1},{8,12},{9,13},{12,... | collective-permute-start | bytes 1966088 | tf_op jit(solution)/shard_map/ppermute | solution.py:399
  102.1 39.5 %collective-permute-start.24 = (bf16[640,640]{1,0:T(8,128)(2,1)}, bf16[640,640]{1,0:T(8,128)(2,1)}, u32[]{:S(2)}, u32[]{:S(2)}) collective-permute-start(bf16[640,640]{1,0:T(8,128)(2,1)} %get-tuple-element.85), channel_id=1, source_target_pairs={{0,8},{8,0},{16,24},{24,16},{1,9},{9,1},{17,25},{25,17},{2,10},{10... | collective-permute-start | bytes 2457608 | tf_op jit(solution)/shard_map/ppermute | solution.py:27
  103.5 53.5 %collective-permute-start.18 = (bf16[640,640]{1,0:T(8,128)(2,1)}, bf16[640,640]{1,0:T(8,128)(2,1)}, u32[]{:S(2)}, u32[]{:S(2)}) collective-permute-start(bf16[640,640]{1,0:T(8,128)(2,1)} %collective-permute-done.17.refs_0_), channel_id=1, source_target_pairs={{0,16},{8,24},{16,0},{24,8},{1,17},{9,25},{17,1},{25,9},{2,18},{10... | collective-permute-start | bytes 2457608 | tf_op jit(solution)/shard_map/ppermute | solution.py:27
  104.8 52.1 %collective-permute-start.20 = (bf16[640,640]{1,0:T(8,128)(2,1)}, bf16[640,640]{1,0:T(8,128)(2,1)}, u32[]{:S(2)}, u32[]{:S(2)}) collective-permute-start(bf16[640,640]{1,0:T(8,128)(2,1)} %collective-permute-done.19.refs_3_), channel_id=1, source_target_pairs={{0,8},{8,0},{16,24},{24,16},{1,9},{9,1},{17,25},{25,17},{2,10},{10... | collective-permute-start | bytes 2457608 | tf_op jit(solution)/shard_map/ppermute | solution.py:27
  113.7 8.9 %copy-start.6 = (bf16[5120,640]{1,0:T(8,128)(2,1)S(1)}, bf16[5120,640]{1,0:T(8,128)(2,1)}, u32[]{:S(2)}) copy-start(bf16[5120,640]{1,0:T(8,128)(2,1)} %copy-done.4) | copy-start | bytes 19660804
  113.7 8.9 %copy-start.35 = (bf16[512,640]{1,0:T(8,128)(2,1)S(1)}, bf16[512,640]{1,0:T(8,128)(2,1)}, u32[]{:S(2)}) copy-start(bf16[512,640]{1,0:T(8,128)(2,1)} %copy-done.34) | copy-start | bytes 1966084
  138.0 3.7 %collective-permute-start.9 = (bf16[512,640]{1,0:T(8,128)(2,1)}, bf16[512,640]{1,0:T(8,128)(2,1)}, u32[]{:S(2)}, u32[]{:S(2)}) collective-permute-start(bf16[512,640]{1,0:T(8,128)(2,1)} %collective-permute-done.8.refs_0_), channel_id=1, source_target_pairs={{0,1},{1,0},{2,3},{3,2},{4,5},{5,4},{6,7},{7,6},{8,9},{9,8},{10,11... | collective-permute-start | bytes 1966088 | tf_op jit(solution)/shard_map/ppermute | solution.py:403
  138.0 3.7 %collective-permute-start.16 = (bf16[512,640]{1,0:T(8,128)(2,1)}, bf16[512,640]{1,0:T(8,128)(2,1)}, u32[]{:S(2)}, u32[]{:S(2)}) collective-permute-start(bf16[512,640]{1,0:T(8,128)(2,1)} %collective-permute-done.11.refs_2_), channel_id=1, source_target_pairs={{0,1},{1,0},{2,3},{3,2},{4,5},{5,4},{6,7},{7,6},{8,9},{9,8},{10,11... | collective-permute-start | bytes 1966088 | tf_op jit(solution)/shard_map/ppermute | solution.py:403
  162.9 23.3 %collective-permute-start.22 = (bf16[640,640]{1,0:T(8,128)(2,1)S(1)}, bf16[640,640]{1,0:T(8,128)(2,1)S(1)}, u32[]{:S(2)}, u32[]{:S(2)}) collective-permute-start(bf16[640,640]{1,0:T(8,128)(2,1)S(1)} %get-tuple-element.76), channel_id=1, source_target_pairs={{0,16},{8,24},{16,0},{24,8},{1,17},{9,25},{17,1},{25,9},{2,18},{10... | collective-permute-start | bytes 2457608 | tf_op jit(solution)/shard_map/ppermute | solution.py:27
  169.1 9.8 %copy-start.10 = (f32[1,2,5120]{1,2,0:T(8,128)S(1)}, f32[1,2,5120]{1,2,0:T(8,128)}, u32[]{:S(2)}) copy-start(f32[1,2,5120]{1,2,0:T(8,128)} %copy.17) | copy-start | bytes 122884
  169.1 9.8 %copy-start.17 = (bf16[1280,640]{1,0:T(8,128)(2,1)S(1)}, bf16[1280,640]{1,0:T(8,128)(2,1)}, u32[]{:S(2)}) copy-start(bf16[1280,640]{1,0:T(8,128)(2,1)} %weight.2) | copy-start | bytes 4915204
  169.1 21.1 %collective-permute-start.21 = (bf16[640,640]{1,0:T(8,128)(2,1)S(1)}, bf16[640,640]{1,0:T(8,128)(2,1)S(1)}, u32[]{:S(2)}, u32[]{:S(2)}) collective-permute-start(bf16[640,640]{1,0:T(8,128)(2,1)S(1)} %get-tuple-element.75), channel_id=1, source_target_pairs={{0,8},{8,0},{16,24},{24,16},{1,9},{9,1},{17,25},{25,17},{2,10},{10... | collective-permute-start | bytes 2457608 | tf_op jit(solution)/shard_map/ppermute | solution.py:27
  175.9 31.8 %collective-permute-start.25 = (bf16[640,640]{1,0:T(8,128)(2,1)}, bf16[640,640]{1,0:T(8,128)(2,1)S(1)}, u32[]{:S(2)}, u32[]{:S(2)}) collective-permute-start(bf16[640,640]{1,0:T(8,128)(2,1)} %get-tuple-element.78), channel_id=1, source_target_pairs={{0,8},{8,0},{16,24},{24,16},{1,9},{9,1},{17,25},{25,17},{2,10},{10... | collective-permute-start | bytes 2457608 | tf_op jit(solution)/shard_map/ppermute | solution.py:27
  177.4 30.4 %collective-permute-start.26 = (bf16[640,640]{1,0:T(8,128)(2,1)S(1)}, bf16[640,640]{1,0:T(8,128)(2,1)S(1)}, u32[]{:S(2)}, u32[]{:S(2)}) collective-permute-start(bf16[640,640]{1,0:T(8,128)(2,1)S(1)} %get-tuple-element.81), channel_id=1, source_target_pairs={{0,16},{8,24},{16,0},{24,8},{1,17},{9,25},{17,1},{25,9},{2,18},{10... | collective-permute-start | bytes 2457608 | tf_op jit(solution)/shard_map/ppermute | solution.py:27
  185.7 10.7 %copy-start.41 = (bf16[5120,640]{1,0:T(8,128)(2,1)}, bf16[5120,640]{1,0:T(8,128)(2,1)S(1)}, u32[]{:S(2)}) copy-start(bf16[5120,640]{1,0:T(8,128)(2,1)S(1)} %get-tuple-element.87) | copy-start | bytes 19660804
  186.4 38.0 %collective-permute-start.31 = (bf16[640,640]{1,0:T(8,128)(2,1)S(1)}, bf16[640,640]{1,0:T(8,128)(2,1)S(1)}, u32[]{:S(2)}, u32[]{:S(2)}) collective-permute-start(bf16[640,640]{1,0:T(8,128)(2,1)S(1)} %add_convert_fusion), channel_id=1, source_target_pairs={{0,8},{8,0},{16,24},{24,16},{1,9},{9,1},{17,25},{25,17},{2,10},{10... | collective-permute-start | bytes 2457608 | tf_op jit(solution)/shard_map/ppermute | solution.py:27
  190.3 34.1 %collective-permute-start.30 = (bf16[640,640]{1,0:T(8,128)(2,1)S(1)}, bf16[640,640]{1,0:T(8,128)(2,1)S(1)}, u32[]{:S(2)}, u32[]{:S(2)}) collective-permute-start(bf16[640,640]{1,0:T(8,128)(2,1)S(1)} %add_convert_fusion.1), channel_id=1, source_target_pairs={{0,16},{8,24},{16,0},{24,8},{1,17},{9,25},{17,1},{25,9},{2,18},{10... | collective-permute-start | bytes 2457608 | tf_op jit(solution)/shard_map/ppermute | solution.py:27
  200.6 19.4 %copy-start.19 = (f32[1024,640]{1,0:T(8,128)S(1)}, f32[1024,640]{1,0:T(8,128)}, u32[]{:S(2)}) copy-start(f32[1024,640]{1,0:T(8,128)} %copy-done.18) | copy-start | bytes 7864324
  200.6 19.4 %copy-start.46 = (bf16[1024,640]{1,0:T(8,128)(2,1)S(1)}, bf16[1024,640]{1,0:T(8,128)(2,1)}, u32[]{:S(2)}) copy-start(bf16[1024,640]{1,0:T(8,128)(2,1)} %param.11) | copy-start | bytes 3932164
  207.7 1.4 collective-permute-start.27
  210.4 3.7 %collective-permute-start.28 = (f32[1,1]{1,0:T(1,128)}, f32[1,1]{1,0:T(1,128)}, u32[]{:S(2)}, u32[]{:S(2)}) collective-permute-start(f32[1,1]{1,0:T(1,128)} %add.111), channel_id=1, source_target_pairs={{0,2},{1,3},{2,0},{3,1},{4,6},{5,7},{6,4},{7,5},{8,10},{9,11},{10,... | collective-permute-start | bytes 20 | tf_op jit(solution)/shard_map/ppermute | solution.py:523
  214.8 4.6 %collective-permute-start.29 = (f32[1,1]{1,0:T(1,128)}, f32[1,1]{1,0:T(1,128)}, u32[]{:S(2)}, u32[]{:S(2)}) collective-permute-start(f32[1,1]{1,0:T(1,128)} %add.112), channel_id=1, source_target_pairs={{0,4},{1,5},{2,6},{3,7},{4,0},{5,1},{6,2},{7,3},{8,12},{9,13},{10,... | collective-permute-start | bytes 20 | tf_op jit(solution)/shard_map/ppermute | solution.py:523
  (32 other events, 63.8 us)

commit v5 on v4

--- a/solution.py
+++ b/solution.py
@@ -13,7 +13,7 @@
 F32 = jnp.float32
 MIB = 1024 * 1024
 CHUNKS = 2
-GATES = {'relay': ('cA1',), 'teacher': ('parts', 'parts1'), 'teacher1': ('far0', 'far1'), 'A2': ('B1',), 'B2': ('A2',), 'A3': ('far0', 'far1'), 'B3': ('A3', 'sums'), 'cB1': ('f0', 'f1'), 'cA2': ('soon',), 'cB2': ('sums',), 'cB3': ('early',), 'teacher relay': ('sums',)}
+GATES = {'relay': ('own',), 'teacher': ('parts', 'parts1'), 'B2': ('f0', 'f1'), 'B3': ('sums', 't00', 't01'), 'cB2': ('far0', 'far1'), 'cA3': ('soon',), 'cB3': ('early', 't10', 't11'), 'teacher relay': ('sums',), 'cA2': ('sums',), 'cB1': ('far0', 'far1')}
 ANY = pl.BlockSpec(memory_space=pl.ANY)
 SMEM = pl.BlockSpec(memory_space=pltpu.SMEM)
 VMEM = pl.BlockSpec(memory_space=pltpu.VMEM)
@@ -59,7 +59,7 @@
 
 def scale_kernel(keys, where, mod, weight, *refs):
     blocks, refs = refs[: len(keys)], refs[len(keys) :]
-    out, sums, full, sems, osems = refs
+    out, sums, full, column, sems, osems = refs
     half_rows = weight.shape[0] // 2
     cols = weight.shape[1]
     loads, drains = [], []
@@ -73,15 +73,18 @@
         loads[-1][0].start()
     tile = 160
     sums[...] = jnp.zeros_like(sums)
-    for (load, spot), drain in zip(loads, drains):
+    for index, ((load, spot), drain) in enumerate(zip(loads, drains)):
+        mask, half = ([(0, 0), (0, 1)] + keys)[index]
+        column[...] = jnp.transpose(mod[where[mask] * 2 + half])
         load.wait()
 
         @pl.loop(0, half_rows // tile)
         def _(step):
-            at = pl.ds(pl.multiple_of(spot + step * tile, tile), tile)
+            low = pl.multiple_of(step * tile, tile)
+            at = pl.ds(pl.multiple_of(spot + low, tile), tile)
             value = full[at, :].astype(F32)
-            shifted = value * mod[at, 0:1]
-            scaled = (value * (1.0 + mod[at, 1:2])).astype(BF16)
+            shifted = value * column[pl.ds(low, tile), 0:1]
+            scaled = (value * (1.0 + column[pl.ds(low, tile), 1:2])).astype(BF16)
             full[at, :] = scaled
             sums[0] += jnp.sum(scaled.astype(F32).reshape(tile // 8, 8, cols), axis=0)
             sums[1] += jnp.sum(shifted.reshape(tile // 8, 8, cols), axis=0)
@@ -96,6 +99,7 @@
 def scale(where, mod, weight, blocks):
     cols = weight.shape[1]
     half_rows = weight.shape[0] // 2
+    mod = jnp.swapaxes(mod.reshape(2, -1, half_rows), 0, 1)
     count = len(blocks) + 2
     width = half_rows * count
     return pl.pallas_call(
@@ -108,12 +112,11 @@
         out_specs=(ANY, VMEM),
         scratch_shapes=[
             pltpu.VMEM((width, cols), BF16),
+            pltpu.VMEM((half_rows, 2), F32),
             pltpu.SemaphoreType.DMA((count,)),
             pltpu.SemaphoreType.DMA((count,)),
         ],
-        compiler_params=pltpu.CompilerParams(
-            vmem_limit_bytes=2 * width * (cols + 256) + 8 * MIB
-        ),
+        compiler_params=pltpu.CompilerParams(vmem_limit_bytes=60 * MIB),
         cost_estimate=pl.CostEstimate(
             flops=1, bytes_accessed=1, transcendentals=0
         ),
@@ -121,23 +124,50 @@
     )(where, mod, weight, *blocks.values())
 
 
+def gradient_halves(flipped, tokens, mod, edge):
+    cols = flipped.shape[0]
+    if len(tokens.shape) == 2:
+        term = jnp.dot(flipped[...], tokens[...], preferred_element_type=F32)
+        terms = [term[:, half * cols : (half + 1) * cols] for half in range(2)]
+        mods = [mod[0][:, half * cols : (half + 1) * cols] for half in range(2)]
+    else:
+        terms = [jnp.dot(flipped[...], tokens[h], preferred_element_type=F32) for h in range(2)]
+        mods = mod
+    return [
+        (term - edge[:, 0:1]) * (1.0 + part[1:2, :]) + edge[:, 1:2] * part[0:1, :]
+        for term, part in zip(terms, mods)
+    ]
+
+
 def project_kernel(
-    prior, last, hops, where, scalars, sums, sample, other, scaled, *refs
+    prior, last, hops, core_at, where, scalars, sums, mod, sample, other, scaled, *refs
 ):
     count = sum(len(hop) for hop in hops)
     pieces, refs = refs[:count], refs[count:]
     if prior:
-        carry, carried, _, *refs = refs
+        carried, carry, _, *refs = refs
+    velocity, inputs, stats, *refs = refs
     if last:
-        velocity, inputs, stats, flipped, edge, *refs = refs
-    else:
-        velocity, inputs, stats, *refs = refs
-    held, full, moments, tail, sems, wsems, osems = refs
+        fars = where.shape[0] - core_at - 1
+        flipped, edge, *refs = refs
+        blocks, refs = refs[: 2 * fars], refs[2 * fars :]
+    held, full, moments, total, sems, wsems, osems, esems, *refs = refs
+    if prior:
+        before, *refs = refs
+    if last:
+        tail, mine, noisy, turned, far = refs
     slots, rows, depth = held.shape
-    cols = velocity.shape[1]
+    cols = total.shape[1]
     width = scaled.shape[0]
     parts = 2 * cols // depth
-    core = where[where.shape[0] - 1]
+    core = where[core_at]
+    span = 2 * cols
+
+    def at_place(place):
+        if parts == 1:
+            return inputs.at[:, pl.ds(pl.multiple_of(place * span, span), span)]
+        return inputs.at[pl.ds(place * 2, 2)]
+
     loads, arrivals, drains = [], [], []
     index = 0
     for n, hop in enumerate(hops):
@@ -155,41 +185,42 @@
             index += 1
         arrivals.append(copies)
         place = where[hop[0][2]]
-        span = 2 * cols
-        loads.append(
-            pltpu.make_async_copy(
-                scaled.at[pl.ds(pl.multiple_of(place * span, span), span)], full.at[n], wsems.at[n]
-            )
-        )
-        drains.append(
-            pltpu.make_async_copy(
-                held.at[pl.ds(n * parts, parts)],
-                inputs.at[pl.ds(place * parts, parts)],
-                osems.at[n],
-            )
-        )
+        low = pl.multiple_of(place * span, span)
+        loads.append(pltpu.make_async_copy(scaled.at[pl.ds(low, span)], full.at[n], wsems.at[n]))
+        here = held.at[n] if parts == 1 else held.at[pl.ds(2 * n, 2)]
+        drains.append(pltpu.make_async_copy(here, at_place(place), osems.at[n]))
     for copies, load in zip(arrivals, loads):
         for copy in copies:
             copy.start()
         load.start()
+    extras = []
+
+    def extra(source, target):
+        extras.append(pltpu.make_async_copy(source, target, esems.at[len(extras)]))
+        extras[-1].start()
+        return extras[-1]
+
+    waits = []
+    if prior:
+        waits.append(extra(carry, before))
+    if last:
+        waits += [extra(sample, mine), extra(other, noisy)]
     piece = 256
     lane = lax.broadcasted_iota(jnp.int32, (piece, 128), 1)
     for n in range(len(hops)):
         for copy in arrivals[n]:
             copy.wait()
+        drains[n].start()
         loads[n].wait()
-        drains[n].start()
         for part in range(parts):
             slot = n * parts + part
             term = jnp.dot(
                 held[slot], full[n, pl.ds(part * depth, depth), :], preferred_element_type=F32
             )
             if slot:
-                velocity[...] += term
-            elif prior:
-                velocity[...] = carry[...] + term
+                total[...] += term
             else:
-                velocity[...] = term
+                total[...] = term
             for low in range(0, rows, piece):
                 at = pl.ds(low, piece)
                 if slot == 0 and prior:
@@ -203,9 +234,17 @@
                 power = jnp.sum(spread * spread, axis=1, keepdims=True)
                 more = jnp.where(lane == 1, sum_, jnp.where(lane == 2, power, 0.0))
                 moments[at, :] += more
+    for copy in waits:
+        copy.wait()
     if not last:
         stats[...] = moments[...]
+        if prior:
+            total[...] += before[...]
+        outs = [extra(total, velocity)]
     else:
+        for copy in drains:
+            copy.wait()
+        nears = [extra(at_place(where[core_at + 1 + j]), far.at[j]) for j in range(fars)]
         tail[...] = jnp.zeros_like(tail)
 
         @pl.loop(0, rows // piece)
@@ -217,77 +256,89 @@
             mean = moments[at, 0:1] + away
             by = lax.rsqrt(power + EPS)
             stats[at, :] = jnp.where(lane == 0, mean, by)
-            value = by * (velocity[at, :] - mean * sums[0, 0:1, :]) + sums[1, 0:1, :]
-            velocity[at, :] = value
-            target = other[at, :].astype(F32) - sample[at, :].astype(F32)
+            value = total[at, :] + before[at, :]
+            value = by * (value - mean * sums[0, 0:1, :]) + sums[1, 0:1, :]
+            total[at, :] = value
+            target = noisy[at, :].astype(F32) - mine[at, :].astype(F32)
             wrong = (value - target) * scalars[1]
             sent = (by * wrong).astype(BF16).astype(F32)
-            flipped[:, at] = jnp.transpose(sent).astype(BF16)
+            turned[:, at] = jnp.transpose(sent).astype(BF16)
             tail[0] += jnp.sum((mean * sent).reshape(piece // 8, 8, cols), axis=0)
             tail[1] += jnp.sum(wrong.reshape(piece // 8, 8, cols), axis=0)
 
+        outs = [extra(turned, flipped), extra(total, velocity)]
         ends = [jnp.sum(jnp.transpose(tail[i]), axis=1, keepdims=True) for i in range(2)]
         edge[...] = jnp.concatenate(ends, axis=1)
-    for copy in drains:
+        for j in range(fars):
+            nears[j].wait()
+            place = where[core_at + 1 + j]
+            mods = [mod[place]] if parts == 1 else [mod[2 * place], mod[2 * place + 1]]
+            for half, term in enumerate(gradient_halves(turned, far.at[j], mods, edge)):
+                blocks[2 * j + half][...] = term.astype(BF16)
+    for copy in outs + ([] if last else drains):
         copy.wait()
 
 
-def project(where, scalars, sums, sample, other, scaled, hops, prior, earlier, last):
+def project(where, scalars, sums, mod, sample, other, scaled, hops, prior, earlier, core_at, last):
     clip_rows, cols = sample.shape
     width = scaled.shape[0]
     group = 1 if cols % 128 else 2
     depth = group * cols
-    places = width // depth
     slots = len(hops) * 2 // group
     pieces = [piece for hop, _ in hops for piece, _, _ in hop]
     plan = [[(low, side, place) for _, low, side in hop] for hop, place in hops]
+    laid = (clip_rows, width) if group == 2 else (width // cols, clip_rows, cols)
+    near = (clip_rows, depth) if group == 2 else (2, clip_rows, cols)
+    fars = where.shape[0] - core_at - 1
     out_shape = [
         jax.ShapeDtypeStruct((clip_rows, cols), F32),
-        jax.ShapeDtypeStruct((places, clip_rows, depth), BF16),
+        jax.ShapeDtypeStruct(laid, BF16),
         jax.ShapeDtypeStruct((clip_rows, 128), F32),
     ]
+    out_specs = [ANY, ANY, VMEM]
+    scratch = [
+        pltpu.VMEM((slots, clip_rows, depth), BF16),
+        pltpu.VMEM((len(hops), 2 * cols, cols), BF16),
+        pltpu.VMEM((clip_rows, 128), F32),
+        pltpu.VMEM((clip_rows, cols), F32),
+        pltpu.SemaphoreType.DMA((len(pieces),)),
+        pltpu.SemaphoreType.DMA((len(hops),)),
+        pltpu.SemaphoreType.DMA((len(hops),)),
+        pltpu.SemaphoreType.DMA((5 + fars,)),
+    ]
+    if prior:
+        velocity, inputs, stats = earlier
+        earlier = [stats, velocity, inputs]
+        scratch.append(pltpu.VMEM((clip_rows, cols), F32))
     if last:
         out_shape.append(jax.ShapeDtypeStruct((cols, clip_rows), BF16))
         out_shape.append(jax.ShapeDtypeStruct((cols, 2), F32))
-    if prior:
-        velocity, inputs, stats = earlier
-        earlier = [velocity, stats, inputs]
-    need = 2 * slots * depth * (clip_rows + cols) + clip_rows * cols * 20 + clip_rows * 128 * 16
+        out_shape += [jax.ShapeDtypeStruct((cols, cols), BF16)] * (2 * fars)
+        out_specs += [ANY, VMEM] + [VMEM] * (2 * fars)
+        scratch += [
+            pltpu.VMEM((2, 8, cols), F32),
+            pltpu.VMEM((clip_rows, cols), BF16),
+            pltpu.VMEM((clip_rows, cols), BF16),
+            pltpu.VMEM((cols, clip_rows), BF16),
+            pltpu.VMEM((fars, *near), BF16),
+        ]
     return pl.pallas_call(
-        functools.partial(project_kernel, prior, last, plan),
+        functools.partial(project_kernel, prior, last, plan, core_at),
         out_shape=out_shape,
-        in_specs=[SMEM, SMEM] + [VMEM] * 3 + [ANY] * (1 + len(pieces))
-        + ([VMEM, VMEM, ANY] if prior else []),
-        out_specs=[VMEM, ANY] + [VMEM] * (len(out_shape) - 2),
-        scratch_shapes=[
-            pltpu.VMEM((slots, clip_rows, depth), BF16),
-            pltpu.VMEM((len(hops), 2 * cols, cols), BF16),
-            pltpu.VMEM((clip_rows, 128), F32),
-            pltpu.VMEM((2, 8, cols), F32),
-            pltpu.SemaphoreType.DMA((len(pieces),)),
-            pltpu.SemaphoreType.DMA((len(hops),)),
-            pltpu.SemaphoreType.DMA((len(hops),)),
-        ],
-        input_output_aliases={6 + len(pieces) + 2: 1} if prior else {},
-        compiler_params=pltpu.CompilerParams(vmem_limit_bytes=need + 8 * MIB),
+        in_specs=[SMEM, SMEM, VMEM, VMEM] + [ANY] * (3 + len(pieces)) + ([VMEM, ANY, ANY] if prior else []),
+        out_specs=out_specs,
+        scratch_shapes=scratch,
+        input_output_aliases={7 + len(pieces) + 2: 1} if prior else {},
+        compiler_params=pltpu.CompilerParams(vmem_limit_bytes=60 * MIB),
         cost_estimate=pl.CostEstimate(flops=1, bytes_accessed=1, transcendentals=0),
         name="project",
-    )(where, scalars, sums, sample, other, scaled, *pieces, *earlier)
+    )(where, scalars, sums, mod, sample, other, scaled, *pieces, *earlier)
 
 
 def outer_kernel(picks, mod, edge, flipped, inputs, *outs):
     del picks
-    cols = flipped.shape[0]
-    if inputs.shape[0] == 1:
-        term = jnp.dot(flipped[...], inputs[0], preferred_element_type=F32)
-        terms = [term[:, half * cols : (half + 1) * cols] for half in range(2)]
-        mods = [mod[0, :, half * cols : (half + 1) * cols] for half in range(2)]
-    else:
-        terms = [jnp.dot(flipped[...], inputs[h], preferred_element_type=F32) for h in range(2)]
-        mods = [mod[0], mod[1]]
-    for half in range(2):
-        shift, gain = mods[half][0:1, :], 1.0 + mods[half][1:2, :]
-        term = (terms[half] - edge[:, 0:1]) * gain + edge[:, 1:2] * shift
+    mods = [mod[i] for i in range(mod.shape[0])]
+    for half, term in enumerate(gradient_halves(flipped, inputs, mods, edge)):
         for i, out in enumerate(outs[half::2]):
 
             @pl.when(pl.program_id(0) == i)
@@ -298,11 +349,15 @@
 def outer(picks, mod, edge, flipped, inputs, dtypes):
     cols, rows = flipped.shape
     count = len(picks)
-    group = inputs.shape[2] // cols
+    group = 2 if len(inputs.shape) == 2 else 1
 
     def spot(i, picks):
         return (picks[i], 0, 0)
 
+    if group == 2:
+        tokens = pl.BlockSpec((rows, 2 * cols), lambda i, picks: (0, picks[i]))
+    else:
+        tokens = pl.BlockSpec((2, rows, cols), spot)
     return pl.pallas_call(
         outer_kernel,
         out_shape=[jax.ShapeDtypeStruct((cols, cols), dtype) for dtype in dtypes],
@@ -313,13 +368,11 @@
                 pl.BlockSpec((2 // group, 2, group * cols), spot),
                 pl.BlockSpec((cols, 2), lambda i, picks: (0, 0)),
                 pl.BlockSpec((cols, rows), lambda i, picks: (0, 0)),
-                pl.BlockSpec((2 // group, rows, group * cols), spot),
+                tokens,
             ],
             out_specs=[pl.BlockSpec((cols, cols), lambda i, picks: (0, 0))] * (2 * count),
         ),
-        compiler_params=pltpu.CompilerParams(
-            vmem_limit_bytes=cols * (rows * 16 + cols * (16 * count + 16)) + 6 * MIB
-        ),
+        compiler_params=pltpu.CompilerParams(vmem_limit_bytes=60 * MIB),
         cost_estimate=pl.CostEstimate(
             flops=4 * rows * cols * cols * count,
             bytes_accessed=4 * rows * cols * (count + 1) + 4 * cols * cols * count,
@@ -422,7 +475,8 @@
     scalars = jnp.stack([sigma, jnp.float32(1.0 / math.sqrt(total_tokens))])
     owners = jnp.stack([clip ^ mask for mask in range(clips)]).astype(jnp.int32)
     where = jnp.stack(places + [shard % 2]).astype(jnp.int32)
-    scaled, sums = scale(owners, jnp.transpose(fake_mod[0]), fake_weight, fake_blocks)
+    by_place = jnp.swapaxes(fake_mod[0].reshape(2, shards // group, group * cols), 0, 1)
+    scaled, sums = scale(owners, fake_mod[0], fake_weight, fake_blocks)
     seen["sums"] = sums
     teacher_parts = {}
     own = gated("teacher", teacher_weight)
@@ -452,12 +506,13 @@
             add_hop(hop)
     cut = max(1, hops - 2)
     done = project(
-        where, scalars, sums, sample, noise, scaled, tokens[:cut], 0, (), False
+        where, scalars, sums, by_place, sample, noise, scaled, tokens[:cut], 0, (), hops, False
     )
     seen["soon"] = done[2]
     if cut < hops - 1:
         done = project(
-            where, scalars, sums, sample, noise, scaled, tokens[cut:], 2 * cols * cut, done, False
+            where, scalars, sums, by_place, sample, noise, scaled, tokens[cut:], 2 * cols * cut,
+            done, hops, False,
         )
     seen["early"] = done[2]
     for key, block in teacher_parts.items():
@@ -466,28 +521,27 @@
     for i in range(CHUNKS):
         cross(hops - 1, i)
     add_hop(hops - 1)
-    fake_velocity, inputs, stats, flipped, edge = project(
-        where, scalars, sums, sample, noise, scaled, tokens[-1:], 2 * cols * (hops - 1), done, True
-    )
-    by_place = jnp.swapaxes(fake_mod[0].reshape(2, shards // group, group * cols), 0, 1)
-    flipped = after(flipped, *(teacher_blocks[key] for key in far))
-
     def going(mask):
         return [bool(mask & order[0]) for _, order in orders]
 
-    held = {}
+    ranks = [[m for m in range(clips) if sum(going(m)) == n] for n in (2, 1, 0)]
+    where = jnp.concatenate([where, jnp.stack([clip ^ mask for mask in ranks[0]]).astype(jnp.int32)])
+    fake_velocity, inputs, stats, flipped, edge, *blocks = project(
+        where, scalars, sums, by_place, sample, noise, scaled, tokens[-1:], 2 * cols * (hops - 1),
+        done, hops, True,
+    )
+
+    held = dict(zip([(mask, half) for mask in ranks[0] for half in range(2)], blocks))
 
     def terms(masks, left):
         dtypes = [BF16 if out else F32 for mask in masks for out in going(mask)]
         got = outer([clip ^ mask for mask in masks], by_place, edge, left, inputs, dtypes)
         held.update(zip([(mask, half) for mask in masks for half in range(2)], got))
 
-    ranks = [[m for m in range(clips) if sum(going(m)) == n] for n in (2, 1, 0)]
-    terms(ranks[0], flipped)
     if ranks[1]:
-        terms(ranks[1], flipped)
+        terms(ranks[1], after(flipped, *blocks))
     ready = list(held.values())
-    halves = []
+    halves, relayed = [], []
     sent = {key: swap_clip(held[key], orders[key[1]][1][0], clips) for key in held if going(key[0])[key[1]]}
     firsts = [sent[key] for key in sent if key[0] in ranks[0]]
     seconds = [sent[key] for key in sent if key[0] not in ranks[0]]
@@ -500,21 +554,28 @@
                 if bit == order[0]:
                     got = sent[mask, half]
                 else:
-                    got = swap_clip(sum(part.astype(F32) for part in block).astype(BF16), bit, clips)
+                    block = sum(part.astype(F32) for part in block).astype(BF16)
+                    relayed.append(block)
+                    got = swap_clip(block, bit, clips)
                 mine[mask ^ bit].append(got)
         halves.append(mine[0])
     fake_grad = finish(halves)
 
     scaled, sums = scale(
-        owners, jnp.transpose(teacher_mod[0]), after(teacher_weight, *ready), teacher_blocks
+        owners, teacher_mod[0], after(teacher_weight, *ready), teacher_blocks
     )
-    depth = group * cols
-    velocity = 0.0
-    for p in range(width // depth):
-        left = inputs[p]
-        left = after(left, *firsts) if p == 0 else after(left, velocity)
-        right = scaled[p * depth : (p + 1) * depth]
-        velocity = velocity + jnp.dot(left, right, preferred_element_type=F32)
+    left = after(inputs, *relayed)
+
+    def add_place(p, total):
+        tokens = lax.dynamic_index_in_dim(left, p, 0, keepdims=False)
+        right = lax.dynamic_slice(scaled, (p * cols, 0), (cols, cols))
+        return total + jnp.dot(tokens, right, preferred_element_type=F32)
+
+    if group == 2:
+        velocity = jnp.dot(left, scaled, preferred_element_type=F32)
+    else:
+        velocity = jnp.zeros((clip_rows, cols), F32)
+        velocity = lax.fori_loop(0, width // cols, add_place, velocity)
     velocity = stats[:, 1:2] * (velocity - stats[:, 0:1] * sums[0, :1]) + sums[1, :1]
     away = sample.astype(F32) - (noised.astype(F32) - sigma * velocity)
     away = after(jnp.sum(jnp.abs(away)).reshape(1, 1), *seconds)

time: 229 us -> 208 us (0.908)
  local copies, waits for them, and re-layouts: 58.2 us -> 7.33 us
  Pallas kernels: 50 us -> 74.3 us
  other arithmetic: 5.58 us -> 12.6 us
  waiting for transfers between devices: 60.6 us -> 56.9 us
  matrix products: 11.9 us -> 14.9 us
    unnamed x98 -> x40, local copies, waits for them, and re-layouts: 49.9 us -> 1.36 us
    pallas_call x3, Pallas kernels: 22 us -> 36.2 us  [project(): pl.pallas_call(functools.partial(project_kernel, prior, last, plan, core_...]
    ppermute x16, waiting for transfers between devices: 10.3 us -> 0.06 us  [swap_clip(): return lax.ppermute(value, 'clip', [(i, i ^ bit) for i in range(count)])]
    pallas_call x2, Pallas kernels: 14.1 us -> 19.6 us  [scale(): pl.pallas_call(functools.partial(scale_kernel, list(blocks)), out_shape=(...]
    ppermute x6, waiting for transfers between devices: 43.5 us -> 48.6 us  [hop_to(): seen[name] = lax.ppermute(gated(name, source), 'fsdp', ring)]
    convert_element_type x2 -> x3, other arithmetic: 0.32 us -> 4.97 us  [the longest x2 3.71 us: per_device(): block = sum((part.astype(F32) for part in block)).astype(BF16)]
    pallas_call x3 -> x2, Pallas kernels: 10.2 us -> 14.7 us  [outer(): pl.pallas_call(outer_kernel, out_shape=[jax.ShapeDtypeStruct((cols, cols)...]
    squeeze x1 -> x0, local copies, waits for them, and re-layouts: 4.16 us -> none  [per_device(): left = inputs[p]]
  transfers between devices with their start and end apart: 32 -> 32, of which waited for: 12 -> 9; matrix products, arithmetic and copies ran while one was open for 14% -> 16% of each run, Pallas kernels for 19% -> 34%
where the time goes in v5:
time: 208 us; the launch traced here: 207 us
  Pallas kernels  74.3 us (36%)
  waiting for transfers between devices  56.9 us (27%)
  starting transfers between devices  36.8 us (18%)
  matrix products  14.9 us (7%)
  other arithmetic  12.6 us (6%)
  local copies, waits for them, and re-layouts  7.33 us (4%)
  between operations  4.28 us (2%)
    ppermute x6, waiting for transfers between devices, hop_to(): seen[name] = lax.ppermute(gated(name, source), 'fsdp', ring)  48.6 us
    pallas_call x3, Pallas kernels, project(): pl.pallas_call(functools.partial(project_kernel, prior, last, plan, core_...  36.2 us
    pallas_call x2, Pallas kernels, scale(): pl.pallas_call(functools.partial(scale_kernel, list(blocks)), out_shape=(...  19.6 us
    ppermute x16, starting transfers between devices, swap_clip(): return lax.ppermute(value, 'clip', [(i, i ^ bit) for i in range(count)])  17.3 us
    ppermute x6, starting transfers between devices, hop_to(): seen[name] = lax.ppermute(gated(name, source), 'fsdp', ring)  15.5 us
    dot_general x1, matrix products, per_device(): velocity = jnp.dot(left, scaled, preferred_element_type=F32)  14.9 us
    pallas_call x2, Pallas kernels, outer(): pl.pallas_call(outer_kernel, out_shape=[jax.ShapeDtypeStruct((cols, cols)...  14.7 us
    ppermute x3, waiting for transfers between devices, per_device(): lax.ppermute(away, 'fsdp', [(i, i ^ bit) for i in range(shards)])  6.95 us
  transfers between devices with their start and end apart: 32, of which 9 were waited for; matrix products, arithmetic and copies ran while one was open for 16% of the time, Pallas kernels for 34%

profile of v5, /device:TPU:0, one launch (start us, length us, event | category | flops | bytes accessed | tf_op | source)
XLA Modules:
  0.0 207.1 jit_solution(5328100742942684593)
XLA Ops:
  0.6 3.0 %collective-permute-start = (bf16[1280,640]{1,0:T(8,128)(2,1)}, bf16[1280,640]{1,0:T(8,128)(2,1)S(1)}, u32[]{:S(2)}, u32[]{:S(2)}) collective-permute-start(bf16[1280,640]{1,0:T(8,128)(2,1)} %weight.1), channel_id=1, source_target_pairs={{0,8},{8,0},{16,24},{24,16},{1,9},{9,1},{17,25},{25,17},{2,10},{10... | collective-permute-start | bytes 4915208 | tf_op jit(solution)/shard_map/ppermute | solution.py:27
  3.6 1.5 collective-permute-start.3
  5.8 2.2 %fusion.1.refs_0_ = bf16[1024,640]{1,0:T(8,128)(2,1)S(1)} fusion(bf16[1024,640]{1,0:T(8,128)(2,1)} %sample.5, bf16[1024,640]{1,0:T(8,128)(2,1)} %other.5, f32[]{:T(128)S(6)} %sub.57, f32[]{:T(128)} %bitcast), kind=kLoop, calls=%fused_computation.3 | loop fusion | flops 3932160 | bytes 3932168 | tf_op jit(solution)/shard_map/convert_element_type | solution.py:426
  8.3 2.6 %collective-permute-start.9 = (bf16[512,640]{1,0:T(8,128)(2,1)S(1)}, bf16[512,640]{1,0:T(8,128)(2,1)S(1)}, u32[]{:S(2)}, u32[]{:S(2)}) collective-permute-start(bf16[512,640]{1,0:T(8,128)(2,1)S(1)} %get-tuple-element.93), channel_id=1, source_target_pairs={{0,4},{1,5},{4,6},{5,7},{6,2},{7,3},{2,0},{3,1},{8,12},{9,13},{12,... | collective-permute-start | bytes 1966088 | tf_op jit(solution)/shard_map/ppermute | solution.py:452
  10.9 1.6 collective-permute-start.5
  12.5 13.5 %collective-permute-done.9.refs_4_ = bf16[512,640]{1,0:T(8,128)(2,1)S(1)} collective-permute-done((bf16[512,640]{1,0:T(8,128)(2,1)S(1)}, bf16[512,640]{1,0:T(8,128)(2,1)S(1)}, u32[]{:S(2)}, u32[]{:S(2)}) %collective-permute-start.9) | collective-permute-done | bytes 655392 | tf_op jit(solution)/shard_map/ppermute | solution.py:452
  26.0 13.6 %collective-permute-done.5.refs_2_ = bf16[512,640]{1,0:T(8,128)(2,1)S(1)} collective-permute-done((bf16[512,640]{1,0:T(8,128)(2,1)S(1)}, bf16[512,640]{1,0:T(8,128)(2,1)S(1)}, u32[]{:S(2)}, u32[]{:S(2)}) %collective-permute-start.5) | collective-permute-done | bytes 655392 | tf_op jit(solution)/shard_map/ppermute | solution.py:452
  39.6 3.4 %collective-permute-start.6 = (bf16[512,640]{1,0:T(8,128)(2,1)S(1)}, bf16[512,640]{1,0:T(8,128)(2,1)}, u32[]{:S(2)}, u32[]{:S(2)}) collective-permute-start(bf16[512,640]{1,0:T(8,128)(2,1)S(1)} %collective-permute-done.5.refs_2_), channel_id=1, source_target_pairs={{0,4},{1,5},{4,6},{5,7},{6,2},{7,3},{2,0},{3,1},{8,12},{9,13},{12,... | collective-permute-start | bytes 1966088 | tf_op jit(solution)/shard_map/ppermute | solution.py:452
  43.1 1.0 collective-permute-start.12
  44.1 1.6 collective-permute-start.2
  45.7 1.2 slice.31
  47.0 0.9 copy-done.17
  47.8 1.5 collective-permute-start.4
  49.3 1.4 fusion.4
  51.3 6.8 %collective-permute-done.6.refs_0_ = bf16[512,640]{1,0:T(8,128)(2,1)} collective-permute-done((bf16[512,640]{1,0:T(8,128)(2,1)S(1)}, bf16[512,640]{1,0:T(8,128)(2,1)}, u32[]{:S(2)}, u32[]{:S(2)}) %collective-permute-start.6) | collective-permute-done | bytes 655392 | tf_op jit(solution)/shard_map/ppermute | solution.py:452
  58.1 1.0 collective-permute-start.14
  59.1 12.6 %collective-permute-done.12.refs_2_ = bf16[512,640]{1,0:T(8,128)(2,1)} collective-permute-done((bf16[512,640]{1,0:T(8,128)(2,1)S(1)}, bf16[512,640]{1,0:T(8,128)(2,1)}, u32[]{:S(2)}, u32[]{:S(2)}) %collective-permute-start.12) | collective-permute-done | bytes 655392 | tf_op jit(solution)/shard_map/ppermute | solution.py:452
  71.7 3.5 %collective-permute-start.7 = (bf16[512,640]{1,0:T(8,128)(2,1)}, bf16[512,640]{1,0:T(8,128)(2,1)}, u32[]{:S(2)}, u32[]{:S(2)}) collective-permute-start(bf16[512,640]{1,0:T(8,128)(2,1)} %collective-permute-done.6.refs_0_), channel_id=1, source_target_pairs={{0,4},{1,5},{4,6},{5,7},{6,2},{7,3},{2,0},{3,1},{8,12},{9,13},{12,... | collective-permute-start | bytes 1966088 | tf_op jit(solution)/shard_map/ppermute | solution.py:452
  76.9 9.7 %scale.2 = (bf16[5120,640]{1,0:T(8,128)(2,1)}, f32[2,8,640]{2,1,0:T(8,128)}) custom-call(s32[4]{0:T(128)} %pad_add_fusion.where, f32[8,2,640]{2,1,0:T(2,128)} %bitcast.25, bf16[1280,640]{1,0:T(8,128)(2,1)} %weight.1, bf16[1280,640]{1,0:T(8,128)(2,1)} %copy-done.5, bf16[640,640]{1,0:T(8,128)(2,1)} %collective-permute-done.2.refs_1_, ...), custom_call_target="tpu_custom_call" | custom-call | flops 1 | bytes 1 | tf_op jit(solution)/shard_map/scale/pallas_call | solution.py:105
  87.2 2.1 %collective-permute-done.7.refs_0_ = bf16[512,640]{1,0:T(8,128)(2,1)} collective-permute-done((bf16[512,640]{1,0:T(8,128)(2,1)}, bf16[512,640]{1,0:T(8,128)(2,1)}, u32[]{:S(2)}, u32[]{:S(2)}) %collective-permute-start.7) | collective-permute-done | bytes 655392 | tf_op jit(solution)/shard_map/ppermute | solution.py:452
  89.3 3.4 %collective-permute-start.15 = (bf16[512,640]{1,0:T(8,128)(2,1)}, bf16[512,640]{1,0:T(8,128)(2,1)}, u32[]{:S(2)}, u32[]{:S(2)}) collective-permute-start(bf16[512,640]{1,0:T(8,128)(2,1)} %collective-permute-done.12.refs_2_), channel_id=1, source_target_pairs={{0,4},{1,5},{4,6},{5,7},{6,2},{7,3},{2,0},{3,1},{8,12},{9,13},{12,... | collective-permute-start | bytes 1966088 | tf_op jit(solution)/shard_map/ppermute | solution.py:452
  92.7 0.6 stack.55.where
  93.3 0.6 pad_maximum_fusion.scalars
  94.0 12.2 %project.3 = (f32[1024,640]{1,0:T(8,128)}, bf16[1024,5120]{1,0:T(8,128)(2,1)}, f32[1024,128]{1,0:T(8,128)}) custom-call(s32[5]{0:T(128)} %stack.55.where, f32[2]{0:T(128)} %pad_maximum_fusion.scalars, f32[2,8,640]{2,1,0:T(8,128)} %get-tuple-element.46.sums, f32[4,2,1280]{2,1,0:T(2,128)} %bitcast.26, bf16[1024,640]{1,0:T(8,128)(2,1)} %sample.5, ...), custom_call_target="tpu_custom_call" | custom-call | flops 1 | bytes 1 | tf_op jit(solution)/shard_map/project/pallas_call | solution.py:325
  106.2 9.4 %project.4 = (f32[1024,640]{1,0:T(8,128)}, bf16[1024,5120]{1,0:T(8,128)(2,1)}, f32[1024,128]{1,0:T(8,128)}) custom-call(s32[5]{0:T(128)} %stack.55.where, f32[2]{0:T(128)} %pad_maximum_fusion.scalars, f32[2,8,640]{2,1,0:T(8,128)} %get-tuple-element.46.sums, f32[4,2,1280]{2,1,0:T(2,128)} %bitcast.27, ...), custom_call_target="tpu_custom_call", output_to_operand_aliasing={{1}: (13, {})} | custom-call | flops 1 | bytes 1 | tf_op jit(solution)/shard_map/project/pallas_call | solution.py:325
  116.4 0.7 concatenate.4.where
  117.1 1.2 collective-permute-done.20.refs_3_
  118.3 14.7 %project.5 = (f32[1024,640]{1,0:T(8,128)}, bf16[1024,5120]{1,0:T(8,128)(2,1)}, f32[1024,128]{1,0:T(8,128)}, bf16[640,1024]{1,0:T(8,128)(2,1)}, f32[640,2]{1,0:T(...) custom-call(s32[6]{0:T(128)} %concatenate.4.where, ...), custom_call_target="tpu_custom_call", output_to_operand_aliasing={{1}: (13, {})} | custom-call | flops 1 | bytes 1 | tf_op jit(solution)/shard_map/project/pallas_call | solution.py:325
  133.0 0.8 collective-permute-start.22
  134.4 1.9 collective-permute-start.21
  136.3 9.4 %outer.2 = (bf16[640,640]{1,0:T(8,128)(2,1)}, f32[640,640]{1,0:T(8,128)}, f32[640,640]{1,0:T(8,128)}, bf16[640,640]{1,0:T(8,128)(2,1)}) custom-call(s32[2]{0:T(128)} %pad_add_fusion.1.picks, f32[4,2,1280]{2,1,0:T(2,128)} %bitcast.29, f32[640,2]{1,0:T(8,128)} %get-tuple-element.63.edge, bf16[640,1024]{1,0:T(8,128)(2,1)} %get-tuple-element.82.flipped, ...), custom_call_target="tpu_custom_call" | custom-call | flops 3355443200 | bytes 11141120 | tf_op jit(solution)/shard_map/outer/pallas_call | solution.py:361
  145.8 1.3 collective-permute-start.26
  147.1 9.9 %scale.3 = (bf16[5120,640]{1,0:T(8,128)(2,1)}, f32[2,8,640]{2,1,0:T(8,128)}) custom-call(s32[4]{0:T(128)} %pad_add_fusion.where, f32[8,2,640]{2,1,0:T(2,128)} %bitcast.31, bf16[1280,640]{1,0:T(8,128)(2,1)} %weight.2, bf16[640,640]{1,0:T(8,128)(2,1)} %copy-done.11, bf16[640,640]{1,0:T(8,128)(2,1)} %collective-permute-done.23.refs_1_, ...), custom_call_target="tpu_custom_call" | custom-call | flops 1 | bytes 1 | tf_op jit(solution)/shard_map/scale/pallas_call | solution.py:105
  157.0 0.9 slice_reduce_fusion.3
  158.5 1.4 add_convert_fusion
  159.9 0.8 collective-permute-start.31
  160.7 2.3 %add_convert_fusion.1 = bf16[640,640]{1,0:T(8,128)(2,1)} fusion(f32[640,640]{1,0:T(8,128)S(1)} %copy-done.8, bf16[640,640]{1,0:T(8,128)(2,1)} %collective-permute-done.21), kind=kLoop, calls=%fused_computation.11 | loop fusion | flops 1228800 | bytes 3276800 | tf_op jit(solution)/shard_map/convert_element_type | solution.py:557
  163.0 2.0 collective-permute-start.30
  164.9 14.9 %fusion.3 = (f32[]{:T(128)}, f32[1024,640]{1,0:T(8,128)}) fusion(bf16[1024,640]{1,0:T(8,128)(2,1)S(1)} %copy-done.2, bf16[1024,640]{1,0:T(8,128)(2,1)S(1)} %copy-done.4, f32[640]{0:T(1024)S(1)} %get-tuple-element.88, f32[640]{0:T(1024)S(1)} %get-tuple-element.87, f32[1024]{0:T(1024)S(1)} %get-tuple-element.86, f32[1024]{0:T(1024)S(1)} %get-tuple-element.85, ...), kind=kOutput, calls=%fused_computation.5 | convolution fusion | flops 6718095360 | bytes 22295560 | tf_op jit(solution)/shard_map/dot_general | solution.py:575
  179.8 5.4 %outer.3 = (f32[640,640]{1,0:T(8,128)}, f32[640,640]{1,0:T(8,128)}) custom-call(s32[1]{0:T(128)} %bitcast.7.picks, f32[4,2,1280]{2,1,0:T(2,128)} %bitcast.30, f32[640,2]{1,0:T(8,128)} %get-tuple-element.63.edge, bf16[640,1024]{1,0:T(8,128)(2,1)} %get-tuple-element.82.flipped, bf16[1024,5120]{1,0:T(8,128)(2,1)} %get-tuple-element.70.inputs), custom_call_target="tpu_custom_call" | custom-call | flops 1677721600 | bytes 6881280 | tf_op jit(solution)/shard_map/outer/pallas_call | solution.py:361
  185.3 1.4 collective-permute-done.27
  187.9 1.4 collective-permute-start.28
  189.3 2.3 %collective-permute-done.28 = f32[1,1]{1,0:T(1,128)} collective-permute-done((f32[1,1]{1,0:T(1,128)}, f32[1,1]{1,0:T(1,128)}, u32[]{:S(2)}, u32[]{:S(2)}) %collective-permute-start.28) | collective-permute-done | bytes 36 | tf_op jit(solution)/shard_map/ppermute | solution.py:584
  192.3 1.4 collective-permute-start.29
  193.7 3.2 %collective-permute-done.29 = f32[1,1]{1,0:T(1,128)} collective-permute-done((f32[1,1]{1,0:T(1,128)}, f32[1,1]{1,0:T(1,128)}, u32[]{:S(2)}, u32[]{:S(2)}) %collective-permute-start.29) | collective-permute-done | bytes 36 | tf_op jit(solution)/shard_map/ppermute | solution.py:584
  197.5 3.5 %multiply_reduce_fusion = (f32[640]{0:T(1024)S(1)}, f32[1024,640]{1,0:T(8,128)S(1)}) fusion(bf16[1024,640]{1,0:T(8,128)(2,1)} %param.11, f32[]{:T(128)} %bitcast.18, f32[1024,640]{1,0:T(8,128)} %get-tuple-element.80, f32[640]{0:T(1024)S(1)} %get-tuple-element.88, f32[1024,640]{1,0:T(8,128)} %get-tuple-element.96, f32[640]{0:T(1024)S(1)} %get-tuple-element.87, ...), kind=kLoop, calls=%fused_computation.6 | loop fusion | flops 6552960 | bytes 9190920 | tf_op jit(solution)/shard_map/reduce_sum | solution.py:589
  201.7 1.3 multiply_convert_fusion
  203.4 3.7 %finish.1 = f32[2,640,640]{2,1,0:T(8,128)} custom-call(f32[640,640]{1,0:T(8,128)S(1)} %copy-done, bf16[640,640]{1,0:T(8,128)(2,1)S(1)} %collective-permute-done.25.refs_1_, bf16[640,640]{1,0:T(8,128)(2,1)S(1)} %collective-permute-done.30.refs_2_, f32[640,640]{1,0:T(8,128)S(1)} %copy-done.1, bf16[640,640]{1,0:T(8,128)(2,1)S(1)} %collective-permute-done.26.refs_4_, ...), custom_call_target="tpu_custom_call" | custom-call | tf_op jit(solution)/shard_map/finish/pallas_call | solution.py:398
  (84 shorter events, 6.4 us)
Async XLA Ops:
  0.6 39.0 %collective-permute-start = (bf16[1280,640]{1,0:T(8,128)(2,1)}, bf16[1280,640]{1,0:T(8,128)(2,1)S(1)}, u32[]{:S(2)}, u32[]{:S(2)}) collective-permute-start(bf16[1280,640]{1,0:T(8,128)(2,1)} %weight.1), channel_id=1, source_target_pairs={{0,8},{8,0},{16,24},{24,16},{1,9},{9,1},{17,25},{25,17},{2,10},{10... | collective-permute-start | bytes 4915208 | tf_op jit(solution)/shard_map/ppermute | solution.py:27
  3.6 39.4 %collective-permute-start.3 = (bf16[1280,640]{1,0:T(8,128)(2,1)}, bf16[1280,640]{1,0:T(8,128)(2,1)}, u32[]{:S(2)}, u32[]{:S(2)}) collective-permute-start(bf16[1280,640]{1,0:T(8,128)(2,1)} %weight.1), channel_id=1, source_target_pairs={{0,16},{8,24},{16,0},{24,8},{1,17},{9,25},{17,1},{25,9},{2,18},{10... | collective-permute-start | bytes 4915208 | tf_op jit(solution)/shard_map/ppermute | solution.py:27
  8.1 38.9 %copy-start.3 = (bf16[1024,640]{1,0:T(8,128)(2,1)}, bf16[1024,640]{1,0:T(8,128)(2,1)S(1)}, u32[]{:S(2)}) copy-start(bf16[1024,640]{1,0:T(8,128)(2,1)S(1)} %fusion.1.refs_0_) | copy-start | bytes 3932164
  8.1 41.3 %copy-start.6 = (bf16[1280,640]{1,0:T(8,128)(2,1)S(1)}, bf16[1280,640]{1,0:T(8,128)(2,1)}, u32[]{:S(2)}) copy-start(bf16[1280,640]{1,0:T(8,128)(2,1)} %weight.2) | copy-start | bytes 4915204
  8.1 36.0 %collective-permute-start.1 = (bf16[1024,640]{1,0:T(8,128)(2,1)S(1)}, bf16[1024,640]{1,0:T(8,128)(2,1)S(1)}, u32[]{:S(2)}, u32[]{:S(2)}) collective-permute-start(bf16[1024,640]{1,0:T(8,128)(2,1)S(1)} %fusion.1.refs_0_), channel_id=1, source_target_pairs={{0,1},{1,0},{2,3},{3,2},{4,5},{5,4},{6,7},{7,6},{8,9},{9,8},{10,11... | collective-permute-start | bytes 3932168 | tf_op jit(solution)/shard_map/ppermute | solution.py:463
  8.3 17.7 %collective-permute-start.9 = (bf16[512,640]{1,0:T(8,128)(2,1)S(1)}, bf16[512,640]{1,0:T(8,128)(2,1)S(1)}, u32[]{:S(2)}, u32[]{:S(2)}) collective-permute-start(bf16[512,640]{1,0:T(8,128)(2,1)S(1)} %get-tuple-element.93), channel_id=1, source_target_pairs={{0,4},{1,5},{4,6},{5,7},{6,2},{7,3},{2,0},{3,1},{8,12},{9,13},{12,... | collective-permute-start | bytes 1966088 | tf_op jit(solution)/shard_map/ppermute | solution.py:452
  10.9 28.7 %collective-permute-start.5 = (bf16[512,640]{1,0:T(8,128)(2,1)S(1)}, bf16[512,640]{1,0:T(8,128)(2,1)S(1)}, u32[]{:S(2)}, u32[]{:S(2)}) collective-permute-start(bf16[512,640]{1,0:T(8,128)(2,1)S(1)} %get-tuple-element.94), channel_id=1, source_target_pairs={{0,4},{1,5},{4,6},{5,7},{6,2},{7,3},{2,0},{3,1},{8,12},{9,13},{12,... | collective-permute-start | bytes 1966088 | tf_op jit(solution)/shard_map/ppermute | solution.py:452
  26.0 24.7 %copy-start.15 = (bf16[512,640]{1,0:T(8,128)(2,1)}, bf16[512,640]{1,0:T(8,128)(2,1)S(1)}, u32[]{:S(2)}) copy-start(bf16[512,640]{1,0:T(8,128)(2,1)S(1)} %collective-permute-done.9.refs_4_) | copy-start | bytes 1966084
  26.0 21.0 %collective-permute-start.10 = (bf16[512,640]{1,0:T(8,128)(2,1)S(1)}, bf16[512,640]{1,0:T(8,128)(2,1)S(1)}, u32[]{:S(2)}, u32[]{:S(2)}) collective-permute-start(bf16[512,640]{1,0:T(8,128)(2,1)S(1)} %collective-permute-done.9.refs_4_), channel_id=1, source_target_pairs={{0,1},{1,0},{2,3},{3,2},{4,5},{5,4},{6,7},{7,6},{8,9},{9,8},{10,11... | collective-permute-start | bytes 1966088 | tf_op jit(solution)/shard_map/ppermute | solution.py:456
  39.6 11.1 %copy-start.16 = (bf16[512,640]{1,0:T(8,128)(2,1)}, bf16[512,640]{1,0:T(8,128)(2,1)S(1)}, u32[]{:S(2)}) copy-start(bf16[512,640]{1,0:T(8,128)(2,1)S(1)} %collective-permute-done.5.refs_2_) | copy-start | bytes 1966084
  39.6 11.1 %collective-permute-start.8 = (bf16[512,640]{1,0:T(8,128)(2,1)S(1)}, bf16[512,640]{1,0:T(8,128)(2,1)S(1)}, u32[]{:S(2)}, u32[]{:S(2)}) collective-permute-start(bf16[512,640]{1,0:T(8,128)(2,1)S(1)} %collective-permute-done.5.refs_2_), channel_id=1, source_target_pairs={{0,1},{1,0},{2,3},{3,2},{4,5},{5,4},{6,7},{7,6},{8,9},{9,8},{10,11... | collective-permute-start | bytes 1966088 | tf_op jit(solution)/shard_map/ppermute | solution.py:456
  39.6 11.0 %copy-start.5 = (bf16[1280,640]{1,0:T(8,128)(2,1)}, bf16[1280,640]{1,0:T(8,128)(2,1)S(1)}, u32[]{:S(2)}) copy-start(bf16[1280,640]{1,0:T(8,128)(2,1)S(1)} %collective-permute-done.refs_0_.refs_5_) | copy-start | bytes 4915204
  39.6 18.5 %collective-permute-start.6 = (bf16[512,640]{1,0:T(8,128)(2,1)S(1)}, bf16[512,640]{1,0:T(8,128)(2,1)}, u32[]{:S(2)}, u32[]{:S(2)}) collective-permute-start(bf16[512,640]{1,0:T(8,128)(2,1)S(1)} %collective-permute-done.5.refs_2_), channel_id=1, source_target_pairs={{0,4},{1,5},{4,6},{5,7},{6,2},{7,3},{2,0},{3,1},{8,12},{9,13},{12,... | collective-permute-start | bytes 1966088 | tf_op jit(solution)/shard_map/ppermute | solution.py:452
  43.1 28.6 %collective-permute-start.12 = (bf16[512,640]{1,0:T(8,128)(2,1)S(1)}, bf16[512,640]{1,0:T(8,128)(2,1)}, u32[]{:S(2)}, u32[]{:S(2)}) collective-permute-start(bf16[512,640]{1,0:T(8,128)(2,1)S(1)} %collective-permute-done.9.refs_4_), channel_id=1, source_target_pairs={{0,4},{1,5},{4,6},{5,7},{6,2},{7,3},{2,0},{3,1},{8,12},{9,13},{12,... | collective-permute-start | bytes 1966088 | tf_op jit(solution)/shard_map/ppermute | solution.py:452
  44.1 6.6 %copy-start.10 = (bf16[1024,640]{1,0:T(8,128)(2,1)}, bf16[1024,640]{1,0:T(8,128)(2,1)S(1)}, u32[]{:S(2)}) copy-start(bf16[1024,640]{1,0:T(8,128)(2,1)S(1)} %collective-permute-done.1.refs_1_) | copy-start | bytes 3932164
  44.1 31.1 %collective-permute-start.2 = (bf16[640,640]{1,0:T(8,128)(2,1)S(1)}, bf16[640,640]{1,0:T(8,128)(2,1)}, u32[]{:S(2)}, u32[]{:S(2)}) collective-permute-start(bf16[640,640]{1,0:T(8,128)(2,1)S(1)} %slice.30), channel_id=1, source_target_pairs={{0,16},{8,24},{16,0},{24,8},{1,17},{9,25},{17,1},{25,9},{2,18},{10... | collective-permute-start | bytes 2457608 | tf_op jit(solution)/shard_map/ppermute | solution.py:27
  47.8 27.9 %collective-permute-start.4 = (bf16[640,640]{1,0:T(8,128)(2,1)S(1)}, bf16[640,640]{1,0:T(8,128)(2,1)}, u32[]{:S(2)}, u32[]{:S(2)}) collective-permute-start(bf16[640,640]{1,0:T(8,128)(2,1)S(1)} %slice.31), channel_id=1, source_target_pairs={{0,8},{8,0},{16,24},{24,16},{1,9},{9,1},{17,25},{25,17},{2,10},{10... | collective-permute-start | bytes 2457608 | tf_op jit(solution)/shard_map/ppermute | solution.py:27
  50.7 25.0 %copy-start.18 = (bf16[512,640]{1,0:T(8,128)(2,1)}, bf16[512,640]{1,0:T(8,128)(2,1)S(1)}, u32[]{:S(2)}) copy-start(bf16[512,640]{1,0:T(8,128)(2,1)S(1)} %collective-permute-done.8.refs_3_) | copy-start | bytes 1966084
  50.7 35.9 %collective-permute-start.13 = (bf16[640,640]{1,0:T(8,128)(2,1)}, bf16[640,640]{1,0:T(8,128)(2,1)S(1)}, u32[]{:S(2)}, u32[]{:S(2)}) collective-permute-start(bf16[640,640]{1,0:T(8,128)(2,1)} %get-tuple-element.92), channel_id=1, source_target_pairs={{0,8},{8,0},{16,24},{24,16},{1,9},{9,1},{17,25},{25,17},{2,10},{10... | collective-permute-start | bytes 2457608 | tf_op jit(solution)/shard_map/ppermute | solution.py:27
  58.1 28.6 %collective-permute-start.14 = (bf16[640,640]{1,0:T(8,128)(2,1)}, bf16[640,640]{1,0:T(8,128)(2,1)S(1)}, u32[]{:S(2)}, u32[]{:S(2)}) collective-permute-start(bf16[640,640]{1,0:T(8,128)(2,1)} %get-tuple-element.91), channel_id=1, source_target_pairs={{0,16},{8,24},{16,0},{24,8},{1,17},{9,25},{17,1},{25,9},{2,18},{10... | collective-permute-start | bytes 2457608 | tf_op jit(solution)/shard_map/ppermute | solution.py:27
  71.7 17.6 %collective-permute-start.7 = (bf16[512,640]{1,0:T(8,128)(2,1)}, bf16[512,640]{1,0:T(8,128)(2,1)}, u32[]{:S(2)}, u32[]{:S(2)}) collective-permute-start(bf16[512,640]{1,0:T(8,128)(2,1)} %collective-permute-done.6.refs_0_), channel_id=1, source_target_pairs={{0,4},{1,5},{4,6},{5,7},{6,2},{7,3},{2,0},{3,1},{8,12},{9,13},{12,... | collective-permute-start | bytes 1966088 | tf_op jit(solution)/shard_map/ppermute | solution.py:452
  75.2 40.4 %collective-permute-start.18 = (bf16[640,640]{1,0:T(8,128)(2,1)}, bf16[640,640]{1,0:T(8,128)(2,1)S(1)}, u32[]{:S(2)}, u32[]{:S(2)}) collective-permute-start(bf16[640,640]{1,0:T(8,128)(2,1)} %get-tuple-element.92), channel_id=1, source_target_pairs={{0,16},{8,24},{16,0},{24,8},{1,17},{9,25},{17,1},{25,9},{2,18},{10... | collective-permute-start | bytes 2457608 | tf_op jit(solution)/shard_map/ppermute | solution.py:27
  75.7 39.9 %collective-permute-start.19 = (bf16[640,640]{1,0:T(8,128)(2,1)}, bf16[640,640]{1,0:T(8,128)(2,1)S(1)}, u32[]{:S(2)}, u32[]{:S(2)}) collective-permute-start(bf16[640,640]{1,0:T(8,128)(2,1)} %get-tuple-element.91), channel_id=1, source_target_pairs={{0,8},{8,0},{16,24},{24,16},{1,9},{9,1},{17,25},{25,17},{2,10},{10... | collective-permute-start | bytes 2457608 | tf_op jit(solution)/shard_map/ppermute | solution.py:27
  86.6 29.6 %copy-start.11 = (bf16[640,640]{1,0:T(8,128)(2,1)}, bf16[640,640]{1,0:T(8,128)(2,1)S(1)}, u32[]{:S(2)}) copy-start(bf16[640,640]{1,0:T(8,128)(2,1)S(1)} %collective-permute-done.13.refs_0_) | copy-start | bytes 2457604
  86.6 19.5 %collective-permute-start.16 = (bf16[512,640]{1,0:T(8,128)(2,1)}, bf16[512,640]{1,0:T(8,128)(2,1)}, u32[]{:S(2)}, u32[]{:S(2)}) collective-permute-start(bf16[512,640]{1,0:T(8,128)(2,1)} %collective-permute-done.6.refs_0_), channel_id=1, source_target_pairs={{0,1},{1,0},{2,3},{3,2},{4,5},{5,4},{6,7},{7,6},{8,9},{9,8},{10,11... | collective-permute-start | bytes 1966088 | tf_op jit(solution)/shard_map/ppermute | solution.py:456
  86.7 29.6 %copy-start.12 = (bf16[640,640]{1,0:T(8,128)(2,1)}, bf16[640,640]{1,0:T(8,128)(2,1)S(1)}, u32[]{:S(2)}) copy-start(bf16[640,640]{1,0:T(8,128)(2,1)S(1)} %collective-permute-done.14.refs_3_) | copy-start | bytes 2457604
  86.7 19.5 %collective-permute-start.17 = (bf16[512,640]{1,0:T(8,128)(2,1)}, bf16[512,640]{1,0:T(8,128)(2,1)}, u32[]{:S(2)}, u32[]{:S(2)}) collective-permute-start(bf16[512,640]{1,0:T(8,128)(2,1)} %collective-permute-done.12.refs_2_), channel_id=1, source_target_pairs={{0,1},{1,0},{2,3},{3,2},{4,5},{5,4},{6,7},{7,6},{8,9},{9,8},{10,11... | collective-permute-start | bytes 1966088 | tf_op jit(solution)/shard_map/ppermute | solution.py:456
  89.3 26.4 %collective-permute-start.15 = (bf16[512,640]{1,0:T(8,128)(2,1)}, bf16[512,640]{1,0:T(8,128)(2,1)}, u32[]{:S(2)}, u32[]{:S(2)}) collective-permute-start(bf16[512,640]{1,0:T(8,128)(2,1)} %collective-permute-done.12.refs_2_), channel_id=1, source_target_pairs={{0,4},{1,5},{4,6},{5,7},{6,2},{7,3},{2,0},{3,1},{8,12},{9,13},{12,... | collective-permute-start | bytes 1966088 | tf_op jit(solution)/shard_map/ppermute | solution.py:452
  106.2 10.9 %collective-permute-start.11 = (bf16[512,640]{1,0:T(8,128)(2,1)}, bf16[512,640]{1,0:T(8,128)(2,1)}, u32[]{:S(2)}, u32[]{:S(2)}) collective-permute-start(bf16[512,640]{1,0:T(8,128)(2,1)} %collective-permute-done.7.refs_0_), channel_id=1, source_target_pairs={{0,1},{1,0},{2,3},{3,2},{4,5},{5,4},{6,7},{7,6},{8,9},{9,8},{10,11... | collective-permute-start | bytes 1966088 | tf_op jit(solution)/shard_map/ppermute | solution.py:456
  115.6 17.3 %copy-start.13 = (bf16[640,640]{1,0:T(8,128)(2,1)}, bf16[640,640]{1,0:T(8,128)(2,1)S(1)}, u32[]{:S(2)}) copy-start(bf16[640,640]{1,0:T(8,128)(2,1)S(1)} %collective-permute-done.18.refs_2_) | copy-start | bytes 2457604
  115.7 17.3 %copy-start.14 = (bf16[640,640]{1,0:T(8,128)(2,1)}, bf16[640,640]{1,0:T(8,128)(2,1)S(1)}, u32[]{:S(2)}) copy-start(bf16[640,640]{1,0:T(8,128)(2,1)S(1)} %collective-permute-done.19.refs_5_) | copy-start | bytes 2457604
  115.7 2.6 %collective-permute-start.20 = (bf16[512,640]{1,0:T(8,128)(2,1)}, bf16[512,640]{1,0:T(8,128)(2,1)}, u32[]{:S(2)}, u32[]{:S(2)}) collective-permute-start(bf16[512,640]{1,0:T(8,128)(2,1)} %collective-permute-done.15.refs_2_), channel_id=1, source_target_pairs={{0,1},{1,0},{2,3},{3,2},{4,5},{5,4},{6,7},{7,6},{8,9},{9,8},{10,11... | collective-permute-start | bytes 1966088 | tf_op jit(solution)/shard_map/ppermute | solution.py:456
  116.2 29.6 %collective-permute-start.23 = (bf16[640,640]{1,0:T(8,128)(2,1)S(1)}, bf16[640,640]{1,0:T(8,128)(2,1)}, u32[]{:S(2)}, u32[]{:S(2)}) collective-permute-start(bf16[640,640]{1,0:T(8,128)(2,1)S(1)} %collective-permute-done.13.refs_0_), channel_id=1, source_target_pairs={{0,16},{8,24},{16,0},{24,8},{1,17},{9,25},{17,1},{25,9},{2,18},{10... | collective-permute-start | bytes 2457608 | tf_op jit(solution)/shard_map/ppermute | solution.py:27
  116.3 30.8 %collective-permute-start.24 = (bf16[640,640]{1,0:T(8,128)(2,1)S(1)}, bf16[640,640]{1,0:T(8,128)(2,1)}, u32[]{:S(2)}, u32[]{:S(2)}) collective-permute-start(bf16[640,640]{1,0:T(8,128)(2,1)S(1)} %collective-permute-done.14.refs_3_), channel_id=1, source_target_pairs={{0,8},{8,0},{16,24},{24,16},{1,9},{9,1},{17,25},{25,17},{2,10},{10... | collective-permute-start | bytes 2457608 | tf_op jit(solution)/shard_map/ppermute | solution.py:27
  118.3 15.5 %copy-start.19 = (f32[1,640]{1,0:T(1,128)S(1)}, f32[1,640]{1,0:T(1,128)}, u32[]{:S(2)}) copy-start(f32[1,640]{1,0:T(1,128)} %param.17) | copy-start | bytes 7684
  133.0 25.5 %collective-permute-start.22 = (bf16[640,640]{1,0:T(8,128)(2,1)}, bf16[640,640]{1,0:T(8,128)(2,1)}, u32[]{:S(2)}, u32[]{:S(2)}) collective-permute-start(bf16[640,640]{1,0:T(8,128)(2,1)} %get-tuple-element.66), channel_id=1, source_target_pairs={{0,16},{8,24},{16,0},{24,8},{1,17},{9,25},{17,1},{25,9},{2,18},{10... | collective-permute-start | bytes 2457608 | tf_op jit(solution)/shard_map/ppermute | solution.py:27
  134.4 26.3 %collective-permute-start.21 = (bf16[640,640]{1,0:T(8,128)(2,1)}, bf16[640,640]{1,0:T(8,128)(2,1)}, u32[]{:S(2)}, u32[]{:S(2)}) collective-permute-start(bf16[640,640]{1,0:T(8,128)(2,1)} %get-tuple-element.65), channel_id=1, source_target_pairs={{0,8},{8,0},{16,24},{24,16},{1,9},{9,1},{17,25},{25,17},{2,10},{10... | collective-permute-start | bytes 2457608 | tf_op jit(solution)/shard_map/ppermute | solution.py:27
  145.7 39.5 %collective-permute-start.25 = (bf16[640,640]{1,0:T(8,128)(2,1)}, bf16[640,640]{1,0:T(8,128)(2,1)S(1)}, u32[]{:S(2)}, u32[]{:S(2)}) collective-permute-start(bf16[640,640]{1,0:T(8,128)(2,1)} %get-tuple-element.71), channel_id=1, source_target_pairs={{0,8},{8,0},{16,24},{24,16},{1,9},{9,1},{17,25},{25,17},{2,10},{10... | collective-permute-start | bytes 2457608 | tf_op jit(solution)/shard_map/ppermute | solution.py:27
  145.8 39.4 %collective-permute-start.26 = (bf16[640,640]{1,0:T(8,128)(2,1)}, bf16[640,640]{1,0:T(8,128)(2,1)S(1)}, u32[]{:S(2)}, u32[]{:S(2)}) collective-permute-start(bf16[640,640]{1,0:T(8,128)(2,1)} %get-tuple-element.72), channel_id=1, source_target_pairs={{0,16},{8,24},{16,0},{24,8},{1,17},{9,25},{17,1},{25,9},{2,18},{10... | collective-permute-start | bytes 2457608 | tf_op jit(solution)/shard_map/ppermute | solution.py:27
  147.1 10.8 %copy-start.7 = (f32[1024,128]{1,0:T(8,128)S(1)}, f32[1024,128]{1,0:T(8,128)}, u32[]{:S(2)}) copy-start(f32[1024,128]{1,0:T(8,128)} %get-tuple-element.61) | copy-start | bytes 1572868
  147.1 11.3 %copy-start.9 = (f32[640,640]{1,0:T(8,128)S(1)}, f32[640,640]{1,0:T(8,128)}, u32[]{:S(2)}) copy-start(f32[640,640]{1,0:T(8,128)} %get-tuple-element.69) | copy-start | bytes 4915204
  158.4 6.5 %copy-start.2 = (bf16[1024,640]{1,0:T(8,128)(2,1)S(1)}, bf16[1024,640]{1,0:T(8,128)(2,1)}, u32[]{:S(2)}) copy-start(bf16[1024,640]{1,0:T(8,128)(2,1)} %sample.5) | copy-start | bytes 3932164
  158.4 6.5 %copy-start.4 = (bf16[1024,640]{1,0:T(8,128)(2,1)S(1)}, bf16[1024,640]{1,0:T(8,128)(2,1)}, u32[]{:S(2)}) copy-start(bf16[1024,640]{1,0:T(8,128)(2,1)} %copy-done.3) | copy-start | bytes 3932164
  159.9 43.0 %collective-permute-start.31 = (bf16[640,640]{1,0:T(8,128)(2,1)S(1)}, bf16[640,640]{1,0:T(8,128)(2,1)S(1)}, u32[]{:S(2)}, u32[]{:S(2)}) collective-permute-start(bf16[640,640]{1,0:T(8,128)(2,1)S(1)} %add_convert_fusion), channel_id=1, source_target_pairs={{0,8},{8,0},{16,24},{24,16},{1,9},{9,1},{17,25},{25,17},{2,10},{10... | collective-permute-start | bytes 2457608 | tf_op jit(solution)/shard_map/ppermute | solution.py:27
  163.0 40.0 %collective-permute-start.30 = (bf16[640,640]{1,0:T(8,128)(2,1)}, bf16[640,640]{1,0:T(8,128)(2,1)S(1)}, u32[]{:S(2)}, u32[]{:S(2)}) collective-permute-start(bf16[640,640]{1,0:T(8,128)(2,1)} %add_convert_fusion.1), channel_id=1, source_target_pairs={{0,16},{8,24},{16,0},{24,8},{1,17},{9,25},{17,1},{25,9},{2,18},{10... | collective-permute-start | bytes 2457608 | tf_op jit(solution)/shard_map/ppermute | solution.py:27
  185.2 1.5 collective-permute-start.27
  187.9 3.7 %collective-permute-start.28 = (f32[1,1]{1,0:T(1,128)}, f32[1,1]{1,0:T(1,128)}, u32[]{:S(2)}, u32[]{:S(2)}) collective-permute-start(f32[1,1]{1,0:T(1,128)} %add.101), channel_id=1, source_target_pairs={{0,2},{1,3},{2,0},{3,1},{4,6},{5,7},{6,4},{7,5},{8,10},{9,11},{10,... | collective-permute-start | bytes 20 | tf_op jit(solution)/shard_map/ppermute | solution.py:584
  192.3 4.6 %collective-permute-start.29 = (f32[1,1]{1,0:T(1,128)}, f32[1,1]{1,0:T(1,128)}, u32[]{:S(2)}, u32[]{:S(2)}) collective-permute-start(f32[1,1]{1,0:T(1,128)} %add.102), channel_id=1, source_target_pairs={{0,4},{1,5},{2,6},{3,7},{4,0},{5,1},{6,2},{7,3},{8,12},{9,13},{10,... | collective-permute-start | bytes 20 | tf_op jit(solution)/shard_map/ppermute | solution.py:584
  (4 other events, 8.7 us)

commit v6 on v5

--- a/solution.py
+++ b/solution.py
@@ -13,7 +13,19 @@
 F32 = jnp.float32
 MIB = 1024 * 1024
 CHUNKS = 2
-GATES = {'relay': ('own',), 'teacher': ('parts', 'parts1'), 'B2': ('f0', 'f1'), 'B3': ('sums', 't00', 't01'), 'cB2': ('far0', 'far1'), 'cA3': ('soon',), 'cB3': ('early', 't10', 't11'), 'teacher relay': ('sums',), 'cA2': ('sums',), 'cB1': ('far0', 'far1')}
+GATES = {
+    "relay": ("own",),
+    "teacher": ("parts", "parts1"),
+    "A3": ("far0", "far1"),
+    "B2": ("A2",),
+    "B3": ("sums", "t00", "t01"),
+    "cB1": ("far0", "far1"),
+    "cA2": ("sums",),
+    "cB2": ("far0", "far1"),
+    "cA3": ("soon",),
+    "cB3": ("early", "t10", "t11"),
+    "teacher relay": ("sums",),
+}
 ANY = pl.BlockSpec(memory_space=pl.ANY)
 SMEM = pl.BlockSpec(memory_space=pltpu.SMEM)
 VMEM = pl.BlockSpec(memory_space=pltpu.VMEM)
@@ -73,25 +85,29 @@
         loads[-1][0].start()
     tile = 160
     sums[...] = jnp.zeros_like(sums)
+    ones = jnp.ones((16, half_rows), BF16)
+    row = lax.broadcasted_iota(jnp.int32, (16, half_rows), 0)
     for index, ((load, spot), drain) in enumerate(zip(loads, drains)):
         mask, half = ([(0, 0), (0, 1)] + keys)[index]
-        column[...] = jnp.transpose(mod[where[mask] * 2 + half])
+        part = mod[where[mask] * 2 + half]
+        column[...] = jnp.transpose(part)
+        shift = part[0:1, :]
+        high = shift.astype(BF16).astype(F32)
+        shift = jnp.where(row == 0, high, jnp.where(row == 1, shift - high, 0.0)).astype(BF16)
         load.wait()
+        whole = pl.ds(spot, half_rows)
+        sums[1] += jnp.dot(shift, full[whole, :], preferred_element_type=F32)
 
         @pl.loop(0, half_rows // tile)
         def _(step):
             low = pl.multiple_of(step * tile, tile)
             at = pl.ds(pl.multiple_of(spot + low, tile), tile)
-            value = full[at, :].astype(F32)
-            shifted = value * column[pl.ds(low, tile), 0:1]
-            scaled = (value * (1.0 + column[pl.ds(low, tile), 1:2])).astype(BF16)
-            full[at, :] = scaled
-            sums[0] += jnp.sum(scaled.astype(F32).reshape(tile // 8, 8, cols), axis=0)
-            sums[1] += jnp.sum(shifted.reshape(tile // 8, 8, cols), axis=0)
+            gain = 1.0 + column[pl.ds(low, tile), 1:2]
+            full[at, :] = (full[at, :].astype(F32) * gain).astype(BF16)
 
         drain.start()
-    for i in range(2):
-        sums[i] = jnp.broadcast_to(jnp.sum(sums[i], axis=0, keepdims=True), (8, cols))
+        sums[0] += jnp.dot(ones, full[whole, :], preferred_element_type=F32)
+    sums[1, 0:1, :] = sums[1, 0:1, :] + sums[1, 1:2, :]
     for drain in drains:
         drain.wait()
 
@@ -106,7 +122,7 @@
         functools.partial(scale_kernel, list(blocks)),
         out_shape=(
             jax.ShapeDtypeStruct((width, cols), BF16),
-            jax.ShapeDtypeStruct((2, 8, cols), F32),
+            jax.ShapeDtypeStruct((2, 16, cols), F32),
         ),
         in_specs=[SMEM, VMEM] + [ANY] * (1 + len(blocks)),
         out_specs=(ANY, VMEM),
@@ -330,7 +346,7 @@
         scratch_shapes=scratch,
         input_output_aliases={7 + len(pieces) + 2: 1} if prior else {},
         compiler_params=pltpu.CompilerParams(vmem_limit_bytes=60 * MIB),
-        cost_estimate=pl.CostEstimate(flops=1, bytes_accessed=1, transcendentals=0),
+        cost_estimate=pl.CostEstimate(flops=4 * slots * clip_rows * depth * cols, bytes_accessed=1, transcendentals=0),
         name="project",
     )(where, scalars, sums, mod, sample, other, scaled, *pieces, *earlier)
 
@@ -577,16 +593,18 @@
         velocity = jnp.zeros((clip_rows, cols), F32)
         velocity = lax.fori_loop(0, width // cols, add_place, velocity)
     velocity = stats[:, 1:2] * (velocity - stats[:, 0:1] * sums[0, :1]) + sums[1, :1]
+    apart = velocity - fake_velocity
+    pulled = jnp.sum(apart * gen_branch.astype(F32), axis=0, keepdims=True)
     away = sample.astype(F32) - (noised.astype(F32) - sigma * velocity)
     away = after(jnp.sum(jnp.abs(away)).reshape(1, 1), *seconds)
-    bit = 1
-    while bit < shards:
-        away = away + lax.ppermute(away, "fsdp", [(i, i ^ bit) for i in range(shards)])
-        bit *= 2
-    gap_value = away / (clip_rows * width)
-    push = sigma * (velocity - fake_velocity) / (gap_value + EPS)
-    branch_cot = (gen_gate * push).astype(BF16)
-    gate_grad = jnp.sum(push * gen_branch.astype(F32), axis=0, keepdims=True) / math.sqrt(clip_rows)
+    away = away + lax.ppermute(away, "fsdp", swap)
+    away = away + sum(
+        lax.ppermute(away, "fsdp", [(i, (i + 2 * k) % shards) for i in range(shards)])
+        for k in range(1, hops)
+    )
+    factor = sigma / (away / (clip_rows * width) + EPS)
+    branch_cot = (gen_gate * factor * apart).astype(BF16)
+    gate_grad = pulled * factor / math.sqrt(clip_rows)
     return (branch_cot, gate_grad, fake_grad)
 
 

time: 208 us -> 208 us (level)
  waiting for transfers between devices: 56.9 us -> 46 us
  starting transfers between devices: 36.8 us -> 45.4 us
    ppermute x6, waiting for transfers between devices: 48.6 us -> 26.3 us  [hop_to(): seen[name] = lax.ppermute(gated(name, source), 'fsdp', ring)]
    ppermute x16, waiting for transfers between devices: 0.06 us -> 19.7 us  [swap_clip(): return lax.ppermute(value, 'clip', [(i, i ^ bit) for i in range(count)])]
    ppermute x3 -> x4, starting transfers between devices: 2.81 us -> 10.3 us  [the longest x3 10.3 us: per_device(): lax.ppermute(away, 'fsdp', [(i, (i + 2 * k) % shards) for i in range(shar...]
    ppermute x3 -> x4, waiting for transfers between devices: 6.95 us -> 0.01 us  [the longest x3 0.01 us: per_device(): lax.ppermute(away, 'fsdp', [(i, (i + 2 * k) % shards) for i in range(shar...]
    reduce_sum x1 -> x0, other arithmetic: 3.51 us -> none  [per_device(): jnp.sum(push * gen_branch.astype(F32), axis=0, keepdims=True)]
    convert_element_type x1, other arithmetic: 1.26 us -> 4.41 us  [per_device(): branch_cot = (gen_gate * factor * apart).astype(BF16)]
  transfers between devices with their start and end apart: 32 -> 33, of which waited for: 9 -> 7; matrix products, arithmetic and copies ran while one was open for 16% -> 17% of each run, Pallas kernels for 34% -> 34%
where the time goes in v6:
time: 208 us
  Pallas kernels  75 us (36%)
  waiting for transfers between devices  46 us (22%)
  starting transfers between devices  45.4 us (22%)
  matrix products  15.4 us (7%)
  other arithmetic  12.2 us (6%)
  local copies, waits for them, and re-layouts  8.82 us (4%)
  between operations  4.85 us (2%)
    pallas_call x3, Pallas kernels, project(): pl.pallas_call(functools.partial(project_kernel, prior, last, plan, core_...  36.4 us
    ppermute x6, waiting for transfers between devices, hop_to(): seen[name] = lax.ppermute(gated(name, source), 'fsdp', ring)  26.3 us
    pallas_call x2, Pallas kernels, scale(): pl.pallas_call(functools.partial(scale_kernel, list(blocks)), out_shape=(...  20.1 us
    ppermute x16, waiting for transfers between devices, swap_clip(): return lax.ppermute(value, 'clip', [(i, i ^ bit) for i in range(count)])  19.7 us
    ppermute x16, starting transfers between devices, swap_clip(): return lax.ppermute(value, 'clip', [(i, i ^ bit) for i in range(count)])  19.1 us
    dot_general x1, matrix products, per_device(): velocity = jnp.dot(left, scaled, preferred_element_type=F32)  15.4 us
    ppermute x6, starting transfers between devices, hop_to(): seen[name] = lax.ppermute(gated(name, source), 'fsdp', ring)  15.2 us
    pallas_call x2, Pallas kernels, outer(): pl.pallas_call(outer_kernel, out_shape=[jax.ShapeDtypeStruct((cols, cols)...  14.7 us
  transfers between devices with their start and end apart: 33, of which 7 were waited for; matrix products, arithmetic and copies ran while one was open for 17% of the time, Pallas kernels for 34%

profile of v6, /device:TPU:0, one launch (start us, length us, event | category | flops | bytes accessed | tf_op | source)
XLA Modules:
  0.0 207.6 jit_solution(4436118717361478335)
XLA Ops:
  0.6 3.0 %collective-permute-start = (bf16[1280,640]{1,0:T(8,128)(2,1)}, bf16[1280,640]{1,0:T(8,128)(2,1)S(1)}, u32[]{:S(2)}, u32[]{:S(2)}) collective-permute-start(bf16[1280,640]{1,0:T(8,128)(2,1)} %weight.1), channel_id=1, source_target_pairs={{0,8},{8,0},{16,24},{24,16},{1,9},{9,1},{17,25},{25,17},{2,10},{10... | collective-permute-start | bytes 4915208 | tf_op jit(solution)/shard_map/ppermute | solution.py:39
  3.6 1.5 collective-permute-start.3
  5.8 2.2 %fusion.1.refs_0_ = bf16[1024,640]{1,0:T(8,128)(2,1)S(1)} fusion(bf16[1024,640]{1,0:T(8,128)(2,1)} %sample.5, bf16[1024,640]{1,0:T(8,128)(2,1)} %other.5, f32[]{:T(128)} %bitcast.1, f32[]{:T(128)S(6)} %sub.47), kind=kLoop, calls=%fused_computation.3 | loop fusion | flops 3932160 | bytes 3932168 | tf_op jit(solution)/shard_map/convert_element_type | solution.py:442
  8.3 2.6 %collective-permute-start.5 = (bf16[512,640]{1,0:T(8,128)(2,1)S(1)}, bf16[512,640]{1,0:T(8,128)(2,1)S(1)}, u32[]{:S(2)}, u32[]{:S(2)}) collective-permute-start(bf16[512,640]{1,0:T(8,128)(2,1)S(1)} %get-tuple-element.96), channel_id=1, source_target_pairs={{0,4},{1,5},{4,6},{5,7},{6,2},{7,3},{2,0},{3,1},{8,12},{9,13},{12,... | collective-permute-start | bytes 1966088 | tf_op jit(solution)/shard_map/ppermute | solution.py:468
  10.9 1.6 collective-permute-start.9
  12.5 13.5 %collective-permute-done.5.refs_2_ = bf16[512,640]{1,0:T(8,128)(2,1)S(1)} collective-permute-done((bf16[512,640]{1,0:T(8,128)(2,1)S(1)}, bf16[512,640]{1,0:T(8,128)(2,1)S(1)}, u32[]{:S(2)}, u32[]{:S(2)}) %collective-permute-start.5) | collective-permute-done | bytes 655392 | tf_op jit(solution)/shard_map/ppermute | solution.py:468
  26.0 3.4 %collective-permute-start.6 = (bf16[512,640]{1,0:T(8,128)(2,1)S(1)}, bf16[512,640]{1,0:T(8,128)(2,1)}, u32[]{:S(2)}, u32[]{:S(2)}) collective-permute-start(bf16[512,640]{1,0:T(8,128)(2,1)S(1)} %collective-permute-done.5.refs_2_), channel_id=1, source_target_pairs={{0,4},{1,5},{4,6},{5,7},{6,2},{7,3},{2,0},{3,1},{8,12},{9,13},{12,... | collective-permute-start | bytes 1966088 | tf_op jit(solution)/shard_map/ppermute | solution.py:468
  29.4 10.3 %collective-permute-done.refs_0_.refs_5_ = bf16[1280,640]{1,0:T(8,128)(2,1)S(1)} collective-permute-done((bf16[1280,640]{1,0:T(8,128)(2,1)}, bf16[1280,640]{1,0:T(8,128)(2,1)S(1)}, u32[]{:S(2)}, u32[]{:S(2)}) %collective-permute-start) | collective-permute-done | bytes 1638432 | tf_op jit(solution)/shard_map/ppermute | solution.py:39
  39.6 1.0 slice.30
  40.7 1.8 collective-permute-start.2
  42.4 1.1 slice.31
  43.5 1.5 collective-permute-start.4
  45.0 8.7 %collective-permute-done.6.refs_0_ = bf16[512,640]{1,0:T(8,128)(2,1)} collective-permute-done((bf16[512,640]{1,0:T(8,128)(2,1)S(1)}, bf16[512,640]{1,0:T(8,128)(2,1)}, u32[]{:S(2)}, u32[]{:S(2)}) %collective-permute-start.6) | collective-permute-done | bytes 655392 | tf_op jit(solution)/shard_map/ppermute | solution.py:468
  53.7 3.5 %collective-permute-start.12 = (bf16[512,640]{1,0:T(8,128)(2,1)}, bf16[512,640]{1,0:T(8,128)(2,1)}, u32[]{:S(2)}, u32[]{:S(2)}) collective-permute-start(bf16[512,640]{1,0:T(8,128)(2,1)} %collective-permute-done.9.refs_4_), channel_id=1, source_target_pairs={{0,4},{1,5},{4,6},{5,7},{6,2},{7,3},{2,0},{3,1},{8,12},{9,13},{12,... | collective-permute-start | bytes 1966088 | tf_op jit(solution)/shard_map/ppermute | solution.py:468
  57.2 1.3 fusion.5
  60.5 4.1 %collective-permute-done.4.refs_4_ = bf16[640,640]{1,0:T(8,128)(2,1)} collective-permute-done((bf16[640,640]{1,0:T(8,128)(2,1)}, bf16[640,640]{1,0:T(8,128)(2,1)}, u32[]{:S(2)}, u32[]{:S(2)}) %collective-permute-start.4) | collective-permute-done | bytes 819232 | tf_op jit(solution)/shard_map/ppermute | solution.py:39
  64.6 10.0 %scale.2 = (bf16[5120,640]{1,0:T(8,128)(2,1)}, f32[2,16,640]{2,1,0:T(8,128)}) custom-call(s32[4]{0:T(128)} %pad_add_fusion.where, f32[8,2,640]{2,1,0:T(2,128)} %bitcast.26, bf16[1280,640]{1,0:T(8,128)(2,1)} %weight.1, bf16[1280,640]{1,0:T(8,128)(2,1)} %copy-done.3, bf16[640,640]{1,0:T(8,128)(2,1)} %collective-permute-done.2.refs_1_, ...), custom_call_target="tpu_custom_call" | custom-call | flops 1 | bytes 1 | tf_op jit(solution)/shard_map/scale/pallas_call | solution.py:121
  75.2 5.0 %collective-permute-done.13.refs_0_ = bf16[640,640]{1,0:T(8,128)(2,1)S(1)} collective-permute-done((bf16[640,640]{1,0:T(8,128)(2,1)}, bf16[640,640]{1,0:T(8,128)(2,1)S(1)}, u32[]{:S(2)}, u32[]{:S(2)}) %collective-permute-start.13) | collective-permute-done | bytes 819232 | tf_op jit(solution)/shard_map/ppermute | solution.py:39
  80.2 0.7 pad_maximum_fusion.scalars
  80.9 0.7 stack.55.where
  82.1 1.4 collective-permute-start.19
  83.6 2.6 %collective-permute-start.15 = (bf16[512,640]{1,0:T(8,128)(2,1)}, bf16[512,640]{1,0:T(8,128)(2,1)}, u32[]{:S(2)}, u32[]{:S(2)}) collective-permute-start(bf16[512,640]{1,0:T(8,128)(2,1)} %collective-permute-done.12.refs_2_), channel_id=1, source_target_pairs={{0,4},{1,5},{4,6},{5,7},{6,2},{7,3},{2,0},{3,1},{8,12},{9,13},{12,... | collective-permute-start | bytes 1966088 | tf_op jit(solution)/shard_map/ppermute | solution.py:468
  86.2 1.6 collective-permute-start.7
  87.7 12.3 %project.3 = (f32[1024,640]{1,0:T(8,128)}, bf16[1024,5120]{1,0:T(8,128)(2,1)}, f32[1024,128]{1,0:T(8,128)}) custom-call(s32[5]{0:T(128)} %stack.55.where, f32[2]{0:T(128)} %pad_maximum_fusion.scalars, f32[2,16,640]{2,1,0:T(8,128)} %get-tuple-element.47.sums, f32[4,2,1280]{2,1,0:T(2,128)} %bitcast.27, bf16[1024,640]{1,0:T(8,128)(2,1)} %sample.5, ...), custom_call_target="tpu_custom_call" | custom-call | flops 6710886400 | bytes 1 | tf_op jit(solution)/shard_map/project/pallas_call | solution.py:341
  100.0 0.8 copy-done.15
  100.9 9.4 %project.4 = (f32[1024,640]{1,0:T(8,128)}, bf16[1024,5120]{1,0:T(8,128)(2,1)}, f32[1024,128]{1,0:T(8,128)}) custom-call(s32[5]{0:T(128)} %stack.55.where, f32[2]{0:T(128)} %pad_maximum_fusion.scalars, f32[2,16,640]{2,1,0:T(8,128)} %get-tuple-element.47.sums, f32[4,2,1280]{2,1,0:T(2,128)} %bitcast.28, ...), custom_call_target="tpu_custom_call", output_to_operand_aliasing={{1}: (13, {})} | custom-call | flops 3355443200 | bytes 1 | tf_op jit(solution)/shard_map/project/pallas_call | solution.py:341
  110.4 4.2 %collective-permute-done.7.refs_0_ = bf16[512,640]{1,0:T(8,128)(2,1)} collective-permute-done((bf16[512,640]{1,0:T(8,128)(2,1)}, bf16[512,640]{1,0:T(8,128)(2,1)}, u32[]{:S(2)}, u32[]{:S(2)}) %collective-permute-start.7) | collective-permute-done | bytes 655392 | tf_op jit(solution)/shard_map/ppermute | solution.py:468
  114.5 0.7 concatenate.4.where
  115.2 1.5 collective-permute-start.23
  117.3 0.8 copy-done.16
  118.3 14.7 %project.5 = (f32[1024,640]{1,0:T(8,128)}, bf16[1024,5120]{1,0:T(8,128)(2,1)}, f32[1024,128]{1,0:T(8,128)}, bf16[640,1024]{1,0:T(8,128)(2,1)}, f32[640,2]{1,0:T(...) custom-call(s32[6]{0:T(128)} %concatenate.4.where, ...), custom_call_target="tpu_custom_call", output_to_operand_aliasing={{1}: (13, {})} | custom-call | flops 3355443200 | bytes 1 | tf_op jit(solution)/shard_map/project/pallas_call | solution.py:341
  133.0 0.9 collective-permute-start.22
  134.6 1.1 collective-permute-start.21
  135.7 9.4 %outer.2 = (bf16[640,640]{1,0:T(8,128)(2,1)}, f32[640,640]{1,0:T(8,128)}, f32[640,640]{1,0:T(8,128)}, bf16[640,640]{1,0:T(8,128)(2,1)}) custom-call(s32[2]{0:T(128)} %pad_add_fusion.1.picks, f32[4,2,1280]{2,1,0:T(2,128)} %bitcast.30, f32[640,2]{1,0:T(8,128)} %get-tuple-element.65.edge, bf16[640,1024]{1,0:T(8,128)(2,1)} %get-tuple-element.84.flipped, ...), custom_call_target="tpu_custom_call" | custom-call | flops 3355443200 | bytes 11141120 | tf_op jit(solution)/shard_map/outer/pallas_call | solution.py:377
  145.1 0.9 collective-permute-start.25
  146.0 1.2 collective-permute-start.26
  147.1 10.1 %scale.3 = (bf16[5120,640]{1,0:T(8,128)(2,1)}, f32[2,16,640]{2,1,0:T(8,128)}) custom-call(s32[4]{0:T(128)} %pad_add_fusion.where, f32[8,2,640]{2,1,0:T(2,128)} %bitcast.32, bf16[1280,640]{1,0:T(8,128)(2,1)} %weight.2, bf16[640,640]{1,0:T(8,128)(2,1)} %copy-done.12, bf16[640,640]{1,0:T(8,128)(2,1)} %collective-permute-done.23.refs_1_, ...), custom_call_target="tpu_custom_call" | custom-call | flops 1 | bytes 1 | tf_op jit(solution)/shard_map/scale/pallas_call | solution.py:121
  157.3 0.9 slice_reduce_fusion.3
  158.7 2.3 %add_convert_fusion = bf16[640,640]{1,0:T(8,128)(2,1)} fusion(f32[640,640]{1,0:T(8,128)S(1)} %copy-done.11, bf16[640,640]{1,0:T(8,128)(2,1)} %collective-permute-done.22), kind=kLoop, calls=%fused_computation.10 | loop fusion | flops 1228800 | bytes 3276800 | tf_op jit(solution)/shard_map/convert_element_type | solution.py:573
  161.1 1.5 collective-permute-start.32
  162.6 1.3 add_convert_fusion.1
  164.5 15.4 %multiply_reduce_fusion = (f32[640]{0:T(1024)S(1)}, f32[]{:T(128)}, f32[1024,640]{1,0:T(8,128)}) fusion(bf16[1024,640]{1,0:T(8,128)(2,1)} %param.11, f32[1024,640]{1,0:T(8,128)S(1)} %copy-done.8, f32[640]{0:T(1024)S(1)} %get-tuple-element.92, f32[640]{0:T(1024)S(1)} %get-tuple-element.91, f32[1024]{0:T(1024)S(1)} %get-tuple-element.90, ...), kind=kOutput, calls=%fused_computation.6 | convolution fusion | flops 6720716288 | bytes 26230280 | tf_op jit(solution)/shard_map/dot_general | solution.py:591
  180.0 5.4 %outer.3 = (f32[640,640]{1,0:T(8,128)}, f32[640,640]{1,0:T(8,128)}) custom-call(s32[1]{0:T(128)} %bitcast.8.picks, f32[4,2,1280]{2,1,0:T(2,128)} %bitcast.31, f32[640,2]{1,0:T(8,128)} %get-tuple-element.65.edge, bf16[640,1024]{1,0:T(8,128)(2,1)} %get-tuple-element.84.flipped, bf16[1024,5120]{1,0:T(8,128)(2,1)} %get-tuple-element.72.inputs), custom_call_target="tpu_custom_call" | custom-call | flops 1677721600 | bytes 6881280 | tf_op jit(solution)/shard_map/outer/pallas_call | solution.py:377
  186.5 3.7 %collective-permute-start.28 = (f32[1,1]{1,0:T(1,128)}, f32[1,1]{1,0:T(1,128)}, u32[]{:S(2)}, u32[]{:S(2)}) collective-permute-start(f32[1,1]{1,0:T(1,128)} %add.104), channel_id=1, source_target_pairs={{0,2},{1,3},{2,4},{3,5},{4,6},{5,7},{6,0},{7,1},{8,10},{9,11},{10,... | collective-permute-start | bytes 20 | tf_op jit(solution)/shard_map/ppermute | solution.py:602
  190.3 3.0 %collective-permute-start.29 = (f32[1,1]{1,0:T(1,128)}, f32[1,1]{1,0:T(1,128)}, u32[]{:S(2)}, u32[]{:S(2)}) collective-permute-start(f32[1,1]{1,0:T(1,128)} %add.104), channel_id=1, source_target_pairs={{0,4},{1,5},{2,6},{3,7},{4,0},{5,1},{6,2},{7,3},{8,12},{9,13},{10,... | collective-permute-start | bytes 20 | tf_op jit(solution)/shard_map/ppermute | solution.py:602
  193.2 3.5 %collective-permute-start.30 = (f32[1,1]{1,0:T(1,128)}, f32[1,1]{1,0:T(1,128)}, u32[]{:S(2)}, u32[]{:S(2)}) collective-permute-start(f32[1,1]{1,0:T(1,128)} %add.104), channel_id=1, source_target_pairs={{0,6},{1,7},{2,0},{3,1},{4,2},{5,3},{6,4},{7,5},{8,14},{9,15},{10,... | collective-permute-start | bytes 20 | tf_op jit(solution)/shard_map/ppermute | solution.py:602
  199.4 4.4 %multiply_convert_fusion = bf16[1024,640]{1,0:T(8,128)(2,1)} fusion(f32[640]{0:T(1024)S(1)} %multiply_reduce_fusion.1, f32[1024,640]{1,0:T(8,128)} %get-tuple-element.83, f32[640]{0:T(1024)S(1)} %get-tuple-element.92, f32[1024,640]{1,0:T(8,128)} %get-tuple-element.97, f32[640]{0:T(1024)S(1)} %get-tuple-element.91, f32[1024]{0:T(1024)S(1)} %get-tuple-element.90, ...), kind=kLoop, calls=%fused_computation.7 | loop fusion | flops 4587520 | bytes 6569472 | tf_op jit(solution)/shard_map/convert_element_type | solution.py:606
  203.9 3.8 %finish.1 = f32[2,640,640]{2,1,0:T(8,128)} custom-call(f32[640,640]{1,0:T(8,128)S(1)} %copy-done, bf16[640,640]{1,0:T(8,128)(2,1)S(1)} %collective-permute-done.25.refs_1_, bf16[640,640]{1,0:T(8,128)(2,1)S(1)} %collective-permute-done.31.refs_2_, f32[640,640]{1,0:T(8,128)S(1)} %copy-done.1, bf16[640,640]{1,0:T(8,128)(2,1)S(1)} %collective-permute-done.26.refs_4_, ...), custom_call_target="tpu_custom_call" | custom-call | tf_op jit(solution)/shard_map/finish/pallas_call | solution.py:414
  (87 shorter events, 6.7 us)
Async XLA Ops:
  0.6 39.0 %collective-permute-start = (bf16[1280,640]{1,0:T(8,128)(2,1)}, bf16[1280,640]{1,0:T(8,128)(2,1)S(1)}, u32[]{:S(2)}, u32[]{:S(2)}) collective-permute-start(bf16[1280,640]{1,0:T(8,128)(2,1)} %weight.1), channel_id=1, source_target_pairs={{0,8},{8,0},{16,24},{24,16},{1,9},{9,1},{17,25},{25,17},{2,10},{10... | collective-permute-start | bytes 4915208 | tf_op jit(solution)/shard_map/ppermute | solution.py:39
  3.6 38.8 %collective-permute-start.3 = (bf16[1280,640]{1,0:T(8,128)(2,1)}, bf16[1280,640]{1,0:T(8,128)(2,1)S(1)}, u32[]{:S(2)}, u32[]{:S(2)}) collective-permute-start(bf16[1280,640]{1,0:T(8,128)(2,1)} %weight.1), channel_id=1, source_target_pairs={{0,16},{8,24},{16,0},{24,8},{1,17},{9,25},{17,1},{25,9},{2,18},{10... | collective-permute-start | bytes 4915208 | tf_op jit(solution)/shard_map/ppermute | solution.py:39
  8.1 35.4 %copy-start.6 = (bf16[1024,640]{1,0:T(8,128)(2,1)}, bf16[1024,640]{1,0:T(8,128)(2,1)S(1)}, u32[]{:S(2)}) copy-start(bf16[1024,640]{1,0:T(8,128)(2,1)S(1)} %fusion.1.refs_0_) | copy-start | bytes 3932164
  8.1 49.1 %copy-start.5 = (bf16[1280,640]{1,0:T(8,128)(2,1)S(1)}, bf16[1280,640]{1,0:T(8,128)(2,1)}, u32[]{:S(2)}) copy-start(bf16[1280,640]{1,0:T(8,128)(2,1)} %weight.2) | copy-start | bytes 4915204
  8.1 21.3 %collective-permute-start.1 = (bf16[1024,640]{1,0:T(8,128)(2,1)S(1)}, bf16[1024,640]{1,0:T(8,128)(2,1)S(1)}, u32[]{:S(2)}, u32[]{:S(2)}) collective-permute-start(bf16[1024,640]{1,0:T(8,128)(2,1)S(1)} %fusion.1.refs_0_), channel_id=1, source_target_pairs={{0,1},{1,0},{2,3},{3,2},{4,5},{5,4},{6,7},{7,6},{8,9},{9,8},{10,11... | collective-permute-start | bytes 3932168 | tf_op jit(solution)/shard_map/ppermute | solution.py:479
  8.3 17.7 %collective-permute-start.5 = (bf16[512,640]{1,0:T(8,128)(2,1)S(1)}, bf16[512,640]{1,0:T(8,128)(2,1)S(1)}, u32[]{:S(2)}, u32[]{:S(2)}) collective-permute-start(bf16[512,640]{1,0:T(8,128)(2,1)S(1)} %get-tuple-element.96), channel_id=1, source_target_pairs={{0,4},{1,5},{4,6},{5,7},{6,2},{7,3},{2,0},{3,1},{8,12},{9,13},{12,... | collective-permute-start | bytes 1966088 | tf_op jit(solution)/shard_map/ppermute | solution.py:468
  10.9 34.1 %collective-permute-start.9 = (bf16[512,640]{1,0:T(8,128)(2,1)S(1)}, bf16[512,640]{1,0:T(8,128)(2,1)}, u32[]{:S(2)}, u32[]{:S(2)}) collective-permute-start(bf16[512,640]{1,0:T(8,128)(2,1)S(1)} %get-tuple-element.95), channel_id=1, source_target_pairs={{0,4},{1,5},{4,6},{5,7},{6,2},{7,3},{2,0},{3,1},{8,12},{9,13},{12,... | collective-permute-start | bytes 1966088 | tf_op jit(solution)/shard_map/ppermute | solution.py:468
  26.0 19.0 %copy-start.20 = (bf16[512,640]{1,0:T(8,128)(2,1)}, bf16[512,640]{1,0:T(8,128)(2,1)S(1)}, u32[]{:S(2)}) copy-start(bf16[512,640]{1,0:T(8,128)(2,1)S(1)} %collective-permute-done.5.refs_2_) | copy-start | bytes 1966084
  26.0 27.7 %collective-permute-start.6 = (bf16[512,640]{1,0:T(8,128)(2,1)S(1)}, bf16[512,640]{1,0:T(8,128)(2,1)}, u32[]{:S(2)}, u32[]{:S(2)}) collective-permute-start(bf16[512,640]{1,0:T(8,128)(2,1)S(1)} %collective-permute-done.5.refs_2_), channel_id=1, source_target_pairs={{0,4},{1,5},{4,6},{5,7},{6,2},{7,3},{2,0},{3,1},{8,12},{9,13},{12,... | collective-permute-start | bytes 1966088 | tf_op jit(solution)/shard_map/ppermute | solution.py:468
  29.4 29.1 %copy-start.19 = (bf16[1024,640]{1,0:T(8,128)(2,1)}, bf16[1024,640]{1,0:T(8,128)(2,1)S(1)}, u32[]{:S(2)}) copy-start(bf16[1024,640]{1,0:T(8,128)(2,1)S(1)} %collective-permute-done.1.refs_1_) | copy-start | bytes 3932164
  39.6 18.9 %copy-start.3 = (bf16[1280,640]{1,0:T(8,128)(2,1)}, bf16[1280,640]{1,0:T(8,128)(2,1)S(1)}, u32[]{:S(2)}) copy-start(bf16[1280,640]{1,0:T(8,128)(2,1)S(1)} %collective-permute-done.refs_0_.refs_5_) | copy-start | bytes 4915204
  40.7 19.9 %collective-permute-start.2 = (bf16[640,640]{1,0:T(8,128)(2,1)}, bf16[640,640]{1,0:T(8,128)(2,1)}, u32[]{:S(2)}, u32[]{:S(2)}) collective-permute-start(bf16[640,640]{1,0:T(8,128)(2,1)} %slice.30), channel_id=1, source_target_pairs={{0,16},{8,24},{16,0},{24,8},{1,17},{9,25},{17,1},{25,9},{2,18},{10... | collective-permute-start | bytes 2457608 | tf_op jit(solution)/shard_map/ppermute | solution.py:39
  42.4 22.2 %copy-start.4 = (bf16[1280,640]{1,0:T(8,128)(2,1)}, bf16[1280,640]{1,0:T(8,128)(2,1)S(1)}, u32[]{:S(2)}) copy-start(bf16[1280,640]{1,0:T(8,128)(2,1)S(1)} %collective-permute-done.3.refs_2_.refs_3_) | copy-start | bytes 4915204
  43.5 21.1 %collective-permute-start.4 = (bf16[640,640]{1,0:T(8,128)(2,1)}, bf16[640,640]{1,0:T(8,128)(2,1)}, u32[]{:S(2)}, u32[]{:S(2)}) collective-permute-start(bf16[640,640]{1,0:T(8,128)(2,1)} %slice.31), channel_id=1, source_target_pairs={{0,8},{8,0},{16,24},{24,16},{1,9},{9,1},{17,25},{25,17},{2,10},{10... | collective-permute-start | bytes 2457608 | tf_op jit(solution)/shard_map/ppermute | solution.py:39
  53.7 20.9 %collective-permute-start.12 = (bf16[512,640]{1,0:T(8,128)(2,1)}, bf16[512,640]{1,0:T(8,128)(2,1)}, u32[]{:S(2)}, u32[]{:S(2)}) collective-permute-start(bf16[512,640]{1,0:T(8,128)(2,1)} %collective-permute-done.9.refs_4_), channel_id=1, source_target_pairs={{0,4},{1,5},{4,6},{5,7},{6,2},{7,3},{2,0},{3,1},{8,12},{9,13},{12,... | collective-permute-start | bytes 1966088 | tf_op jit(solution)/shard_map/ppermute | solution.py:468
  58.5 21.7 %collective-permute-start.13 = (bf16[640,640]{1,0:T(8,128)(2,1)}, bf16[640,640]{1,0:T(8,128)(2,1)S(1)}, u32[]{:S(2)}, u32[]{:S(2)}) collective-permute-start(bf16[640,640]{1,0:T(8,128)(2,1)} %get-tuple-element.94), channel_id=1, source_target_pairs={{0,8},{8,0},{16,24},{24,16},{1,9},{9,1},{17,25},{25,17},{2,10},{10... | collective-permute-start | bytes 2457608 | tf_op jit(solution)/shard_map/ppermute | solution.py:39
  59.0 22.5 %collective-permute-start.14 = (bf16[640,640]{1,0:T(8,128)(2,1)}, bf16[640,640]{1,0:T(8,128)(2,1)S(1)}, u32[]{:S(2)}, u32[]{:S(2)}) collective-permute-start(bf16[640,640]{1,0:T(8,128)(2,1)} %get-tuple-element.93), channel_id=1, source_target_pairs={{0,16},{8,24},{16,0},{24,8},{1,17},{9,25},{17,1},{25,9},{2,18},{10... | collective-permute-start | bytes 2457608 | tf_op jit(solution)/shard_map/ppermute | solution.py:39
  60.5 23.0 %collective-permute-start.8 = (bf16[512,640]{1,0:T(8,128)(2,1)}, bf16[512,640]{1,0:T(8,128)(2,1)}, u32[]{:S(2)}, u32[]{:S(2)}) collective-permute-start(bf16[512,640]{1,0:T(8,128)(2,1)} %copy-done.20), channel_id=1, source_target_pairs={{0,1},{1,0},{2,3},{3,2},{4,5},{5,4},{6,7},{7,6},{8,9},{9,8},{10,11... | collective-permute-start | bytes 1966088 | tf_op jit(solution)/shard_map/ppermute | solution.py:472
  64.6 17.5 %collective-permute-start.10 = (bf16[512,640]{1,0:T(8,128)(2,1)}, bf16[512,640]{1,0:T(8,128)(2,1)}, u32[]{:S(2)}, u32[]{:S(2)}) collective-permute-start(bf16[512,640]{1,0:T(8,128)(2,1)} %collective-permute-done.9.refs_4_), channel_id=1, source_target_pairs={{0,1},{1,0},{2,3},{3,2},{4,5},{5,4},{6,7},{7,6},{8,9},{9,8},{10,11... | collective-permute-start | bytes 1966088 | tf_op jit(solution)/shard_map/ppermute | solution.py:472
  74.6 11.5 %collective-permute-start.16 = (bf16[512,640]{1,0:T(8,128)(2,1)}, bf16[512,640]{1,0:T(8,128)(2,1)S(1)}, u32[]{:S(2)}, u32[]{:S(2)}) collective-permute-start(bf16[512,640]{1,0:T(8,128)(2,1)} %collective-permute-done.6.refs_0_), channel_id=1, source_target_pairs={{0,1},{1,0},{2,3},{3,2},{4,5},{5,4},{6,7},{7,6},{8,9},{9,8},{10,11... | collective-permute-start | bytes 1966088 | tf_op jit(solution)/shard_map/ppermute | solution.py:472
  80.2 35.0 %copy-start.12 = (bf16[640,640]{1,0:T(8,128)(2,1)}, bf16[640,640]{1,0:T(8,128)(2,1)S(1)}, u32[]{:S(2)}) copy-start(bf16[640,640]{1,0:T(8,128)(2,1)S(1)} %collective-permute-done.13.refs_0_) | copy-start | bytes 2457604
  80.2 19.8 %collective-permute-start.17 = (bf16[512,640]{1,0:T(8,128)(2,1)}, bf16[512,640]{1,0:T(8,128)(2,1)S(1)}, u32[]{:S(2)}, u32[]{:S(2)}) collective-permute-start(bf16[512,640]{1,0:T(8,128)(2,1)} %collective-permute-done.12.refs_2_), channel_id=1, source_target_pairs={{0,1},{1,0},{2,3},{3,2},{4,5},{5,4},{6,7},{7,6},{8,9},{9,8},{10,11... | collective-permute-start | bytes 1966088 | tf_op jit(solution)/shard_map/ppermute | solution.py:472
  81.6 35.2 %copy-start.13 = (bf16[640,640]{1,0:T(8,128)(2,1)}, bf16[640,640]{1,0:T(8,128)(2,1)S(1)}, u32[]{:S(2)}) copy-start(bf16[640,640]{1,0:T(8,128)(2,1)S(1)} %collective-permute-done.14.refs_3_) | copy-start | bytes 2457604
  81.6 28.7 %collective-permute-start.18 = (bf16[640,640]{1,0:T(8,128)(2,1)}, bf16[640,640]{1,0:T(8,128)(2,1)}, u32[]{:S(2)}, u32[]{:S(2)}) collective-permute-start(bf16[640,640]{1,0:T(8,128)(2,1)} %get-tuple-element.94), channel_id=1, source_target_pairs={{0,16},{8,24},{16,0},{24,8},{1,17},{9,25},{17,1},{25,9},{2,18},{10... | collective-permute-start | bytes 2457608 | tf_op jit(solution)/shard_map/ppermute | solution.py:39
  82.1 28.2 %collective-permute-start.19 = (bf16[640,640]{1,0:T(8,128)(2,1)}, bf16[640,640]{1,0:T(8,128)(2,1)}, u32[]{:S(2)}, u32[]{:S(2)}) collective-permute-start(bf16[640,640]{1,0:T(8,128)(2,1)} %get-tuple-element.93), channel_id=1, source_target_pairs={{0,8},{8,0},{16,24},{24,16},{1,9},{9,1},{17,25},{25,17},{2,10},{10... | collective-permute-start | bytes 2457608 | tf_op jit(solution)/shard_map/ppermute | solution.py:39
  83.6 26.7 %collective-permute-start.15 = (bf16[512,640]{1,0:T(8,128)(2,1)}, bf16[512,640]{1,0:T(8,128)(2,1)}, u32[]{:S(2)}, u32[]{:S(2)}) collective-permute-start(bf16[512,640]{1,0:T(8,128)(2,1)} %collective-permute-done.12.refs_2_), channel_id=1, source_target_pairs={{0,4},{1,5},{4,6},{5,7},{6,2},{7,3},{2,0},{3,1},{8,12},{9,13},{12,... | collective-permute-start | bytes 1966088 | tf_op jit(solution)/shard_map/ppermute | solution.py:468
  86.2 13.9 %copy-start.14 = (bf16[512,640]{1,0:T(8,128)(2,1)}, bf16[512,640]{1,0:T(8,128)(2,1)S(1)}, u32[]{:S(2)}) copy-start(bf16[512,640]{1,0:T(8,128)(2,1)S(1)} %collective-permute-done.16.refs_1_) | copy-start | bytes 1966084
  86.2 28.4 %collective-permute-start.7 = (bf16[512,640]{1,0:T(8,128)(2,1)}, bf16[512,640]{1,0:T(8,128)(2,1)}, u32[]{:S(2)}, u32[]{:S(2)}) collective-permute-start(bf16[512,640]{1,0:T(8,128)(2,1)} %collective-permute-done.6.refs_0_), channel_id=1, source_target_pairs={{0,4},{1,5},{4,6},{5,7},{6,2},{7,3},{2,0},{3,1},{8,12},{9,13},{12,... | collective-permute-start | bytes 1966088 | tf_op jit(solution)/shard_map/ppermute | solution.py:468
  110.3 7.0 %collective-permute-start.20 = (bf16[512,640]{1,0:T(8,128)(2,1)}, bf16[512,640]{1,0:T(8,128)(2,1)S(1)}, u32[]{:S(2)}, u32[]{:S(2)}) collective-permute-start(bf16[512,640]{1,0:T(8,128)(2,1)} %collective-permute-done.15.refs_2_), channel_id=1, source_target_pairs={{0,1},{1,0},{2,3},{3,2},{4,5},{5,4},{6,7},{7,6},{8,9},{9,8},{10,11... | collective-permute-start | bytes 1966088 | tf_op jit(solution)/shard_map/ppermute | solution.py:472
  114.5 2.8 %collective-permute-start.11 = (bf16[512,640]{1,0:T(8,128)(2,1)}, bf16[512,640]{1,0:T(8,128)(2,1)S(1)}, u32[]{:S(2)}, u32[]{:S(2)}) collective-permute-start(bf16[512,640]{1,0:T(8,128)(2,1)} %collective-permute-done.7.refs_0_), channel_id=1, source_target_pairs={{0,1},{1,0},{2,3},{3,2},{4,5},{5,4},{6,7},{7,6},{8,9},{9,8},{10,11... | collective-permute-start | bytes 1966088 | tf_op jit(solution)/shard_map/ppermute | solution.py:472
  115.2 30.7 %collective-permute-start.23 = (bf16[640,640]{1,0:T(8,128)(2,1)S(1)}, bf16[640,640]{1,0:T(8,128)(2,1)}, u32[]{:S(2)}, u32[]{:S(2)}) collective-permute-start(bf16[640,640]{1,0:T(8,128)(2,1)S(1)} %collective-permute-done.13.refs_0_), channel_id=1, source_target_pairs={{0,16},{8,24},{16,0},{24,8},{1,17},{9,25},{17,1},{25,9},{2,18},{10... | collective-permute-start | bytes 2457608 | tf_op jit(solution)/shard_map/ppermute | solution.py:39
  116.8 30.4 %collective-permute-start.24 = (bf16[640,640]{1,0:T(8,128)(2,1)S(1)}, bf16[640,640]{1,0:T(8,128)(2,1)}, u32[]{:S(2)}, u32[]{:S(2)}) collective-permute-start(bf16[640,640]{1,0:T(8,128)(2,1)S(1)} %collective-permute-done.14.refs_3_), channel_id=1, source_target_pairs={{0,8},{8,0},{16,24},{24,16},{1,9},{9,1},{17,25},{25,17},{2,10},{10... | collective-permute-start | bytes 2457608 | tf_op jit(solution)/shard_map/ppermute | solution.py:39
  133.0 25.7 %collective-permute-start.22 = (bf16[640,640]{1,0:T(8,128)(2,1)}, bf16[640,640]{1,0:T(8,128)(2,1)}, u32[]{:S(2)}, u32[]{:S(2)}) collective-permute-start(bf16[640,640]{1,0:T(8,128)(2,1)} %get-tuple-element.68), channel_id=1, source_target_pairs={{0,16},{8,24},{16,0},{24,8},{1,17},{9,25},{17,1},{25,9},{2,18},{10... | collective-permute-start | bytes 2457608 | tf_op jit(solution)/shard_map/ppermute | solution.py:39
  134.6 28.0 %collective-permute-start.21 = (bf16[640,640]{1,0:T(8,128)(2,1)}, bf16[640,640]{1,0:T(8,128)(2,1)}, u32[]{:S(2)}, u32[]{:S(2)}) collective-permute-start(bf16[640,640]{1,0:T(8,128)(2,1)} %get-tuple-element.67), channel_id=1, source_target_pairs={{0,8},{8,0},{16,24},{24,16},{1,9},{9,1},{17,25},{25,17},{2,10},{10... | collective-permute-start | bytes 2457608 | tf_op jit(solution)/shard_map/ppermute | solution.py:39
  145.1 34.8 %collective-permute-start.25 = (bf16[640,640]{1,0:T(8,128)(2,1)}, bf16[640,640]{1,0:T(8,128)(2,1)S(1)}, u32[]{:S(2)}, u32[]{:S(2)}) collective-permute-start(bf16[640,640]{1,0:T(8,128)(2,1)} %get-tuple-element.73), channel_id=1, source_target_pairs={{0,8},{8,0},{16,24},{24,16},{1,9},{9,1},{17,25},{25,17},{2,10},{10... | collective-permute-start | bytes 2457608 | tf_op jit(solution)/shard_map/ppermute | solution.py:39
  146.0 33.9 %collective-permute-start.26 = (bf16[640,640]{1,0:T(8,128)(2,1)}, bf16[640,640]{1,0:T(8,128)(2,1)S(1)}, u32[]{:S(2)}, u32[]{:S(2)}) collective-permute-start(bf16[640,640]{1,0:T(8,128)(2,1)} %get-tuple-element.74), channel_id=1, source_target_pairs={{0,16},{8,24},{16,0},{24,8},{1,17},{9,25},{17,1},{25,9},{2,18},{10... | collective-permute-start | bytes 2457608 | tf_op jit(solution)/shard_map/ppermute | solution.py:39
  147.1 11.1 %copy-start.9 = (f32[1024,128]{1,0:T(8,128)S(1)}, f32[1024,128]{1,0:T(8,128)}, u32[]{:S(2)}) copy-start(f32[1024,128]{1,0:T(8,128)} %get-tuple-element.63) | copy-start | bytes 1572868
  147.1 11.6 %copy-start.11 = (f32[640,640]{1,0:T(8,128)S(1)}, f32[640,640]{1,0:T(8,128)}, u32[]{:S(2)}) copy-start(f32[640,640]{1,0:T(8,128)} %get-tuple-element.71) | copy-start | bytes 4915204
  158.7 5.8 %copy-start.2 = (bf16[1024,640]{1,0:T(8,128)(2,1)S(1)}, bf16[1024,640]{1,0:T(8,128)(2,1)}, u32[]{:S(2)}) copy-start(bf16[1024,640]{1,0:T(8,128)(2,1)} %sample.5) | copy-start | bytes 3932164
  158.7 5.8 %copy-start.7 = (bf16[1024,640]{1,0:T(8,128)(2,1)S(1)}, bf16[1024,640]{1,0:T(8,128)(2,1)}, u32[]{:S(2)}) copy-start(bf16[1024,640]{1,0:T(8,128)(2,1)} %copy-done.6) | copy-start | bytes 3932164
  158.7 5.8 %copy-start.8 = (f32[1024,640]{1,0:T(8,128)S(1)}, f32[1024,640]{1,0:T(8,128)}, u32[]{:S(2)}) copy-start(f32[1024,640]{1,0:T(8,128)} %get-tuple-element.83) | copy-start | bytes 7864324
  161.1 42.8 %collective-permute-start.32 = (bf16[640,640]{1,0:T(8,128)(2,1)}, bf16[640,640]{1,0:T(8,128)(2,1)S(1)}, u32[]{:S(2)}, u32[]{:S(2)}) collective-permute-start(bf16[640,640]{1,0:T(8,128)(2,1)} %add_convert_fusion), channel_id=1, source_target_pairs={{0,8},{8,0},{16,24},{24,16},{1,9},{9,1},{17,25},{25,17},{2,10},{10... | collective-permute-start | bytes 2457608 | tf_op jit(solution)/shard_map/ppermute | solution.py:39
  163.9 40.0 %collective-permute-start.31 = (bf16[640,640]{1,0:T(8,128)(2,1)S(1)}, bf16[640,640]{1,0:T(8,128)(2,1)S(1)}, u32[]{:S(2)}, u32[]{:S(2)}) collective-permute-start(bf16[640,640]{1,0:T(8,128)(2,1)S(1)} %add_convert_fusion.1), channel_id=1, source_target_pairs={{0,16},{8,24},{16,0},{24,8},{1,17},{9,25},{17,1},{25,9},{2,18},{10... | collective-permute-start | bytes 2457608 | tf_op jit(solution)/shard_map/ppermute | solution.py:39
  179.9 19.5 %copy-start.18 = (f32[1,640]{1,0:T(1,128)S(1)}, f32[1,640]{1,0:T(1,128)}, u32[]{:S(2)}) copy-start(f32[1,640]{1,0:T(1,128)} %param.17) | copy-start | bytes 7684
  179.9 5.4 %collective-permute-start.27 = (f32[1,1]{1,0:T(1,128)}, f32[1,1]{1,0:T(1,128)}, u32[]{:S(2)}, u32[]{:S(2)}) collective-permute-start(f32[1,1]{1,0:T(1,128)} %bitcast.18), channel_id=1, source_target_pairs={{0,1},{1,0},{2,3},{3,2},{4,5},{5,4},{6,7},{7,6},{8,9},{9,8},{10,11... | collective-permute-start | bytes 20 | tf_op jit(solution)/shard_map/ppermute | solution.py:600
  186.5 10.3 %collective-permute-start.28 = (f32[1,1]{1,0:T(1,128)}, f32[1,1]{1,0:T(1,128)}, u32[]{:S(2)}, u32[]{:S(2)}) collective-permute-start(f32[1,1]{1,0:T(1,128)} %add.104), channel_id=1, source_target_pairs={{0,2},{1,3},{2,4},{3,5},{4,6},{5,7},{6,0},{7,1},{8,10},{9,11},{10,... | collective-permute-start | bytes 20 | tf_op jit(solution)/shard_map/ppermute | solution.py:602
  190.3 6.5 %collective-permute-start.29 = (f32[1,1]{1,0:T(1,128)}, f32[1,1]{1,0:T(1,128)}, u32[]{:S(2)}, u32[]{:S(2)}) collective-permute-start(f32[1,1]{1,0:T(1,128)} %add.104), channel_id=1, source_target_pairs={{0,4},{1,5},{2,6},{3,7},{4,0},{5,1},{6,2},{7,3},{8,12},{9,13},{10,... | collective-permute-start | bytes 20 | tf_op jit(solution)/shard_map/ppermute | solution.py:602
  193.2 4.9 %collective-permute-start.30 = (f32[1,1]{1,0:T(1,128)}, f32[1,1]{1,0:T(1,128)}, u32[]{:S(2)}, u32[]{:S(2)}) collective-permute-start(f32[1,1]{1,0:T(1,128)} %add.104), channel_id=1, source_target_pairs={{0,6},{1,7},{2,0},{3,1},{4,2},{5,3},{6,4},{7,5},{8,14},{9,15},{10,... | collective-permute-start | bytes 20 | tf_op jit(solution)/shard_map/ppermute | solution.py:602
  (6 other events, 16.9 us)

commit v7 on v5

--- a/solution.py
+++ b/solution.py
@@ -13,7 +13,19 @@
 F32 = jnp.float32
 MIB = 1024 * 1024
 CHUNKS = 2
-GATES = {'relay': ('own',), 'teacher': ('parts', 'parts1'), 'B2': ('f0', 'f1'), 'B3': ('sums', 't00', 't01'), 'cB2': ('far0', 'far1'), 'cA3': ('soon',), 'cB3': ('early', 't10', 't11'), 'teacher relay': ('sums',), 'cA2': ('sums',), 'cB1': ('far0', 'far1')}
+GATES = {
+    "relay": ("own",),
+    "teacher": ("parts", "parts1"),
+    "A3": ("far0", "far1"),
+    "B2": ("A2",),
+    "B3": ("sums", "t00", "t01"),
+    "cB1": ("far0", "far1"),
+    "cA2": ("sums",),
+    "cB2": ("far0", "far1"),
+    "cA3": ("soon",),
+    "cB3": ("early", "t10", "t11"),
+    "teacher relay": ("sums",),
+}
 ANY = pl.BlockSpec(memory_space=pl.ANY)
 SMEM = pl.BlockSpec(memory_space=pltpu.SMEM)
 VMEM = pl.BlockSpec(memory_space=pltpu.VMEM)
@@ -71,24 +83,20 @@
         loads.append((pltpu.make_async_copy(source, full.at[at], sems.at[index]), spot))
         drains.append(pltpu.make_async_copy(full.at[at], out.at[at], osems.at[index]))
         loads[-1][0].start()
-    tile = 160
     sums[...] = jnp.zeros_like(sums)
+    tile = half_rows // 2
     for index, ((load, spot), drain) in enumerate(zip(loads, drains)):
         mask, half = ([(0, 0), (0, 1)] + keys)[index]
         column[...] = jnp.transpose(mod[where[mask] * 2 + half])
         load.wait()
-
-        @pl.loop(0, half_rows // tile)
-        def _(step):
-            low = pl.multiple_of(step * tile, tile)
+        for low in range(0, half_rows, tile):
             at = pl.ds(pl.multiple_of(spot + low, tile), tile)
             value = full[at, :].astype(F32)
-            shifted = value * column[pl.ds(low, tile), 0:1]
-            scaled = (value * (1.0 + column[pl.ds(low, tile), 1:2])).astype(BF16)
+            shifted = value * column[low : low + tile, 0:1]
+            scaled = (value * (1.0 + column[low : low + tile, 1:2])).astype(BF16)
             full[at, :] = scaled
             sums[0] += jnp.sum(scaled.astype(F32).reshape(tile // 8, 8, cols), axis=0)
             sums[1] += jnp.sum(shifted.reshape(tile // 8, 8, cols), axis=0)
-
         drain.start()
     for i in range(2):
         sums[i] = jnp.broadcast_to(jnp.sum(sums[i], axis=0, keepdims=True), (8, cols))
@@ -330,7 +338,7 @@
         scratch_shapes=scratch,
         input_output_aliases={7 + len(pieces) + 2: 1} if prior else {},
         compiler_params=pltpu.CompilerParams(vmem_limit_bytes=60 * MIB),
-        cost_estimate=pl.CostEstimate(flops=1, bytes_accessed=1, transcendentals=0),
+        cost_estimate=pl.CostEstimate(flops=4 * slots * clip_rows * depth * cols, bytes_accessed=1, transcendentals=0),
         name="project",
     )(where, scalars, sums, mod, sample, other, scaled, *pieces, *earlier)
 
@@ -577,16 +585,19 @@
         velocity = jnp.zeros((clip_rows, cols), F32)
         velocity = lax.fori_loop(0, width // cols, add_place, velocity)
     velocity = stats[:, 1:2] * (velocity - stats[:, 0:1] * sums[0, :1]) + sums[1, :1]
+    apart = velocity - fake_velocity
+    pulled = jnp.sum(apart * gen_branch.astype(F32), axis=0, keepdims=True)
     away = sample.astype(F32) - (noised.astype(F32) - sigma * velocity)
     away = after(jnp.sum(jnp.abs(away)).reshape(1, 1), *seconds)
     bit = 1
     while bit < shards:
+        if bit == 2:
+            away = after(away, fake_grad)
         away = away + lax.ppermute(away, "fsdp", [(i, i ^ bit) for i in range(shards)])
         bit *= 2
-    gap_value = away / (clip_rows * width)
-    push = sigma * (velocity - fake_velocity) / (gap_value + EPS)
-    branch_cot = (gen_gate * push).astype(BF16)
-    gate_grad = jnp.sum(push * gen_branch.astype(F32), axis=0, keepdims=True) / math.sqrt(clip_rows)
+    factor = sigma / (away / (clip_rows * width) + EPS)
+    branch_cot = (gen_gate * factor * apart).astype(BF16)
+    gate_grad = pulled * factor / math.sqrt(clip_rows)
     return (branch_cot, gate_grad, fake_grad)
 
 

time: 208 us -> 209 us (level)
  starting transfers between devices: 36.8 us -> 43.4 us
  local copies, waits for them, and re-layouts: 7.33 us -> 11.6 us
  waiting for transfers between devices: 56.9 us -> 53.1 us
  other arithmetic: 12.6 us -> 9.37 us
  Pallas kernels: 74.3 us -> 71.5 us
    ppermute x16, waiting for transfers between devices: 0.06 us -> 26.1 us  [swap_clip(): return lax.ppermute(value, 'clip', [(i, i ^ bit) for i in range(count)])]
    ppermute x6, waiting for transfers between devices: 48.6 us -> 26.3 us  [hop_to(): seen[name] = lax.ppermute(gated(name, source), 'fsdp', ring)]
    ppermute x3, waiting for transfers between devices: 6.95 us -> 0.66 us  [per_device(): lax.ppermute(away, 'fsdp', [(i, i ^ bit) for i in range(shards)])]
    ppermute x3, starting transfers between devices: 2.81 us -> 8.06 us  [per_device(): lax.ppermute(away, 'fsdp', [(i, i ^ bit) for i in range(shards)])]
    reduce_sum x1 -> x0, other arithmetic: 3.51 us -> none  [per_device(): jnp.sum(push * gen_branch.astype(F32), axis=0, keepdims=True)]
    unnamed x40 -> x46, local copies, waits for them, and re-layouts: 1.36 us -> 4.85 us
    pallas_call x2, Pallas kernels: 19.6 us -> 16.8 us  [scale(): pl.pallas_call(functools.partial(scale_kernel, list(blocks)), out_shape=(...]
  transfers between devices with their start and end apart: 32 -> 32, of which waited for: 9 -> 10; matrix products, arithmetic and copies ran while one was open for 16% -> 14% of each run, Pallas kernels for 34% -> 32%
where the time goes in v7:
time: 209 us
  Pallas kernels  71.5 us (34%)
  waiting for transfers between devices  53.1 us (25%)
  starting transfers between devices  43.4 us (21%)
  matrix products  15.7 us (8%)
  local copies, waits for them, and re-layouts  11.6 us (6%)
  other arithmetic  9.37 us (4%)
  between operations  4.11 us (2%)
    pallas_call x3, Pallas kernels, project(): pl.pallas_call(functools.partial(project_kernel, prior, last, plan, core_...  36.3 us
    ppermute x6, waiting for transfers between devices, hop_to(): seen[name] = lax.ppermute(gated(name, source), 'fsdp', ring)  26.3 us
    ppermute x16, waiting for transfers between devices, swap_clip(): return lax.ppermute(value, 'clip', [(i, i ^ bit) for i in range(count)])  26.1 us
    ppermute x16, starting transfers between devices, swap_clip(): return lax.ppermute(value, 'clip', [(i, i ^ bit) for i in range(count)])  19.3 us
    pallas_call x2, Pallas kernels, scale(): pl.pallas_call(functools.partial(scale_kernel, list(blocks)), out_shape=(...  16.8 us
    dot_general x1, matrix products, per_device(): velocity = jnp.dot(left, scaled, preferred_element_type=F32)  15.7 us
    ppermute x6, starting transfers between devices, hop_to(): seen[name] = lax.ppermute(gated(name, source), 'fsdp', ring)  15.3 us
    pallas_call x2, Pallas kernels, outer(): pl.pallas_call(outer_kernel, out_shape=[jax.ShapeDtypeStruct((cols, cols)...  14.7 us
  transfers between devices with their start and end apart: 32, of which 10 were waited for; matrix products, arithmetic and copies ran while one was open for 14% of the time, Pallas kernels for 32%

profile of v7, /device:TPU:0, one launch (start us, length us, event | category | flops | bytes accessed | tf_op | source)
XLA Modules:
  0.0 208.7 jit_solution(10417458322074037703)
XLA Ops:
  0.6 3.0 %collective-permute-start = (bf16[1280,640]{1,0:T(8,128)(2,1)}, bf16[1280,640]{1,0:T(8,128)(2,1)S(1)}, u32[]{:S(2)}, u32[]{:S(2)}) collective-permute-start(bf16[1280,640]{1,0:T(8,128)(2,1)} %weight.1), channel_id=1, source_target_pairs={{0,8},{8,0},{16,24},{24,16},{1,9},{9,1},{17,25},{25,17},{2,10},{10... | collective-permute-start | bytes 4915208 | tf_op jit(solution)/shard_map/ppermute | solution.py:39
  3.6 1.5 collective-permute-start.3
  5.8 2.2 %fusion.1.refs_0_ = bf16[1024,640]{1,0:T(8,128)(2,1)S(1)} fusion(bf16[1024,640]{1,0:T(8,128)(2,1)} %sample.5, bf16[1024,640]{1,0:T(8,128)(2,1)} %other.5, f32[]{:T(128)} %bitcast.1, f32[]{:T(128)S(6)} %sub.47), kind=kLoop, calls=%fused_computation.3 | loop fusion | flops 3932160 | bytes 3932168 | tf_op jit(solution)/shard_map/convert_element_type | solution.py:434
  8.3 2.6 %collective-permute-start.5 = (bf16[512,640]{1,0:T(8,128)(2,1)S(1)}, bf16[512,640]{1,0:T(8,128)(2,1)S(1)}, u32[]{:S(2)}, u32[]{:S(2)}) collective-permute-start(bf16[512,640]{1,0:T(8,128)(2,1)S(1)} %get-tuple-element.98), channel_id=1, source_target_pairs={{0,4},{1,5},{4,6},{5,7},{6,2},{7,3},{2,0},{3,1},{8,12},{9,13},{12,... | collective-permute-start | bytes 1966088 | tf_op jit(solution)/shard_map/ppermute | solution.py:460
  10.9 1.6 collective-permute-start.9
  12.5 13.5 %collective-permute-done.5.refs_2_ = bf16[512,640]{1,0:T(8,128)(2,1)S(1)} collective-permute-done((bf16[512,640]{1,0:T(8,128)(2,1)S(1)}, bf16[512,640]{1,0:T(8,128)(2,1)S(1)}, u32[]{:S(2)}, u32[]{:S(2)}) %collective-permute-start.5) | collective-permute-done | bytes 655392 | tf_op jit(solution)/shard_map/ppermute | solution.py:460
  26.0 3.4 %collective-permute-start.6 = (bf16[512,640]{1,0:T(8,128)(2,1)S(1)}, bf16[512,640]{1,0:T(8,128)(2,1)}, u32[]{:S(2)}, u32[]{:S(2)}) collective-permute-start(bf16[512,640]{1,0:T(8,128)(2,1)S(1)} %collective-permute-done.5.refs_2_), channel_id=1, source_target_pairs={{0,4},{1,5},{4,6},{5,7},{6,2},{7,3},{2,0},{3,1},{8,12},{9,13},{12,... | collective-permute-start | bytes 1966088 | tf_op jit(solution)/shard_map/ppermute | solution.py:460
  29.4 10.3 %collective-permute-done.refs_0_.refs_5_ = bf16[1280,640]{1,0:T(8,128)(2,1)S(1)} collective-permute-done((bf16[1280,640]{1,0:T(8,128)(2,1)}, bf16[1280,640]{1,0:T(8,128)(2,1)S(1)}, u32[]{:S(2)}, u32[]{:S(2)}) %collective-permute-start) | collective-permute-done | bytes 1638432 | tf_op jit(solution)/shard_map/ppermute | solution.py:39
  39.6 1.1 slice.30
  40.7 1.8 collective-permute-start.2
  42.5 1.0 slice.31
  43.5 1.5 collective-permute-start.4
  45.0 8.6 %collective-permute-done.6.refs_0_ = bf16[512,640]{1,0:T(8,128)(2,1)} collective-permute-done((bf16[512,640]{1,0:T(8,128)(2,1)S(1)}, bf16[512,640]{1,0:T(8,128)(2,1)}, u32[]{:S(2)}, u32[]{:S(2)}) %collective-permute-start.6) | collective-permute-done | bytes 655392 | tf_op jit(solution)/shard_map/ppermute | solution.py:460
  53.7 3.5 %collective-permute-start.12 = (bf16[512,640]{1,0:T(8,128)(2,1)}, bf16[512,640]{1,0:T(8,128)(2,1)}, u32[]{:S(2)}, u32[]{:S(2)}) collective-permute-start(bf16[512,640]{1,0:T(8,128)(2,1)} %collective-permute-done.9.refs_4_), channel_id=1, source_target_pairs={{0,4},{1,5},{4,6},{5,7},{6,2},{7,3},{2,0},{3,1},{8,12},{9,13},{12,... | collective-permute-start | bytes 1966088 | tf_op jit(solution)/shard_map/ppermute | solution.py:460
  57.2 1.3 fusion.5
  60.6 4.1 %collective-permute-done.4.refs_4_ = bf16[640,640]{1,0:T(8,128)(2,1)} collective-permute-done((bf16[640,640]{1,0:T(8,128)(2,1)}, bf16[640,640]{1,0:T(8,128)(2,1)}, u32[]{:S(2)}, u32[]{:S(2)}) %collective-permute-start.4) | collective-permute-done | bytes 819232 | tf_op jit(solution)/shard_map/ppermute | solution.py:39
  64.7 8.3 %scale.2 = (bf16[5120,640]{1,0:T(8,128)(2,1)}, f32[2,8,640]{2,1,0:T(8,128)}) custom-call(s32[4]{0:T(128)} %pad_add_fusion.where, f32[8,2,640]{2,1,0:T(2,128)} %bitcast.26, bf16[1280,640]{1,0:T(8,128)(2,1)} %weight.1, bf16[1280,640]{1,0:T(8,128)(2,1)} %copy-done.3, bf16[640,640]{1,0:T(8,128)(2,1)} %collective-permute-done.2.refs_1_, ...), custom_call_target="tpu_custom_call" | custom-call | flops 1 | bytes 1 | tf_op jit(solution)/shard_map/scale/pallas_call | solution.py:113
  73.6 6.6 %collective-permute-done.13.refs_0_ = bf16[640,640]{1,0:T(8,128)(2,1)S(1)} collective-permute-done((bf16[640,640]{1,0:T(8,128)(2,1)}, bf16[640,640]{1,0:T(8,128)(2,1)S(1)}, u32[]{:S(2)}, u32[]{:S(2)}) %collective-permute-start.13) | collective-permute-done | bytes 819232 | tf_op jit(solution)/shard_map/ppermute | solution.py:39
  82.1 1.4 collective-permute-start.19
  83.5 2.6 %collective-permute-start.15 = (bf16[512,640]{1,0:T(8,128)(2,1)}, bf16[512,640]{1,0:T(8,128)(2,1)S(1)}, u32[]{:S(2)}, u32[]{:S(2)}) collective-permute-start(bf16[512,640]{1,0:T(8,128)(2,1)} %collective-permute-done.12.refs_2_), channel_id=1, source_target_pairs={{0,4},{1,5},{4,6},{5,7},{6,2},{7,3},{2,0},{3,1},{8,12},{9,13},{12,... | collective-permute-start | bytes 1966088 | tf_op jit(solution)/shard_map/ppermute | solution.py:460
  86.1 1.6 collective-permute-start.7
  87.7 12.2 %project.3 = (f32[1024,640]{1,0:T(8,128)}, bf16[1024,5120]{1,0:T(8,128)(2,1)}, f32[1024,128]{1,0:T(8,128)}) custom-call(s32[5]{0:T(128)} %stack.55.where, f32[2]{0:T(128)} %pad_maximum_fusion.scalars, f32[2,8,640]{2,1,0:T(8,128)} %get-tuple-element.48.sums, f32[4,2,1280]{2,1,0:T(2,128)} %bitcast.27, bf16[1024,640]{1,0:T(8,128)(2,1)} %sample.5, ...), custom_call_target="tpu_custom_call" | custom-call | flops 6710886400 | bytes 1 | tf_op jit(solution)/shard_map/project/pallas_call | solution.py:333
  99.9 0.8 copy-done.18
  100.7 9.4 %project.4 = (f32[1024,640]{1,0:T(8,128)}, bf16[1024,5120]{1,0:T(8,128)(2,1)}, f32[1024,128]{1,0:T(8,128)}) custom-call(s32[5]{0:T(128)} %stack.55.where, f32[2]{0:T(128)} %pad_maximum_fusion.scalars, f32[2,8,640]{2,1,0:T(8,128)} %get-tuple-element.48.sums, f32[4,2,1280]{2,1,0:T(2,128)} %bitcast.28, ...), custom_call_target="tpu_custom_call", output_to_operand_aliasing={{1}: (13, {})} | custom-call | flops 3355443200 | bytes 1 | tf_op jit(solution)/shard_map/project/pallas_call | solution.py:333
  110.3 4.2 %collective-permute-done.7.refs_0_ = bf16[512,640]{1,0:T(8,128)(2,1)} collective-permute-done((bf16[512,640]{1,0:T(8,128)(2,1)}, bf16[512,640]{1,0:T(8,128)(2,1)}, u32[]{:S(2)}, u32[]{:S(2)}) %collective-permute-start.7) | collective-permute-done | bytes 655392 | tf_op jit(solution)/shard_map/ppermute | solution.py:460
  115.1 1.5 collective-permute-start.23
  117.2 14.7 %project.5 = (f32[1024,640]{1,0:T(8,128)}, bf16[1024,5120]{1,0:T(8,128)(2,1)}, f32[1024,128]{1,0:T(8,128)}, bf16[640,1024]{1,0:T(8,128)(2,1)}, f32[640,2]{1,0:T(...) custom-call(s32[6]{0:T(128)} %concatenate.4.where, ...), custom_call_target="tpu_custom_call", output_to_operand_aliasing={{1}: (13, {})} | custom-call | flops 3355443200 | bytes 1 | tf_op jit(solution)/shard_map/project/pallas_call | solution.py:333
  131.8 1.3 collective-permute-start.22
  133.8 0.7 collective-permute-start.21
  134.5 9.4 %outer.2 = (bf16[640,640]{1,0:T(8,128)(2,1)}, f32[640,640]{1,0:T(8,128)}, f32[640,640]{1,0:T(8,128)}, bf16[640,640]{1,0:T(8,128)(2,1)}) custom-call(s32[2]{0:T(128)} %pad_add_fusion.1.picks, f32[4,2,1280]{2,1,0:T(2,128)} %bitcast.30, f32[640,2]{1,0:T(8,128)} %get-tuple-element.66.edge, bf16[640,1024]{1,0:T(8,128)(2,1)} %get-tuple-element.84.flipped, ...), custom_call_target="tpu_custom_call" | custom-call | flops 3355443200 | bytes 11141120 | tf_op jit(solution)/shard_map/outer/pallas_call | solution.py:369
  143.9 1.3 collective-permute-start.25
  145.2 0.8 collective-permute-start.26
  146.1 0.9 copy-done.16
  147.0 8.5 %scale.3 = (bf16[5120,640]{1,0:T(8,128)(2,1)}, f32[2,8,640]{2,1,0:T(8,128)}) custom-call(s32[4]{0:T(128)} %pad_add_fusion.where, f32[8,2,640]{2,1,0:T(2,128)} %bitcast.32, bf16[1280,640]{1,0:T(8,128)(2,1)} %weight.2, bf16[640,640]{1,0:T(8,128)(2,1)} %copy-done.14, bf16[640,640]{1,0:T(8,128)(2,1)} %copy-done.15, ...), custom_call_target="tpu_custom_call" | custom-call | flops 1 | bytes 1 | tf_op jit(solution)/shard_map/scale/pallas_call | solution.py:113
  155.5 0.9 slice_reduce_fusion.3
  157.0 2.3 %add_convert_fusion = bf16[640,640]{1,0:T(8,128)(2,1)} fusion(f32[640,640]{1,0:T(8,128)S(1)} %copy-done.13, bf16[640,640]{1,0:T(8,128)(2,1)} %collective-permute-done.22), kind=kLoop, calls=%fused_computation.10 | loop fusion | flops 1228800 | bytes 3276800 | tf_op jit(solution)/shard_map/convert_element_type | solution.py:565
  159.3 1.3 collective-permute-start.29
  160.7 1.3 add_convert_fusion.1
  162.0 1.0 collective-permute-start.28
  163.0 15.7 %multiply_reduce_fusion = (f32[640]{0:T(1024)S(1)}, f32[]{:T(128)}, f32[1024,640]{1,0:T(8,128)}) fusion(bf16[1024,640]{1,0:T(8,128)(2,1)} %param.11, f32[1024,640]{1,0:T(8,128)S(1)} %copy-done.8, f32[640]{0:T(1024)S(1)} %get-tuple-element.94, f32[640]{0:T(1024)S(1)} %get-tuple-element.93, f32[1024]{0:T(1024)S(1)} %get-tuple-element.92, ...), kind=kOutput, calls=%fused_computation.6 | convolution fusion | flops 6720716288 | bytes 26230280 | tf_op jit(solution)/shard_map/dot_general | solution.py:583
  178.7 5.3 %outer.3 = (f32[640,640]{1,0:T(8,128)}, f32[640,640]{1,0:T(8,128)}) custom-call(s32[1]{0:T(128)} %bitcast.8.picks, f32[4,2,1280]{2,1,0:T(2,128)} %bitcast.31, f32[640,2]{1,0:T(8,128)} %get-tuple-element.66.edge, bf16[640,1024]{1,0:T(8,128)(2,1)} %get-tuple-element.84.flipped, bf16[1024,5120]{1,0:T(8,128)(2,1)} %get-tuple-element.73.inputs), custom_call_target="tpu_custom_call" | custom-call | flops 1677721600 | bytes 6881280 | tf_op jit(solution)/shard_map/outer/pallas_call | solution.py:369
  185.4 4.5 %collective-permute-done.29.refs_5_ = bf16[640,640]{1,0:T(8,128)(2,1)S(1)} collective-permute-done((bf16[640,640]{1,0:T(8,128)(2,1)}, bf16[640,640]{1,0:T(8,128)(2,1)S(1)}, u32[]{:S(2)}, u32[]{:S(2)}) %collective-permute-start.29) | collective-permute-done | bytes 819232 | tf_op jit(solution)/shard_map/ppermute | solution.py:39
  189.9 1.4 copy-done
  191.3 1.4 copy-done.1
  192.7 3.7 %finish.1 = f32[2,640,640]{2,1,0:T(8,128)} custom-call(f32[640,640]{1,0:T(8,128)S(1)} %copy-done, bf16[640,640]{1,0:T(8,128)(2,1)S(1)} %collective-permute-done.25.refs_1_, bf16[640,640]{1,0:T(8,128)(2,1)S(1)} %collective-permute-done.28.refs_2_, f32[640,640]{1,0:T(8,128)S(1)} %copy-done.1, bf16[640,640]{1,0:T(8,128)(2,1)S(1)} %collective-permute-done.26.refs_4_, ...), custom_call_target="tpu_custom_call" | custom-call | tf_op jit(solution)/shard_map/finish/pallas_call | solution.py:406
  196.5 3.7 %collective-permute-start.30 = (f32[1,1]{1,0:T(1,128)}, f32[1,1]{1,0:T(1,128)}, u32[]{:S(2)}, u32[]{:S(2)}) collective-permute-start(f32[1,1]{1,0:T(1,128)} %add.101), channel_id=1, source_target_pairs={{0,2},{1,3},{2,0},{3,1},{4,6},{5,7},{6,4},{7,5},{8,10},{9,11},{10,... | collective-permute-start | bytes 20 | tf_op jit(solution)/shard_map/ppermute | solution.py:596
  201.0 4.4 %collective-permute-start.31 = (f32[1,1]{1,0:T(1,128)}, f32[1,1]{1,0:T(1,128)}, u32[]{:S(2)}, u32[]{:S(2)}) collective-permute-start(f32[1,1]{1,0:T(1,128)} %add.102), channel_id=1, source_target_pairs={{0,4},{1,5},{2,6},{3,7},{4,0},{5,1},{6,2},{7,3},{8,12},{9,13},{10,... | collective-permute-start | bytes 20 | tf_op jit(solution)/shard_map/ppermute | solution.py:596
  207.0 1.7 multiply_convert_fusion
  (89 shorter events, 8.6 us)
Async XLA Ops:
  0.6 39.0 %collective-permute-start = (bf16[1280,640]{1,0:T(8,128)(2,1)}, bf16[1280,640]{1,0:T(8,128)(2,1)S(1)}, u32[]{:S(2)}, u32[]{:S(2)}) collective-permute-start(bf16[1280,640]{1,0:T(8,128)(2,1)} %weight.1), channel_id=1, source_target_pairs={{0,8},{8,0},{16,24},{24,16},{1,9},{9,1},{17,25},{25,17},{2,10},{10... | collective-permute-start | bytes 4915208 | tf_op jit(solution)/shard_map/ppermute | solution.py:39
  3.6 38.8 %collective-permute-start.3 = (bf16[1280,640]{1,0:T(8,128)(2,1)}, bf16[1280,640]{1,0:T(8,128)(2,1)S(1)}, u32[]{:S(2)}, u32[]{:S(2)}) collective-permute-start(bf16[1280,640]{1,0:T(8,128)(2,1)} %weight.1), channel_id=1, source_target_pairs={{0,16},{8,24},{16,0},{24,8},{1,17},{9,25},{17,1},{25,9},{2,18},{10... | collective-permute-start | bytes 4915208 | tf_op jit(solution)/shard_map/ppermute | solution.py:39
  8.1 35.5 %copy-start.6 = (bf16[1024,640]{1,0:T(8,128)(2,1)}, bf16[1024,640]{1,0:T(8,128)(2,1)S(1)}, u32[]{:S(2)}) copy-start(bf16[1024,640]{1,0:T(8,128)(2,1)S(1)} %fusion.1.refs_0_) | copy-start | bytes 3932164
  8.1 49.1 %copy-start.5 = (bf16[1280,640]{1,0:T(8,128)(2,1)S(1)}, bf16[1280,640]{1,0:T(8,128)(2,1)}, u32[]{:S(2)}) copy-start(bf16[1280,640]{1,0:T(8,128)(2,1)} %weight.2) | copy-start | bytes 4915204
  8.1 21.3 %collective-permute-start.1 = (bf16[1024,640]{1,0:T(8,128)(2,1)S(1)}, bf16[1024,640]{1,0:T(8,128)(2,1)S(1)}, u32[]{:S(2)}, u32[]{:S(2)}) collective-permute-start(bf16[1024,640]{1,0:T(8,128)(2,1)S(1)} %fusion.1.refs_0_), channel_id=1, source_target_pairs={{0,1},{1,0},{2,3},{3,2},{4,5},{5,4},{6,7},{7,6},{8,9},{9,8},{10,11... | collective-permute-start | bytes 3932168 | tf_op jit(solution)/shard_map/ppermute | solution.py:471
  8.3 17.7 %collective-permute-start.5 = (bf16[512,640]{1,0:T(8,128)(2,1)S(1)}, bf16[512,640]{1,0:T(8,128)(2,1)S(1)}, u32[]{:S(2)}, u32[]{:S(2)}) collective-permute-start(bf16[512,640]{1,0:T(8,128)(2,1)S(1)} %get-tuple-element.98), channel_id=1, source_target_pairs={{0,4},{1,5},{4,6},{5,7},{6,2},{7,3},{2,0},{3,1},{8,12},{9,13},{12,... | collective-permute-start | bytes 1966088 | tf_op jit(solution)/shard_map/ppermute | solution.py:460
  10.9 34.1 %collective-permute-start.9 = (bf16[512,640]{1,0:T(8,128)(2,1)S(1)}, bf16[512,640]{1,0:T(8,128)(2,1)}, u32[]{:S(2)}, u32[]{:S(2)}) collective-permute-start(bf16[512,640]{1,0:T(8,128)(2,1)S(1)} %get-tuple-element.97), channel_id=1, source_target_pairs={{0,4},{1,5},{4,6},{5,7},{6,2},{7,3},{2,0},{3,1},{8,12},{9,13},{12,... | collective-permute-start | bytes 1966088 | tf_op jit(solution)/shard_map/ppermute | solution.py:460
  26.0 19.1 %copy-start.22 = (bf16[512,640]{1,0:T(8,128)(2,1)}, bf16[512,640]{1,0:T(8,128)(2,1)S(1)}, u32[]{:S(2)}) copy-start(bf16[512,640]{1,0:T(8,128)(2,1)S(1)} %collective-permute-done.5.refs_2_) | copy-start | bytes 1966084
  26.0 27.7 %collective-permute-start.6 = (bf16[512,640]{1,0:T(8,128)(2,1)S(1)}, bf16[512,640]{1,0:T(8,128)(2,1)}, u32[]{:S(2)}, u32[]{:S(2)}) collective-permute-start(bf16[512,640]{1,0:T(8,128)(2,1)S(1)} %collective-permute-done.5.refs_2_), channel_id=1, source_target_pairs={{0,4},{1,5},{4,6},{5,7},{6,2},{7,3},{2,0},{3,1},{8,12},{9,13},{12,... | collective-permute-start | bytes 1966088 | tf_op jit(solution)/shard_map/ppermute | solution.py:460
  29.4 29.1 %copy-start.21 = (bf16[1024,640]{1,0:T(8,128)(2,1)}, bf16[1024,640]{1,0:T(8,128)(2,1)S(1)}, u32[]{:S(2)}) copy-start(bf16[1024,640]{1,0:T(8,128)(2,1)S(1)} %collective-permute-done.1.refs_1_) | copy-start | bytes 3932164
  39.6 18.8 %copy-start.3 = (bf16[1280,640]{1,0:T(8,128)(2,1)}, bf16[1280,640]{1,0:T(8,128)(2,1)S(1)}, u32[]{:S(2)}) copy-start(bf16[1280,640]{1,0:T(8,128)(2,1)S(1)} %collective-permute-done.refs_0_.refs_5_) | copy-start | bytes 4915204
  40.7 19.9 %collective-permute-start.2 = (bf16[640,640]{1,0:T(8,128)(2,1)}, bf16[640,640]{1,0:T(8,128)(2,1)}, u32[]{:S(2)}, u32[]{:S(2)}) collective-permute-start(bf16[640,640]{1,0:T(8,128)(2,1)} %slice.30), channel_id=1, source_target_pairs={{0,16},{8,24},{16,0},{24,8},{1,17},{9,25},{17,1},{25,9},{2,18},{10... | collective-permute-start | bytes 2457608 | tf_op jit(solution)/shard_map/ppermute | solution.py:39
  42.5 22.2 %copy-start.4 = (bf16[1280,640]{1,0:T(8,128)(2,1)}, bf16[1280,640]{1,0:T(8,128)(2,1)S(1)}, u32[]{:S(2)}) copy-start(bf16[1280,640]{1,0:T(8,128)(2,1)S(1)} %collective-permute-done.3.refs_2_.refs_3_) | copy-start | bytes 4915204
  43.5 21.2 %collective-permute-start.4 = (bf16[640,640]{1,0:T(8,128)(2,1)}, bf16[640,640]{1,0:T(8,128)(2,1)}, u32[]{:S(2)}, u32[]{:S(2)}) collective-permute-start(bf16[640,640]{1,0:T(8,128)(2,1)} %slice.31), channel_id=1, source_target_pairs={{0,8},{8,0},{16,24},{24,16},{1,9},{9,1},{17,25},{25,17},{2,10},{10... | collective-permute-start | bytes 2457608 | tf_op jit(solution)/shard_map/ppermute | solution.py:39
  53.7 19.4 %collective-permute-start.12 = (bf16[512,640]{1,0:T(8,128)(2,1)}, bf16[512,640]{1,0:T(8,128)(2,1)}, u32[]{:S(2)}, u32[]{:S(2)}) collective-permute-start(bf16[512,640]{1,0:T(8,128)(2,1)} %collective-permute-done.9.refs_4_), channel_id=1, source_target_pairs={{0,4},{1,5},{4,6},{5,7},{6,2},{7,3},{2,0},{3,1},{8,12},{9,13},{12,... | collective-permute-start | bytes 1966088 | tf_op jit(solution)/shard_map/ppermute | solution.py:460
  58.5 21.8 %collective-permute-start.13 = (bf16[640,640]{1,0:T(8,128)(2,1)}, bf16[640,640]{1,0:T(8,128)(2,1)S(1)}, u32[]{:S(2)}, u32[]{:S(2)}) collective-permute-start(bf16[640,640]{1,0:T(8,128)(2,1)} %get-tuple-element.96), channel_id=1, source_target_pairs={{0,8},{8,0},{16,24},{24,16},{1,9},{9,1},{17,25},{25,17},{2,10},{10... | collective-permute-start | bytes 2457608 | tf_op jit(solution)/shard_map/ppermute | solution.py:39
  59.0 22.5 %collective-permute-start.14 = (bf16[640,640]{1,0:T(8,128)(2,1)}, bf16[640,640]{1,0:T(8,128)(2,1)}, u32[]{:S(2)}, u32[]{:S(2)}) collective-permute-start(bf16[640,640]{1,0:T(8,128)(2,1)} %get-tuple-element.95), channel_id=1, source_target_pairs={{0,16},{8,24},{16,0},{24,8},{1,17},{9,25},{17,1},{25,9},{2,18},{10... | collective-permute-start | bytes 2457608 | tf_op jit(solution)/shard_map/ppermute | solution.py:39
  60.6 22.9 %collective-permute-start.8 = (bf16[512,640]{1,0:T(8,128)(2,1)}, bf16[512,640]{1,0:T(8,128)(2,1)}, u32[]{:S(2)}, u32[]{:S(2)}) collective-permute-start(bf16[512,640]{1,0:T(8,128)(2,1)} %copy-done.22), channel_id=1, source_target_pairs={{0,1},{1,0},{2,3},{3,2},{4,5},{5,4},{6,7},{7,6},{8,9},{9,8},{10,11... | collective-permute-start | bytes 1966088 | tf_op jit(solution)/shard_map/ppermute | solution.py:464
  64.7 17.4 %collective-permute-start.10 = (bf16[512,640]{1,0:T(8,128)(2,1)}, bf16[512,640]{1,0:T(8,128)(2,1)}, u32[]{:S(2)}, u32[]{:S(2)}) collective-permute-start(bf16[512,640]{1,0:T(8,128)(2,1)} %collective-permute-done.9.refs_4_), channel_id=1, source_target_pairs={{0,1},{1,0},{2,3},{3,2},{4,5},{5,4},{6,7},{7,6},{8,9},{9,8},{10,11... | collective-permute-start | bytes 1966088 | tf_op jit(solution)/shard_map/ppermute | solution.py:464
  73.1 13.0 %collective-permute-start.16 = (bf16[512,640]{1,0:T(8,128)(2,1)}, bf16[512,640]{1,0:T(8,128)(2,1)S(1)}, u32[]{:S(2)}, u32[]{:S(2)}) collective-permute-start(bf16[512,640]{1,0:T(8,128)(2,1)} %collective-permute-done.6.refs_0_), channel_id=1, source_target_pairs={{0,1},{1,0},{2,3},{3,2},{4,5},{5,4},{6,7},{7,6},{8,9},{9,8},{10,11... | collective-permute-start | bytes 1966088 | tf_op jit(solution)/shard_map/ppermute | solution.py:464
  80.2 34.9 %copy-start.14 = (bf16[640,640]{1,0:T(8,128)(2,1)}, bf16[640,640]{1,0:T(8,128)(2,1)S(1)}, u32[]{:S(2)}) copy-start(bf16[640,640]{1,0:T(8,128)(2,1)S(1)} %collective-permute-done.13.refs_0_) | copy-start | bytes 2457604
  80.2 19.6 %collective-permute-start.17 = (bf16[512,640]{1,0:T(8,128)(2,1)}, bf16[512,640]{1,0:T(8,128)(2,1)S(1)}, u32[]{:S(2)}, u32[]{:S(2)}) collective-permute-start(bf16[512,640]{1,0:T(8,128)(2,1)} %collective-permute-done.12.refs_2_), channel_id=1, source_target_pairs={{0,1},{1,0},{2,3},{3,2},{4,5},{5,4},{6,7},{7,6},{8,9},{9,8},{10,11... | collective-permute-start | bytes 1966088 | tf_op jit(solution)/shard_map/ppermute | solution.py:464
  81.5 28.7 %collective-permute-start.18 = (bf16[640,640]{1,0:T(8,128)(2,1)}, bf16[640,640]{1,0:T(8,128)(2,1)}, u32[]{:S(2)}, u32[]{:S(2)}) collective-permute-start(bf16[640,640]{1,0:T(8,128)(2,1)} %get-tuple-element.96), channel_id=1, source_target_pairs={{0,16},{8,24},{16,0},{24,8},{1,17},{9,25},{17,1},{25,9},{2,18},{10... | collective-permute-start | bytes 2457608 | tf_op jit(solution)/shard_map/ppermute | solution.py:39
  82.1 28.1 %collective-permute-start.19 = (bf16[640,640]{1,0:T(8,128)(2,1)}, bf16[640,640]{1,0:T(8,128)(2,1)}, u32[]{:S(2)}, u32[]{:S(2)}) collective-permute-start(bf16[640,640]{1,0:T(8,128)(2,1)} %get-tuple-element.95), channel_id=1, source_target_pairs={{0,8},{8,0},{16,24},{24,16},{1,9},{9,1},{17,25},{25,17},{2,10},{10... | collective-permute-start | bytes 2457608 | tf_op jit(solution)/shard_map/ppermute | solution.py:39
  83.5 26.7 %collective-permute-start.15 = (bf16[512,640]{1,0:T(8,128)(2,1)}, bf16[512,640]{1,0:T(8,128)(2,1)S(1)}, u32[]{:S(2)}, u32[]{:S(2)}) collective-permute-start(bf16[512,640]{1,0:T(8,128)(2,1)} %collective-permute-done.12.refs_2_), channel_id=1, source_target_pairs={{0,4},{1,5},{4,6},{5,7},{6,2},{7,3},{2,0},{3,1},{8,12},{9,13},{12,... | collective-permute-start | bytes 1966088 | tf_op jit(solution)/shard_map/ppermute | solution.py:460
  86.1 13.8 %copy-start.17 = (bf16[512,640]{1,0:T(8,128)(2,1)}, bf16[512,640]{1,0:T(8,128)(2,1)S(1)}, u32[]{:S(2)}) copy-start(bf16[512,640]{1,0:T(8,128)(2,1)S(1)} %collective-permute-done.16.refs_1_) | copy-start | bytes 1966084
  86.1 28.4 %collective-permute-start.7 = (bf16[512,640]{1,0:T(8,128)(2,1)}, bf16[512,640]{1,0:T(8,128)(2,1)}, u32[]{:S(2)}, u32[]{:S(2)}) collective-permute-start(bf16[512,640]{1,0:T(8,128)(2,1)} %collective-permute-done.6.refs_0_), channel_id=1, source_target_pairs={{0,4},{1,5},{4,6},{5,7},{6,2},{7,3},{2,0},{3,1},{8,12},{9,13},{12,... | collective-permute-start | bytes 1966088 | tf_op jit(solution)/shard_map/ppermute | solution.py:460
  110.2 7.0 %copy-start.19 = (bf16[512,640]{1,0:T(8,128)(2,1)}, bf16[512,640]{1,0:T(8,128)(2,1)S(1)}, u32[]{:S(2)}) copy-start(bf16[512,640]{1,0:T(8,128)(2,1)S(1)} %collective-permute-done.15.refs_2_) | copy-start | bytes 1966084
  110.2 7.0 %collective-permute-start.20 = (bf16[512,640]{1,0:T(8,128)(2,1)S(1)}, bf16[512,640]{1,0:T(8,128)(2,1)}, u32[]{:S(2)}, u32[]{:S(2)}) collective-permute-start(bf16[512,640]{1,0:T(8,128)(2,1)S(1)} %collective-permute-done.15.refs_2_), channel_id=1, source_target_pairs={{0,1},{1,0},{2,3},{3,2},{4,5},{5,4},{6,7},{7,6},{8,9},{9,8},{10,11... | collective-permute-start | bytes 1966088 | tf_op jit(solution)/shard_map/ppermute | solution.py:464
  114.5 2.7 %collective-permute-start.11 = (bf16[512,640]{1,0:T(8,128)(2,1)}, bf16[512,640]{1,0:T(8,128)(2,1)}, u32[]{:S(2)}, u32[]{:S(2)}) collective-permute-start(bf16[512,640]{1,0:T(8,128)(2,1)} %collective-permute-done.7.refs_0_), channel_id=1, source_target_pairs={{0,1},{1,0},{2,3},{3,2},{4,5},{5,4},{6,7},{7,6},{8,9},{9,8},{10,11... | collective-permute-start | bytes 1966088 | tf_op jit(solution)/shard_map/ppermute | solution.py:464
  115.1 30.1 %collective-permute-start.23 = (bf16[640,640]{1,0:T(8,128)(2,1)S(1)}, bf16[640,640]{1,0:T(8,128)(2,1)S(1)}, u32[]{:S(2)}, u32[]{:S(2)}) collective-permute-start(bf16[640,640]{1,0:T(8,128)(2,1)S(1)} %collective-permute-done.13.refs_0_), channel_id=1, source_target_pairs={{0,16},{8,24},{16,0},{24,8},{1,17},{9,25},{17,1},{25,9},{2,18},{10... | collective-permute-start | bytes 2457608 | tf_op jit(solution)/shard_map/ppermute | solution.py:39
  116.6 29.3 %collective-permute-start.24 = (bf16[640,640]{1,0:T(8,128)(2,1)}, bf16[640,640]{1,0:T(8,128)(2,1)S(1)}, u32[]{:S(2)}, u32[]{:S(2)}) collective-permute-start(bf16[640,640]{1,0:T(8,128)(2,1)} %collective-permute-done.14.refs_3_), channel_id=1, source_target_pairs={{0,8},{8,0},{16,24},{24,16},{1,9},{9,1},{17,25},{25,17},{2,10},{10... | collective-permute-start | bytes 2457608 | tf_op jit(solution)/shard_map/ppermute | solution.py:39
  131.8 25.1 %collective-permute-start.22 = (bf16[640,640]{1,0:T(8,128)(2,1)}, bf16[640,640]{1,0:T(8,128)(2,1)}, u32[]{:S(2)}, u32[]{:S(2)}) collective-permute-start(bf16[640,640]{1,0:T(8,128)(2,1)} %get-tuple-element.69), channel_id=1, source_target_pairs={{0,16},{8,24},{16,0},{24,8},{1,17},{9,25},{17,1},{25,9},{2,18},{10... | collective-permute-start | bytes 2457608 | tf_op jit(solution)/shard_map/ppermute | solution.py:39
  133.8 26.9 %collective-permute-start.21 = (bf16[640,640]{1,0:T(8,128)(2,1)}, bf16[640,640]{1,0:T(8,128)(2,1)}, u32[]{:S(2)}, u32[]{:S(2)}) collective-permute-start(bf16[640,640]{1,0:T(8,128)(2,1)} %get-tuple-element.68), channel_id=1, source_target_pairs={{0,8},{8,0},{16,24},{24,16},{1,9},{9,1},{17,25},{25,17},{2,10},{10... | collective-permute-start | bytes 2457608 | tf_op jit(solution)/shard_map/ppermute | solution.py:39
  143.9 34.8 %collective-permute-start.25 = (bf16[640,640]{1,0:T(8,128)(2,1)}, bf16[640,640]{1,0:T(8,128)(2,1)S(1)}, u32[]{:S(2)}, u32[]{:S(2)}) collective-permute-start(bf16[640,640]{1,0:T(8,128)(2,1)} %get-tuple-element.74), channel_id=1, source_target_pairs={{0,8},{8,0},{16,24},{24,16},{1,9},{9,1},{17,25},{25,17},{2,10},{10... | collective-permute-start | bytes 2457608 | tf_op jit(solution)/shard_map/ppermute | solution.py:39
  145.2 33.5 %collective-permute-start.26 = (bf16[640,640]{1,0:T(8,128)(2,1)}, bf16[640,640]{1,0:T(8,128)(2,1)S(1)}, u32[]{:S(2)}, u32[]{:S(2)}) collective-permute-start(bf16[640,640]{1,0:T(8,128)(2,1)} %get-tuple-element.75), channel_id=1, source_target_pairs={{0,16},{8,24},{16,0},{24,8},{1,17},{9,25},{17,1},{25,9},{2,18},{10... | collective-permute-start | bytes 2457608 | tf_op jit(solution)/shard_map/ppermute | solution.py:39
  147.0 9.4 %copy-start.11 = (f32[1024,128]{1,0:T(8,128)S(1)}, f32[1024,128]{1,0:T(8,128)}, u32[]{:S(2)}) copy-start(f32[1024,128]{1,0:T(8,128)} %get-tuple-element.64) | copy-start | bytes 1572868
  147.0 9.9 %copy-start.13 = (f32[640,640]{1,0:T(8,128)S(1)}, f32[640,640]{1,0:T(8,128)}, u32[]{:S(2)}) copy-start(f32[640,640]{1,0:T(8,128)} %get-tuple-element.72) | copy-start | bytes 4915204
  156.9 6.0 %copy-start.2 = (bf16[1024,640]{1,0:T(8,128)(2,1)S(1)}, bf16[1024,640]{1,0:T(8,128)(2,1)}, u32[]{:S(2)}) copy-start(bf16[1024,640]{1,0:T(8,128)(2,1)} %sample.5) | copy-start | bytes 3932164
  156.9 6.0 %copy-start.7 = (bf16[1024,640]{1,0:T(8,128)(2,1)S(1)}, bf16[1024,640]{1,0:T(8,128)(2,1)}, u32[]{:S(2)}) copy-start(bf16[1024,640]{1,0:T(8,128)(2,1)} %copy-done.6) | copy-start | bytes 3932164
  159.3 30.6 %collective-permute-start.29 = (bf16[640,640]{1,0:T(8,128)(2,1)}, bf16[640,640]{1,0:T(8,128)(2,1)S(1)}, u32[]{:S(2)}, u32[]{:S(2)}) collective-permute-start(bf16[640,640]{1,0:T(8,128)(2,1)} %add_convert_fusion), channel_id=1, source_target_pairs={{0,8},{8,0},{16,24},{24,16},{1,9},{9,1},{17,25},{25,17},{2,10},{10... | collective-permute-start | bytes 2457608 | tf_op jit(solution)/shard_map/ppermute | solution.py:39
  162.0 27.9 %collective-permute-start.28 = (bf16[640,640]{1,0:T(8,128)(2,1)S(1)}, bf16[640,640]{1,0:T(8,128)(2,1)S(1)}, u32[]{:S(2)}, u32[]{:S(2)}) collective-permute-start(bf16[640,640]{1,0:T(8,128)(2,1)S(1)} %add_convert_fusion.1), channel_id=1, source_target_pairs={{0,16},{8,24},{16,0},{24,8},{1,17},{9,25},{17,1},{25,9},{2,18},{10... | collective-permute-start | bytes 2457608 | tf_op jit(solution)/shard_map/ppermute | solution.py:39
  178.7 5.4 %collective-permute-start.27 = (f32[1,1]{1,0:T(1,128)}, f32[1,1]{1,0:T(1,128)}, u32[]{:S(2)}, u32[]{:S(2)}) collective-permute-start(f32[1,1]{1,0:T(1,128)} %bitcast.18), channel_id=1, source_target_pairs={{0,1},{1,0},{2,3},{3,2},{4,5},{5,4},{6,7},{7,6},{8,9},{9,8},{10,11... | collective-permute-start | bytes 20 | tf_op jit(solution)/shard_map/ppermute | solution.py:596
  192.7 14.2 %copy-start.20 = (f32[1,640]{1,0:T(1,128)S(1)}, f32[1,640]{1,0:T(1,128)}, u32[]{:S(2)}) copy-start(f32[1,640]{1,0:T(1,128)} %param.17) | copy-start | bytes 7684
  192.7 14.2 %copy-start.9 = (f32[1024,640]{1,0:T(8,128)S(1)}, f32[1024,640]{1,0:T(8,128)}, u32[]{:S(2)}) copy-start(f32[1024,640]{1,0:T(8,128)} %get-tuple-element.88) | copy-start | bytes 7864324
  192.7 14.2 %copy-start.10 = (f32[1024,640]{1,0:T(8,128)S(1)}, f32[1024,640]{1,0:T(8,128)}, u32[]{:S(2)}) copy-start(f32[1024,640]{1,0:T(8,128)} %get-tuple-element.99) | copy-start | bytes 7864324
  196.5 4.0 %collective-permute-start.30 = (f32[1,1]{1,0:T(1,128)}, f32[1,1]{1,0:T(1,128)}, u32[]{:S(2)}, u32[]{:S(2)}) collective-permute-start(f32[1,1]{1,0:T(1,128)} %add.101), channel_id=1, source_target_pairs={{0,2},{1,3},{2,0},{3,1},{4,6},{5,7},{6,4},{7,5},{8,10},{9,11},{10,... | collective-permute-start | bytes 20 | tf_op jit(solution)/shard_map/ppermute | solution.py:596
  201.0 4.7 %collective-permute-start.31 = (f32[1,1]{1,0:T(1,128)}, f32[1,1]{1,0:T(1,128)}, u32[]{:S(2)}, u32[]{:S(2)}) collective-permute-start(f32[1,1]{1,0:T(1,128)} %add.102), channel_id=1, source_target_pairs={{0,4},{1,5},{2,6},{3,7},{4,0},{5,1},{6,2},{7,3},{8,12},{9,13},{10,... | collective-permute-start | bytes 20 | tf_op jit(solution)/shard_map/ppermute | solution.py:596
  (7 other events, 16.7 us)

commit v8 on v7

--- a/solution.py
+++ b/solution.py
@@ -16,15 +16,15 @@
 GATES = {
     "relay": ("own",),
     "teacher": ("parts", "parts1"),
-    "A3": ("far0", "far1"),
     "B2": ("A2",),
-    "B3": ("sums", "t00", "t01"),
-    "cB1": ("far0", "far1"),
-    "cA2": ("sums",),
     "cB2": ("far0", "far1"),
     "cA3": ("soon",),
+    "teacher relay": ("sums",),
+    "cA2": ("sums",),
+    "cB1": ("far0", "far1"),
+    "B3": ("sums",),
     "cB3": ("early", "t10", "t11"),
-    "teacher relay": ("sums",),
+    "A3": ("far0", "far1"),
 }
 ANY = pl.BlockSpec(memory_space=pl.ANY)
 SMEM = pl.BlockSpec(memory_space=pltpu.SMEM)
@@ -126,7 +126,7 @@
         ],
         compiler_params=pltpu.CompilerParams(vmem_limit_bytes=60 * MIB),
         cost_estimate=pl.CostEstimate(
-            flops=1, bytes_accessed=1, transcendentals=0
+            flops=2700 * width * cols, bytes_accessed=7 * width * cols, transcendentals=0
         ),
         name="scale",
     )(where, mod, weight, *blocks.values())
@@ -338,7 +338,7 @@
         scratch_shapes=scratch,
         input_output_aliases={7 + len(pieces) + 2: 1} if prior else {},
         compiler_params=pltpu.CompilerParams(vmem_limit_bytes=60 * MIB),
-        cost_estimate=pl.CostEstimate(flops=4 * slots * clip_rows * depth * cols, bytes_accessed=1, transcendentals=0),
+        cost_estimate=pl.CostEstimate(flops=1, bytes_accessed=1, transcendentals=0),
         name="project",
     )(where, scalars, sums, mod, sample, other, scaled, *pieces, *earlier)
 
@@ -591,8 +591,6 @@
     away = after(jnp.sum(jnp.abs(away)).reshape(1, 1), *seconds)
     bit = 1
     while bit < shards:
-        if bit == 2:
-            away = after(away, fake_grad)
         away = away + lax.ppermute(away, "fsdp", [(i, i ^ bit) for i in range(shards)])
         bit *= 2
     factor = sigma / (away / (clip_rows * width) + EPS)

time: 209 us -> 201 us (0.962)
  waiting for transfers between devices: 53.1 us -> 42 us
  other arithmetic: 9.37 us -> 12.1 us
    ppermute x16, waiting for transfers between devices: 26.1 us -> 20.2 us  [swap_clip(): return lax.ppermute(value, 'clip', [(i, i ^ bit) for i in range(count)])]
    ppermute x6, waiting for transfers between devices: 26.3 us -> 20.6 us  [hop_to(): seen[name] = lax.ppermute(gated(name, source), 'fsdp', ring)]
    unnamed x46 -> x40, local copies, waits for them, and re-layouts: 4.85 us -> 1.11 us
    convert_element_type x1, other arithmetic: 1.74 us -> 4.42 us  [per_device(): branch_cot = (gen_gate * factor * apart).astype(BF16)]
    slice x2, local copies, waits for them, and re-layouts: 2.11 us -> 4.24 us  [relay_parts(): parts[bit, half] = block[half * rows:(half + 1) * rows]]
  transfers between devices with their start and end apart: 32 -> 32, of which waited for: 10 -> 10; matrix products, arithmetic and copies ran while one was open for 14% -> 19% of each run, Pallas kernels for 32% -> 34%
where the time goes in v8:
time: 201 us; the launch traced here: 200 us
  Pallas kernels  71.6 us (36%)
  starting transfers between devices  44.1 us (22%)
  waiting for transfers between devices  42 us (21%)
  matrix products  15.7 us (8%)
  other arithmetic  12.1 us (6%)
  local copies, waits for them, and re-layouts  10.8 us (5%)
  between operations  4.15 us (2%)
    pallas_call x3, Pallas kernels, project(): pl.pallas_call(functools.partial(project_kernel, prior, last, plan, core_...  36.2 us
    ppermute x16, starting transfers between devices, swap_clip(): return lax.ppermute(value, 'clip', [(i, i ^ bit) for i in range(count)])  20.7 us
    ppermute x6, waiting for transfers between devices, hop_to(): seen[name] = lax.ppermute(gated(name, source), 'fsdp', ring)  20.6 us
    ppermute x16, waiting for transfers between devices, swap_clip(): return lax.ppermute(value, 'clip', [(i, i ^ bit) for i in range(count)])  20.2 us
    pallas_call x2, Pallas kernels, scale(): pl.pallas_call(functools.partial(scale_kernel, list(blocks)), out_shape=(...  16.9 us
    dot_general x1, matrix products, per_device(): velocity = jnp.dot(left, scaled, preferred_element_type=F32)  15.7 us
    ppermute x6, starting transfers between devices, hop_to(): seen[name] = lax.ppermute(gated(name, source), 'fsdp', ring)  15.2 us
    pallas_call x2, Pallas kernels, outer(): pl.pallas_call(outer_kernel, out_shape=[jax.ShapeDtypeStruct((cols, cols)...  14.7 us
  transfers between devices with their start and end apart: 32, of which 10 were waited for; matrix products, arithmetic and copies ran while one was open for 19% of the time, Pallas kernels for 34%

profile of v8, /device:TPU:0, one launch (start us, length us, event | category | flops | bytes accessed | tf_op | source)
XLA Modules:
  0.0 200.5 jit_solution(1108610803943447559)
XLA Ops:
  0.6 3.0 %collective-permute-start = (bf16[1280,640]{1,0:T(8,128)(2,1)}, bf16[1280,640]{1,0:T(8,128)(2,1)}, u32[]{:S(2)}, u32[]{:S(2)}) collective-permute-start(bf16[1280,640]{1,0:T(8,128)(2,1)} %weight.1), channel_id=1, source_target_pairs={{0,8},{8,0},{16,24},{24,16},{1,9},{9,1},{17,25},{25,17},{2,10},{10... | collective-permute-start | bytes 4915208 | tf_op jit(solution)/shard_map/ppermute | solution.py:39
  3.6 1.5 collective-permute-start.3
  5.8 2.2 %fusion.1.refs_0_ = bf16[1024,640]{1,0:T(8,128)(2,1)S(1)} fusion(bf16[1024,640]{1,0:T(8,128)(2,1)} %sample.5, bf16[1024,640]{1,0:T(8,128)(2,1)} %other.5, f32[]{:T(128)} %bitcast.1, f32[]{:T(128)S(6)} %sub.47), kind=kLoop, calls=%fused_computation.3 | loop fusion | flops 3932160 | bytes 3932168 | tf_op jit(solution)/shard_map/convert_element_type | solution.py:434
  8.2 1.0 fusion.6
  9.1 2.6 %collective-permute-start.5 = (bf16[512,640]{1,0:T(8,128)(2,1)S(1)}, bf16[512,640]{1,0:T(8,128)(2,1)}, u32[]{:S(2)}, u32[]{:S(2)}) collective-permute-start(bf16[512,640]{1,0:T(8,128)(2,1)S(1)} %get-tuple-element.96), channel_id=1, source_target_pairs={{0,4},{1,5},{4,6},{5,7},{6,2},{7,3},{2,0},{3,1},{8,12},{9,13},{12,... | collective-permute-start | bytes 1966088 | tf_op jit(solution)/shard_map/ppermute | solution.py:460
  11.7 1.6 collective-permute-start.9
  13.3 13.5 %collective-permute-done.5.refs_2_ = bf16[512,640]{1,0:T(8,128)(2,1)} collective-permute-done((bf16[512,640]{1,0:T(8,128)(2,1)S(1)}, bf16[512,640]{1,0:T(8,128)(2,1)}, u32[]{:S(2)}, u32[]{:S(2)}) %collective-permute-start.5) | collective-permute-done | bytes 655392 | tf_op jit(solution)/shard_map/ppermute | solution.py:460
  26.8 3.5 %collective-permute-start.6 = (bf16[512,640]{1,0:T(8,128)(2,1)}, bf16[512,640]{1,0:T(8,128)(2,1)}, u32[]{:S(2)}, u32[]{:S(2)}) collective-permute-start(bf16[512,640]{1,0:T(8,128)(2,1)} %collective-permute-done.5.refs_2_), channel_id=1, source_target_pairs={{0,4},{1,5},{4,6},{5,7},{6,2},{7,3},{2,0},{3,1},{8,12},{9,13},{12,... | collective-permute-start | bytes 1966088 | tf_op jit(solution)/shard_map/ppermute | solution.py:460
  30.3 9.5 %collective-permute-done.refs_0_.refs_5_ = bf16[1280,640]{1,0:T(8,128)(2,1)} collective-permute-done((bf16[1280,640]{1,0:T(8,128)(2,1)}, bf16[1280,640]{1,0:T(8,128)(2,1)}, u32[]{:S(2)}, u32[]{:S(2)}) %collective-permute-start) | collective-permute-done | bytes 1638432 | tf_op jit(solution)/shard_map/ppermute | solution.py:39
  39.8 2.1 %slice.30 = bf16[640,640]{1,0:T(8,128)(2,1)} slice(bf16[1280,640]{1,0:T(8,128)(2,1)} %collective-permute-done.refs_0_.refs_5_), slice={[0:640], [0:640]} | slice | bytes 1638400 | tf_op jit(solution)/shard_map/slice | solution.py:55
  41.9 1.8 collective-permute-start.2
  43.6 2.1 %slice.31 = bf16[640,640]{1,0:T(8,128)(2,1)} slice(bf16[1280,640]{1,0:T(8,128)(2,1)} %collective-permute-done.3.refs_2_.refs_3_), slice={[640:1280], [0:640]} | slice | bytes 1638400 | tf_op jit(solution)/shard_map/slice | solution.py:55
  45.8 1.5 collective-permute-start.4
  47.3 0.7 pad_add_fusion.where
  48.4 6.1 %collective-permute-done.6.refs_0_ = bf16[512,640]{1,0:T(8,128)(2,1)} collective-permute-done((bf16[512,640]{1,0:T(8,128)(2,1)}, bf16[512,640]{1,0:T(8,128)(2,1)}, u32[]{:S(2)}, u32[]{:S(2)}) %collective-permute-start.6) | collective-permute-done | bytes 655392 | tf_op jit(solution)/shard_map/ppermute | solution.py:460
  54.6 3.4 %collective-permute-start.12 = (bf16[512,640]{1,0:T(8,128)(2,1)}, bf16[512,640]{1,0:T(8,128)(2,1)}, u32[]{:S(2)}, u32[]{:S(2)}) collective-permute-start(bf16[512,640]{1,0:T(8,128)(2,1)} %collective-permute-done.9.refs_4_), channel_id=1, source_target_pairs={{0,4},{1,5},{4,6},{5,7},{6,2},{7,3},{2,0},{3,1},{8,12},{9,13},{12,... | collective-permute-start | bytes 1966088 | tf_op jit(solution)/shard_map/ppermute | solution.py:460
  57.9 1.3 fusion.5
  59.3 2.3 %collective-permute-done.2.refs_1_ = bf16[640,640]{1,0:T(8,128)(2,1)} collective-permute-done((bf16[640,640]{1,0:T(8,128)(2,1)}, bf16[640,640]{1,0:T(8,128)(2,1)}, u32[]{:S(2)}, u32[]{:S(2)}) %collective-permute-start.2) | collective-permute-done | bytes 819232 | tf_op jit(solution)/shard_map/ppermute | solution.py:39
  61.6 1.4 collective-permute-start.16
  63.1 1.9 collective-permute-done.4.refs_4_
  64.9 8.4 %scale.2 = (bf16[5120,640]{1,0:T(8,128)(2,1)}, f32[2,8,640]{2,1,0:T(8,128)}) custom-call(s32[4]{0:T(128)} %pad_add_fusion.where, f32[8,2,640]{2,1,0:T(2,128)} %bitcast.26, bf16[1280,640]{1,0:T(8,128)(2,1)} %weight.1, bf16[1280,640]{1,0:T(8,128)(2,1)} %collective-permute-done.refs_0_.refs_5_, bf16[640,640]{1,0:T(8,128)(2,1)} %collective-permute-done.2.refs_1_, ...), custom_call_target="tpu_custom_call" | custom-call | flops 8847360000 | bytes 22937600 | tf_op jit(solution)/shard_map/scale/pallas_call | solution.py:113
  73.9 1.5 collective-permute-start.17
  76.0 4.4 %collective-permute-done.16.refs_2_ = bf16[640,640]{1,0:T(8,128)(2,1)S(1)} collective-permute-done((bf16[640,640]{1,0:T(8,128)(2,1)}, bf16[640,640]{1,0:T(8,128)(2,1)S(1)}, u32[]{:S(2)}, u32[]{:S(2)}) %collective-permute-start.16) | collective-permute-done | bytes 819232 | tf_op jit(solution)/shard_map/ppermute | solution.py:39
  80.3 1.2 collective-permute-start.23
  81.6 2.6 %collective-permute-start.13 = (bf16[512,640]{1,0:T(8,128)(2,1)}, bf16[512,640]{1,0:T(8,128)(2,1)S(1)}, u32[]{:S(2)}, u32[]{:S(2)}) collective-permute-start(bf16[512,640]{1,0:T(8,128)(2,1)} %collective-permute-done.12.refs_2_), channel_id=1, source_target_pairs={{0,4},{1,5},{4,6},{5,7},{6,2},{7,3},{2,0},{3,1},{8,12},{9,13},{12,... | collective-permute-start | bytes 1966088 | tf_op jit(solution)/shard_map/ppermute | solution.py:460
  84.2 1.6 collective-permute-start.7
  87.0 12.2 %project.3 = (f32[1024,640]{1,0:T(8,128)}, bf16[1024,5120]{1,0:T(8,128)(2,1)}, f32[1024,128]{1,0:T(8,128)}) custom-call(s32[5]{0:T(128)} %stack.55.where, f32[2]{0:T(128)} %pad_maximum_fusion.scalars, f32[2,8,640]{2,1,0:T(8,128)} %get-tuple-element.47.sums, f32[4,2,1280]{2,1,0:T(2,128)} %bitcast.27, bf16[1024,640]{1,0:T(8,128)(2,1)} %sample.5, ...), custom_call_target="tpu_custom_call" | custom-call | flops 1 | bytes 1 | tf_op jit(solution)/shard_map/project/pallas_call | solution.py:333
  99.2 9.4 %project.4 = (f32[1024,640]{1,0:T(8,128)}, bf16[1024,5120]{1,0:T(8,128)(2,1)}, f32[1024,128]{1,0:T(8,128)}) custom-call(s32[5]{0:T(128)} %stack.55.where, f32[2]{0:T(128)} %pad_maximum_fusion.scalars, f32[2,8,640]{2,1,0:T(8,128)} %get-tuple-element.47.sums, f32[4,2,1280]{2,1,0:T(2,128)} %bitcast.28, ...), custom_call_target="tpu_custom_call", output_to_operand_aliasing={{1}: (13, {})} | custom-call | flops 1 | bytes 1 | tf_op jit(solution)/shard_map/project/pallas_call | solution.py:333
  108.7 1.0 collective-permute-done.7.refs_0_
  109.7 2.2 %collective-permute-done.21.refs_0_ = bf16[640,640]{1,0:T(8,128)(2,1)} collective-permute-done((bf16[640,640]{1,0:T(8,128)(2,1)}, bf16[640,640]{1,0:T(8,128)(2,1)}, u32[]{:S(2)}, u32[]{:S(2)}) %collective-permute-start.21) | collective-permute-done | bytes 819232 | tf_op jit(solution)/shard_map/ppermute | solution.py:39
  112.4 1.4 collective-permute-start.24
  115.1 0.8 copy-done.16
  116.1 14.6 %project.5 = (f32[1024,640]{1,0:T(8,128)}, bf16[1024,5120]{1,0:T(8,128)(2,1)}, f32[1024,128]{1,0:T(8,128)}, bf16[640,1024]{1,0:T(8,128)(2,1)}, f32[640,2]{1,0:T(...) custom-call(s32[6]{0:T(128)} %concatenate.4.where, ...), custom_call_target="tpu_custom_call", output_to_operand_aliasing={{1}: (13, {})} | custom-call | flops 1 | bytes 1 | tf_op jit(solution)/shard_map/project/pallas_call | solution.py:333
  130.7 0.7 collective-permute-start.19
  131.4 1.5 collective-permute-start.20
  132.8 9.4 %outer.2 = (bf16[640,640]{1,0:T(8,128)(2,1)}, f32[640,640]{1,0:T(8,128)}, f32[640,640]{1,0:T(8,128)}, bf16[640,640]{1,0:T(8,128)(2,1)}) custom-call(s32[2]{0:T(128)} %pad_add_fusion.1.picks, f32[4,2,1280]{2,1,0:T(2,128)} %bitcast.30, f32[640,2]{1,0:T(8,128)} %get-tuple-element.65.edge, bf16[640,1024]{1,0:T(8,128)(2,1)} %get-tuple-element.84.flipped, ...), custom_call_target="tpu_custom_call" | custom-call | flops 3355443200 | bytes 11141120 | tf_op jit(solution)/shard_map/outer/pallas_call | solution.py:369
  142.2 1.5 collective-permute-start.25
  144.2 8.5 %scale.3 = (bf16[5120,640]{1,0:T(8,128)(2,1)}, f32[2,8,640]{2,1,0:T(8,128)}) custom-call(s32[4]{0:T(128)} %pad_add_fusion.where, f32[8,2,640]{2,1,0:T(2,128)} %bitcast.32, bf16[1280,640]{1,0:T(8,128)(2,1)} %weight.2, bf16[640,640]{1,0:T(8,128)(2,1)} %collective-permute-done.21.refs_0_, bf16[640,640]{1,0:T(8,128)(2,1)} %collective-permute-done.22.refs_1_, ...), custom_call_target="tpu_custom_call" | custom-call | flops 8847360000 | bytes 22937600 | tf_op jit(solution)/shard_map/scale/pallas_call | solution.py:113
  152.8 0.9 slice_reduce_fusion.3
  154.2 2.3 %add_convert_fusion = bf16[640,640]{1,0:T(8,128)(2,1)} fusion(f32[640,640]{1,0:T(8,128)S(1)} %copy-done.9, bf16[640,640]{1,0:T(8,128)(2,1)} %collective-permute-done.20), kind=kLoop, calls=%fused_computation.10 | loop fusion | flops 1228800 | bytes 3276800 | tf_op jit(solution)/shard_map/convert_element_type | solution.py:565
  157.1 1.3 add_convert_fusion.1
  158.4 1.5 collective-permute-start.30
  160.0 15.7 %multiply_reduce_fusion = (f32[640]{0:T(1024)S(1)}, f32[]{:T(128)}, f32[1024,640]{1,0:T(8,128)}) fusion(bf16[1024,640]{1,0:T(8,128)(2,1)} %param.11, f32[1024,640]{1,0:T(8,128)S(1)} %copy-done.5, f32[640]{0:T(1024)S(1)} %get-tuple-element.92, f32[640]{0:T(1024)S(1)} %get-tuple-element.91, f32[1024]{0:T(1024)S(1)} %get-tuple-element.90, ...), kind=kOutput, calls=%fused_computation.6 | convolution fusion | flops 6720716288 | bytes 26230280 | tf_op jit(solution)/shard_map/dot_general | solution.py:583
  175.7 5.4 %outer.3 = (f32[640,640]{1,0:T(8,128)}, f32[640,640]{1,0:T(8,128)}) custom-call(s32[1]{0:T(128)} %bitcast.8.picks, f32[4,2,1280]{2,1,0:T(2,128)} %bitcast.31, f32[640,2]{1,0:T(8,128)} %get-tuple-element.65.edge, bf16[640,1024]{1,0:T(8,128)(2,1)} %get-tuple-element.84.flipped, bf16[1024,5120]{1,0:T(8,128)(2,1)} %get-tuple-element.72.inputs), custom_call_target="tpu_custom_call" | custom-call | flops 1677721600 | bytes 6881280 | tf_op jit(solution)/shard_map/outer/pallas_call | solution.py:369
  182.3 2.9 %collective-permute-start.28 = (f32[1,1]{1,0:T(1,128)}, f32[1,1]{1,0:T(1,128)}, u32[]{:S(2)}, u32[]{:S(2)}) collective-permute-start(f32[1,1]{1,0:T(1,128)} %add.101), channel_id=1, source_target_pairs={{0,2},{1,3},{2,0},{3,1},{4,6},{5,7},{6,4},{7,5},{8,10},{9,11},{10,... | collective-permute-start | bytes 20 | tf_op jit(solution)/shard_map/ppermute | solution.py:594
  186.5 3.9 %collective-permute-start.29 = (f32[1,1]{1,0:T(1,128)}, f32[1,1]{1,0:T(1,128)}, u32[]{:S(2)}, u32[]{:S(2)}) collective-permute-start(f32[1,1]{1,0:T(1,128)} %add.102), channel_id=1, source_target_pairs={{0,4},{1,5},{2,6},{3,7},{4,0},{5,1},{6,2},{7,3},{8,12},{9,13},{10,... | collective-permute-start | bytes 20 | tf_op jit(solution)/shard_map/ppermute | solution.py:594
  192.3 4.4 %multiply_convert_fusion = bf16[1024,640]{1,0:T(8,128)(2,1)} fusion(f32[640]{0:T(1024)S(1)} %multiply_reduce_fusion.1, f32[1024,640]{1,0:T(8,128)} %get-tuple-element.83, f32[640]{0:T(1024)S(1)} %get-tuple-element.92, f32[1024,640]{1,0:T(8,128)} %get-tuple-element.97, f32[640]{0:T(1024)S(1)} %get-tuple-element.91, f32[1024]{0:T(1024)S(1)} %get-tuple-element.90, ...), kind=kLoop, calls=%fused_computation.7 | loop fusion | flops 4587520 | bytes 6569472 | tf_op jit(solution)/shard_map/convert_element_type | solution.py:597
  196.7 3.8 %finish.1 = f32[2,640,640]{2,1,0:T(8,128)} custom-call(f32[640,640]{1,0:T(8,128)S(1)} %copy-done, bf16[640,640]{1,0:T(8,128)(2,1)S(1)} %collective-permute-done.25.refs_1_, bf16[640,640]{1,0:T(8,128)(2,1)S(1)} %collective-permute-done.30.refs_2_, f32[640,640]{1,0:T(8,128)S(1)} %copy-done.1, bf16[640,640]{1,0:T(8,128)(2,1)S(1)} %collective-permute-done.26.refs_4_, ...), custom_call_target="tpu_custom_call" | custom-call | tf_op jit(solution)/shard_map/finish/pallas_call | solution.py:406
  (83 shorter events, 8.5 us)
Async XLA Ops:
  0.6 39.1 %collective-permute-start = (bf16[1280,640]{1,0:T(8,128)(2,1)}, bf16[1280,640]{1,0:T(8,128)(2,1)}, u32[]{:S(2)}, u32[]{:S(2)}) collective-permute-start(bf16[1280,640]{1,0:T(8,128)(2,1)} %weight.1), channel_id=1, source_target_pairs={{0,8},{8,0},{16,24},{24,16},{1,9},{9,1},{17,25},{25,17},{2,10},{10... | collective-permute-start | bytes 4915208 | tf_op jit(solution)/shard_map/ppermute | solution.py:39
  3.6 40.0 %collective-permute-start.3 = (bf16[1280,640]{1,0:T(8,128)(2,1)}, bf16[1280,640]{1,0:T(8,128)(2,1)}, u32[]{:S(2)}, u32[]{:S(2)}) collective-permute-start(bf16[1280,640]{1,0:T(8,128)(2,1)} %weight.1), channel_id=1, source_target_pairs={{0,16},{8,24},{16,0},{24,8},{1,17},{9,25},{17,1},{25,9},{2,18},{10... | collective-permute-start | bytes 4915208 | tf_op jit(solution)/shard_map/ppermute | solution.py:39
  8.1 37.7 %copy-start.3 = (bf16[1024,640]{1,0:T(8,128)(2,1)}, bf16[1024,640]{1,0:T(8,128)(2,1)S(1)}, u32[]{:S(2)}) copy-start(bf16[1024,640]{1,0:T(8,128)(2,1)S(1)} %fusion.1.refs_0_) | copy-start | bytes 3932164
  8.1 49.9 %copy-start.7 = (bf16[1280,640]{1,0:T(8,128)(2,1)S(1)}, bf16[1280,640]{1,0:T(8,128)(2,1)}, u32[]{:S(2)}) copy-start(bf16[1280,640]{1,0:T(8,128)(2,1)} %weight.2) | copy-start | bytes 4915204
  8.1 22.2 %collective-permute-start.1 = (bf16[1024,640]{1,0:T(8,128)(2,1)S(1)}, bf16[1024,640]{1,0:T(8,128)(2,1)S(1)}, u32[]{:S(2)}, u32[]{:S(2)}) collective-permute-start(bf16[1024,640]{1,0:T(8,128)(2,1)S(1)} %fusion.1.refs_0_), channel_id=1, source_target_pairs={{0,1},{1,0},{2,3},{3,2},{4,5},{5,4},{6,7},{7,6},{8,9},{9,8},{10,11... | collective-permute-start | bytes 3932168 | tf_op jit(solution)/shard_map/ppermute | solution.py:471
  9.1 17.6 %collective-permute-start.5 = (bf16[512,640]{1,0:T(8,128)(2,1)S(1)}, bf16[512,640]{1,0:T(8,128)(2,1)}, u32[]{:S(2)}, u32[]{:S(2)}) collective-permute-start(bf16[512,640]{1,0:T(8,128)(2,1)S(1)} %get-tuple-element.96), channel_id=1, source_target_pairs={{0,4},{1,5},{4,6},{5,7},{6,2},{7,3},{2,0},{3,1},{8,12},{9,13},{12,... | collective-permute-start | bytes 1966088 | tf_op jit(solution)/shard_map/ppermute | solution.py:460
  11.7 36.2 %collective-permute-start.9 = (bf16[512,640]{1,0:T(8,128)(2,1)}, bf16[512,640]{1,0:T(8,128)(2,1)}, u32[]{:S(2)}, u32[]{:S(2)}) collective-permute-start(bf16[512,640]{1,0:T(8,128)(2,1)} %get-tuple-element.95), channel_id=1, source_target_pairs={{0,4},{1,5},{4,6},{5,7},{6,2},{7,3},{2,0},{3,1},{8,12},{9,13},{12,... | collective-permute-start | bytes 1966088 | tf_op jit(solution)/shard_map/ppermute | solution.py:460
  26.8 27.8 %collective-permute-start.6 = (bf16[512,640]{1,0:T(8,128)(2,1)}, bf16[512,640]{1,0:T(8,128)(2,1)}, u32[]{:S(2)}, u32[]{:S(2)}) collective-permute-start(bf16[512,640]{1,0:T(8,128)(2,1)} %collective-permute-done.5.refs_2_), channel_id=1, source_target_pairs={{0,4},{1,5},{4,6},{5,7},{6,2},{7,3},{2,0},{3,1},{8,12},{9,13},{12,... | collective-permute-start | bytes 1966088 | tf_op jit(solution)/shard_map/ppermute | solution.py:460
  30.3 29.0 %copy-start.10 = (bf16[1024,640]{1,0:T(8,128)(2,1)}, bf16[1024,640]{1,0:T(8,128)(2,1)S(1)}, u32[]{:S(2)}) copy-start(bf16[1024,640]{1,0:T(8,128)(2,1)S(1)} %collective-permute-done.1.refs_1_) | copy-start | bytes 3932164
  41.9 19.7 %collective-permute-start.2 = (bf16[640,640]{1,0:T(8,128)(2,1)}, bf16[640,640]{1,0:T(8,128)(2,1)}, u32[]{:S(2)}, u32[]{:S(2)}) collective-permute-start(bf16[640,640]{1,0:T(8,128)(2,1)} %slice.30), channel_id=1, source_target_pairs={{0,16},{8,24},{16,0},{24,8},{1,17},{9,25},{17,1},{25,9},{2,18},{10... | collective-permute-start | bytes 2457608 | tf_op jit(solution)/shard_map/ppermute | solution.py:39
  45.8 19.1 %collective-permute-start.4 = (bf16[640,640]{1,0:T(8,128)(2,1)}, bf16[640,640]{1,0:T(8,128)(2,1)}, u32[]{:S(2)}, u32[]{:S(2)}) collective-permute-start(bf16[640,640]{1,0:T(8,128)(2,1)} %slice.31), channel_id=1, source_target_pairs={{0,8},{8,0},{16,24},{24,16},{1,9},{9,1},{17,25},{25,17},{2,10},{10... | collective-permute-start | bytes 2457608 | tf_op jit(solution)/shard_map/ppermute | solution.py:39
  47.9 27.5 %collective-permute-start.8 = (bf16[512,640]{1,0:T(8,128)(2,1)}, bf16[512,640]{1,0:T(8,128)(2,1)}, u32[]{:S(2)}, u32[]{:S(2)}) collective-permute-start(bf16[512,640]{1,0:T(8,128)(2,1)} %collective-permute-done.5.refs_2_), channel_id=1, source_target_pairs={{0,1},{1,0},{2,3},{3,2},{4,5},{5,4},{6,7},{7,6},{8,9},{9,8},{10,11... | collective-permute-start | bytes 1966088 | tf_op jit(solution)/shard_map/ppermute | solution.py:464
  47.9 26.0 %collective-permute-start.10 = (bf16[512,640]{1,0:T(8,128)(2,1)}, bf16[512,640]{1,0:T(8,128)(2,1)}, u32[]{:S(2)}, u32[]{:S(2)}) collective-permute-start(bf16[512,640]{1,0:T(8,128)(2,1)} %collective-permute-done.9.refs_4_), channel_id=1, source_target_pairs={{0,1},{1,0},{2,3},{3,2},{4,5},{5,4},{6,7},{7,6},{8,9},{9,8},{10,11... | collective-permute-start | bytes 1966088 | tf_op jit(solution)/shard_map/ppermute | solution.py:464
  54.6 18.9 %collective-permute-start.12 = (bf16[512,640]{1,0:T(8,128)(2,1)}, bf16[512,640]{1,0:T(8,128)(2,1)}, u32[]{:S(2)}, u32[]{:S(2)}) collective-permute-start(bf16[512,640]{1,0:T(8,128)(2,1)} %collective-permute-done.9.refs_4_), channel_id=1, source_target_pairs={{0,4},{1,5},{4,6},{5,7},{6,2},{7,3},{2,0},{3,1},{8,12},{9,13},{12,... | collective-permute-start | bytes 1966088 | tf_op jit(solution)/shard_map/ppermute | solution.py:460
  61.6 18.7 %collective-permute-start.16 = (bf16[640,640]{1,0:T(8,128)(2,1)}, bf16[640,640]{1,0:T(8,128)(2,1)S(1)}, u32[]{:S(2)}, u32[]{:S(2)}) collective-permute-start(bf16[640,640]{1,0:T(8,128)(2,1)} %get-tuple-element.94), channel_id=1, source_target_pairs={{0,16},{8,24},{16,0},{24,8},{1,17},{9,25},{17,1},{25,9},{2,18},{10... | collective-permute-start | bytes 2457608 | tf_op jit(solution)/shard_map/ppermute | solution.py:39
  64.9 9.0 %copy-start.11 = (bf16[640,640]{1,0:T(8,128)(2,1)S(1)}, bf16[640,640]{1,0:T(8,128)(2,1)}, u32[]{:S(2)}) copy-start(bf16[640,640]{1,0:T(8,128)(2,1)} %get-tuple-element.93) | copy-start | bytes 2457604
  73.3 8.2 %collective-permute-start.14 = (bf16[512,640]{1,0:T(8,128)(2,1)}, bf16[512,640]{1,0:T(8,128)(2,1)S(1)}, u32[]{:S(2)}, u32[]{:S(2)}) collective-permute-start(bf16[512,640]{1,0:T(8,128)(2,1)} %collective-permute-done.6.refs_0_), channel_id=1, source_target_pairs={{0,1},{1,0},{2,3},{3,2},{4,5},{5,4},{6,7},{7,6},{8,9},{9,8},{10,11... | collective-permute-start | bytes 1966088 | tf_op jit(solution)/shard_map/ppermute | solution.py:464
  73.4 10.8 %collective-permute-start.15 = (bf16[512,640]{1,0:T(8,128)(2,1)}, bf16[512,640]{1,0:T(8,128)(2,1)S(1)}, u32[]{:S(2)}, u32[]{:S(2)}) collective-permute-start(bf16[512,640]{1,0:T(8,128)(2,1)} %collective-permute-done.12.refs_2_), channel_id=1, source_target_pairs={{0,1},{1,0},{2,3},{3,2},{4,5},{5,4},{6,7},{7,6},{8,9},{9,8},{10,11... | collective-permute-start | bytes 1966088 | tf_op jit(solution)/shard_map/ppermute | solution.py:464
  73.9 34.6 %collective-permute-start.17 = (bf16[640,640]{1,0:T(8,128)(2,1)S(1)}, bf16[640,640]{1,0:T(8,128)(2,1)}, u32[]{:S(2)}, u32[]{:S(2)}) collective-permute-start(bf16[640,640]{1,0:T(8,128)(2,1)S(1)} %copy-done.11), channel_id=1, source_target_pairs={{0,8},{8,0},{16,24},{24,16},{1,9},{9,1},{17,25},{25,17},{2,10},{10... | collective-permute-start | bytes 2457608 | tf_op jit(solution)/shard_map/ppermute | solution.py:39
  75.4 36.4 %collective-permute-start.21 = (bf16[640,640]{1,0:T(8,128)(2,1)}, bf16[640,640]{1,0:T(8,128)(2,1)}, u32[]{:S(2)}, u32[]{:S(2)}) collective-permute-start(bf16[640,640]{1,0:T(8,128)(2,1)} %get-tuple-element.94), channel_id=1, source_target_pairs={{0,8},{8,0},{16,24},{24,16},{1,9},{9,1},{17,25},{25,17},{2,10},{10... | collective-permute-start | bytes 2457608 | tf_op jit(solution)/shard_map/ppermute | solution.py:39
  80.3 32.1 %collective-permute-start.23 = (bf16[640,640]{1,0:T(8,128)(2,1)S(1)}, bf16[640,640]{1,0:T(8,128)(2,1)}, u32[]{:S(2)}, u32[]{:S(2)}) collective-permute-start(bf16[640,640]{1,0:T(8,128)(2,1)S(1)} %copy-done.11), channel_id=1, source_target_pairs={{0,16},{8,24},{16,0},{24,8},{1,17},{9,25},{17,1},{25,9},{2,18},{10... | collective-permute-start | bytes 2457608 | tf_op jit(solution)/shard_map/ppermute | solution.py:39
  81.6 17.6 %copy-start.14 = (bf16[512,640]{1,0:T(8,128)(2,1)}, bf16[512,640]{1,0:T(8,128)(2,1)S(1)}, u32[]{:S(2)}) copy-start(bf16[512,640]{1,0:T(8,128)(2,1)S(1)} %collective-permute-done.14.refs_1_) | copy-start | bytes 1966084
  81.6 27.0 %collective-permute-start.13 = (bf16[512,640]{1,0:T(8,128)(2,1)}, bf16[512,640]{1,0:T(8,128)(2,1)S(1)}, u32[]{:S(2)}, u32[]{:S(2)}) collective-permute-start(bf16[512,640]{1,0:T(8,128)(2,1)} %collective-permute-done.12.refs_2_), channel_id=1, source_target_pairs={{0,4},{1,5},{4,6},{5,7},{6,2},{7,3},{2,0},{3,1},{8,12},{9,13},{12,... | collective-permute-start | bytes 1966088 | tf_op jit(solution)/shard_map/ppermute | solution.py:460
  84.2 15.0 %copy-start.15 = (bf16[512,640]{1,0:T(8,128)(2,1)}, bf16[512,640]{1,0:T(8,128)(2,1)S(1)}, u32[]{:S(2)}) copy-start(bf16[512,640]{1,0:T(8,128)(2,1)S(1)} %collective-permute-done.15.refs_3_) | copy-start | bytes 1966084
  84.2 25.4 %collective-permute-start.7 = (bf16[512,640]{1,0:T(8,128)(2,1)}, bf16[512,640]{1,0:T(8,128)(2,1)S(1)}, u32[]{:S(2)}, u32[]{:S(2)}) collective-permute-start(bf16[512,640]{1,0:T(8,128)(2,1)} %collective-permute-done.6.refs_0_), channel_id=1, source_target_pairs={{0,4},{1,5},{4,6},{5,7},{6,2},{7,3},{2,0},{3,1},{8,12},{9,13},{12,... | collective-permute-start | bytes 1966088 | tf_op jit(solution)/shard_map/ppermute | solution.py:460
  108.6 6.5 %copy-start.12 = (bf16[512,640]{1,0:T(8,128)(2,1)}, bf16[512,640]{1,0:T(8,128)(2,1)S(1)}, u32[]{:S(2)}) copy-start(bf16[512,640]{1,0:T(8,128)(2,1)S(1)} %collective-permute-done.13.refs_2_) | copy-start | bytes 1966084
  108.6 6.4 %collective-permute-start.18 = (bf16[512,640]{1,0:T(8,128)(2,1)S(1)}, bf16[512,640]{1,0:T(8,128)(2,1)S(1)}, u32[]{:S(2)}, u32[]{:S(2)}) collective-permute-start(bf16[512,640]{1,0:T(8,128)(2,1)S(1)} %collective-permute-done.13.refs_2_), channel_id=1, source_target_pairs={{0,1},{1,0},{2,3},{3,2},{4,5},{5,4},{6,7},{7,6},{8,9},{9,8},{10,11... | collective-permute-start | bytes 1966088 | tf_op jit(solution)/shard_map/ppermute | solution.py:464
  109.7 5.4 %copy-start.13 = (bf16[512,640]{1,0:T(8,128)(2,1)}, bf16[512,640]{1,0:T(8,128)(2,1)S(1)}, u32[]{:S(2)}) copy-start(bf16[512,640]{1,0:T(8,128)(2,1)S(1)} %collective-permute-done.7.refs_0_) | copy-start | bytes 1966084
  109.7 5.4 %collective-permute-start.11 = (bf16[512,640]{1,0:T(8,128)(2,1)S(1)}, bf16[512,640]{1,0:T(8,128)(2,1)S(1)}, u32[]{:S(2)}, u32[]{:S(2)}) collective-permute-start(bf16[512,640]{1,0:T(8,128)(2,1)S(1)} %collective-permute-done.7.refs_0_), channel_id=1, source_target_pairs={{0,1},{1,0},{2,3},{3,2},{4,5},{5,4},{6,7},{7,6},{8,9},{9,8},{10,11... | collective-permute-start | bytes 1966088 | tf_op jit(solution)/shard_map/ppermute | solution.py:464
  111.8 31.9 %collective-permute-start.22 = (bf16[640,640]{1,0:T(8,128)(2,1)}, bf16[640,640]{1,0:T(8,128)(2,1)}, u32[]{:S(2)}, u32[]{:S(2)}) collective-permute-start(bf16[640,640]{1,0:T(8,128)(2,1)} %collective-permute-done.21.refs_0_), channel_id=1, source_target_pairs={{0,16},{8,24},{16,0},{24,8},{1,17},{9,25},{17,1},{25,9},{2,18},{10... | collective-permute-start | bytes 2457608 | tf_op jit(solution)/shard_map/ppermute | solution.py:39
  112.4 31.8 %collective-permute-start.24 = (bf16[640,640]{1,0:T(8,128)(2,1)}, bf16[640,640]{1,0:T(8,128)(2,1)}, u32[]{:S(2)}, u32[]{:S(2)}) collective-permute-start(bf16[640,640]{1,0:T(8,128)(2,1)} %collective-permute-done.23.refs_3_), channel_id=1, source_target_pairs={{0,8},{8,0},{16,24},{24,16},{1,9},{9,1},{17,25},{25,17},{2,10},{10... | collective-permute-start | bytes 2457608 | tf_op jit(solution)/shard_map/ppermute | solution.py:39
  130.7 26.4 %collective-permute-start.19 = (bf16[640,640]{1,0:T(8,128)(2,1)}, bf16[640,640]{1,0:T(8,128)(2,1)}, u32[]{:S(2)}, u32[]{:S(2)}) collective-permute-start(bf16[640,640]{1,0:T(8,128)(2,1)} %get-tuple-element.67), channel_id=1, source_target_pairs={{0,8},{8,0},{16,24},{24,16},{1,9},{9,1},{17,25},{25,17},{2,10},{10... | collective-permute-start | bytes 2457608 | tf_op jit(solution)/shard_map/ppermute | solution.py:39
  131.4 22.8 %collective-permute-start.20 = (bf16[640,640]{1,0:T(8,128)(2,1)}, bf16[640,640]{1,0:T(8,128)(2,1)}, u32[]{:S(2)}, u32[]{:S(2)}) collective-permute-start(bf16[640,640]{1,0:T(8,128)(2,1)} %get-tuple-element.68), channel_id=1, source_target_pairs={{0,16},{8,24},{16,0},{24,8},{1,17},{9,25},{17,1},{25,9},{2,18},{10... | collective-permute-start | bytes 2457608 | tf_op jit(solution)/shard_map/ppermute | solution.py:39
  142.2 33.4 %collective-permute-start.25 = (bf16[640,640]{1,0:T(8,128)(2,1)}, bf16[640,640]{1,0:T(8,128)(2,1)S(1)}, u32[]{:S(2)}, u32[]{:S(2)}) collective-permute-start(bf16[640,640]{1,0:T(8,128)(2,1)} %get-tuple-element.73), channel_id=1, source_target_pairs={{0,8},{8,0},{16,24},{24,16},{1,9},{9,1},{17,25},{25,17},{2,10},{10... | collective-permute-start | bytes 2457608 | tf_op jit(solution)/shard_map/ppermute | solution.py:39
  143.7 32.0 %collective-permute-start.26 = (bf16[640,640]{1,0:T(8,128)(2,1)}, bf16[640,640]{1,0:T(8,128)(2,1)S(1)}, u32[]{:S(2)}, u32[]{:S(2)}) collective-permute-start(bf16[640,640]{1,0:T(8,128)(2,1)} %get-tuple-element.74), channel_id=1, source_target_pairs={{0,16},{8,24},{16,0},{24,8},{1,17},{9,25},{17,1},{25,9},{2,18},{10... | collective-permute-start | bytes 2457608 | tf_op jit(solution)/shard_map/ppermute | solution.py:39
  144.2 9.4 %copy-start.6 = (f32[1024,128]{1,0:T(8,128)S(1)}, f32[1024,128]{1,0:T(8,128)}, u32[]{:S(2)}) copy-start(f32[1024,128]{1,0:T(8,128)} %get-tuple-element.63) | copy-start | bytes 1572868
  144.2 10.0 %copy-start.9 = (f32[640,640]{1,0:T(8,128)S(1)}, f32[640,640]{1,0:T(8,128)}, u32[]{:S(2)}) copy-start(f32[640,640]{1,0:T(8,128)} %get-tuple-element.71) | copy-start | bytes 4915204
  154.2 5.8 %copy-start.2 = (bf16[1024,640]{1,0:T(8,128)(2,1)S(1)}, bf16[1024,640]{1,0:T(8,128)(2,1)}, u32[]{:S(2)}) copy-start(bf16[1024,640]{1,0:T(8,128)(2,1)} %sample.5) | copy-start | bytes 3932164
  154.2 5.8 %copy-start.4 = (bf16[1024,640]{1,0:T(8,128)(2,1)S(1)}, bf16[1024,640]{1,0:T(8,128)(2,1)}, u32[]{:S(2)}) copy-start(bf16[1024,640]{1,0:T(8,128)(2,1)} %copy-done.3) | copy-start | bytes 3932164
  154.2 5.8 %copy-start.5 = (f32[1024,640]{1,0:T(8,128)S(1)}, f32[1024,640]{1,0:T(8,128)}, u32[]{:S(2)}) copy-start(f32[1024,640]{1,0:T(8,128)} %get-tuple-element.83) | copy-start | bytes 7864324
  156.5 40.2 %collective-permute-start.31 = (bf16[640,640]{1,0:T(8,128)(2,1)}, bf16[640,640]{1,0:T(8,128)(2,1)S(1)}, u32[]{:S(2)}, u32[]{:S(2)}) collective-permute-start(bf16[640,640]{1,0:T(8,128)(2,1)} %add_convert_fusion), channel_id=1, source_target_pairs={{0,8},{8,0},{16,24},{24,16},{1,9},{9,1},{17,25},{25,17},{2,10},{10... | collective-permute-start | bytes 2457608 | tf_op jit(solution)/shard_map/ppermute | solution.py:39
  158.4 38.3 %collective-permute-start.30 = (bf16[640,640]{1,0:T(8,128)(2,1)S(1)}, bf16[640,640]{1,0:T(8,128)(2,1)S(1)}, u32[]{:S(2)}, u32[]{:S(2)}) collective-permute-start(bf16[640,640]{1,0:T(8,128)(2,1)S(1)} %add_convert_fusion.1), channel_id=1, source_target_pairs={{0,16},{8,24},{16,0},{24,8},{1,17},{9,25},{17,1},{25,9},{2,18},{10... | collective-permute-start | bytes 2457608 | tf_op jit(solution)/shard_map/ppermute | solution.py:39
  175.7 16.6 %copy-start.18 = (f32[1,640]{1,0:T(1,128)S(1)}, f32[1,640]{1,0:T(1,128)}, u32[]{:S(2)}) copy-start(f32[1,640]{1,0:T(1,128)} %param.17) | copy-start | bytes 7684
  175.7 5.4 %collective-permute-start.27 = (f32[1,1]{1,0:T(1,128)}, f32[1,1]{1,0:T(1,128)}, u32[]{:S(2)}, u32[]{:S(2)}) collective-permute-start(f32[1,1]{1,0:T(1,128)} %bitcast.18), channel_id=1, source_target_pairs={{0,1},{1,0},{2,3},{3,2},{4,5},{5,4},{6,7},{7,6},{8,9},{9,8},{10,11... | collective-permute-start | bytes 20 | tf_op jit(solution)/shard_map/ppermute | solution.py:594
  182.3 3.6 %collective-permute-start.28 = (f32[1,1]{1,0:T(1,128)}, f32[1,1]{1,0:T(1,128)}, u32[]{:S(2)}, u32[]{:S(2)}) collective-permute-start(f32[1,1]{1,0:T(1,128)} %add.101), channel_id=1, source_target_pairs={{0,2},{1,3},{2,0},{3,1},{4,6},{5,7},{6,4},{7,5},{8,10},{9,11},{10,... | collective-permute-start | bytes 20 | tf_op jit(solution)/shard_map/ppermute | solution.py:594
  186.5 4.5 %collective-permute-start.29 = (f32[1,1]{1,0:T(1,128)}, f32[1,1]{1,0:T(1,128)}, u32[]{:S(2)}, u32[]{:S(2)}) collective-permute-start(f32[1,1]{1,0:T(1,128)} %add.102), channel_id=1, source_target_pairs={{0,4},{1,5},{2,6},{3,7},{4,0},{5,1},{6,2},{7,3},{8,12},{9,13},{10,... | collective-permute-start | bytes 20 | tf_op jit(solution)/shard_map/ppermute | solution.py:594
  192.3 4.4 %copy-start = (f32[640,640]{1,0:T(8,128)S(1)}, f32[640,640]{1,0:T(8,128)}, u32[]{:S(2)}) copy-start(f32[640,640]{1,0:T(8,128)} %get-tuple-element.85.refs_0_) | copy-start | bytes 4915204
  192.3 4.4 %copy-start.1 = (f32[640,640]{1,0:T(8,128)S(1)}, f32[640,640]{1,0:T(8,128)}, u32[]{:S(2)}) copy-start(f32[640,640]{1,0:T(8,128)} %get-tuple-element.86.refs_3_) | copy-start | bytes 4915204
  (4 other events, 7.5 us)

commit v9 on v8

--- a/solution.py
+++ b/solution.py
@@ -19,7 +19,7 @@
     "B2": ("A2",),
     "cB2": ("far0", "far1"),
     "cA3": ("soon",),
-    "teacher relay": ("sums",),
+    "teacher relay": ("cA2",),
     "cA2": ("sums",),
     "cB1": ("far0", "far1"),
     "B3": ("sums",),

time: 201 us -> 202 us (level)
  starting transfers between devices: 44.1 us -> 46.4 us
  waiting for transfers between devices: 42 us -> 39.9 us
  transfers between devices with their start and end apart: 32 -> 32, of which waited for: 10 -> 9; matrix products, arithmetic and copies ran while one was open for 19% -> 19% of each run, Pallas kernels for 34% -> 34%
where the time goes in v9:
time: 202 us
  Pallas kernels  71.7 us (35%)
  starting transfers between devices  46.4 us (23%)
  waiting for transfers between devices  39.9 us (20%)
  matrix products  15.5 us (8%)
  other arithmetic  13.4 us (7%)
  local copies, waits for them, and re-layouts  10.8 us (5%)
  between operations  4 us (2%)
    pallas_call x3, Pallas kernels, project(): pl.pallas_call(functools.partial(project_kernel, prior, last, plan, core_...  36.2 us
    ppermute x16, starting transfers between devices, swap_clip(): return lax.ppermute(value, 'clip', [(i, i ^ bit) for i in range(count)])  22 us
    ppermute x6, waiting for transfers between devices, hop_to(): seen[name] = lax.ppermute(gated(name, source), 'fsdp', ring)  19.6 us
    ppermute x16, waiting for transfers between devices, swap_clip(): return lax.ppermute(value, 'clip', [(i, i ^ bit) for i in range(count)])  18.8 us
    pallas_call x2, Pallas kernels, scale(): pl.pallas_call(functools.partial(scale_kernel, list(blocks)), out_shape=(...  16.9 us
    ppermute x6, starting transfers between devices, hop_to(): seen[name] = lax.ppermute(gated(name, source), 'fsdp', ring)  15.8 us
    dot_general x1, matrix products, per_device(): velocity = jnp.dot(left, scaled, preferred_element_type=F32)  15.5 us
    pallas_call x2, Pallas kernels, outer(): pl.pallas_call(outer_kernel, out_shape=[jax.ShapeDtypeStruct((cols, cols)...  14.8 us
  transfers between devices with their start and end apart: 32, of which 9 were waited for; matrix products, arithmetic and copies ran while one was open for 19% of the time, Pallas kernels for 34%

profile of v9, /device:TPU:0, one launch (start us, length us, event | category | flops | bytes accessed | tf_op | source)
XLA Modules:
  0.0 201.6 jit_solution(5524566825436054187)
XLA Ops:
  0.6 3.0 %collective-permute-start = (bf16[1280,640]{1,0:T(8,128)(2,1)}, bf16[1280,640]{1,0:T(8,128)(2,1)}, u32[]{:S(2)}, u32[]{:S(2)}) collective-permute-start(bf16[1280,640]{1,0:T(8,128)(2,1)} %weight.1), channel_id=1, source_target_pairs={{0,8},{8,0},{16,24},{24,16},{1,9},{9,1},{17,25},{25,17},{2,10},{10... | collective-permute-start | bytes 4915208 | tf_op jit(solution)/shard_map/ppermute | solution.py:39
  3.6 1.5 collective-permute-start.3
  5.8 2.2 %fusion.1.refs_0_ = bf16[1024,640]{1,0:T(8,128)(2,1)S(1)} fusion(bf16[1024,640]{1,0:T(8,128)(2,1)} %sample.5, bf16[1024,640]{1,0:T(8,128)(2,1)} %other.5, f32[]{:T(128)} %bitcast.1, f32[]{:T(128)S(6)} %sub.47), kind=kLoop, calls=%fused_computation.3 | loop fusion | flops 3932160 | bytes 3932168 | tf_op jit(solution)/shard_map/convert_element_type | solution.py:434
  8.2 1.0 fusion.6
  9.1 2.6 %collective-permute-start.5 = (bf16[512,640]{1,0:T(8,128)(2,1)S(1)}, bf16[512,640]{1,0:T(8,128)(2,1)}, u32[]{:S(2)}, u32[]{:S(2)}) collective-permute-start(bf16[512,640]{1,0:T(8,128)(2,1)S(1)} %get-tuple-element.96), channel_id=1, source_target_pairs={{0,4},{1,5},{4,6},{5,7},{6,2},{7,3},{2,0},{3,1},{8,12},{9,13},{12,... | collective-permute-start | bytes 1966088 | tf_op jit(solution)/shard_map/ppermute | solution.py:460
  11.7 1.6 collective-permute-start.9
  13.3 13.5 %collective-permute-done.5.refs_2_ = bf16[512,640]{1,0:T(8,128)(2,1)} collective-permute-done((bf16[512,640]{1,0:T(8,128)(2,1)S(1)}, bf16[512,640]{1,0:T(8,128)(2,1)}, u32[]{:S(2)}, u32[]{:S(2)}) %collective-permute-start.5) | collective-permute-done | bytes 655392 | tf_op jit(solution)/shard_map/ppermute | solution.py:460
  26.8 3.5 %collective-permute-start.6 = (bf16[512,640]{1,0:T(8,128)(2,1)}, bf16[512,640]{1,0:T(8,128)(2,1)}, u32[]{:S(2)}, u32[]{:S(2)}) collective-permute-start(bf16[512,640]{1,0:T(8,128)(2,1)} %collective-permute-done.5.refs_2_), channel_id=1, source_target_pairs={{0,4},{1,5},{4,6},{5,7},{6,2},{7,3},{2,0},{3,1},{8,12},{9,13},{12,... | collective-permute-start | bytes 1966088 | tf_op jit(solution)/shard_map/ppermute | solution.py:460
  30.3 9.5 %collective-permute-done.refs_0_.refs_5_ = bf16[1280,640]{1,0:T(8,128)(2,1)} collective-permute-done((bf16[1280,640]{1,0:T(8,128)(2,1)}, bf16[1280,640]{1,0:T(8,128)(2,1)}, u32[]{:S(2)}, u32[]{:S(2)}) %collective-permute-start) | collective-permute-done | bytes 1638432 | tf_op jit(solution)/shard_map/ppermute | solution.py:39
  39.8 2.1 %slice.30 = bf16[640,640]{1,0:T(8,128)(2,1)} slice(bf16[1280,640]{1,0:T(8,128)(2,1)} %collective-permute-done.refs_0_.refs_5_), slice={[0:640], [0:640]} | slice | bytes 1638400 | tf_op jit(solution)/shard_map/slice | solution.py:55
  41.9 1.8 collective-permute-start.2
  43.6 2.1 %slice.31 = bf16[640,640]{1,0:T(8,128)(2,1)} slice(bf16[1280,640]{1,0:T(8,128)(2,1)} %collective-permute-done.3.refs_2_.refs_3_), slice={[640:1280], [0:640]} | slice | bytes 1638400 | tf_op jit(solution)/shard_map/slice | solution.py:55
  45.7 1.5 collective-permute-start.4
  48.4 6.1 %collective-permute-done.6.refs_0_ = bf16[512,640]{1,0:T(8,128)(2,1)} collective-permute-done((bf16[512,640]{1,0:T(8,128)(2,1)}, bf16[512,640]{1,0:T(8,128)(2,1)}, u32[]{:S(2)}, u32[]{:S(2)}) %collective-permute-start.6) | collective-permute-done | bytes 655392 | tf_op jit(solution)/shard_map/ppermute | solution.py:460
  54.6 3.4 %collective-permute-start.12 = (bf16[512,640]{1,0:T(8,128)(2,1)}, bf16[512,640]{1,0:T(8,128)(2,1)}, u32[]{:S(2)}, u32[]{:S(2)}) collective-permute-start(bf16[512,640]{1,0:T(8,128)(2,1)} %collective-permute-done.9.refs_4_), channel_id=1, source_target_pairs={{0,4},{1,5},{4,6},{5,7},{6,2},{7,3},{2,0},{3,1},{8,12},{9,13},{12,... | collective-permute-start | bytes 1966088 | tf_op jit(solution)/shard_map/ppermute | solution.py:460
  58.0 1.4 fusion.5
  59.3 2.3 %collective-permute-done.2.refs_1_ = bf16[640,640]{1,0:T(8,128)(2,1)} collective-permute-done((bf16[640,640]{1,0:T(8,128)(2,1)}, bf16[640,640]{1,0:T(8,128)(2,1)}, u32[]{:S(2)}, u32[]{:S(2)}) %collective-permute-start.2) | collective-permute-done | bytes 819232 | tf_op jit(solution)/shard_map/ppermute | solution.py:39
  61.6 1.4 collective-permute-start.16
  63.1 1.8 collective-permute-done.4.refs_4_
  64.9 8.4 %scale.2 = (bf16[5120,640]{1,0:T(8,128)(2,1)}, f32[2,8,640]{2,1,0:T(8,128)}) custom-call(s32[4]{0:T(128)} %pad_add_fusion.where, f32[8,2,640]{2,1,0:T(2,128)} %bitcast.26, bf16[1280,640]{1,0:T(8,128)(2,1)} %weight.1, bf16[1280,640]{1,0:T(8,128)(2,1)} %collective-permute-done.refs_0_.refs_5_, bf16[640,640]{1,0:T(8,128)(2,1)} %collective-permute-done.2.refs_1_, ...), custom_call_target="tpu_custom_call" | custom-call | flops 8847360000 | bytes 22937600 | tf_op jit(solution)/shard_map/scale/pallas_call | solution.py:113
  73.9 1.5 collective-permute-start.17
  75.4 2.6 %collective-permute-start.13 = (bf16[512,640]{1,0:T(8,128)(2,1)}, bf16[512,640]{1,0:T(8,128)(2,1)S(1)}, u32[]{:S(2)}, u32[]{:S(2)}) collective-permute-start(bf16[512,640]{1,0:T(8,128)(2,1)} %collective-permute-done.12.refs_2_), channel_id=1, source_target_pairs={{0,4},{1,5},{4,6},{5,7},{6,2},{7,3},{2,0},{3,1},{8,12},{9,13},{12,... | collective-permute-start | bytes 1966088 | tf_op jit(solution)/shard_map/ppermute | solution.py:460
  78.0 2.4 %collective-permute-done.16.refs_2_ = bf16[640,640]{1,0:T(8,128)(2,1)} collective-permute-done((bf16[640,640]{1,0:T(8,128)(2,1)}, bf16[640,640]{1,0:T(8,128)(2,1)}, u32[]{:S(2)}, u32[]{:S(2)}) %collective-permute-start.16) | collective-permute-done | bytes 819232 | tf_op jit(solution)/shard_map/ppermute | solution.py:39
  80.4 2.2 %collective-permute-start.7 = (bf16[512,640]{1,0:T(8,128)(2,1)}, bf16[512,640]{1,0:T(8,128)(2,1)S(1)}, u32[]{:S(2)}, u32[]{:S(2)}) collective-permute-start(bf16[512,640]{1,0:T(8,128)(2,1)} %collective-permute-done.6.refs_0_), channel_id=1, source_target_pairs={{0,4},{1,5},{4,6},{5,7},{6,2},{7,3},{2,0},{3,1},{8,12},{9,13},{12,... | collective-permute-start | bytes 1966088 | tf_op jit(solution)/shard_map/ppermute | solution.py:460
  82.6 1.5 collective-permute-start.21
  84.1 1.5 collective-permute-start.23
  85.7 0.7 stack.55.where
  86.9 12.2 %project.3 = (f32[1024,640]{1,0:T(8,128)}, bf16[1024,5120]{1,0:T(8,128)(2,1)}, f32[1024,128]{1,0:T(8,128)}) custom-call(s32[5]{0:T(128)} %stack.55.where, f32[2]{0:T(128)} %pad_maximum_fusion.scalars, f32[2,8,640]{2,1,0:T(8,128)} %get-tuple-element.47.sums, f32[4,2,1280]{2,1,0:T(2,128)} %bitcast.27, bf16[1024,640]{1,0:T(8,128)(2,1)} %sample.5, ...), custom_call_target="tpu_custom_call" | custom-call | flops 1 | bytes 1 | tf_op jit(solution)/shard_map/project/pallas_call | solution.py:333
  99.1 9.4 %project.4 = (f32[1024,640]{1,0:T(8,128)}, bf16[1024,5120]{1,0:T(8,128)(2,1)}, f32[1024,128]{1,0:T(8,128)}) custom-call(s32[5]{0:T(128)} %stack.55.where, f32[2]{0:T(128)} %pad_maximum_fusion.scalars, f32[2,8,640]{2,1,0:T(8,128)} %get-tuple-element.47.sums, f32[4,2,1280]{2,1,0:T(2,128)} %bitcast.28, ...), custom_call_target="tpu_custom_call", output_to_operand_aliasing={{1}: (13, {})} | custom-call | flops 1 | bytes 1 | tf_op jit(solution)/shard_map/project/pallas_call | solution.py:333
  109.1 2.7 %collective-permute-done.21.refs_0_ = bf16[640,640]{1,0:T(8,128)(2,1)} collective-permute-done((bf16[640,640]{1,0:T(8,128)(2,1)}, bf16[640,640]{1,0:T(8,128)(2,1)}, u32[]{:S(2)}, u32[]{:S(2)}) %collective-permute-start.21) | collective-permute-done | bytes 819232 | tf_op jit(solution)/shard_map/ppermute | solution.py:39
  112.4 1.4 collective-permute-start.24
  115.1 0.8 copy-done.15
  116.1 14.6 %project.5 = (f32[1024,640]{1,0:T(8,128)}, bf16[1024,5120]{1,0:T(8,128)(2,1)}, f32[1024,128]{1,0:T(8,128)}, bf16[640,1024]{1,0:T(8,128)(2,1)}, f32[640,2]{1,0:T(...) custom-call(s32[6]{0:T(128)} %concatenate.4.where, ...), custom_call_target="tpu_custom_call", output_to_operand_aliasing={{1}: (13, {})} | custom-call | flops 1 | bytes 1 | tf_op jit(solution)/shard_map/project/pallas_call | solution.py:333
  131.4 1.5 collective-permute-start.20
  132.9 9.5 %outer.2 = (bf16[640,640]{1,0:T(8,128)(2,1)}, f32[640,640]{1,0:T(8,128)}, f32[640,640]{1,0:T(8,128)}, bf16[640,640]{1,0:T(8,128)(2,1)}) custom-call(s32[2]{0:T(128)} %pad_add_fusion.1.picks, f32[4,2,1280]{2,1,0:T(2,128)} %bitcast.30, f32[640,2]{1,0:T(8,128)} %get-tuple-element.65.edge, bf16[640,1024]{1,0:T(8,128)(2,1)} %get-tuple-element.84.flipped, ...), custom_call_target="tpu_custom_call" | custom-call | flops 3355443200 | bytes 11141120 | tf_op jit(solution)/shard_map/outer/pallas_call | solution.py:369
  142.4 1.5 collective-permute-start.25
  144.9 8.5 %scale.3 = (bf16[5120,640]{1,0:T(8,128)(2,1)}, f32[2,8,640]{2,1,0:T(8,128)}) custom-call(s32[4]{0:T(128)} %pad_add_fusion.where, f32[8,2,640]{2,1,0:T(2,128)} %bitcast.32, bf16[1280,640]{1,0:T(8,128)(2,1)} %weight.2, bf16[640,640]{1,0:T(8,128)(2,1)} %collective-permute-done.21.refs_0_, bf16[640,640]{1,0:T(8,128)(2,1)} %collective-permute-done.22.refs_1_, ...), custom_call_target="tpu_custom_call" | custom-call | flops 8847360000 | bytes 22937600 | tf_op jit(solution)/shard_map/scale/pallas_call | solution.py:113
  153.4 0.8 slice_reduce_fusion.3
  154.2 2.6 %add_convert_fusion = bf16[640,640]{1,0:T(8,128)(2,1)} fusion(f32[640,640]{1,0:T(8,128)} %get-tuple-element.71, bf16[640,640]{1,0:T(8,128)(2,1)S(1)} %collective-permute-done.20), kind=kLoop, calls=%fused_computation.10 | loop fusion | flops 1228800 | bytes 3276800 | tf_op jit(solution)/shard_map/convert_element_type | solution.py:565
  157.4 2.2 %add_convert_fusion.1 = bf16[640,640]{1,0:T(8,128)(2,1)} fusion(f32[640,640]{1,0:T(8,128)S(1)} %copy-done.8, bf16[640,640]{1,0:T(8,128)(2,1)} %collective-permute-done.19), kind=kLoop, calls=%fused_computation.11 | loop fusion | flops 1228800 | bytes 3276800 | tf_op jit(solution)/shard_map/convert_element_type | solution.py:565
  159.7 1.5 collective-permute-start.30
  161.2 15.5 %multiply_reduce_fusion = (f32[640]{0:T(1024)S(1)}, f32[]{:T(128)}, f32[1024,640]{1,0:T(8,128)}) fusion(bf16[1024,640]{1,0:T(8,128)(2,1)S(1)} %copy-done.18, f32[1024,640]{1,0:T(8,128)S(1)} %copy-done.5, f32[640]{0:T(1024)S(1)} %get-tuple-element.92, f32[640]{0:T(1024)S(1)} %get-tuple-element.91, f32[1024]{0:T(1024)S(1)} %get-tuple-element.90, ...), kind=kOutput, calls=%fused_computation.6 | convolution fusion | flops 6720716288 | bytes 26230280 | tf_op jit(solution)/shard_map/dot_general | solution.py:583
  176.7 5.4 %outer.3 = (f32[640,640]{1,0:T(8,128)}, f32[640,640]{1,0:T(8,128)}) custom-call(s32[1]{0:T(128)} %bitcast.8.picks, f32[4,2,1280]{2,1,0:T(2,128)} %bitcast.31, f32[640,2]{1,0:T(8,128)} %get-tuple-element.65.edge, bf16[640,1024]{1,0:T(8,128)(2,1)} %get-tuple-element.84.flipped, bf16[1024,5120]{1,0:T(8,128)(2,1)} %get-tuple-element.72.inputs), custom_call_target="tpu_custom_call" | custom-call | flops 1677721600 | bytes 6881280 | tf_op jit(solution)/shard_map/outer/pallas_call | solution.py:369
  183.3 2.9 %collective-permute-start.28 = (f32[1,1]{1,0:T(1,128)}, f32[1,1]{1,0:T(1,128)}, u32[]{:S(2)}, u32[]{:S(2)}) collective-permute-start(f32[1,1]{1,0:T(1,128)} %add.101), channel_id=1, source_target_pairs={{0,2},{1,3},{2,0},{3,1},{4,6},{5,7},{6,4},{7,5},{8,10},{9,11},{10,... | collective-permute-start | bytes 20 | tf_op jit(solution)/shard_map/ppermute | solution.py:594
  186.2 0.8 collective-permute-done.28
  187.6 3.9 %collective-permute-start.29 = (f32[1,1]{1,0:T(1,128)}, f32[1,1]{1,0:T(1,128)}, u32[]{:S(2)}, u32[]{:S(2)}) collective-permute-start(f32[1,1]{1,0:T(1,128)} %add.102), channel_id=1, source_target_pairs={{0,4},{1,5},{2,6},{3,7},{4,0},{5,1},{6,2},{7,3},{8,12},{9,13},{10,... | collective-permute-start | bytes 20 | tf_op jit(solution)/shard_map/ppermute | solution.py:594
  193.4 4.4 %multiply_convert_fusion = bf16[1024,640]{1,0:T(8,128)(2,1)} fusion(f32[640]{0:T(1024)S(1)} %multiply_reduce_fusion.1, f32[1024,640]{1,0:T(8,128)} %get-tuple-element.83, f32[640]{0:T(1024)S(1)} %get-tuple-element.92, f32[1024,640]{1,0:T(8,128)} %get-tuple-element.97, f32[640]{0:T(1024)S(1)} %get-tuple-element.91, f32[1024]{0:T(1024)S(1)} %get-tuple-element.90, ...), kind=kLoop, calls=%fused_computation.7 | loop fusion | flops 4587520 | bytes 6569472 | tf_op jit(solution)/shard_map/convert_element_type | solution.py:597
  197.8 3.8 %finish.1 = f32[2,640,640]{2,1,0:T(8,128)} custom-call(f32[640,640]{1,0:T(8,128)S(1)} %copy-done, bf16[640,640]{1,0:T(8,128)(2,1)S(1)} %collective-permute-done.25.refs_1_, bf16[640,640]{1,0:T(8,128)(2,1)S(1)} %collective-permute-done.30.refs_2_, f32[640,640]{1,0:T(8,128)S(1)} %copy-done.1, bf16[640,640]{1,0:T(8,128)(2,1)S(1)} %collective-permute-done.26.refs_4_, ...), custom_call_target="tpu_custom_call" | custom-call | tf_op jit(solution)/shard_map/finish/pallas_call | solution.py:406
  (81 shorter events, 8.7 us)
Async XLA Ops:
  0.6 39.1 %collective-permute-start = (bf16[1280,640]{1,0:T(8,128)(2,1)}, bf16[1280,640]{1,0:T(8,128)(2,1)}, u32[]{:S(2)}, u32[]{:S(2)}) collective-permute-start(bf16[1280,640]{1,0:T(8,128)(2,1)} %weight.1), channel_id=1, source_target_pairs={{0,8},{8,0},{16,24},{24,16},{1,9},{9,1},{17,25},{25,17},{2,10},{10... | collective-permute-start | bytes 4915208 | tf_op jit(solution)/shard_map/ppermute | solution.py:39
  3.6 40.0 %collective-permute-start.3 = (bf16[1280,640]{1,0:T(8,128)(2,1)}, bf16[1280,640]{1,0:T(8,128)(2,1)}, u32[]{:S(2)}, u32[]{:S(2)}) collective-permute-start(bf16[1280,640]{1,0:T(8,128)(2,1)} %weight.1), channel_id=1, source_target_pairs={{0,16},{8,24},{16,0},{24,8},{1,17},{9,25},{17,1},{25,9},{2,18},{10... | collective-permute-start | bytes 4915208 | tf_op jit(solution)/shard_map/ppermute | solution.py:39
  8.1 37.7 %copy-start.3 = (bf16[1024,640]{1,0:T(8,128)(2,1)}, bf16[1024,640]{1,0:T(8,128)(2,1)S(1)}, u32[]{:S(2)}) copy-start(bf16[1024,640]{1,0:T(8,128)(2,1)S(1)} %fusion.1.refs_0_) | copy-start | bytes 3932164
  8.1 49.9 %copy-start.7 = (bf16[1280,640]{1,0:T(8,128)(2,1)S(1)}, bf16[1280,640]{1,0:T(8,128)(2,1)}, u32[]{:S(2)}) copy-start(bf16[1280,640]{1,0:T(8,128)(2,1)} %weight.2) | copy-start | bytes 4915204
  8.1 22.2 %collective-permute-start.1 = (bf16[1024,640]{1,0:T(8,128)(2,1)S(1)}, bf16[1024,640]{1,0:T(8,128)(2,1)S(1)}, u32[]{:S(2)}, u32[]{:S(2)}) collective-permute-start(bf16[1024,640]{1,0:T(8,128)(2,1)S(1)} %fusion.1.refs_0_), channel_id=1, source_target_pairs={{0,1},{1,0},{2,3},{3,2},{4,5},{5,4},{6,7},{7,6},{8,9},{9,8},{10,11... | collective-permute-start | bytes 3932168 | tf_op jit(solution)/shard_map/ppermute | solution.py:471
  9.1 17.6 %collective-permute-start.5 = (bf16[512,640]{1,0:T(8,128)(2,1)S(1)}, bf16[512,640]{1,0:T(8,128)(2,1)}, u32[]{:S(2)}, u32[]{:S(2)}) collective-permute-start(bf16[512,640]{1,0:T(8,128)(2,1)S(1)} %get-tuple-element.96), channel_id=1, source_target_pairs={{0,4},{1,5},{4,6},{5,7},{6,2},{7,3},{2,0},{3,1},{8,12},{9,13},{12,... | collective-permute-start | bytes 1966088 | tf_op jit(solution)/shard_map/ppermute | solution.py:460
  11.7 36.2 %collective-permute-start.9 = (bf16[512,640]{1,0:T(8,128)(2,1)}, bf16[512,640]{1,0:T(8,128)(2,1)}, u32[]{:S(2)}, u32[]{:S(2)}) collective-permute-start(bf16[512,640]{1,0:T(8,128)(2,1)} %get-tuple-element.95), channel_id=1, source_target_pairs={{0,4},{1,5},{4,6},{5,7},{6,2},{7,3},{2,0},{3,1},{8,12},{9,13},{12,... | collective-permute-start | bytes 1966088 | tf_op jit(solution)/shard_map/ppermute | solution.py:460
  26.8 27.8 %collective-permute-start.6 = (bf16[512,640]{1,0:T(8,128)(2,1)}, bf16[512,640]{1,0:T(8,128)(2,1)}, u32[]{:S(2)}, u32[]{:S(2)}) collective-permute-start(bf16[512,640]{1,0:T(8,128)(2,1)} %collective-permute-done.5.refs_2_), channel_id=1, source_target_pairs={{0,4},{1,5},{4,6},{5,7},{6,2},{7,3},{2,0},{3,1},{8,12},{9,13},{12,... | collective-permute-start | bytes 1966088 | tf_op jit(solution)/shard_map/ppermute | solution.py:460
  30.3 29.1 %copy-start.9 = (bf16[1024,640]{1,0:T(8,128)(2,1)}, bf16[1024,640]{1,0:T(8,128)(2,1)S(1)}, u32[]{:S(2)}) copy-start(bf16[1024,640]{1,0:T(8,128)(2,1)S(1)} %collective-permute-done.1.refs_1_) | copy-start | bytes 3932164
  41.9 19.7 %collective-permute-start.2 = (bf16[640,640]{1,0:T(8,128)(2,1)}, bf16[640,640]{1,0:T(8,128)(2,1)}, u32[]{:S(2)}, u32[]{:S(2)}) collective-permute-start(bf16[640,640]{1,0:T(8,128)(2,1)} %slice.30), channel_id=1, source_target_pairs={{0,16},{8,24},{16,0},{24,8},{1,17},{9,25},{17,1},{25,9},{2,18},{10... | collective-permute-start | bytes 2457608 | tf_op jit(solution)/shard_map/ppermute | solution.py:39
  45.7 19.1 %collective-permute-start.4 = (bf16[640,640]{1,0:T(8,128)(2,1)}, bf16[640,640]{1,0:T(8,128)(2,1)}, u32[]{:S(2)}, u32[]{:S(2)}) collective-permute-start(bf16[640,640]{1,0:T(8,128)(2,1)} %slice.31), channel_id=1, source_target_pairs={{0,8},{8,0},{16,24},{24,16},{1,9},{9,1},{17,25},{25,17},{2,10},{10... | collective-permute-start | bytes 2457608 | tf_op jit(solution)/shard_map/ppermute | solution.py:39
  47.9 27.5 %collective-permute-start.8 = (bf16[512,640]{1,0:T(8,128)(2,1)}, bf16[512,640]{1,0:T(8,128)(2,1)}, u32[]{:S(2)}, u32[]{:S(2)}) collective-permute-start(bf16[512,640]{1,0:T(8,128)(2,1)} %collective-permute-done.5.refs_2_), channel_id=1, source_target_pairs={{0,1},{1,0},{2,3},{3,2},{4,5},{5,4},{6,7},{7,6},{8,9},{9,8},{10,11... | collective-permute-start | bytes 1966088 | tf_op jit(solution)/shard_map/ppermute | solution.py:464
  47.9 26.0 %collective-permute-start.10 = (bf16[512,640]{1,0:T(8,128)(2,1)}, bf16[512,640]{1,0:T(8,128)(2,1)}, u32[]{:S(2)}, u32[]{:S(2)}) collective-permute-start(bf16[512,640]{1,0:T(8,128)(2,1)} %collective-permute-done.9.refs_4_), channel_id=1, source_target_pairs={{0,1},{1,0},{2,3},{3,2},{4,5},{5,4},{6,7},{7,6},{8,9},{9,8},{10,11... | collective-permute-start | bytes 1966088 | tf_op jit(solution)/shard_map/ppermute | solution.py:464
  54.6 18.8 %collective-permute-start.12 = (bf16[512,640]{1,0:T(8,128)(2,1)}, bf16[512,640]{1,0:T(8,128)(2,1)}, u32[]{:S(2)}, u32[]{:S(2)}) collective-permute-start(bf16[512,640]{1,0:T(8,128)(2,1)} %collective-permute-done.9.refs_4_), channel_id=1, source_target_pairs={{0,4},{1,5},{4,6},{5,7},{6,2},{7,3},{2,0},{3,1},{8,12},{9,13},{12,... | collective-permute-start | bytes 1966088 | tf_op jit(solution)/shard_map/ppermute | solution.py:460
  61.6 18.8 %collective-permute-start.16 = (bf16[640,640]{1,0:T(8,128)(2,1)}, bf16[640,640]{1,0:T(8,128)(2,1)}, u32[]{:S(2)}, u32[]{:S(2)}) collective-permute-start(bf16[640,640]{1,0:T(8,128)(2,1)} %get-tuple-element.94), channel_id=1, source_target_pairs={{0,16},{8,24},{16,0},{24,8},{1,17},{9,25},{17,1},{25,9},{2,18},{10... | collective-permute-start | bytes 2457608 | tf_op jit(solution)/shard_map/ppermute | solution.py:39
  64.9 9.0 %copy-start.10 = (bf16[640,640]{1,0:T(8,128)(2,1)S(1)}, bf16[640,640]{1,0:T(8,128)(2,1)}, u32[]{:S(2)}) copy-start(bf16[640,640]{1,0:T(8,128)(2,1)} %get-tuple-element.93) | copy-start | bytes 2457604
  73.3 9.3 %collective-permute-start.14 = (bf16[512,640]{1,0:T(8,128)(2,1)}, bf16[512,640]{1,0:T(8,128)(2,1)S(1)}, u32[]{:S(2)}, u32[]{:S(2)}) collective-permute-start(bf16[512,640]{1,0:T(8,128)(2,1)} %collective-permute-done.6.refs_0_), channel_id=1, source_target_pairs={{0,1},{1,0},{2,3},{3,2},{4,5},{5,4},{6,7},{7,6},{8,9},{9,8},{10,11... | collective-permute-start | bytes 1966088 | tf_op jit(solution)/shard_map/ppermute | solution.py:464
  73.4 10.7 %collective-permute-start.15 = (bf16[512,640]{1,0:T(8,128)(2,1)}, bf16[512,640]{1,0:T(8,128)(2,1)S(1)}, u32[]{:S(2)}, u32[]{:S(2)}) collective-permute-start(bf16[512,640]{1,0:T(8,128)(2,1)} %collective-permute-done.12.refs_2_), channel_id=1, source_target_pairs={{0,1},{1,0},{2,3},{3,2},{4,5},{5,4},{6,7},{7,6},{8,9},{9,8},{10,11... | collective-permute-start | bytes 1966088 | tf_op jit(solution)/shard_map/ppermute | solution.py:464
  73.9 34.6 %collective-permute-start.17 = (bf16[640,640]{1,0:T(8,128)(2,1)S(1)}, bf16[640,640]{1,0:T(8,128)(2,1)}, u32[]{:S(2)}, u32[]{:S(2)}) collective-permute-start(bf16[640,640]{1,0:T(8,128)(2,1)S(1)} %copy-done.10), channel_id=1, source_target_pairs={{0,8},{8,0},{16,24},{24,16},{1,9},{9,1},{17,25},{25,17},{2,10},{10... | collective-permute-start | bytes 2457608 | tf_op jit(solution)/shard_map/ppermute | solution.py:39
  75.4 33.1 %collective-permute-start.13 = (bf16[512,640]{1,0:T(8,128)(2,1)}, bf16[512,640]{1,0:T(8,128)(2,1)S(1)}, u32[]{:S(2)}, u32[]{:S(2)}) collective-permute-start(bf16[512,640]{1,0:T(8,128)(2,1)} %collective-permute-done.12.refs_2_), channel_id=1, source_target_pairs={{0,4},{1,5},{4,6},{5,7},{6,2},{7,3},{2,0},{3,1},{8,12},{9,13},{12,... | collective-permute-start | bytes 1966088 | tf_op jit(solution)/shard_map/ppermute | solution.py:460
  80.4 28.2 %collective-permute-start.7 = (bf16[512,640]{1,0:T(8,128)(2,1)}, bf16[512,640]{1,0:T(8,128)(2,1)S(1)}, u32[]{:S(2)}, u32[]{:S(2)}) collective-permute-start(bf16[512,640]{1,0:T(8,128)(2,1)} %collective-permute-done.6.refs_0_), channel_id=1, source_target_pairs={{0,4},{1,5},{4,6},{5,7},{6,2},{7,3},{2,0},{3,1},{8,12},{9,13},{12,... | collective-permute-start | bytes 1966088 | tf_op jit(solution)/shard_map/ppermute | solution.py:460
  82.6 16.5 %copy-start.13 = (bf16[512,640]{1,0:T(8,128)(2,1)}, bf16[512,640]{1,0:T(8,128)(2,1)S(1)}, u32[]{:S(2)}) copy-start(bf16[512,640]{1,0:T(8,128)(2,1)S(1)} %collective-permute-done.14.refs_1_) | copy-start | bytes 1966084
  82.6 29.2 %collective-permute-start.21 = (bf16[640,640]{1,0:T(8,128)(2,1)}, bf16[640,640]{1,0:T(8,128)(2,1)}, u32[]{:S(2)}, u32[]{:S(2)}) collective-permute-start(bf16[640,640]{1,0:T(8,128)(2,1)} %get-tuple-element.94), channel_id=1, source_target_pairs={{0,8},{8,0},{16,24},{24,16},{1,9},{9,1},{17,25},{25,17},{2,10},{10... | collective-permute-start | bytes 2457608 | tf_op jit(solution)/shard_map/ppermute | solution.py:39
  84.1 15.0 %copy-start.14 = (bf16[512,640]{1,0:T(8,128)(2,1)}, bf16[512,640]{1,0:T(8,128)(2,1)S(1)}, u32[]{:S(2)}) copy-start(bf16[512,640]{1,0:T(8,128)(2,1)S(1)} %collective-permute-done.15.refs_3_) | copy-start | bytes 1966084
  84.1 28.2 %collective-permute-start.23 = (bf16[640,640]{1,0:T(8,128)(2,1)S(1)}, bf16[640,640]{1,0:T(8,128)(2,1)}, u32[]{:S(2)}, u32[]{:S(2)}) collective-permute-start(bf16[640,640]{1,0:T(8,128)(2,1)S(1)} %copy-done.10), channel_id=1, source_target_pairs={{0,16},{8,24},{16,0},{24,8},{1,17},{9,25},{17,1},{25,9},{2,18},{10... | collective-permute-start | bytes 2457608 | tf_op jit(solution)/shard_map/ppermute | solution.py:39
  108.5 6.5 %copy-start.11 = (bf16[512,640]{1,0:T(8,128)(2,1)}, bf16[512,640]{1,0:T(8,128)(2,1)S(1)}, u32[]{:S(2)}) copy-start(bf16[512,640]{1,0:T(8,128)(2,1)S(1)} %collective-permute-done.13.refs_2_) | copy-start | bytes 1966084
  108.5 6.5 %collective-permute-start.18 = (bf16[512,640]{1,0:T(8,128)(2,1)S(1)}, bf16[512,640]{1,0:T(8,128)(2,1)S(1)}, u32[]{:S(2)}, u32[]{:S(2)}) collective-permute-start(bf16[512,640]{1,0:T(8,128)(2,1)S(1)} %collective-permute-done.13.refs_2_), channel_id=1, source_target_pairs={{0,1},{1,0},{2,3},{3,2},{4,5},{5,4},{6,7},{7,6},{8,9},{9,8},{10,11... | collective-permute-start | bytes 1966088 | tf_op jit(solution)/shard_map/ppermute | solution.py:464
  108.6 6.5 %copy-start.12 = (bf16[512,640]{1,0:T(8,128)(2,1)}, bf16[512,640]{1,0:T(8,128)(2,1)S(1)}, u32[]{:S(2)}) copy-start(bf16[512,640]{1,0:T(8,128)(2,1)S(1)} %collective-permute-done.7.refs_0_) | copy-start | bytes 1966084
  108.6 6.4 %collective-permute-start.11 = (bf16[512,640]{1,0:T(8,128)(2,1)S(1)}, bf16[512,640]{1,0:T(8,128)(2,1)S(1)}, u32[]{:S(2)}, u32[]{:S(2)}) collective-permute-start(bf16[512,640]{1,0:T(8,128)(2,1)S(1)} %collective-permute-done.7.refs_0_), channel_id=1, source_target_pairs={{0,1},{1,0},{2,3},{3,2},{4,5},{5,4},{6,7},{7,6},{8,9},{9,8},{10,11... | collective-permute-start | bytes 1966088 | tf_op jit(solution)/shard_map/ppermute | solution.py:464
  111.8 32.5 %collective-permute-start.22 = (bf16[640,640]{1,0:T(8,128)(2,1)}, bf16[640,640]{1,0:T(8,128)(2,1)}, u32[]{:S(2)}, u32[]{:S(2)}) collective-permute-start(bf16[640,640]{1,0:T(8,128)(2,1)} %collective-permute-done.21.refs_0_), channel_id=1, source_target_pairs={{0,16},{8,24},{16,0},{24,8},{1,17},{9,25},{17,1},{25,9},{2,18},{10... | collective-permute-start | bytes 2457608 | tf_op jit(solution)/shard_map/ppermute | solution.py:39
  112.4 32.6 %collective-permute-start.24 = (bf16[640,640]{1,0:T(8,128)(2,1)}, bf16[640,640]{1,0:T(8,128)(2,1)}, u32[]{:S(2)}, u32[]{:S(2)}) collective-permute-start(bf16[640,640]{1,0:T(8,128)(2,1)} %collective-permute-done.23.refs_3_), channel_id=1, source_target_pairs={{0,8},{8,0},{16,24},{24,16},{1,9},{9,1},{17,25},{25,17},{2,10},{10... | collective-permute-start | bytes 2457608 | tf_op jit(solution)/shard_map/ppermute | solution.py:39
  130.7 26.7 %collective-permute-start.19 = (bf16[640,640]{1,0:T(8,128)(2,1)}, bf16[640,640]{1,0:T(8,128)(2,1)}, u32[]{:S(2)}, u32[]{:S(2)}) collective-permute-start(bf16[640,640]{1,0:T(8,128)(2,1)} %get-tuple-element.67), channel_id=1, source_target_pairs={{0,8},{8,0},{16,24},{24,16},{1,9},{9,1},{17,25},{25,17},{2,10},{10... | collective-permute-start | bytes 2457608 | tf_op jit(solution)/shard_map/ppermute | solution.py:39
  131.4 22.8 %collective-permute-start.20 = (bf16[640,640]{1,0:T(8,128)(2,1)}, bf16[640,640]{1,0:T(8,128)(2,1)S(1)}, u32[]{:S(2)}, u32[]{:S(2)}) collective-permute-start(bf16[640,640]{1,0:T(8,128)(2,1)} %get-tuple-element.68), channel_id=1, source_target_pairs={{0,16},{8,24},{16,0},{24,8},{1,17},{9,25},{17,1},{25,9},{2,18},{10... | collective-permute-start | bytes 2457608 | tf_op jit(solution)/shard_map/ppermute | solution.py:39
  132.9 11.0 %copy-start.6 = (f32[1024,128]{1,0:T(8,128)S(1)}, f32[1024,128]{1,0:T(8,128)}, u32[]{:S(2)}) copy-start(f32[1024,128]{1,0:T(8,128)} %get-tuple-element.63) | copy-start | bytes 1572868
  142.4 34.3 %collective-permute-start.25 = (bf16[640,640]{1,0:T(8,128)(2,1)}, bf16[640,640]{1,0:T(8,128)(2,1)S(1)}, u32[]{:S(2)}, u32[]{:S(2)}) collective-permute-start(bf16[640,640]{1,0:T(8,128)(2,1)} %get-tuple-element.73), channel_id=1, source_target_pairs={{0,8},{8,0},{16,24},{24,16},{1,9},{9,1},{17,25},{25,17},{2,10},{10... | collective-permute-start | bytes 2457608 | tf_op jit(solution)/shard_map/ppermute | solution.py:39
  144.4 32.3 %collective-permute-start.26 = (bf16[640,640]{1,0:T(8,128)(2,1)}, bf16[640,640]{1,0:T(8,128)(2,1)S(1)}, u32[]{:S(2)}, u32[]{:S(2)}) collective-permute-start(bf16[640,640]{1,0:T(8,128)(2,1)} %get-tuple-element.74), channel_id=1, source_target_pairs={{0,16},{8,24},{16,0},{24,8},{1,17},{9,25},{17,1},{25,9},{2,18},{10... | collective-permute-start | bytes 2457608 | tf_op jit(solution)/shard_map/ppermute | solution.py:39
  144.9 12.5 %copy-start.8 = (f32[640,640]{1,0:T(8,128)S(1)}, f32[640,640]{1,0:T(8,128)}, u32[]{:S(2)}) copy-start(f32[640,640]{1,0:T(8,128)} %get-tuple-element.70) | copy-start | bytes 4915204
  154.2 7.0 %copy-start.2 = (bf16[1024,640]{1,0:T(8,128)(2,1)S(1)}, bf16[1024,640]{1,0:T(8,128)(2,1)}, u32[]{:S(2)}) copy-start(bf16[1024,640]{1,0:T(8,128)(2,1)} %sample.5) | copy-start | bytes 3932164
  154.2 7.0 %copy-start.4 = (bf16[1024,640]{1,0:T(8,128)(2,1)S(1)}, bf16[1024,640]{1,0:T(8,128)(2,1)}, u32[]{:S(2)}) copy-start(bf16[1024,640]{1,0:T(8,128)(2,1)} %copy-done.3) | copy-start | bytes 3932164
  154.2 7.0 %copy-start.5 = (f32[1024,640]{1,0:T(8,128)S(1)}, f32[1024,640]{1,0:T(8,128)}, u32[]{:S(2)}) copy-start(f32[1024,640]{1,0:T(8,128)} %get-tuple-element.83) | copy-start | bytes 7864324
  154.2 7.0 %copy-start.18 = (bf16[1024,640]{1,0:T(8,128)(2,1)S(1)}, bf16[1024,640]{1,0:T(8,128)(2,1)}, u32[]{:S(2)}) copy-start(bf16[1024,640]{1,0:T(8,128)(2,1)} %param.11) | copy-start | bytes 3932164
  156.9 40.9 %collective-permute-start.31 = (bf16[640,640]{1,0:T(8,128)(2,1)}, bf16[640,640]{1,0:T(8,128)(2,1)S(1)}, u32[]{:S(2)}, u32[]{:S(2)}) collective-permute-start(bf16[640,640]{1,0:T(8,128)(2,1)} %add_convert_fusion), channel_id=1, source_target_pairs={{0,8},{8,0},{16,24},{24,16},{1,9},{9,1},{17,25},{25,17},{2,10},{10... | collective-permute-start | bytes 2457608 | tf_op jit(solution)/shard_map/ppermute | solution.py:39
  159.7 38.1 %collective-permute-start.30 = (bf16[640,640]{1,0:T(8,128)(2,1)}, bf16[640,640]{1,0:T(8,128)(2,1)S(1)}, u32[]{:S(2)}, u32[]{:S(2)}) collective-permute-start(bf16[640,640]{1,0:T(8,128)(2,1)} %add_convert_fusion.1), channel_id=1, source_target_pairs={{0,16},{8,24},{16,0},{24,8},{1,17},{9,25},{17,1},{25,9},{2,18},{10... | collective-permute-start | bytes 2457608 | tf_op jit(solution)/shard_map/ppermute | solution.py:39
  176.6 16.7 %copy-start.17 = (f32[1,640]{1,0:T(1,128)S(1)}, f32[1,640]{1,0:T(1,128)}, u32[]{:S(2)}) copy-start(f32[1,640]{1,0:T(1,128)} %param.17) | copy-start | bytes 7684
  176.6 5.4 %collective-permute-start.27 = (f32[1,1]{1,0:T(1,128)}, f32[1,1]{1,0:T(1,128)}, u32[]{:S(2)}, u32[]{:S(2)}) collective-permute-start(f32[1,1]{1,0:T(1,128)} %bitcast.18), channel_id=1, source_target_pairs={{0,1},{1,0},{2,3},{3,2},{4,5},{5,4},{6,7},{7,6},{8,9},{9,8},{10,11... | collective-permute-start | bytes 20 | tf_op jit(solution)/shard_map/ppermute | solution.py:594
  183.3 3.7 %collective-permute-start.28 = (f32[1,1]{1,0:T(1,128)}, f32[1,1]{1,0:T(1,128)}, u32[]{:S(2)}, u32[]{:S(2)}) collective-permute-start(f32[1,1]{1,0:T(1,128)} %add.101), channel_id=1, source_target_pairs={{0,2},{1,3},{2,0},{3,1},{4,6},{5,7},{6,4},{7,5},{8,10},{9,11},{10,... | collective-permute-start | bytes 20 | tf_op jit(solution)/shard_map/ppermute | solution.py:594
  187.6 4.6 %collective-permute-start.29 = (f32[1,1]{1,0:T(1,128)}, f32[1,1]{1,0:T(1,128)}, u32[]{:S(2)}, u32[]{:S(2)}) collective-permute-start(f32[1,1]{1,0:T(1,128)} %add.102), channel_id=1, source_target_pairs={{0,4},{1,5},{2,6},{3,7},{4,0},{5,1},{6,2},{7,3},{8,12},{9,13},{10,... | collective-permute-start | bytes 20 | tf_op jit(solution)/shard_map/ppermute | solution.py:594
  193.4 4.4 %copy-start = (f32[640,640]{1,0:T(8,128)S(1)}, f32[640,640]{1,0:T(8,128)}, u32[]{:S(2)}) copy-start(f32[640,640]{1,0:T(8,128)} %get-tuple-element.85.refs_0_) | copy-start | bytes 4915204
  (3 other events, 6.4 us)
